TPU v7x, 512 devices: a whole 4x8x8 slice. The times are simulated.
512 devices in a mesh: dom: 128 (over x, y, z_hi), feat: 4 (over z_lo, core).
Axes of the slice: x: 4, y: 8, z: 8 (z_hi: 4, z_lo: 2; z = z_hi * 2 + z_lo), core: 2. Of those that a mesh axis runs over, the one named last changes fastest.
Arguments:
- node_state: bfloat16 [131072, 512], P('dom', 'feat'), may hold values from -6 to 6
- w_dst: bfloat16 [2, 512, 512], P(None, None, 'feat'), may hold values from -0.25 to 0.25
- w_src: bfloat16 [2, 512, 512], P(None, None, 'feat'), may hold values from -0.25 to 0.25
- w_msg: bfloat16 [2, 512, 512], replicated, may hold values from -0.25 to 0.25
- w_node_in: bfloat16 [2, 1024, 512], P(None, None, 'feat'), may hold values from -0.1875 to 0.1875
- w_node_out: bfloat16 [2, 512, 512], P(None, None, 'feat'), may hold values from -0.25 to 0.25
- msg_vectors: float32 [2, 2, 512], replicated, may hold values from -3 to 3
- msg_gain: float32 [2, 512], replicated, may hold values from 0.1 to 1.9
- node_vectors: float32 [2, 4, 512], P(None, None, 'feat'), may hold values from -3 to 3
- node_gain: float32 [2, 512], P(None, 'feat'), may hold values from 0.1 to 1.9
- nbr_blocks: int32 [1024, 6], P('dom'), may hold values from 0 to 1023, as said below
- edge_count: int32 [1024, 6], P('dom'), may hold values from 1 to 128, as said below
- edge_src: int32 [1024, 6, 128], P('dom'), may hold values from 0 to 127
- edge_dst: int32 [1024, 6, 128], P('dom'), may hold values from 0 to 127
Outputs:
- new_state: bfloat16 [131072, 512], P('dom', 'feat')
Inputs may be any that keep to these rules, and one draw needn't show every extreme that they name: `nbr_blocks`: each row names 6 different blocks within 8 blocks of its own block b; its first entry is b. `edge_count`: the first entry of every row is 128.
All inputs are finite; a program needn't handle non-finite values.
Results may differ from a plain program's by a relative error of at most 0.017.
Values may be sent and summed in bfloat16 or wider, within the bound.
No kernel may reach another device: no remote copies, remote signals or barrier semaphores. Data moves between devices by JAX's collectives and lax.ppermute only.
A program may use at most 64 MiB of HBM per device.

v0:
```python
import jax
import jax.numpy as jnp
from jax import lax
from jax.sharding import PartitionSpec as P

LAYERS = 2


epsilon = 1e-05


def with_halo(block, sides, width):
    for axis, dim in sides:
        count = lax.axis_size(axis)
        forward = [(i, i + 1) for i in range(count - 1)]
        backward = [(target, source) for source, target in forward]
        low = lax.ppermute(
            lax.slice_in_dim(block, block.shape[dim] - width, None, axis=dim), axis, forward
        )
        high = lax.ppermute(lax.slice_in_dim(block, 0, width, axis=dim), axis, backward)
        block = jnp.concatenate([low, block, high], axis=dim)
    return block


def normalize(values, gain_vec, shift_vec):
    centre = jnp.mean(values, axis=-1, keepdims=True)
    shifted = values - centre
    spread = jnp.mean(shifted * shifted, axis=-1, keepdims=True)
    return shifted * lax.rsqrt(spread + epsilon) * gain_vec + shift_vec


def collect_rows(receivers, live_flags, positions, values):
    one_hot = ((receivers[:, None, :] == positions[None, :, None]) & live_flags[:, None, :]).astype(
        jnp.bfloat16
    )
    upper = values.astype(jnp.bfloat16)
    lower = (values - upper.astype(jnp.float32)).astype(jnp.bfloat16)
    summed = jnp.einsum("bne,bed->bnd", one_hot, upper, preferred_element_type=jnp.float32)
    return summed + jnp.einsum("bne,bed->bnd", one_hot, lower, preferred_element_type=jnp.float32)


def per_device(
    node_state,
    w_dst,
    w_src,
    w_msg,
    w_node_in,
    w_node_out,
    msg_vectors,
    msg_gain,
    node_vectors,
    node_gain,
    nbr_blocks,
    edge_count,
    edge_src,
    edge_dst,
):
    row_count, panel_width = node_state.shape
    full_width = w_msg.shape[1]
    block_count = nbr_blocks.shape[0]
    block_len = row_count // block_count
    slot_count = edge_src.shape[1] * edge_src.shape[2]
    part_slots = slot_count // lax.axis_size("feat")
    feat_rank = lax.axis_index("feat")
    first_row = lax.axis_index("dom") * row_count
    src_rows = (
        (nbr_blocks[:, :, None] * block_len + edge_src).reshape(block_count, slot_count)
        - first_row
        + row_count
    )
    dst_local = edge_dst.reshape(block_count, slot_count)
    dst_rows = dst_local + (jnp.arange(block_count, dtype=jnp.int32) * block_len)[:, None]
    edge_live = (
        jnp.arange(edge_src.shape[2], dtype=jnp.int32)[None, None, :] < edge_count[:, :, None]
    ).reshape(block_count, slot_count)
    positions = jnp.arange(block_len, dtype=jnp.int32)
    dst_part = lax.dynamic_slice_in_dim(dst_local, feat_rank * part_slots, part_slots, 1)
    live_part = lax.dynamic_slice_in_dim(edge_live, feat_rank * part_slots, part_slots, 1)
    latent = node_state
    for layer_index in range(LAYERS):
        weight_dst = w_dst[layer_index]
        weight_src = w_src[layer_index]
        weight_in = w_node_in[layer_index]
        weight_out = w_node_out[layer_index]
        gathered_rows = lax.all_gather(latent, "feat", axis=1, tiled=True)
        banded = with_halo(gathered_rows, (("dom", 0),), row_count)
        dst_terms = (
            jnp.dot(gathered_rows, weight_dst, preferred_element_type=jnp.float32)
            + node_vectors[layer_index, 0]
        ).astype(jnp.bfloat16)
        src_terms = jnp.dot(banded, weight_src, preferred_element_type=jnp.float32).astype(
            jnp.bfloat16
        )
        direct = jnp.dot(gathered_rows, weight_in[:full_width], preferred_element_type=jnp.float32)
        edge_hidden = jax.nn.relu(
            dst_terms[dst_rows].astype(jnp.float32) + src_terms[src_rows].astype(jnp.float32)
        ).astype(jnp.bfloat16)
        mixed_here = (
            jnp.einsum(
                "bed,df->bef",
                lax.all_to_all(edge_hidden, "feat", split_axis=1, concat_axis=2, tiled=True),
                w_msg[layer_index],
                preferred_element_type=jnp.float32,
            )
            + msg_vectors[layer_index, 0]
        )
        messages = normalize(mixed_here, msg_gain[layer_index], msg_vectors[layer_index, 1])
        partial_value = collect_rows(dst_part, live_part, positions, messages).reshape(
            row_count, full_width
        )
        aggregate = lax.psum_scatter(
            partial_value.astype(jnp.bfloat16), "feat", scatter_dimension=1, tiled=True
        )
        shard_piece = lax.all_gather(aggregate, "feat", axis=1, tiled=True)
        rows_in = lax.dynamic_slice_in_dim(weight_in, full_width, shard_piece.shape[1], 0)
        pre_act = direct + jnp.dot(shard_piece, rows_in, preferred_element_type=jnp.float32)
        inner_act = jax.nn.relu(pre_act + node_vectors[layer_index, 1]).astype(jnp.bfloat16)
        node_output = (
            jnp.dot(
                lax.all_gather(inner_act, "feat", axis=1, tiled=True),
                weight_out,
                preferred_element_type=jnp.float32,
            )
            + node_vectors[layer_index, 2]
        )
        totals, squares = lax.psum(
            (jnp.sum(node_output, axis=-1), jnp.sum(node_output * node_output, axis=-1)), "feat"
        )
        centre = totals / full_width
        spread = squares / full_width - centre * centre
        normed_node = (node_output - centre[:, None]) * lax.rsqrt(spread + epsilon)[
            :, None
        ] * node_gain[layer_index] + node_vectors[layer_index, 3]
        latent = (latent.astype(jnp.float32) + normed_node).astype(jnp.bfloat16)
    return latent


def solution(mesh):
    placed = (
        P("dom", "feat"),
        P(None, None, "feat"),
        P(None, None, "feat"),
        P(),
        P(None, None, "feat"),
        P(None, None, "feat"),
        P(),
        P(),
        P(None, None, "feat"),
        P(None, "feat"),
        P("dom", None),
        P("dom", None),
        P("dom", None, None),
        P("dom", None, None),
    )
    return jax.shard_map(
        per_device, mesh=mesh, in_specs=placed, out_specs=P("dom", "feat"), check_vma=False
    )
```

profile of v0, /device:TPU:6, one launch (start us, length us, event | category | flops | bytes accessed | tf_op | source)
XLA Modules:
  0.0 501.4 jit_solution(13476057632991830729)
XLA Ops:
  8.9 31.4 %all-gather.7.cloned.1.call-done = bf16[1024,512]{1,0:T(8,128)(2,1)} async-done(((bf16[1024,128]{1,0:T(8,128)(2,1)}), bf16[1024,512]{1,0:T(8,128)(2,1)}) %all-gather.7.cloned.1.call-update) | async-done | bytes 1048592 | tf_op jit(solution)/shard_map/all_gather | solution.py:85
  40.3 9.1 %collective-permute-start.1 = (bf16[1024,512]{1,0:T(8,128)(2,1)}, bf16[1024,512]{1,0:T(8,128)(2,1)}, u32[]{:S(2)}, u32[]{:S(2)}) collective-permute-start(bf16[1024,512]{1,0:T(8,128)(2,1)} %all-gather.7.cloned.1.call-done), channel_id=1, source_target_pairs={{4,0},{8,4},{12,8},{16,12},{20,16},{24,20},{28,24},{32,28},{36,32}... | collective-permute-start | bytes 3145736 | tf_op jit(solution)/shard_map/ppermute | solution.py:20
  54.7 18.1 %gather_fusion = bf16[6144,128]{1,0:T(8,128)(2,1)S(1)} fusion(bf16[1024,128]{1,0:T(8,128)(2,1)S(1)} %fusion.34, s32[6144]{0:T(1024)S(1)} %broadcast_clamp_fusion.1), kind=kCustom, calls=%fused_computation | custom fusion | bytes 3170304 | tf_op jit(solution)/shard_map/gather | solution.py:96
  72.8 21.3 %collective-permute-done.1 = bf16[1024,512]{1,0:T(8,128)(2,1)} collective-permute-done((bf16[1024,512]{1,0:T(8,128)(2,1)}, bf16[1024,512]{1,0:T(8,128)(2,1)}, u32[]{:S(2)}, u32[]{:S(2)}) %collective-permute-start.1) | collective-permute-done | bytes 1048608 | tf_op jit(solution)/shard_map/ppermute | solution.py:20
  94.2 9.4 %collective-permute-done = bf16[1024,512]{1,0:T(8,128)(2,1)} collective-permute-done((bf16[1024,512]{1,0:T(8,128)(2,1)}, bf16[1024,512]{1,0:T(8,128)(2,1)}, u32[]{:S(2)}, u32[]{:S(2)}) %collective-permute-start) | collective-permute-done | bytes 1048608 | tf_op jit(solution)/shard_map/ppermute | solution.py:17
  103.6 2.5 convolution_convert_fusion.1
  106.1 22.2 %gather_fusion.1 = bf16[6144,128]{1,0:T(8,128)(2,1)} fusion(bf16[3072,128]{1,0:T(8,128)(2,1)S(1)} %convolution_convert_fusion.1, s32[6144]{0:T(1024)S(1)} %broadcast_clamp_fusion), kind=kCustom, calls=%fused_computation.1 | custom fusion | bytes 3170304 | tf_op jit(solution)/shard_map/gather | solution.py:96
  130.3 2.2 copy.28
  132.5 3.6 all-to-all-start
  137.2 18.8 %all-to-all-done = bf16[8,768,128]{2,0,1:T(8,128)(2,1)S(1)} async-done(((bf16[8,768,128]{2,0,1:T(8,128)(2,1)}), bf16[8,768,128]{2,0,1:T(8,128)(2,1)S(1)}, u32[]{:S(2)}, u32[]{:S(2)}) %all-to-all-start) | async-done | bytes 1572896 | tf_op jit(solution)/shard_map/all_to_all | solution.py:101
  158.0 2.1 add_reduce_fusion.1
  162.5 2.3 add_convert_fusion.1
  166.2 18.7 %reduce-scatter.7.cloned.1.call-done = bf16[128,1024]{1,0:T(8,128)(2,1)} async-done(((bf16[512,1024]{1,0:T(8,128)(2,1)}), bf16[128,1024]{1,0:T(8,128)(2,1)}) %reduce-scatter.7.cloned.1.call-update) | async-done | bytes 262160
  187.2 26.7 %all-gather.9.cloned.1.call-done = bf16[1024,512]{1,0:T(8,128)(2,1)} async-done(((bf16[1024,128]{1,0:T(8,128)(2,1)}), bf16[1024,512]{1,0:T(8,128)(2,1)}) %all-gather.9.cloned.1.call-update) | async-done | bytes 1048592 | tf_op jit(solution)/shard_map/all_gather | solution.py:114
  214.0 2.4 fusion.33
  216.6 27.5 %all-gather.11.cloned.1.call-done = bf16[1024,512]{1,0:T(8,128)(2,1)} async-done(((bf16[1024,128]{1,0:T(8,128)(2,1)}), bf16[1024,512]{1,0:T(8,128)(2,1)}) %all-gather.11.cloned.1.call-update) | async-done | bytes 1048592 | tf_op jit(solution)/shard_map/all_gather | solution.py:120
  245.8 7.3 %all-reduce.1 = (f32[1024]{0:T(1024)S(1)}, f32[1024]{0:T(1024)S(1)}) all-reduce(f32[1024]{0:T(1024)S(1)} %get-tuple-element.8, f32[1024]{0:T(1024)S(1)} %get-tuple-element.7), channel_id=1, replica_groups=mesh['dom'=128,'feat'=4] {'feat'}, use_global_device_ids=true, to_apply=%region_6.7 | all-reduce | flops 2048 | bytes 16384 | tf_op jit(solution)/shard_map/psum | solution.py:126
  254.1 26.7 %all-gather.13.cloned.1.call-done = bf16[1024,512]{0,1:T(8,128)(2,1)} async-done(((bf16[1024,128]{0,1:T(8,128)(2,1)}), bf16[1024,512]{0,1:T(8,128)(2,1)}) %all-gather.13.cloned.1.call-update) | async-done | bytes 1048592 | tf_op jit(solution)/shard_map/all_gather | solution.py:85
  280.9 8.6 %collective-permute-start.3 = (bf16[1024,512]{0,1:T(8,128)(2,1)}, bf16[1024,512]{0,1:T(8,128)(2,1)}, u32[]{:S(2)}, u32[]{:S(2)}) collective-permute-start(bf16[1024,512]{0,1:T(8,128)(2,1)} %all-gather.13.cloned.1.call-done), channel_id=1, source_target_pairs={{4,0},{8,4},{12,8},{16,12},{20,16},{24,20},{28,24},{32,28},{36,32}... | collective-permute-start | bytes 3145736 | tf_op jit(solution)/shard_map/ppermute | solution.py:20
  293.3 18.1 %gather_fusion.2 = bf16[6144,128]{1,0:T(8,128)(2,1)S(1)} fusion(bf16[1024,128]{1,0:T(8,128)(2,1)S(1)} %fusion.35, s32[6144]{0:T(1024)S(1)} %broadcast_clamp_fusion.1), kind=kCustom, calls=%fused_computation.2 | custom fusion | bytes 3170304 | tf_op jit(solution)/shard_map/gather | solution.py:96
  311.4 23.6 %collective-permute-done.3 = bf16[1024,512]{0,1:T(8,128)(2,1)} collective-permute-done((bf16[1024,512]{0,1:T(8,128)(2,1)}, bf16[1024,512]{0,1:T(8,128)(2,1)}, u32[]{:S(2)}, u32[]{:S(2)}) %collective-permute-start.3) | collective-permute-done | bytes 1048608 | tf_op jit(solution)/shard_map/ppermute | solution.py:20
  335.0 8.7 %collective-permute-done.2 = bf16[1024,512]{0,1:T(8,128)(2,1)} collective-permute-done((bf16[1024,512]{0,1:T(8,128)(2,1)}, bf16[1024,512]{0,1:T(8,128)(2,1)}, u32[]{:S(2)}, u32[]{:S(2)}) %collective-permute-start.2) | collective-permute-done | bytes 1048608 | tf_op jit(solution)/shard_map/ppermute | solution.py:17
  343.8 2.6 convolution_convert_fusion
  346.3 22.2 %gather_fusion.3 = bf16[6144,128]{1,0:T(8,128)(2,1)} fusion(bf16[3072,128]{1,0:T(8,128)(2,1)S(1)} %convolution_convert_fusion, s32[6144]{0:T(1024)S(1)} %broadcast_clamp_fusion), kind=kCustom, calls=%fused_computation.3 | custom fusion | bytes 3170304 | tf_op jit(solution)/shard_map/gather | solution.py:96
  371.5 22.5 %all_to_all.36 = bf16[8,768,128]{2,0,1:T(8,128)(2,1)S(1)} all-to-all(bf16[8,768,128]{2,0,1:T(8,128)(2,1)S(1)} %copy.31), channel_id=1, replica_groups=mesh['dom'=128,'feat'=4] {'feat'}, dimensions={1} | all-to-all | bytes 3145728 | tf_op jit(solution)/shard_map/all_to_all | solution.py:101
  397.2 2.6 add_reduce_fusion
  402.2 2.3 add_convert_fusion
  406.0 19.5 %reduce-scatter.9.cloned.1.call-done = bf16[128,1024]{1,0:T(8,128)(2,1)} async-done(((bf16[512,1024]{1,0:T(8,128)(2,1)}), bf16[128,1024]{1,0:T(8,128)(2,1)}) %reduce-scatter.9.cloned.1.call-update) | async-done | bytes 262160
  427.9 26.3 %all-gather.15.cloned.1.call-done = bf16[1024,512]{1,0:T(8,128)(2,1)} async-done(((bf16[1024,128]{1,0:T(8,128)(2,1)}), bf16[1024,512]{1,0:T(8,128)(2,1)}) %all-gather.15.cloned.1.call-update) | async-done | bytes 1048592 | tf_op jit(solution)/shard_map/all_gather | solution.py:114
  454.2 2.4 fusion.32
  456.7 27.7 %all-gather.17.cloned.1.call-done = bf16[1024,512]{1,0:T(8,128)(2,1)} async-done(((bf16[1024,128]{1,0:T(8,128)(2,1)}), bf16[1024,512]{1,0:T(8,128)(2,1)}) %all-gather.17.cloned.1.call-update) | async-done | bytes 1048592 | tf_op jit(solution)/shard_map/all_gather | solution.py:120
  486.1 7.3 %all-reduce = (f32[1024]{0:T(1024)S(1)}, f32[1024]{0:T(1024)S(1)}) all-reduce(f32[1024]{0:T(1024)S(1)} %get-tuple-element.6, f32[1024]{0:T(1024)S(1)} %get-tuple-element.5), channel_id=1, replica_groups=mesh['dom'=128,'feat'=4] {'feat'}, use_global_device_ids=true, to_apply=%region_13.14 | all-reduce | flops 2048 | bytes 16384 | tf_op jit(solution)/shard_map/psum | solution.py:126
  (96 shorter events, 40.6 us)
Async XLA Ops:
  6.5 33.7 %all-gather.7.cloned.1.call-start = ((), (), s32[]{:S(2)}) async-start(), calls=%async_computation.4 | async-start | bytes 1310720 | tf_op jit(solution)/shard_map/all_gather | solution.py:85
  40.3 53.9 %collective-permute-start.1 = (bf16[1024,512]{1,0:T(8,128)(2,1)}, bf16[1024,512]{1,0:T(8,128)(2,1)}, u32[]{:S(2)}, u32[]{:S(2)}) collective-permute-start(bf16[1024,512]{1,0:T(8,128)(2,1)} %all-gather.7.cloned.1.call-done), channel_id=1, source_target_pairs={{4,0},{8,4},{12,8},{16,12},{20,16},{24,20},{28,24},{32,28},{36,32}... | collective-permute-start | bytes 3145736 | tf_op jit(solution)/shard_map/ppermute | solution.py:20
  49.4 54.2 %collective-permute-start = (bf16[1024,512]{1,0:T(8,128)(2,1)}, bf16[1024,512]{1,0:T(8,128)(2,1)}, u32[]{:S(2)}, u32[]{:S(2)}) collective-permute-start(bf16[1024,512]{1,0:T(8,128)(2,1)} %all-gather.7.cloned.1.call-done), channel_id=1, source_target_pairs={{0,4},{4,8},{8,12},{12,16},{16,20},{20,24},{24,28},{28,32},{32,36}... | collective-permute-start | bytes 3145736 | tf_op jit(solution)/shard_map/ppermute | solution.py:17
  54.7 48.9 %copy-start = (bf16[1024,512]{1,0:T(8,128)(2,1)S(1)}, bf16[1024,512]{1,0:T(8,128)(2,1)}, u32[]{:S(2)}) copy-start(bf16[1024,512]{1,0:T(8,128)(2,1)} %all-gather.7.cloned.1.call-done) | copy-start | bytes 3145732
  130.3 5.8 %copy-start.11 = (s32[8,6]{1,0:T(8,128)S(1)}, s32[8,6]{1,0:T(8,128)}, u32[]{:S(2)}) copy-start(s32[8,6]{1,0:T(8,128)} %param.25) | copy-start | bytes 580
  130.3 6.9 %copy-start.12 = (f32[2,512]{1,0:T(2,128)S(1)}, f32[2,512]{1,0:T(2,128)}, u32[]{:S(2)}) copy-start(f32[2,512]{1,0:T(2,128)} %param.21) | copy-start | bytes 12292
  130.3 6.9 %copy-start.10 = (f32[2,2,512]{2,1,0:T(2,128)S(1)}, f32[2,2,512]{2,1,0:T(2,128)}, u32[]{:S(2)}) copy-start(f32[2,2,512]{2,1,0:T(2,128)} %param.20) | copy-start | bytes 24580
  132.5 23.6 %all-to-all-start = ((bf16[8,768,128]{2,0,1:T(8,128)(2,1)}), bf16[8,768,128]{2,0,1:T(8,128)(2,1)S(1)}, u32[]{:S(2)}, u32[]{:S(2)}) async-start(bf16[8,768,128]{2,0,1:T(8,128)(2,1)} %copy.28), calls=%async_computation | async-start | bytes 3145728 | tf_op jit(solution)/shard_map/all_to_all | solution.py:101
  136.0 48.8 %reduce-scatter.7.cloned.1.call-start = ((), (), s32[]{:S(2)}) async-start(), calls=%async_computation.10 | async-start | bytes 1310720
  164.8 22.0 %copy-start.1 = (bf16[1024,512]{1,0:T(8,128)(2,1)S(1)}, bf16[1024,512]{1,0:T(8,128)(2,1)}, u32[]{:S(2)}) copy-start(bf16[1024,512]{1,0:T(8,128)(2,1)} %all-gather.7.cloned.1.call-done) | copy-start | bytes 3145732
  164.8 22.0 %copy-start.5 = (bf16[2,1024,128]{2,1,0:T(8,128)(2,1)S(1)}, bf16[2,1024,128]{2,1,0:T(8,128)(2,1)}, u32[]{:S(2)}) copy-start(bf16[2,1024,128]{2,1,0:T(8,128)(2,1)} %param.18) | copy-start | bytes 1572868
  166.2 50.2 %copy-start.4 = (bf16[1024,128]{1,0:T(8,128)(2,1)S(1)}, bf16[1024,128]{1,0:T(8,128)(2,1)}, u32[]{:S(2)}) copy-start(bf16[1024,128]{1,0:T(8,128)(2,1)} %param.14) | copy-start | bytes 786436
  166.2 50.4 %copy-start.13 = (f32[2,128]{1,0:T(2,128)S(1)}, f32[2,128]{1,0:T(2,128)}, u32[]{:S(2)}) copy-start(f32[2,128]{1,0:T(2,128)} %param.23) | copy-start | bytes 3076
  166.2 77.9 %copy-start.7 = (bf16[2,512,128]{2,1,0:T(8,128)(2,1)S(1)}, bf16[2,512,128]{2,1,0:T(8,128)(2,1)}, u32[]{:S(2)}) copy-start(bf16[2,512,128]{2,1,0:T(8,128)(2,1)} %param.19) | copy-start | bytes 786436
  166.2 47.8 %all-gather.9.cloned.1.call-start = ((), (), s32[]{:S(2)}) async-start(), calls=%async_computation.5 | async-start | bytes 1310720 | tf_op jit(solution)/shard_map/all_gather | solution.py:114
  186.7 57.3 %all-gather.11.cloned.1.call-start = ((), (), s32[]{:S(2)}) async-start(), calls=%async_computation.6 | async-start | bytes 1310720 | tf_op jit(solution)/shard_map/all_gather | solution.py:120
  187.2 104.3 %copy-start.9 = (bf16[2,512,128]{2,1,0:T(8,128)(2,1)S(1)}, bf16[2,512,128]{2,1,0:T(8,128)(2,1)}, u32[]{:S(2)}) copy-start(bf16[2,512,128]{2,1,0:T(8,128)(2,1)} %param.15) | copy-start | bytes 786436
  216.3 64.5 %all-gather.13.cloned.1.call-start = ((), (), s32[]{:S(2)}) async-start(), calls=%async_computation.7 | async-start | bytes 1310720 | tf_op jit(solution)/shard_map/all_gather | solution.py:85
  254.1 171.4 %reduce-scatter.9.cloned.1.call-start = ((), (), s32[]{:S(2)}) async-start(), calls=%async_computation.11 | async-start | bytes 1310720
  280.9 54.1 %collective-permute-start.3 = (bf16[1024,512]{0,1:T(8,128)(2,1)}, bf16[1024,512]{0,1:T(8,128)(2,1)}, u32[]{:S(2)}, u32[]{:S(2)}) collective-permute-start(bf16[1024,512]{0,1:T(8,128)(2,1)} %all-gather.13.cloned.1.call-done), channel_id=1, source_target_pairs={{4,0},{8,4},{12,8},{16,12},{20,16},{24,20},{28,24},{32,28},{36,32}... | collective-permute-start | bytes 3145736 | tf_op jit(solution)/shard_map/ppermute | solution.py:20
  289.4 54.3 %collective-permute-start.2 = (bf16[1024,512]{0,1:T(8,128)(2,1)}, bf16[1024,512]{0,1:T(8,128)(2,1)}, u32[]{:S(2)}, u32[]{:S(2)}) collective-permute-start(bf16[1024,512]{0,1:T(8,128)(2,1)} %all-gather.13.cloned.1.call-done), channel_id=1, source_target_pairs={{0,4},{4,8},{8,12},{12,16},{16,20},{20,24},{24,28},{28,32},{32,36}... | collective-permute-start | bytes 3145736 | tf_op jit(solution)/shard_map/ppermute | solution.py:17
  293.3 50.5 %copy-start.2 = (bf16[1024,512]{0,1:T(8,128)(2,1)S(1)}, bf16[1024,512]{0,1:T(8,128)(2,1)}, u32[]{:S(2)}) copy-start(bf16[1024,512]{0,1:T(8,128)(2,1)} %all-gather.13.cloned.1.call-done) | copy-start | bytes 3145732
  404.5 22.9 %copy-start.6 = (bf16[2,1024,128]{2,1,0:T(8,128)(2,1)S(1)}, bf16[2,1024,128]{2,1,0:T(8,128)(2,1)}, u32[]{:S(2)}) copy-start(bf16[2,1024,128]{2,1,0:T(8,128)(2,1)} %param.18) | copy-start | bytes 1572868
  405.9 78.5 %copy-start.8 = (bf16[2,512,128]{2,1,0:T(8,128)(2,1)S(1)}, bf16[2,512,128]{2,1,0:T(8,128)(2,1)}, u32[]{:S(2)}) copy-start(bf16[2,512,128]{2,1,0:T(8,128)(2,1)} %param.19) | copy-start | bytes 786436
  405.9 48.3 %all-gather.15.cloned.1.call-start = ((), (), s32[]{:S(2)}) async-start(), calls=%async_computation.8 | async-start | bytes 1310720 | tf_op jit(solution)/shard_map/all_gather | solution.py:114
  425.5 67.9 %copy-start.3 = (bf16[1024,128]{0,1:T(8,128)(2,1)S(1)}, bf16[1024,128]{0,1:T(8,128)(2,1)}, u32[]{:S(2)}) copy-start(bf16[1024,128]{0,1:T(8,128)(2,1)} %add_convert_fusion.3) | copy-start | bytes 786436
  427.4 57.0 %all-gather.17.cloned.1.call-start = ((), (), s32[]{:S(2)}) async-start(), calls=%async_computation.9 | async-start | bytes 1310720 | tf_op jit(solution)/shard_map/all_gather | solution.py:120
Sparse Core Ops, SparseCore 0:
  9.4 30.7 all-gather.6
  166.3 18.5 reduce-scatter.6
  187.2 26.7 all-gather.8
  216.5 27.5 all-gather.10
  254.2 26.5 all-gather.12
  406.0 19.4 reduce-scatter.8
  427.6 26.6 all-gather.14
  456.8 27.5 all-gather.16
where the time goes:
time: 502 us; the launch traced here: 501 us
  waiting for transfers between devices  287 us (57%)
  local copies, waits for them, and re-layouts  98.3 us (20%)
  blocking collectives  37.2 us (7%)
  matrix products  29.9 us (6%)
  starting transfers between devices  25.6 us (5%)
  between operations  13.9 us (3%)
  other arithmetic  9.11 us (2%)
    all_gather x2, waiting for transfers between devices, per_device(): gathered_rows = lax.all_gather(latent, 'feat', axis=1, tiled=True)  58.1 us
    all_gather x2, waiting for transfers between devices, per_device(): lax.all_gather(inner_act, 'feat', axis=1, tiled=True)  55.1 us
    all_gather x2, waiting for transfers between devices, per_device(): shard_piece = lax.all_gather(aggregate, 'feat', axis=1, tiled=True)  53.1 us
    ppermute x2, waiting for transfers between devices, with_halo(): lax.ppermute(lax.slice_in_dim(block, 0, width, axis=dim), axis, backward)  45 us
    gather x2, local copies, waits for them, and re-layouts, per_device(): src_terms[src_rows].astype(jnp.float32)  44.4 us
    unnamed x10, waiting for transfers between devices  39 us
    gather x2, local copies, waits for them, and re-layouts, per_device(): dst_terms[dst_rows].astype(jnp.float32)  36.2 us
    all_to_all x1, blocking collectives, per_device(): lax.all_to_all(edge_hidden, 'feat', split_axis=1, concat_axis=2, tiled=True)  22.5 us
  transfers between devices with their start and end apart: 13, of which 13 were waited for; matrix products, arithmetic and copies ran while one was open for 9% of the time, Pallas kernels for 0%

commit v1 on v0

v1 whole, which is shorter than its diff:
```python
import jax
import jax.numpy as jnp
from jax import lax
from jax.experimental import pallas as pl
from jax.experimental.pallas import tpu as pltpu
from jax.sharding import PartitionSpec as P

LAYERS = 2
EPSILON = 1e-05
BOTH = ("dom", "feat")
F32 = jnp.float32
BF16 = jnp.bfloat16
VECTOR_ROWS = 16


def dot(a, b):
    return jnp.dot(a, b, preferred_element_type=F32)


def exchange(value, mask):
    total = lax.axis_size(BOTH)
    return lax.ppermute(value, BOTH, [(i, i ^ mask) for i in range(total)])


def shifted(value, step):
    total = lax.axis_size(BOTH)
    return lax.ppermute(value, BOTH, [(i, i - step) for i in range(total) if 0 <= i - step < total])


def prepare_kernel(count_ref, src_ref, dst_ref, dst_row_ref, gather_ref, collect_ref):
    blocks, slots, edges, _ = gather_ref.shape
    lanes = lax.broadcasted_iota(jnp.int32, (edges, edges), 1)
    rows = lax.broadcasted_iota(jnp.int32, (edges, edges), 0)
    for j in range(blocks):
        for k in range(slots):
            to = dst_ref[j][:, k : k + 1] == lanes
            frm = src_ref[j][:, k : k + 1] == lanes
            gather_ref[j, k, :, :edges] = to.astype(F32).astype(BF16)
            gather_ref[j, k, :, edges:] = frm.astype(F32).astype(BF16)
            live = (dst_row_ref[j, k : k + 1, :] == rows) & (lanes < count_ref[j, k])
            collect_ref[j, :, k * edges : (k + 1) * edges] = live.astype(F32).astype(BF16)


def layer_kernel(layer, first, *refs):
    (place_ref, nbr_ref, h_ref, m4, m2, p2, p4, mate, mates, w0, w1, w2, w3, vec_in, wmsg_ref, mvec_ref,
     mgain_ref, gather_ref, collect_ref) = refs[:19]
    if first:
        out_ref, vec_ref, window, receive, hidden, normed, agg = refs[19:]
    else:
        out_ref, window, receive, hidden, normed, agg = refs[19:]
    f = place_ref[0]
    side = place_ref[1]
    base = place_ref[2]
    shards = (w0, w1, w2, w3)
    blocks, slots, edges, _ = gather_ref.shape
    width = wmsg_ref.shape[-1]
    part = width // 4

    def cols(lo, hi):
        return jnp.concatenate([w[lo:hi, :] for w in shards], axis=1)

    def wide(ref):
        return jnp.concatenate([ref[i] for i in range(4)], axis=1)

    if first:
        end = 5 * width
        for m, w in enumerate(shards):
            rows = w[end : end + 3 * VECTOR_ROWS, :].astype(F32)
            vec_ref[m] = (
                rows[:VECTOR_ROWS] + rows[VECTOR_ROWS : 2 * VECTOR_ROWS] + rows[2 * VECTOR_ROWS :]
            )
        vectors = vec_ref
    else:
        vectors = vec_in

    def vector(i):
        row = layer * 5 + i
        return jnp.concatenate([vectors[m, row : row + 1, :] for m in range(4)], axis=1)

    own = wide(h_ref)
    w_src = cols(0, width)
    pieces = [(h_ref, 5), (m4, 1), (m2, 3), (p2, 7), (p4, 9)]
    for ref, at in pieces:
        window[pl.ds(2 * at * edges, 2 * edges), :] = dot(wide(ref), w_src).astype(BF16)
    over = 1 - 2 * side
    for i, s in enumerate((None, -4, -2, 2, 4)):
        at = 5 + (0 if s is None else s) + over
        ref = mate if s is None else mates.at[i - 1]
        window[pl.ds(pl.multiple_of(2 * at * edges, 2 * edges), 2 * edges), :] = dot(wide(ref), w_src).astype(BF16)
    receive[...] = (dot(own, cols(width, 2 * width)) + vector(0)).astype(BF16)

    w_msg = jnp.concatenate([wmsg_ref[f ^ m] for m in range(4)], axis=0)
    bias = mvec_ref[layer, 0:1, :]
    offset = mvec_ref[layer, 1:2, :]
    gain = mgain_ref[layer : layer + 1, :]
    for j in range(blocks):
        to = receive[j * edges : (j + 1) * edges, :]
        for k in range(slots):
            at = (nbr_ref[2 * f + j, k] - base) * edges
            frm = window[pl.ds(pl.multiple_of(at, edges), edges), :]
            terms = dot(gather_ref[j, k], jnp.concatenate([to, frm], axis=0))
            hidden[k * edges : (k + 1) * edges, :] = jnp.maximum(terms, 0.0).astype(BF16)
        for k in range(0, slots, 2):
            rows = slice(k * edges, (k + 2) * edges)
            message = dot(hidden[rows, :], w_msg) + bias
            centred = message - jnp.mean(message, axis=1, keepdims=True)
            spread = jnp.mean(centred * centred, axis=1, keepdims=True)
            normed[rows, :] = (centred * lax.rsqrt(spread + EPSILON)).astype(BF16)
        collect = collect_ref[j]
        degree = jnp.sum(collect.astype(F32), axis=1, keepdims=True)
        total = dot(collect, normed[...]) * gain + degree * offset
        agg[j * edges : (j + 1) * edges, :] = total.astype(BF16)

    pre = dot(own, cols(2 * width, 3 * width)) + dot(agg[...], cols(3 * width, 4 * width)) + vector(1)
    inner = jnp.maximum(pre, 0.0).astype(BF16)

    def out_rows(w):
        at = 4 * width
        return jnp.concatenate(
            [w[pl.ds(pl.multiple_of(at + (f ^ m) * part, part), part), :] for m in range(4)], axis=0
        )

    w_out = jnp.concatenate([out_rows(w) for w in shards], axis=1)
    node = dot(inner, w_out) + vector(2)
    centred = node - jnp.mean(node, axis=1, keepdims=True)
    spread = jnp.mean(centred * centred, axis=1, keepdims=True)
    change = centred * lax.rsqrt(spread + EPSILON) * vector(4) + vector(3)
    for m in range(4):
        piece = change[:, m * part : (m + 1) * part]
        out_ref[f ^ m] = (h_ref[f ^ m].astype(F32) + piece).astype(BF16)


def per_device(
    node_state,
    w_dst,
    w_src,
    w_msg,
    w_node_in,
    w_node_out,
    msg_vectors,
    msg_gain,
    node_vectors,
    node_gain,
    nbr_blocks,
    edge_count,
    edge_src,
    edge_dst,
):
    width = w_msg.shape[1]
    part = width // 4
    block_count, slots = nbr_blocks.shape
    edges = edge_src.shape[2]
    mine = block_count // 4
    rows = mine * edges
    feat = lax.axis_index("feat")
    chain = lax.axis_index("dom") * 4 + feat
    place = jnp.stack([feat, feat % 2, mine * (chain - 5)]).astype(jnp.int32)

    vec = jnp.concatenate([node_vectors, node_gain[:, None, :]], axis=1).reshape(LAYERS * 5, part)
    vec = jnp.pad(vec, ((0, VECTOR_ROWS - LAYERS * 5), (0, 0)))
    high = lax.reduce_precision(vec, 8, 7)
    middle = lax.reduce_precision(vec - high, 8, 7)
    low = vec - high - middle
    packs = []
    for layer in range(LAYERS):
        group = [w_src[layer], w_dst[layer], w_node_in[layer], w_node_out[layer]]
        if layer == 0:
            group += [high.astype(BF16), middle.astype(BF16), low.astype(BF16)]
        packs.append(jnp.concatenate(group, axis=0))

    def spread_weights(pack):
        across = exchange(pack, 2)
        return pack, exchange(pack, 1), across, exchange(across, 1)

    src = lax.dynamic_slice_in_dim(edge_src, feat * mine, mine, 0)
    dst = lax.dynamic_slice_in_dim(edge_dst, feat * mine, mine, 0)
    count = lax.dynamic_slice_in_dim(edge_count, feat * mine, mine, 0)
    vmem = pl.BlockSpec(memory_space=pltpu.VMEM)
    smem = pl.BlockSpec(memory_space=pltpu.SMEM)
    gather, collect = pl.pallas_call(
        prepare_kernel,
        out_shape=(
            jax.ShapeDtypeStruct((mine, slots, edges, 2 * edges), BF16),
            jax.ShapeDtypeStruct((mine, edges, slots * edges), BF16),
        ),
        in_specs=[smem, vmem, vmem, vmem],
        out_specs=(vmem, vmem),
        name="one_hots",
    )(count, jnp.swapaxes(src, 1, 2), jnp.swapaxes(dst, 1, 2), dst)

    latent = lax.all_to_all(node_state.reshape(4, rows, part), "feat", split_axis=0, concat_axis=0, tiled=True)
    weights = spread_weights(packs[0])
    vectors = jnp.zeros((8, 128), F32)
    for layer in range(LAYERS):
        near = [shifted(latent, s) for s in (-4, -2, 2, 4)]
        mate = exchange(latent, 1)
        mates = exchange(jnp.stack(near), 1)
        if layer == 0:
            later, mates = lax.optimization_barrier((packs[1], mates))
        out_shape = [jax.ShapeDtypeStruct((4, rows, part), BF16)]
        if layer == 0:
            out_shape.append(jax.ShapeDtypeStruct((4, VECTOR_ROWS, part), F32))
        result = pl.pallas_call(
            lambda *refs, layer=layer: layer_kernel(layer, layer == 0, *refs),
            out_shape=out_shape,
            in_specs=[smem, smem] + [vmem] * 17,
            out_specs=[vmem] * len(out_shape),
            scratch_shapes=[
                pltpu.VMEM((22 * edges, width), BF16),
                pltpu.VMEM((rows, width), BF16),
                pltpu.VMEM((slots * edges, width), BF16),
                pltpu.VMEM((slots * edges, width), BF16),
                pltpu.VMEM((rows, width), BF16),
            ],
            compiler_params=pltpu.CompilerParams(vmem_limit_bytes=48 * 1024 * 1024),
            name=f"layer{layer}",
        )(
            place, nbr_blocks, latent, *near, mate, mates, *weights, vectors,
            w_msg[layer].reshape(4, part, width), msg_vectors, msg_gain, gather, collect,
        )
        if layer == 0:
            latent, vectors = result
            weights = spread_weights(later)
        else:
            latent = result[0]
    out = lax.all_to_all(latent, "feat", split_axis=0, concat_axis=0, tiled=True)
    return out.reshape(4 * rows, part)


def solution(mesh):
    placed = (
        P("dom", "feat"),
        P(None, None, "feat"),
        P(None, None, "feat"),
        P(),
        P(None, None, "feat"),
        P(None, None, "feat"),
        P(),
        P(),
        P(None, None, "feat"),
        P(None, "feat"),
        P("dom", None),
        P("dom", None),
        P("dom", None, None),
        P("dom", None, None),
    )
    return jax.shard_map(
        per_device, mesh=mesh, in_specs=placed, out_specs=P("dom", "feat"), check_vma=False
    )
```

time: 502 us -> 138 us (0.27)
  waiting for transfers between devices: 287 us -> 36.3 us
  local copies, waits for them, and re-layouts: 98.3 us -> 8.68 us
  starting transfers between devices: 25.6 us -> 65.1 us
  matrix products: 29.9 us -> 0 us
  blocking collectives: 37.2 us -> 8.42 us
  Pallas kernels: 0 us -> 14.8 us
  between operations: 13.9 us -> 0.39 us
  other arithmetic: 9.11 us -> 3.29 us
    all_gather x6 -> x0, waiting for transfers between devices: 166 us -> none  [the longest x2 58.1 us: per_device(): gathered_rows = lax.all_gather(latent, 'feat', axis=1, tiled=True)]
    gather x4 -> x0, local copies, waits for them, and re-layouts: 80.6 us -> none  [the longest x2 44.4 us: per_device(): src_terms[src_rows].astype(jnp.float32)]
    ppermute x4 -> x18, starting transfers between devices: 21.7 us -> 61.3 us  [the longest x8 38.3 us: shifted(): lax.ppermute(value, BOTH, [(i, i - step) for i in range(total) if 0 <= i...]
    unnamed x10 -> x0, waiting for transfers between devices: 39 us -> none
    dot_general x16 -> x0, matrix products: 29.9 us -> none  [the longest x2 5.09 us: per_device(): jnp.dot(banded, weight_src, preferred_element_type=jnp.float32)]
    ppermute x4 -> x18, waiting for transfers between devices: 63.2 us -> 36.3 us  [the longest x8 26.6 us: shifted(): lax.ppermute(value, BOTH, [(i, i - step) for i in range(total) if 0 <= i...]
    all_to_all x1, waiting for transfers between devices: 18.8 us -> 0.01 us  [per_device(): lax.all_to_all(node_state.reshape(4, rows, part), 'feat', split_axis=0, c...]
    pallas_call x0 -> x3, Pallas kernels: none -> 14.8 us  [the longest x2 12.2 us: per_device(): pl.pallas_call(lambda *refs, layer=layer: layer_kernel(layer, layer == 0,...]
  transfers between devices with their start and end apart: 13 -> 19, of which waited for: 13 -> 9; matrix products, arithmetic and copies ran while one was open for 9% -> 7% of each run, Pallas kernels for 0% -> 2%
where the time goes in v1:
time: 138 us; the launch traced here: 137 us
  starting transfers between devices  65.1 us (47%)
  waiting for transfers between devices  36.3 us (26%)
  Pallas kernels  14.8 us (11%)
  local copies, waits for them, and re-layouts  8.68 us (6%)
  blocking collectives  8.42 us (6%)
  other arithmetic  3.29 us (2%)
    ppermute x8, starting transfers between devices, shifted(): lax.ppermute(value, BOTH, [(i, i - step) for i in range(total) if 0 <= i...  38.3 us
    ppermute x8, waiting for transfers between devices, shifted(): lax.ppermute(value, BOTH, [(i, i - step) for i in range(total) if 0 <= i...  26.6 us
    ppermute x10, starting transfers between devices, exchange(): return lax.ppermute(value, BOTH, [(i, i ^ mask) for i in range(total)])  23 us
    pallas_call x2, Pallas kernels, per_device(): pl.pallas_call(lambda *refs, layer=layer: layer_kernel(layer, layer == 0,...  12.2 us
    ppermute x10, waiting for transfers between devices, exchange(): return lax.ppermute(value, BOTH, [(i, i ^ mask) for i in range(total)])  9.7 us
    all_to_all x1, blocking collectives, per_device(): lax.all_to_all(latent, 'feat', split_axis=0, concat_axis=0, tiled=True)  8.42 us
    unnamed x33, local copies, waits for them, and re-layouts  5 us
    all_to_all x1, starting transfers between devices, per_device(): lax.all_to_all(node_state.reshape(4, rows, part), 'feat', split_axis=0, c...  3.78 us
  transfers between devices with their start and end apart: 19, of which 9 were waited for; matrix products, arithmetic and copies ran while one was open for 7% of the time, Pallas kernels for 2%

profile of v1, /device:TPU:6, one launch (start us, length us, event | category | flops | bytes accessed | tf_op | source)
XLA Modules:
  0.0 136.9 jit_solution(15474569566132405835)
XLA Ops:
  0.0 3.8 %all-to-all-start = ((bf16[4,256,128]{2,1,0:T(8,128)(2,1)}), bf16[4,256,128]{2,1,0:T(8,128)(2,1)S(1)}, u32[]{:S(2)}, u32[]{:S(2)}) async-start(bf16[4,256,128]{2,1,0:T(8,128)(2,1)} %bitcast.50), calls=%async_computation | async-start | bytes 524288 | tf_op jit(solution)/shard_map/all_to_all | solution.py:191
  6.6 4.1 %collective-permute-start.7 = (bf16[2608,128]{1,0:T(8,128)(2,1)S(1)}, bf16[2608,128]{1,0:T(8,128)(2,1)S(1)}, u32[]{:S(2)}, u32[]{:S(2)}) collective-permute-start(bf16[2608,128]{1,0:T(8,128)(2,1)S(1)} %constant_dynamic-update-slice_fusion.refs_9_), channel_id=1, source_target_pairs={{0,2},{1,3},{2,0},{3,1},{4,6},{5,7},{6,4},{7,5},{8,10},{9,11},{10,... | collective-permute-start | bytes 2002952 | tf_op jit(solution)/shard_map/ppermute | solution.py:22
  11.4 12.3 %collective-permute-start.2 = (bf16[4,256,128]{2,1,0:T(8,128)(2,1)S(1)}, bf16[4,256,128]{2,1,0:T(8,128)(2,1)S(1)}, u32[]{:S(2)}, u32[]{:S(2)}) collective-permute-start(bf16[4,256,128]{2,1,0:T(8,128)(2,1)S(1)} %all-to-all-done.refs_2_), channel_id=1, source_target_pairs={{2,0},{3,1},{4,2},{5,3},{6,4},{7,5},{8,6},{9,7},{10,8},{11,9},{12,... | collective-permute-start | bytes 786440 | tf_op jit(solution)/shard_map/ppermute | solution.py:27
  23.7 3.3 %collective-permute-start.3 = (bf16[4,256,128]{2,1,0:T(8,128)(2,1)S(1)}, bf16[4,256,128]{2,1,0:T(8,128)(2,1)S(1)}, u32[]{:S(2)}, u32[]{:S(2)}) collective-permute-start(bf16[4,256,128]{2,1,0:T(8,128)(2,1)S(1)} %all-to-all-done.refs_2_), channel_id=1, source_target_pairs={{4,0},{5,1},{6,2},{7,3},{8,4},{9,5},{10,6},{11,7},{12,8},{13,9},{1... | collective-permute-start | bytes 786440 | tf_op jit(solution)/shard_map/ppermute | solution.py:27
  27.0 3.4 %collective-permute-start = (bf16[4,256,128]{2,1,0:T(8,128)(2,1)S(1)}, bf16[4,256,128]{2,1,0:T(8,128)(2,1)S(1)}, u32[]{:S(2)}, u32[]{:S(2)}) collective-permute-start(bf16[4,256,128]{2,1,0:T(8,128)(2,1)S(1)} %all-to-all-done.refs_2_), channel_id=1, source_target_pairs={{0,4},{1,5},{2,6},{3,7},{4,8},{5,9},{6,10},{7,11},{8,12},{9,13},{1... | collective-permute-start | bytes 786440 | tf_op jit(solution)/shard_map/ppermute | solution.py:27
  30.4 2.4 %collective-permute-start.1 = (bf16[4,256,128]{2,1,0:T(8,128)(2,1)S(1)}, bf16[4,256,128]{2,1,0:T(8,128)(2,1)S(1)}, u32[]{:S(2)}, u32[]{:S(2)}) collective-permute-start(bf16[4,256,128]{2,1,0:T(8,128)(2,1)S(1)} %all-to-all-done.refs_2_), channel_id=1, source_target_pairs={{0,2},{1,3},{2,4},{3,5},{4,6},{5,7},{6,8},{7,9},{8,10},{9,11},{10,... | collective-permute-start | bytes 786440 | tf_op jit(solution)/shard_map/ppermute | solution.py:27
  33.7 9.0 %collective-permute-done.2.refs_5_ = bf16[4,256,128]{2,1,0:T(8,128)(2,1)S(1)} collective-permute-done((bf16[4,256,128]{2,1,0:T(8,128)(2,1)S(1)}, bf16[4,256,128]{2,1,0:T(8,128)(2,1)S(1)}, u32[]{:S(2)}, u32[]{:S(2)}) %collective-permute-start.2) | collective-permute-done | bytes 262176 | tf_op jit(solution)/shard_map/ppermute | solution.py:27
  42.7 1.9 %collective-permute-start.6 = (bf16[2608,128]{1,0:T(8,128)(2,1)S(1)}, bf16[2608,128]{1,0:T(8,128)(2,1)S(1)}, u32[]{:S(2)}, u32[]{:S(2)}) collective-permute-start(bf16[2608,128]{1,0:T(8,128)(2,1)S(1)} %constant_dynamic-update-slice_fusion.refs_9_), channel_id=1, source_target_pairs={{0,1},{1,0},{2,3},{3,2},{4,5},{5,4},{6,7},{7,6},{8,9},{9,8},{10,11... | collective-permute-start | bytes 2002952 | tf_op jit(solution)/shard_map/ppermute | solution.py:22
  44.6 3.0 %collective-permute-done.refs_3_ = bf16[4,256,128]{2,1,0:T(8,128)(2,1)S(1)} collective-permute-done((bf16[4,256,128]{2,1,0:T(8,128)(2,1)S(1)}, bf16[4,256,128]{2,1,0:T(8,128)(2,1)S(1)}, u32[]{:S(2)}, u32[]{:S(2)}) %collective-permute-start) | collective-permute-done | bytes 262176 | tf_op jit(solution)/shard_map/ppermute | solution.py:27
  47.6 5.5 %collective-permute-done.1.refs_4_ = bf16[4,256,128]{2,1,0:T(8,128)(2,1)S(1)} collective-permute-done((bf16[4,256,128]{2,1,0:T(8,128)(2,1)S(1)}, bf16[4,256,128]{2,1,0:T(8,128)(2,1)S(1)}, u32[]{:S(2)}, u32[]{:S(2)}) %collective-permute-start.1) | collective-permute-done | bytes 262176 | tf_op jit(solution)/shard_map/ppermute | solution.py:27
  54.3 1.9 %collective-permute-start.5 = (bf16[4,4,256,128]{3,2,1,0:T(8,128)(2,1)}, bf16[4,4,256,128]{3,2,1,0:T(8,128)(2,1)}, u32[]{:S(2)}, u32[]{:S(2)}) collective-permute-start(bf16[4,4,256,128]{3,2,1,0:T(8,128)(2,1)} %pad_maximum_fusion), channel_id=1, source_target_pairs={{0,1},{1,0},{2,3},{3,2},{4,5},{5,4},{6,7},{7,6},{8,9},{9,8},{10,11... | collective-permute-start | bytes 3145736 | tf_op jit(solution)/shard_map/ppermute | solution.py:22
  57.5 2.4 %collective-permute-start.8 = (bf16[2608,128]{1,0:T(8,128)(2,1)S(1)}, bf16[2608,128]{1,0:T(8,128)(2,1)}, u32[]{:S(2)}, u32[]{:S(2)}) collective-permute-start(bf16[2608,128]{1,0:T(8,128)(2,1)S(1)} %collective-permute-done.7.refs_11_), channel_id=1, source_target_pairs={{0,1},{1,0},{2,3},{3,2},{4,5},{5,4},{6,7},{7,6},{8,9},{9,8},{10,11... | collective-permute-start | bytes 2002952 | tf_op jit(solution)/shard_map/ppermute | solution.py:22
  62.1 2.5 %one_hots.1 = (bf16[2,6,128,256]{3,2,1,0:T(8,128)(2,1)}, bf16[2,128,768]{2,1,0:T(8,128)(2,1)}) custom-call(s32[2,6]{1,0:T(2,128)} %constant_dynamic-slice_fusion.2.count_ref, s32[2,128,6]{2,1,0:T(8,128)} %bitcast.49, s32[2,128,6]{2,1,0:T(8,128)} %bitcast.48, s32[2,6,128]{2,1,0:T(8,128)} %copy.20.dst_row_ref), custom_call_target="tpu_custom_call" | custom-call | tf_op jit(solution)/shard_map/one_hots/pallas_call | solution.py:180
  64.7 1.2 pad_maximum_fusion.2.refs_9_
  65.9 2.1 %collective-permute-start.4 = (bf16[4,256,128]{2,1,0:T(8,128)(2,1)S(1)}, bf16[4,256,128]{2,1,0:T(8,128)(2,1)S(1)}, u32[]{:S(2)}, u32[]{:S(2)}) collective-permute-start(bf16[4,256,128]{2,1,0:T(8,128)(2,1)S(1)} %all-to-all-done.refs_2_), channel_id=1, source_target_pairs={{0,1},{1,0},{2,3},{3,2},{4,5},{5,4},{6,7},{7,6},{8,9},{9,8},{10,11... | collective-permute-start | bytes 786440 | tf_op jit(solution)/shard_map/ppermute | solution.py:22
  68.1 1.4 %collective-permute-done.4.refs_7_ = bf16[4,256,128]{2,1,0:T(8,128)(2,1)S(1)} collective-permute-done((bf16[4,256,128]{2,1,0:T(8,128)(2,1)S(1)}, bf16[4,256,128]{2,1,0:T(8,128)(2,1)S(1)}, u32[]{:S(2)}, u32[]{:S(2)}) %collective-permute-start.4) | collective-permute-done | bytes 262176 | tf_op jit(solution)/shard_map/ppermute | solution.py:22
  69.5 6.4 %layer0.1 = (bf16[4,256,128]{2,1,0:T(8,128)(2,1)S(1)}, f32[4,16,128]{2,1,0:T(8,128)S(1)}) custom-call(s32[3]{0:T(128)S(1)} %pad_add_fusion.refs_0_, s32[8,6]{1,0:T(8,128)S(1)} %copy-done.4, bf16[4,256,128]{2,1,0:T(8,128)(2,1)S(1)} %all-to-all-done.refs_2_, bf16[4,256,128]{2,1,0:T(8,128)(2,1)S(1)} %collective-permute-done.refs_3_, ...), custom_call_target="tpu_custom_call" | custom-call | tf_op jit(solution)/shard_map/layer0/pallas_call | solution.py:203
  75.9 1.9 %collective-permute-start.9 = (bf16[4,256,128]{2,1,0:T(8,128)(2,1)S(1)}, bf16[4,256,128]{2,1,0:T(8,128)(2,1)S(1)}, u32[]{:S(2)}, u32[]{:S(2)}) collective-permute-start(bf16[4,256,128]{2,1,0:T(8,128)(2,1)S(1)} %get-tuple-element.14.refs_2_), channel_id=1, source_target_pairs={{0,4},{1,5},{2,6},{3,7},{4,8},{5,9},{6,10},{7,11},{8,12},{9,13},{1... | collective-permute-start | bytes 786440 | tf_op jit(solution)/shard_map/ppermute | solution.py:27
  77.8 1.9 %collective-permute-start.10 = (bf16[4,256,128]{2,1,0:T(8,128)(2,1)S(1)}, bf16[4,256,128]{2,1,0:T(8,128)(2,1)S(1)}, u32[]{:S(2)}, u32[]{:S(2)}) collective-permute-start(bf16[4,256,128]{2,1,0:T(8,128)(2,1)S(1)} %get-tuple-element.14.refs_2_), channel_id=1, source_target_pairs={{0,2},{1,3},{2,4},{3,5},{4,6},{5,7},{6,8},{7,9},{8,10},{9,11},{10,... | collective-permute-start | bytes 786440 | tf_op jit(solution)/shard_map/ppermute | solution.py:27
  79.7 8.1 %collective-permute-start.11 = (bf16[4,256,128]{2,1,0:T(8,128)(2,1)S(1)}, bf16[4,256,128]{2,1,0:T(8,128)(2,1)S(1)}, u32[]{:S(2)}, u32[]{:S(2)}) collective-permute-start(bf16[4,256,128]{2,1,0:T(8,128)(2,1)S(1)} %get-tuple-element.14.refs_2_), channel_id=1, source_target_pairs={{2,0},{3,1},{4,2},{5,3},{6,4},{7,5},{8,6},{9,7},{10,8},{11,9},{12,... | collective-permute-start | bytes 786440 | tf_op jit(solution)/shard_map/ppermute | solution.py:27
  87.9 4.8 %collective-permute-start.12 = (bf16[4,256,128]{2,1,0:T(8,128)(2,1)S(1)}, bf16[4,256,128]{2,1,0:T(8,128)(2,1)S(1)}, u32[]{:S(2)}, u32[]{:S(2)}) collective-permute-start(bf16[4,256,128]{2,1,0:T(8,128)(2,1)S(1)} %get-tuple-element.14.refs_2_), channel_id=1, source_target_pairs={{4,0},{5,1},{6,2},{7,3},{8,4},{9,5},{10,6},{11,7},{12,8},{13,9},{1... | collective-permute-start | bytes 786440 | tf_op jit(solution)/shard_map/ppermute | solution.py:27
  92.7 1.9 %collective-permute-start.16 = (bf16[2560,128]{1,0:T(8,128)(2,1)S(1)}, bf16[2560,128]{1,0:T(8,128)(2,1)S(1)}, u32[]{:S(2)}, u32[]{:S(2)}) collective-permute-start(bf16[2560,128]{1,0:T(8,128)(2,1)S(1)} %pad_maximum_fusion.2.refs_9_), channel_id=1, source_target_pairs={{0,2},{1,3},{2,0},{3,1},{4,6},{5,7},{6,4},{7,5},{8,10},{9,11},{10,... | collective-permute-start | bytes 1966088 | tf_op jit(solution)/shard_map/ppermute | solution.py:22
  94.6 2.6 %collective-permute-done.9.refs_3_ = bf16[4,256,128]{2,1,0:T(8,128)(2,1)S(1)} collective-permute-done((bf16[4,256,128]{2,1,0:T(8,128)(2,1)S(1)}, bf16[4,256,128]{2,1,0:T(8,128)(2,1)S(1)}, u32[]{:S(2)}, u32[]{:S(2)}) %collective-permute-start.9) | collective-permute-done | bytes 262176 | tf_op jit(solution)/shard_map/ppermute | solution.py:27
  97.3 1.4 collective-permute-done.10.refs_4_
  98.6 5.0 %collective-permute-done.12.refs_6_ = bf16[4,256,128]{2,1,0:T(8,128)(2,1)S(1)} collective-permute-done((bf16[4,256,128]{2,1,0:T(8,128)(2,1)S(1)}, bf16[4,256,128]{2,1,0:T(8,128)(2,1)S(1)}, u32[]{:S(2)}, u32[]{:S(2)}) %collective-permute-start.12) | collective-permute-done | bytes 262176 | tf_op jit(solution)/shard_map/ppermute | solution.py:27
  103.8 2.1 %collective-permute-start.14 = (bf16[4,4,256,128]{3,2,1,0:T(8,128)(2,1)S(1)}, bf16[4,4,256,128]{3,2,1,0:T(8,128)(2,1)S(1)}, u32[]{:S(2)}, u32[]{:S(2)}) collective-permute-start(bf16[4,4,256,128]{3,2,1,0:T(8,128)(2,1)S(1)} %pad_maximum_fusion.1), channel_id=1, source_target_pairs={{0,1},{1,0},{2,3},{3,2},{4,5},{5,4},{6,7},{7,6},{8,9},{9,8},{10,11... | collective-permute-start | bytes 3145736 | tf_op jit(solution)/shard_map/ppermute | solution.py:22
  105.9 2.4 %collective-permute-start.15 = (bf16[2560,128]{1,0:T(8,128)(2,1)S(1)}, bf16[2560,128]{1,0:T(8,128)(2,1)S(1)}, u32[]{:S(2)}, u32[]{:S(2)}) collective-permute-start(bf16[2560,128]{1,0:T(8,128)(2,1)S(1)} %pad_maximum_fusion.2.refs_9_), channel_id=1, source_target_pairs={{0,1},{1,0},{2,3},{3,2},{4,5},{5,4},{6,7},{7,6},{8,9},{9,8},{10,11... | collective-permute-start | bytes 1966088 | tf_op jit(solution)/shard_map/ppermute | solution.py:22
  108.3 7.1 %collective-permute-done.16.refs_11_ = bf16[2560,128]{1,0:T(8,128)(2,1)S(1)} collective-permute-done((bf16[2560,128]{1,0:T(8,128)(2,1)S(1)}, bf16[2560,128]{1,0:T(8,128)(2,1)S(1)}, u32[]{:S(2)}, u32[]{:S(2)}) %collective-permute-start.16) | collective-permute-done | bytes 655392 | tf_op jit(solution)/shard_map/ppermute | solution.py:22
  115.4 1.9 %collective-permute-start.17 = (bf16[2560,128]{1,0:T(8,128)(2,1)S(1)}, bf16[2560,128]{1,0:T(8,128)(2,1)S(1)}, u32[]{:S(2)}, u32[]{:S(2)}) collective-permute-start(bf16[2560,128]{1,0:T(8,128)(2,1)S(1)} %collective-permute-done.16.refs_11_), channel_id=1, source_target_pairs={{0,1},{1,0},{2,3},{3,2},{4,5},{5,4},{6,7},{7,6},{8,9},{9,8},{10,11... | collective-permute-start | bytes 1966088 | tf_op jit(solution)/shard_map/ppermute | solution.py:22
  117.3 2.4 %collective-permute-start.13 = (bf16[4,256,128]{2,1,0:T(8,128)(2,1)S(1)}, bf16[4,256,128]{2,1,0:T(8,128)(2,1)S(1)}, u32[]{:S(2)}, u32[]{:S(2)}) collective-permute-start(bf16[4,256,128]{2,1,0:T(8,128)(2,1)S(1)} %get-tuple-element.14.refs_2_), channel_id=1, source_target_pairs={{0,1},{1,0},{2,3},{3,2},{4,5},{5,4},{6,7},{7,6},{8,9},{9,8},{10,11... | collective-permute-start | bytes 786440 | tf_op jit(solution)/shard_map/ppermute | solution.py:22
  121.9 5.9 %layer1.1 = bf16[4,256,128]{2,1,0:T(8,128)(2,1)S(1)} custom-call(s32[3]{0:T(128)S(1)} %pad_add_fusion.refs_0_, s32[8,6]{1,0:T(8,128)S(1)} %copy-done.4, bf16[4,256,128]{2,1,0:T(8,128)(2,1)S(1)} %get-tuple-element.14.refs_2_, bf16[4,256,128]{2,1,0:T(8,128)(2,1)S(1)} %collective-permute-done.9.refs_3_, ...), custom_call_target="tpu_custom_call" | custom-call | tf_op jit(solution)/shard_map/layer1/pallas_call | solution.py:203
  127.8 8.4 %all_to_all.10 = bf16[4,256,128]{2,1,0:T(8,128)(2,1)S(1)} all-to-all(bf16[4,256,128]{2,1,0:T(8,128)(2,1)S(1)} %layer1.1), channel_id=1, replica_groups=mesh['dom'=128,'feat'=4] {'feat'}, dimensions={0} | all-to-all | bytes 524288 | tf_op jit(solution)/shard_map/all_to_all | solution.py:226
  (60 shorter events, 12.0 us)
Async XLA Ops:
  0.0 56.2 %copy-start = (s32[8,6]{1,0:T(8,128)S(1)}, s32[8,6]{1,0:T(8,128)}, u32[]{:S(2)}) copy-start(s32[8,6]{1,0:T(8,128)} %param.25) | copy-start | bytes 580
  0.0 10.6 %copy-start.11 = (bf16[2,512,128]{2,1,0:T(8,128)(2,1)S(1)}, bf16[2,512,128]{2,1,0:T(8,128)(2,1)}, u32[]{:S(2)}) copy-start(bf16[2,512,128]{2,1,0:T(8,128)(2,1)} %param.15) | copy-start | bytes 786436
  0.0 6.4 %copy-start.8 = (bf16[2,1024,128]{2,1,0:T(8,128)(2,1)S(1)}, bf16[2,1024,128]{2,1,0:T(8,128)(2,1)}, u32[]{:S(2)}) copy-start(bf16[2,1024,128]{2,1,0:T(8,128)(2,1)} %param.18) | copy-start | bytes 1572868
  0.0 6.5 %copy-start.12 = (bf16[2,512,128]{2,1,0:T(8,128)(2,1)S(1)}, bf16[2,512,128]{2,1,0:T(8,128)(2,1)}, u32[]{:S(2)}) copy-start(bf16[2,512,128]{2,1,0:T(8,128)(2,1)} %param.19) | copy-start | bytes 786436
  0.0 11.3 %all-to-all-start = ((bf16[4,256,128]{2,1,0:T(8,128)(2,1)}), bf16[4,256,128]{2,1,0:T(8,128)(2,1)S(1)}, u32[]{:S(2)}, u32[]{:S(2)}) async-start(bf16[4,256,128]{2,1,0:T(8,128)(2,1)} %bitcast.50), calls=%async_computation | async-start | bytes 524288 | tf_op jit(solution)/shard_map/all_to_all | solution.py:191
  3.8 29.9 %copy-start.10 = (bf16[2,512,128]{2,1,0:T(8,128)(2,1)S(1)}, bf16[2,512,128]{2,1,0:T(8,128)(2,1)}, u32[]{:S(2)}) copy-start(bf16[2,512,128]{2,1,0:T(8,128)(2,1)} %param.16) | copy-start | bytes 786436
  6.6 50.9 %collective-permute-start.7 = (bf16[2608,128]{1,0:T(8,128)(2,1)S(1)}, bf16[2608,128]{1,0:T(8,128)(2,1)S(1)}, u32[]{:S(2)}, u32[]{:S(2)}) collective-permute-start(bf16[2608,128]{1,0:T(8,128)(2,1)S(1)} %constant_dynamic-update-slice_fusion.refs_9_), channel_id=1, source_target_pairs={{0,2},{1,3},{2,0},{3,1},{4,6},{5,7},{6,4},{7,5},{8,10},{9,11},{10,... | collective-permute-start | bytes 2002952 | tf_op jit(solution)/shard_map/ppermute | solution.py:22
  11.4 31.3 %collective-permute-start.2 = (bf16[4,256,128]{2,1,0:T(8,128)(2,1)S(1)}, bf16[4,256,128]{2,1,0:T(8,128)(2,1)S(1)}, u32[]{:S(2)}, u32[]{:S(2)}) collective-permute-start(bf16[4,256,128]{2,1,0:T(8,128)(2,1)S(1)} %all-to-all-done.refs_2_), channel_id=1, source_target_pairs={{2,0},{3,1},{4,2},{5,3},{6,4},{7,5},{8,6},{9,7},{10,8},{11,9},{12,... | collective-permute-start | bytes 786440 | tf_op jit(solution)/shard_map/ppermute | solution.py:27
  23.7 21.0 %collective-permute-start.3 = (bf16[4,256,128]{2,1,0:T(8,128)(2,1)S(1)}, bf16[4,256,128]{2,1,0:T(8,128)(2,1)S(1)}, u32[]{:S(2)}, u32[]{:S(2)}) collective-permute-start(bf16[4,256,128]{2,1,0:T(8,128)(2,1)S(1)} %all-to-all-done.refs_2_), channel_id=1, source_target_pairs={{4,0},{5,1},{6,2},{7,3},{8,4},{9,5},{10,6},{11,7},{12,8},{13,9},{1... | collective-permute-start | bytes 786440 | tf_op jit(solution)/shard_map/ppermute | solution.py:27
  27.0 20.6 %collective-permute-start = (bf16[4,256,128]{2,1,0:T(8,128)(2,1)S(1)}, bf16[4,256,128]{2,1,0:T(8,128)(2,1)S(1)}, u32[]{:S(2)}, u32[]{:S(2)}) collective-permute-start(bf16[4,256,128]{2,1,0:T(8,128)(2,1)S(1)} %all-to-all-done.refs_2_), channel_id=1, source_target_pairs={{0,4},{1,5},{2,6},{3,7},{4,8},{5,9},{6,10},{7,11},{8,12},{9,13},{1... | collective-permute-start | bytes 786440 | tf_op jit(solution)/shard_map/ppermute | solution.py:27
  30.4 22.7 %collective-permute-start.1 = (bf16[4,256,128]{2,1,0:T(8,128)(2,1)S(1)}, bf16[4,256,128]{2,1,0:T(8,128)(2,1)S(1)}, u32[]{:S(2)}, u32[]{:S(2)}) collective-permute-start(bf16[4,256,128]{2,1,0:T(8,128)(2,1)S(1)} %all-to-all-done.refs_2_), channel_id=1, source_target_pairs={{0,2},{1,3},{2,4},{3,5},{4,6},{5,7},{6,8},{7,9},{8,10},{9,11},{10,... | collective-permute-start | bytes 786440 | tf_op jit(solution)/shard_map/ppermute | solution.py:27
  42.7 26.8 %collective-permute-start.6 = (bf16[2608,128]{1,0:T(8,128)(2,1)S(1)}, bf16[2608,128]{1,0:T(8,128)(2,1)S(1)}, u32[]{:S(2)}, u32[]{:S(2)}) collective-permute-start(bf16[2608,128]{1,0:T(8,128)(2,1)S(1)} %constant_dynamic-update-slice_fusion.refs_9_), channel_id=1, source_target_pairs={{0,1},{1,0},{2,3},{3,2},{4,5},{5,4},{6,7},{7,6},{8,9},{9,8},{10,11... | collective-permute-start | bytes 2002952 | tf_op jit(solution)/shard_map/ppermute | solution.py:22
  53.2 3.6 %copy-start.9 = (bf16[2,1024,128]{2,1,0:T(8,128)(2,1)S(1)}, bf16[2,1024,128]{2,1,0:T(8,128)(2,1)}, u32[]{:S(2)}) copy-start(bf16[2,1024,128]{2,1,0:T(8,128)(2,1)} %param.18) | copy-start | bytes 1572868
  54.3 13.8 %collective-permute-start.5 = (bf16[4,4,256,128]{3,2,1,0:T(8,128)(2,1)}, bf16[4,4,256,128]{3,2,1,0:T(8,128)(2,1)}, u32[]{:S(2)}, u32[]{:S(2)}) collective-permute-start(bf16[4,4,256,128]{3,2,1,0:T(8,128)(2,1)} %pad_maximum_fusion), channel_id=1, source_target_pairs={{0,1},{1,0},{2,3},{3,2},{4,5},{5,4},{6,7},{7,6},{8,9},{9,8},{10,11... | collective-permute-start | bytes 3145736 | tf_op jit(solution)/shard_map/ppermute | solution.py:22
  57.5 12.0 %collective-permute-start.8 = (bf16[2608,128]{1,0:T(8,128)(2,1)S(1)}, bf16[2608,128]{1,0:T(8,128)(2,1)}, u32[]{:S(2)}, u32[]{:S(2)}) collective-permute-start(bf16[2608,128]{1,0:T(8,128)(2,1)S(1)} %collective-permute-done.7.refs_11_), channel_id=1, source_target_pairs={{0,1},{1,0},{2,3},{3,2},{4,5},{5,4},{6,7},{7,6},{8,9},{9,8},{10,11... | collective-permute-start | bytes 2002952 | tf_op jit(solution)/shard_map/ppermute | solution.py:22
  64.7 3.3 %copy-start.7 = (bf16[2,512,512]{2,1,0:T(8,128)(2,1)S(1)}, bf16[2,512,512]{2,1,0:T(8,128)(2,1)}, u32[]{:S(2)}) copy-start(bf16[2,512,512]{2,1,0:T(8,128)(2,1)} %param.17) | copy-start | bytes 3145732
  65.9 3.6 %copy-start.2 = (bf16[2,128,768]{2,1,0:T(8,128)(2,1)S(1)}, bf16[2,128,768]{2,1,0:T(8,128)(2,1)}, u32[]{:S(2)}) copy-start(bf16[2,128,768]{2,1,0:T(8,128)(2,1)} %get-tuple-element.13.refs_18_) | copy-start | bytes 1179652
  65.9 3.6 %copy-start.3 = (f32[2,2,512]{2,1,0:T(2,128)S(1)}, f32[2,2,512]{2,1,0:T(2,128)}, u32[]{:S(2)}) copy-start(f32[2,2,512]{2,1,0:T(2,128)} %refs_15_.3) | copy-start | bytes 24580
  65.9 3.6 %copy-start.4 = (s32[8,6]{1,0:T(8,128)S(1)}, s32[8,6]{1,0:T(8,128)}, u32[]{:S(2)}) copy-start(s32[8,6]{1,0:T(8,128)} %refs_1_.3) | copy-start | bytes 580
  65.9 3.6 %copy-start.5 = (f32[2,512]{1,0:T(2,128)S(1)}, f32[2,512]{1,0:T(2,128)}, u32[]{:S(2)}) copy-start(f32[2,512]{1,0:T(2,128)} %refs_16_.3) | copy-start | bytes 12292
  65.9 3.6 %collective-permute-start.4 = (bf16[4,256,128]{2,1,0:T(8,128)(2,1)S(1)}, bf16[4,256,128]{2,1,0:T(8,128)(2,1)S(1)}, u32[]{:S(2)}, u32[]{:S(2)}) collective-permute-start(bf16[4,256,128]{2,1,0:T(8,128)(2,1)S(1)} %all-to-all-done.refs_2_), channel_id=1, source_target_pairs={{0,1},{1,0},{2,3},{3,2},{4,5},{5,4},{6,7},{7,6},{8,9},{9,8},{10,11... | collective-permute-start | bytes 786440 | tf_op jit(solution)/shard_map/ppermute | solution.py:22
  75.9 21.4 %collective-permute-start.9 = (bf16[4,256,128]{2,1,0:T(8,128)(2,1)S(1)}, bf16[4,256,128]{2,1,0:T(8,128)(2,1)S(1)}, u32[]{:S(2)}, u32[]{:S(2)}) collective-permute-start(bf16[4,256,128]{2,1,0:T(8,128)(2,1)S(1)} %get-tuple-element.14.refs_2_), channel_id=1, source_target_pairs={{0,4},{1,5},{2,6},{3,7},{4,8},{5,9},{6,10},{7,11},{8,12},{9,13},{1... | collective-permute-start | bytes 786440 | tf_op jit(solution)/shard_map/ppermute | solution.py:27
  77.8 20.8 %collective-permute-start.10 = (bf16[4,256,128]{2,1,0:T(8,128)(2,1)S(1)}, bf16[4,256,128]{2,1,0:T(8,128)(2,1)S(1)}, u32[]{:S(2)}, u32[]{:S(2)}) collective-permute-start(bf16[4,256,128]{2,1,0:T(8,128)(2,1)S(1)} %get-tuple-element.14.refs_2_), channel_id=1, source_target_pairs={{0,2},{1,3},{2,4},{3,5},{4,6},{5,7},{6,8},{7,9},{8,10},{9,11},{10,... | collective-permute-start | bytes 786440 | tf_op jit(solution)/shard_map/ppermute | solution.py:27
  79.7 18.9 %collective-permute-start.11 = (bf16[4,256,128]{2,1,0:T(8,128)(2,1)S(1)}, bf16[4,256,128]{2,1,0:T(8,128)(2,1)S(1)}, u32[]{:S(2)}, u32[]{:S(2)}) collective-permute-start(bf16[4,256,128]{2,1,0:T(8,128)(2,1)S(1)} %get-tuple-element.14.refs_2_), channel_id=1, source_target_pairs={{2,0},{3,1},{4,2},{5,3},{6,4},{7,5},{8,6},{9,7},{10,8},{11,9},{12,... | collective-permute-start | bytes 786440 | tf_op jit(solution)/shard_map/ppermute | solution.py:27
  87.9 15.8 %collective-permute-start.12 = (bf16[4,256,128]{2,1,0:T(8,128)(2,1)S(1)}, bf16[4,256,128]{2,1,0:T(8,128)(2,1)S(1)}, u32[]{:S(2)}, u32[]{:S(2)}) collective-permute-start(bf16[4,256,128]{2,1,0:T(8,128)(2,1)S(1)} %get-tuple-element.14.refs_2_), channel_id=1, source_target_pairs={{4,0},{5,1},{6,2},{7,3},{8,4},{9,5},{10,6},{11,7},{12,8},{13,9},{1... | collective-permute-start | bytes 786440 | tf_op jit(solution)/shard_map/ppermute | solution.py:27
  92.7 22.7 %collective-permute-start.16 = (bf16[2560,128]{1,0:T(8,128)(2,1)S(1)}, bf16[2560,128]{1,0:T(8,128)(2,1)S(1)}, u32[]{:S(2)}, u32[]{:S(2)}) collective-permute-start(bf16[2560,128]{1,0:T(8,128)(2,1)S(1)} %pad_maximum_fusion.2.refs_9_), channel_id=1, source_target_pairs={{0,2},{1,3},{2,0},{3,1},{4,6},{5,7},{6,4},{7,5},{8,10},{9,11},{10,... | collective-permute-start | bytes 1966088 | tf_op jit(solution)/shard_map/ppermute | solution.py:22
  103.7 18.2 %copy-start.1 = (bf16[2,6,128,256]{3,2,1,0:T(8,128)(2,1)S(1)}, bf16[2,6,128,256]{3,2,1,0:T(8,128)(2,1)}, u32[]{:S(2)}) copy-start(bf16[2,6,128,256]{3,2,1,0:T(8,128)(2,1)} %get-tuple-element.12.refs_17_) | copy-start | bytes 2359300
  103.8 17.1 %collective-permute-start.14 = (bf16[4,4,256,128]{3,2,1,0:T(8,128)(2,1)S(1)}, bf16[4,4,256,128]{3,2,1,0:T(8,128)(2,1)S(1)}, u32[]{:S(2)}, u32[]{:S(2)}) collective-permute-start(bf16[4,4,256,128]{3,2,1,0:T(8,128)(2,1)S(1)} %pad_maximum_fusion.1), channel_id=1, source_target_pairs={{0,1},{1,0},{2,3},{3,2},{4,5},{5,4},{6,7},{7,6},{8,9},{9,8},{10,11... | collective-permute-start | bytes 3145736 | tf_op jit(solution)/shard_map/ppermute | solution.py:22
  105.9 15.0 %collective-permute-start.15 = (bf16[2560,128]{1,0:T(8,128)(2,1)S(1)}, bf16[2560,128]{1,0:T(8,128)(2,1)S(1)}, u32[]{:S(2)}, u32[]{:S(2)}) collective-permute-start(bf16[2560,128]{1,0:T(8,128)(2,1)S(1)} %pad_maximum_fusion.2.refs_9_), channel_id=1, source_target_pairs={{0,1},{1,0},{2,3},{3,2},{4,5},{5,4},{6,7},{7,6},{8,9},{9,8},{10,11... | collective-permute-start | bytes 1966088 | tf_op jit(solution)/shard_map/ppermute | solution.py:22
  115.4 5.5 %collective-permute-start.17 = (bf16[2560,128]{1,0:T(8,128)(2,1)S(1)}, bf16[2560,128]{1,0:T(8,128)(2,1)S(1)}, u32[]{:S(2)}, u32[]{:S(2)}) collective-permute-start(bf16[2560,128]{1,0:T(8,128)(2,1)S(1)} %collective-permute-done.16.refs_11_), channel_id=1, source_target_pairs={{0,1},{1,0},{2,3},{3,2},{4,5},{5,4},{6,7},{7,6},{8,9},{9,8},{10,11... | collective-permute-start | bytes 1966088 | tf_op jit(solution)/shard_map/ppermute | solution.py:22
  117.3 3.6 %collective-permute-start.13 = (bf16[4,256,128]{2,1,0:T(8,128)(2,1)S(1)}, bf16[4,256,128]{2,1,0:T(8,128)(2,1)S(1)}, u32[]{:S(2)}, u32[]{:S(2)}) collective-permute-start(bf16[4,256,128]{2,1,0:T(8,128)(2,1)S(1)} %get-tuple-element.14.refs_2_), channel_id=1, source_target_pairs={{0,1},{1,0},{2,3},{3,2},{4,5},{5,4},{6,7},{7,6},{8,9},{9,8},{10,11... | collective-permute-start | bytes 786440 | tf_op jit(solution)/shard_map/ppermute | solution.py:22
  120.9 1.0 copy-start.6

commit v2 on v1

v2 whole, which is shorter than its diff:
```python
import jax
import jax.numpy as jnp
from jax import lax
from jax.experimental import pallas as pl
from jax.experimental.pallas import tpu as pltpu
from jax.sharding import PartitionSpec as P

LAYERS = 2
EPSILON = 1e-05
BOTH = ("dom", "feat")
F32 = jnp.float32
BF16 = jnp.bfloat16
VECTOR_ROWS = 16
ORDER = (0, 2, 1, 3)
FLIPPED = (1, 0, 3, 2)
STRAIGHT = (0, 1, 2, 3)
UNROLL = 4
LIST = 32
VMEM = pl.BlockSpec(memory_space=pltpu.VMEM)
SMEM = pl.BlockSpec(memory_space=pltpu.SMEM)


def dot(a, b):
    return jnp.dot(a, b, preferred_element_type=F32)


def exchange(value, mask):
    total = lax.axis_size(BOTH)
    return lax.ppermute(value, BOTH, [(i, i ^ mask) for i in range(total)])


def pass_on(value):
    total = lax.axis_size(BOTH)
    pairs = [(i, i + (2 if i % 2 == 0 else -2)) for i in range(total)]
    return lax.ppermute(value, BOTH, [(i, t) for i, t in pairs if 0 <= t < total])


def prepare_kernel(place_ref, nbr_ref, count_ref, src_ref, dst_ref, dst_row_ref, gather_ref, collect_ref, degree_ref, meta_ref):
    last, edges, _ = gather_ref.shape
    slots = nbr_ref.shape[1]
    blocks = last // slots
    core, first, base = place_ref[1], place_ref[2], place_ref[3]
    lanes = lax.broadcasted_iota(jnp.int32, (edges, edges), 1)
    rows = lax.broadcasted_iota(jnp.int32, (edges, edges), 0)
    for i in range(LIST):
        meta_ref[0, i] = last - 1
        meta_ref[1, i] = last - 1
        meta_ref[2, i] = 0
    near, far = jnp.int32(0), jnp.int32(0)
    for j in range(blocks):
        to = dst_ref[first + j]
        frm = src_ref[first + j]
        to_row = dst_row_ref[first + j]
        degree = jnp.zeros((edges, edges), F32)
        for k in range(slots):
            s = j * slots + k
            gather_ref[s, :, :edges] = (to[:, k : k + 1] == lanes).astype(F32).astype(BF16)
            gather_ref[s, :, edges:] = (frm[:, k : k + 1] == lanes).astype(F32).astype(BF16)
            live = ((to_row[k : k + 1, :] == rows) & (lanes < count_ref[first + j, k])).astype(F32)
            collect_ref[s] = live.astype(BF16)
            degree = degree + live
            place = nbr_ref[first + j, k] - base
            step = (place + 2 * blocks) // blocks - 2
            hops = jnp.abs(step)
            meta_ref[2, s] = hops * blocks + place - step * blocks
            mine = jnp.where(step == 0, core == j // (blocks // 2), (step > 0) == (core == 1))
            is_far = mine & (hops == 2)
            is_near = mine & (hops < 2)

            @pl.when(is_near)
            def _():
                meta_ref[0, near] = s

            @pl.when(is_far)
            def _():
                meta_ref[1, far] = s

            near = near + is_near.astype(jnp.int32)
            far = far + is_far.astype(jnp.int32)
        degree_ref[j * edges : (j + 1) * edges, :] = jnp.broadcast_to(
            jnp.sum(degree, axis=1, keepdims=True), (edges, edges)
        )
    meta_ref[3, 0] = near
    meta_ref[3, 1] = far
    gather_ref[last - 1] = jnp.zeros(gather_ref.shape[1:], BF16)
    collect_ref[last - 1] = jnp.zeros(collect_ref.shape[1:], BF16)


def wide(ref, order=STRAIGHT):
    return jnp.concatenate([ref[i] for i in order], axis=1)


def weight(shards, f, half, base, mixed):
    part = shards[0].shape[-1]
    rows = []
    for i in range(4):
        g = f ^ ORDER[i] if mixed else i
        cols = []
        for m, w in enumerate(shards):
            at = g // 2 if m < 2 else (g // 2) ^ half
            start = base + (g % 2) * part
            if mixed:
                start = pl.multiple_of(start, part)
            cols.append(w[at, pl.ds(start, part), :])
        rows.append(jnp.concatenate(cols, axis=1))
    return jnp.concatenate(rows, axis=0)


def vector(vectors, layer, i):
    row = layer * 5 + i
    return jnp.concatenate([vectors[m, row : row + 1, :] for m in range(4)], axis=1)


def run_edges(which, shift, layer, f, meta_ref, receive, window, gather_ref, collect_ref, wmsg_ref, mvec_ref, hidden, normed, acc):
    slots = 6
    edges = gather_ref.shape[1]
    w_msg = jnp.concatenate([wmsg_ref[f ^ m] for m in range(4)], axis=0)
    bias = mvec_ref[layer, 0:1, :]

    def body(step, carry):
        ids = [meta_ref[which, step * UNROLL + u] for u in range(UNROLL)]
        blocks = [jnp.minimum(s // slots, 3) for s in ids]
        for u, (s, j) in enumerate(zip(ids, blocks)):
            at = meta_ref[2, s] - shift
            if which == 1:
                at = jnp.maximum(at, 0)
            to = receive[pl.ds(pl.multiple_of(j * edges, edges), edges), :]
            frm = window[pl.ds(pl.multiple_of(at * edges, edges), edges), :]
            terms = dot(gather_ref[s], jnp.concatenate([to, frm], axis=0))
            hidden[u * edges : (u + 1) * edges, :] = jnp.maximum(terms, 0.0).astype(BF16)
        for v in range(0, UNROLL, 2):
            rows = slice(v * edges, (v + 2) * edges)
            message = dot(hidden[rows, :], w_msg) + bias
            centred = message - jnp.mean(message, axis=1, keepdims=True)
            spread = jnp.mean(centred * centred, axis=1, keepdims=True)
            normed[rows, :] = (centred * lax.rsqrt(spread + EPSILON)).astype(BF16)
        for u, (s, j) in enumerate(zip(ids, blocks)):
            rows = pl.ds(pl.multiple_of(j * edges, edges), edges)
            acc[rows, :] = acc[rows, :] + dot(collect_ref[s], normed[u * edges : (u + 1) * edges, :])
        return carry

    lax.fori_loop(0, (meta_ref[3, which] + UNROLL - 1) // UNROLL, body, 0)


def near_kernel(layer, first, place_ref, meta_ref, h_ref, next_ref, w0, w1, w2, w3, *refs):
    if first:
        wmsg_ref, mvec_ref, gather_ref, collect_ref, acc, receive, vectors, window, hidden, normed = refs
    else:
        vectors, wmsg_ref, mvec_ref, gather_ref, collect_ref, acc, receive, window, hidden, normed = refs
    f, half = place_ref[0], place_ref[4]
    shards = (w0, w1, w2, w3)
    edges = gather_ref.shape[1]
    if first:
        end = w0.shape[1] - 3 * VECTOR_ROWS
        for m, w in enumerate(shards):
            rows = w[0, end : end + 3 * VECTOR_ROWS, :].astype(F32)
            vectors[m] = rows[:VECTOR_ROWS] + rows[VECTOR_ROWS : 2 * VECTOR_ROWS] + rows[2 * VECTOR_ROWS :]
    w_src = weight(shards, f, half, 0, True)
    own = wide(h_ref)
    block = own.shape[0]
    window[:block, :] = dot(own, w_src).astype(BF16)
    window[block:, :] = dot(wide(next_ref, FLIPPED), w_src).astype(BF16)
    receive[...] = (dot(own, weight(shards, f, half, 2 * edges, True)) + vector(vectors, layer, 0)).astype(BF16)
    acc[...] = jnp.zeros_like(acc)
    run_edges(0, 0, layer, f, meta_ref, receive, window, gather_ref, collect_ref, wmsg_ref, mvec_ref, hidden, normed, acc)


def far_kernel(layer, place_ref, meta_ref, after_ref, w0, w1, w2, w3, wmsg_ref, mvec_ref, gather_ref, collect_ref, acc_in, receive, out_ref, window, hidden, normed, acc):
    f, half = place_ref[0], place_ref[4]
    edges = gather_ref.shape[1]
    window[...] = dot(wide(after_ref), weight((w0, w1, w2, w3), f, half, 0, True)).astype(BF16)
    acc[...] = acc_in[...]
    run_edges(1, 8, layer, f, meta_ref, receive, window, gather_ref, collect_ref, wmsg_ref, mvec_ref, hidden, normed, acc)
    out_ref[...] = acc[...].astype(BF16)


def node_kernel(layer, final, place_ref, h_ref, part_a, part_b, degree_ref, w0, w1, w2, w3, vectors, mvec_ref, mgain_ref, *outs):
    f, half = place_ref[0], place_ref[4]
    shards = (w0, w1, w2, w3)
    part = h_ref.shape[-1]
    step = 2 * part
    total = part_a[...].astype(F32) + part_b[...].astype(F32)
    agg = total * mgain_ref[layer : layer + 1, :] + degree_ref[:, 0:1] * mvec_ref[layer, 1:2, :]
    pre = dot(wide(h_ref), weight(shards, f, half, 2 * step, True))
    pre = pre + dot(agg.astype(BF16), weight(shards, f, half, 3 * step, False)) + vector(vectors, layer, 1)
    inner = jnp.maximum(pre, 0.0).astype(BF16)
    inner = jnp.concatenate([inner[:, m * part : (m + 1) * part] for m in ORDER], axis=1)
    node = dot(inner, weight(shards, f, half, 4 * step, True)) + vector(vectors, layer, 2)
    centred = node - jnp.mean(node, axis=1, keepdims=True)
    spread = jnp.mean(centred * centred, axis=1, keepdims=True)
    change = centred * lax.rsqrt(spread + EPSILON) * vector(vectors, layer, 4) + vector(vectors, layer, 3)
    for i, m in enumerate(ORDER):
        if final and m not in (0, 2):
            continue
        new = (h_ref[i].astype(F32) + change[:, m * part : (m + 1) * part]).astype(BF16)
        if final:
            outs[m // 2][...] = new
        else:
            outs[0][i] = new


def join_kernel(place_ref, own_ref, other_ref, out_ref):
    rows = own_ref.shape[0]
    side = place_ref[5]
    out_ref[pl.ds(pl.multiple_of(side * rows, rows), rows), :] = own_ref[...]
    out_ref[pl.ds(pl.multiple_of((1 - side) * rows, rows), rows), :] = other_ref[...]


def call(kernel, name, inputs, spaces, outs, out_spaces, scratch=()):
    return pl.pallas_call(
        kernel,
        out_shape=outs,
        in_specs=spaces,
        out_specs=out_spaces,
        scratch_shapes=list(scratch),
        compiler_params=pltpu.CompilerParams(vmem_limit_bytes=32 * 1024 * 1024),
        name=name,
    )(*inputs)


def per_device(
    node_state,
    w_dst,
    w_src,
    w_msg,
    w_node_in,
    w_node_out,
    msg_vectors,
    msg_gain,
    node_vectors,
    node_gain,
    nbr_blocks,
    edge_count,
    edge_src,
    edge_dst,
):
    width = w_msg.shape[1]
    part = width // 4
    block_count, slots = nbr_blocks.shape
    edges = edge_src.shape[2]
    mine = block_count // 2
    rows = mine * edges
    feat = lax.axis_index("feat")
    dom = lax.axis_index("dom")
    side = feat // 2
    half = (dom // 4) % 2
    place = jnp.stack(
        [feat, feat % 2, side * mine, dom * block_count + side * mine, half, side]
    ).astype(jnp.int32)

    vec = jnp.concatenate([node_vectors, node_gain[:, None, :]], axis=1).reshape(LAYERS * 5, part)
    vec = jnp.pad(vec, ((0, VECTOR_ROWS - LAYERS * 5), (0, 0)))
    high = lax.reduce_precision(vec, 8, 7)
    middle = lax.reduce_precision(vec - high, 8, 7)
    low = vec - high - middle
    thirds = jnp.concatenate([high, middle, low], axis=0).astype(BF16)
    packs = []
    for layer in range(LAYERS):
        group = [
            w.reshape(2, width // 2, part)
            for w in (
                w_src[layer], w_dst[layer], w_node_in[layer, :width], w_node_in[layer, width:], w_node_out[layer],
            )
        ]
        if layer == 0:
            group.append(jnp.broadcast_to(thirds[None], (2,) + thirds.shape))
        packs.append(jnp.concatenate(group, axis=1))

    def spread_weights(pack, share):
        beside = exchange(pack, 1)
        across = exchange(share, 2)
        across = jnp.stack([across, exchange(across, 16)])
        return pack, beside, across, exchange(across, 1)

    def share_of(pack):
        return lax.dynamic_index_in_dim(pack, half, 0, keepdims=False)

    halves = node_state.reshape(2, rows, part)
    own = lax.dynamic_index_in_dim(halves, side, 0, keepdims=False)
    other = lax.dynamic_index_in_dim(halves, 1 - side, 0, keepdims=False)
    pair = jnp.stack([own, exchange(other, 2)])
    latent = jnp.concatenate([pair, exchange(pair, 1)], axis=0)
    weights = spread_weights(packs[0], share_of(packs[0]))

    all_slots = mine * slots + 1
    gather, collect, degree, meta = call(
        prepare_kernel,
        "one_hots",
        (place, nbr_blocks, edge_count, jnp.swapaxes(edge_src, 1, 2), jnp.swapaxes(edge_dst, 1, 2), edge_dst),
        [SMEM] * 3 + [VMEM] * 3,
        (
            jax.ShapeDtypeStruct((all_slots, edges, 2 * edges), BF16),
            jax.ShapeDtypeStruct((all_slots, edges, edges), BF16),
            jax.ShapeDtypeStruct((rows, edges), F32),
            jax.ShapeDtypeStruct((4, LIST), jnp.int32),
        ),
        (VMEM, VMEM, VMEM, SMEM),
    )

    vectors = None
    for layer in range(LAYERS):
        final = layer == LAYERS - 1
        after = pass_on(latent)
        beyond = pass_on(after)
        if not final:
            beyond, share = lax.optimization_barrier((beyond, share_of(packs[layer + 1])))
        messages = w_msg[layer].reshape(4, part, width)
        outs = [jax.ShapeDtypeStruct((rows, width), F32), jax.ShapeDtypeStruct((rows, width), BF16)]
        inputs = [place, meta, latent, after, *weights]
        if layer == 0:
            outs.append(jax.ShapeDtypeStruct((4, VECTOR_ROWS, part), F32))
        else:
            inputs.append(vectors)
        inputs += [messages, msg_vectors, gather, collect]
        result = call(
            lambda *refs, layer=layer: near_kernel(layer, layer == 0, *refs),
            f"near{layer}",
            inputs,
            [SMEM, SMEM] + [VMEM] * (len(inputs) - 2),
            outs,
            [VMEM] * len(outs),
            [
                pltpu.VMEM((2 * rows, width), BF16),
                pltpu.VMEM((UNROLL * edges, width), BF16),
                pltpu.VMEM((UNROLL * edges, width), BF16),
            ],
        )
        acc, receive = result[0], result[1]
        if layer == 0:
            vectors = result[2]
        partial = call(
            lambda *refs, layer=layer: far_kernel(layer, *refs),
            f"far{layer}",
            [place, meta, beyond, *weights, messages, msg_vectors, gather, collect, acc, receive],
            [SMEM, SMEM] + [VMEM] * 11,
            jax.ShapeDtypeStruct((rows, width), BF16),
            VMEM,
            [
                pltpu.VMEM((rows, width), BF16),
                pltpu.VMEM((UNROLL * edges, width), BF16),
                pltpu.VMEM((UNROLL * edges, width), BF16),
                pltpu.VMEM((rows, width), F32),
            ],
        )
        theirs = exchange(partial, 1)
        if final:
            outs = [jax.ShapeDtypeStruct((rows, part), BF16)] * 2
        else:
            outs = [jax.ShapeDtypeStruct((4, rows, part), BF16)]
        result = call(
            lambda *refs, layer=layer, final=final: node_kernel(layer, final, *refs),
            f"node{layer}",
            [place, latent, partial, theirs, degree, *weights, vectors, msg_vectors, msg_gain],
            [SMEM] + [VMEM] * 11,
            outs,
            [VMEM] * len(outs),
        )
        if final:
            return call(
                join_kernel,
                "join",
                [place, result[0], exchange(result[1], 2)],
                [SMEM, VMEM, VMEM],
                jax.ShapeDtypeStruct((2 * rows, part), BF16),
                VMEM,
            )
        latent = result[0]
        weights = spread_weights(packs[layer + 1], share)


def solution(mesh):
    placed = (
        P("dom", "feat"),
        P(None, None, "feat"),
        P(None, None, "feat"),
        P(),
        P(None, None, "feat"),
        P(None, None, "feat"),
        P(),
        P(),
        P(None, None, "feat"),
        P(None, "feat"),
        P("dom", None),
        P("dom", None),
        P("dom", None, None),
        P("dom", None, None),
    )
    return jax.shard_map(
        per_device, mesh=mesh, in_specs=placed, out_specs=P("dom", "feat"), check_vma=False
    )
```

time: 138 us -> 131 us (0.949)
  starting transfers between devices: 65.1 us -> 46.2 us
  waiting for transfers between devices: 36.3 us -> 46.3 us
  Pallas kernels: 14.8 us -> 23.8 us
  blocking collectives: 8.42 us -> 0 us
  other arithmetic: 3.29 us -> 1.14 us
  local copies, waits for them, and re-layouts: 8.68 us -> 10.8 us
    ppermute x8 -> x4, starting transfers between devices: 38.3 us -> 8.21 us  [pass_on(): lax.ppermute(value, BOTH, [(i, t) for i, t in pairs if 0 <= t < total])]
    ppermute x10 -> x13, waiting for transfers between devices: 9.7 us -> 26.6 us  [exchange(): return lax.ppermute(value, BOTH, [(i, i ^ mask) for i in range(total)])]
    ppermute x10 -> x13, starting transfers between devices: 23 us -> 38 us  [exchange(): return lax.ppermute(value, BOTH, [(i, i ^ mask) for i in range(total)])]
    pallas_call x3 -> x8, Pallas kernels: 14.8 us -> 23.8 us  [call(): pl.pallas_call(kernel, out_shape=outs, in_specs=spaces, out_specs=out_spa...]
    all_to_all x1 -> x0, blocking collectives: 8.42 us -> none  [per_device(): lax.all_to_all(latent, 'feat', split_axis=0, concat_axis=0, tiled=True)]
    ppermute x8 -> x4, waiting for transfers between devices: 26.6 us -> 19.8 us  [pass_on(): lax.ppermute(value, BOTH, [(i, t) for i, t in pairs if 0 <= t < total])]
    all_to_all x1 -> x0, starting transfers between devices: 3.78 us -> none  [per_device(): lax.all_to_all(node_state.reshape(4, rows, part), 'feat', split_axis=0, c...]
    slice x1 -> x5, local copies, waits for them, and re-layouts: 0.07 us -> 2.82 us  [the longest x1 0.99 us: per_device(): w_src[layer]]
  transfers between devices with their start and end apart: 19 -> 17, of which waited for: 9 -> 9; matrix products, arithmetic and copies ran while one was open for 7% -> 6% of each run, Pallas kernels for 2% -> 12%
where the time goes in v2:
time: 131 us; the launch traced here: 129 us
  waiting for transfers between devices  46.3 us (35%)
  starting transfers between devices  46.2 us (35%)
  Pallas kernels  23.8 us (18%)
  local copies, waits for them, and re-layouts  10.8 us (8%)
    ppermute x13, starting transfers between devices, exchange(): return lax.ppermute(value, BOTH, [(i, i ^ mask) for i in range(total)])  38 us
    ppermute x13, waiting for transfers between devices, exchange(): return lax.ppermute(value, BOTH, [(i, i ^ mask) for i in range(total)])  26.6 us
    pallas_call x8, Pallas kernels, call(): pl.pallas_call(kernel, out_shape=outs, in_specs=spaces, out_specs=out_spa...  23.8 us
    ppermute x4, waiting for transfers between devices, pass_on(): lax.ppermute(value, BOTH, [(i, t) for i, t in pairs if 0 <= t < total])  19.8 us
    ppermute x4, starting transfers between devices, pass_on(): lax.ppermute(value, BOTH, [(i, t) for i, t in pairs if 0 <= t < total])  8.21 us
    unnamed x46, local copies, waits for them, and re-layouts  6.76 us
  transfers between devices with their start and end apart: 17, of which 9 were waited for; matrix products, arithmetic and copies ran while one was open for 6% of the time, Pallas kernels for 12%

profile of v2, /device:TPU:6, one launch (start us, length us, event | category | flops | bytes accessed | tf_op | source)
XLA Modules:
  0.0 128.9 jit_solution(15794431947403471600)
XLA Ops:
  1.1 4.3 %collective-permute-start = (bf16[512,128]{1,0:T(8,128)(2,1)S(1)}, bf16[512,128]{1,0:T(8,128)(2,1)S(1)}, u32[]{:S(2)}, u32[]{:S(2)}) collective-permute-start(bf16[512,128]{1,0:T(8,128)(2,1)S(1)} %get-tuple-element.44), channel_id=1, source_target_pairs={{0,2},{1,3},{2,0},{3,1},{4,6},{5,7},{6,4},{7,5},{8,10},{9,11},{10,... | collective-permute-start | bytes 393224 | tf_op jit(solution)/shard_map/ppermute | solution.py:29
  8.4 1.9 %collective-permute-start.5 = (bf16[1328,128]{1,0:T(8,128)(2,1)S(1)}, bf16[1328,128]{1,0:T(8,128)(2,1)S(1)}, u32[]{:S(2)}, u32[]{:S(2)}) collective-permute-start(bf16[1328,128]{1,0:T(8,128)(2,1)S(1)} %dynamic-slice_bitcast_fusion), channel_id=1, source_target_pairs={{0,2},{1,3},{2,0},{3,1},{4,6},{5,7},{6,4},{7,5},{8,10},{9,11},{10,... | collective-permute-start | bytes 1019912 | tf_op jit(solution)/shard_map/ppermute | solution.py:29
  10.4 2.1 %collective-permute-start.1 = (bf16[2,512,128]{2,1,0:T(8,128)(2,1)S(1)}, bf16[2,512,128]{2,1,0:T(8,128)(2,1)S(1)}, u32[]{:S(2)}, u32[]{:S(2)}) collective-permute-start(bf16[2,512,128]{2,1,0:T(8,128)(2,1)S(1)} %pad_maximum_fusion.3), channel_id=1, source_target_pairs={{0,1},{1,0},{2,3},{3,2},{4,5},{5,4},{6,7},{7,6},{8,9},{9,8},{10,11... | collective-permute-start | bytes 786440 | tf_op jit(solution)/shard_map/ppermute | solution.py:29
  12.5 2.4 %collective-permute-start.4 = (bf16[2,1328,128]{2,1,0:T(8,128)(2,1)S(1)}, bf16[2,1328,128]{2,1,0:T(8,128)(2,1)S(1)}, u32[]{:S(2)}, u32[]{:S(2)}) collective-permute-start(bf16[2,1328,128]{2,1,0:T(8,128)(2,1)S(1)} %constant_dynamic-update-slice_fusion.5.refs_4_.refs_3_.refs_5_), channel_id=1, source_target_pairs={{0,1},{1,0},{2,3},{3,2},{4,5},{5,4},{6,7},{7,6},{8,9},{9,8},{10,11... | collective-permute-start | bytes 2039816 | tf_op jit(solution)/shard_map/ppermute | solution.py:29
  15.0 4.8 %collective-permute-done.5 = bf16[1328,128]{1,0:T(8,128)(2,1)S(1)} collective-permute-done((bf16[1328,128]{1,0:T(8,128)(2,1)S(1)}, bf16[1328,128]{1,0:T(8,128)(2,1)S(1)}, u32[]{:S(2)}, u32[]{:S(2)}) %collective-permute-start.5) | collective-permute-done | bytes 340000 | tf_op jit(solution)/shard_map/ppermute | solution.py:29
  19.8 3.5 %collective-permute-start.6 = (bf16[1328,128]{1,0:T(8,128)(2,1)S(1)}, bf16[1328,128]{1,0:T(8,128)(2,1)S(1)}, u32[]{:S(2)}, u32[]{:S(2)}) collective-permute-start(bf16[1328,128]{1,0:T(8,128)(2,1)S(1)} %collective-permute-done.5), channel_id=1, source_target_pairs={{0,16},{1,17},{2,18},{3,19},{4,20},{5,21},{6,22},{7,23},{8,24},{9,... | collective-permute-start | bytes 1019912 | tf_op jit(solution)/shard_map/ppermute | solution.py:29
  24.2 2.2 %collective-permute-start.2 = (bf16[4,512,128]{2,1,0:T(8,128)(2,1)S(1)}, bf16[4,512,128]{2,1,0:T(8,128)(2,1)}, u32[]{:S(2)}, u32[]{:S(2)}) collective-permute-start(bf16[4,512,128]{2,1,0:T(8,128)(2,1)S(1)} %pad_maximum_fusion.2.refs_2_.refs_1_), channel_id=1, source_target_pairs={{0,2},{2,4},{3,1},{4,6},{5,3},{6,8},{7,5},{8,10},{9,7},{10,12},{11... | collective-permute-start | bytes 1572872 | tf_op jit(solution)/shard_map/ppermute | solution.py:35
  26.5 3.6 %collective-permute-done.6 = bf16[1328,128]{1,0:T(8,128)(2,1)S(1)} collective-permute-done((bf16[1328,128]{1,0:T(8,128)(2,1)S(1)}, bf16[1328,128]{1,0:T(8,128)(2,1)S(1)}, u32[]{:S(2)}, u32[]{:S(2)}) %collective-permute-start.6) | collective-permute-done | bytes 340000 | tf_op jit(solution)/shard_map/ppermute | solution.py:29
  30.2 6.2 %collective-permute-start.7 = (bf16[2,1328,128]{2,1,0:T(8,128)(2,1)S(1)}, bf16[2,1328,128]{2,1,0:T(8,128)(2,1)S(1)}, u32[]{:S(2)}, u32[]{:S(2)}) collective-permute-start(bf16[2,1328,128]{2,1,0:T(8,128)(2,1)S(1)} %pad_maximum_fusion.refs_6_.refs_5_.refs_7_), channel_id=1, source_target_pairs={{0,1},{1,0},{2,3},{3,2},{4,5},{5,4},{6,7},{7,6},{8,9},{9,8},{10,11... | collective-permute-start | bytes 2039816 | tf_op jit(solution)/shard_map/ppermute | solution.py:29
  36.5 7.0 %collective-permute-done.2.refs_3_ = bf16[4,512,128]{2,1,0:T(8,128)(2,1)} collective-permute-done((bf16[4,512,128]{2,1,0:T(8,128)(2,1)S(1)}, bf16[4,512,128]{2,1,0:T(8,128)(2,1)}, u32[]{:S(2)}, u32[]{:S(2)}) %collective-permute-start.2) | collective-permute-done | bytes 524320 | tf_op jit(solution)/shard_map/ppermute | solution.py:35
  43.6 1.9 %collective-permute-start.3 = (bf16[4,512,128]{2,1,0:T(8,128)(2,1)}, bf16[4,512,128]{2,1,0:T(8,128)(2,1)}, u32[]{:S(2)}, u32[]{:S(2)}) collective-permute-start(bf16[4,512,128]{2,1,0:T(8,128)(2,1)} %collective-permute-done.2.refs_3_), channel_id=1, source_target_pairs={{0,2},{2,4},{3,1},{4,6},{5,3},{6,8},{7,5},{8,10},{9,7},{10,12},{11... | collective-permute-start | bytes 1572872 | tf_op jit(solution)/shard_map/ppermute | solution.py:35
  51.3 2.4 %one_hots.1 = (bf16[25,128,256]{2,1,0:T(8,128)(2,1)S(1)}, bf16[25,128,128]{2,1,0:T(8,128)(2,1)S(1)}, f32[512,128]{1,0:T(8,128)S(1)}, s32[4,32]{1,0:T(4,128)S(1)}) custom-call(s32[6]{0:T(128)S(1)} %stack.52.place_ref.refs_0_, s32[8,6]{1,0:T(8,128)S(1)} %copy-done.6, s32[8,6]{1,0:T(8,128)S(1)} %copy-done.7, s32[8,128,6]{2,1,0:T(8,128)S(1)} %bitcast.40, ...), custom_call_target="tpu_custom_call" | custom-call | tf_op jit(solution)/shard_map/one_hots/pallas_call | solution.py:210
  54.7 6.1 %near0.1 = (f32[512,512]{1,0:T(8,128)S(1)}, bf16[512,512]{1,0:T(8,128)(2,1)S(1)}, f32[4,16,128]{2,1,0:T(8,128)S(1)}) custom-call(s32[6]{0:T(128)S(1)} %stack.52.place_ref.refs_0_, s32[4,32]{1,0:T(4,128)S(1)} %get-tuple-element.18.refs_1_, bf16[4,512,128]{2,1,0:T(8,128)(2,1)S(1)} %copy-done.1, bf16[4,512,128]{2,1,0:T(8,128)(2,1)} %collective-permute-done.2.refs_3_, ...), custom_call_target="tpu_custom_call" | custom-call | tf_op jit(solution)/shard_map/near0/pallas_call | solution.py:210
  60.9 2.6 %far0.1.refs_2_ = bf16[512,512]{1,0:T(8,128)(2,1)S(1)} custom-call(s32[6]{0:T(128)S(1)} %stack.52.place_ref.refs_0_, s32[4,32]{1,0:T(4,128)S(1)} %get-tuple-element.18.refs_1_, bf16[4,512,128]{2,1,0:T(8,128)(2,1)} %collective-permute-done.3.refs_2_, bf16[2,1328,128]{2,1,0:T(8,128)(2,1)S(1)} %constant_dynamic-update-slice_fusion.5.refs_4_.refs_3_.refs_5_, ...), custom_call_target="tpu_custom_call" | custom-call | tf_op jit(solution)/shard_map/far0/pallas_call | solution.py:210
  63.5 3.1 %collective-permute-start.8 = (bf16[512,512]{1,0:T(8,128)(2,1)S(1)}, bf16[512,512]{1,0:T(8,128)(2,1)S(1)}, u32[]{:S(2)}, u32[]{:S(2)}) collective-permute-start(bf16[512,512]{1,0:T(8,128)(2,1)S(1)} %far0.1.refs_2_), channel_id=1, source_target_pairs={{0,1},{1,0},{2,3},{3,2},{4,5},{5,4},{6,7},{7,6},{8,9},{9,8},{10,11... | collective-permute-start | bytes 1572872 | tf_op jit(solution)/shard_map/ppermute | solution.py:29
  66.5 1.9 %collective-permute-start.12 = (bf16[1280,128]{1,0:T(8,128)(2,1)S(1)}, bf16[1280,128]{1,0:T(8,128)(2,1)S(1)}, u32[]{:S(2)}, u32[]{:S(2)}) collective-permute-start(bf16[1280,128]{1,0:T(8,128)(2,1)S(1)} %dynamic-slice_bitcast_fusion.1), channel_id=1, source_target_pairs={{0,2},{1,3},{2,0},{3,1},{4,6},{5,7},{6,4},{7,5},{8,10},{9,11},{10,... | collective-permute-start | bytes 983048 | tf_op jit(solution)/shard_map/ppermute | solution.py:29
  68.5 9.6 %collective-permute-done.12 = bf16[1280,128]{1,0:T(8,128)(2,1)S(1)} collective-permute-done((bf16[1280,128]{1,0:T(8,128)(2,1)S(1)}, bf16[1280,128]{1,0:T(8,128)(2,1)S(1)}, u32[]{:S(2)}, u32[]{:S(2)}) %collective-permute-start.12) | collective-permute-done | bytes 327712 | tf_op jit(solution)/shard_map/ppermute | solution.py:29
  78.0 1.9 %collective-permute-start.13 = (bf16[1280,128]{1,0:T(8,128)(2,1)S(1)}, bf16[1280,128]{1,0:T(8,128)(2,1)S(1)}, u32[]{:S(2)}, u32[]{:S(2)}) collective-permute-start(bf16[1280,128]{1,0:T(8,128)(2,1)S(1)} %collective-permute-done.12), channel_id=1, source_target_pairs={{0,16},{1,17},{2,18},{3,19},{4,20},{5,21},{6,22},{7,23},{8,24},{9,... | collective-permute-start | bytes 983048 | tf_op jit(solution)/shard_map/ppermute | solution.py:29
  80.0 1.9 %node0.1.refs_2_.refs_1_ = bf16[4,512,128]{2,1,0:T(8,128)(2,1)S(1)} custom-call(s32[6]{0:T(128)S(1)} %stack.52.place_ref.refs_0_, bf16[4,512,128]{2,1,0:T(8,128)(2,1)S(1)} %copy-done.1, bf16[512,512]{1,0:T(8,128)(2,1)S(1)} %far0.1.refs_2_, bf16[512,512]{1,0:T(8,128)(2,1)S(1)} %collective-permute-done.8.refs_3_, f32[512,128]{1,0:T(8,128)S(1)} %get-tuple-element.24.refs_4_, ...), custom_call_target="tpu_custom_call" | custom-call | tf_op jit(solution)/shard_map/node0/pallas_call | solution.py:210
  81.9 2.2 %collective-permute-start.9 = (bf16[4,512,128]{2,1,0:T(8,128)(2,1)S(1)}, bf16[4,512,128]{2,1,0:T(8,128)(2,1)S(1)}, u32[]{:S(2)}, u32[]{:S(2)}) collective-permute-start(bf16[4,512,128]{2,1,0:T(8,128)(2,1)S(1)} %node0.1.refs_2_.refs_1_), channel_id=1, source_target_pairs={{0,2},{2,4},{3,1},{4,6},{5,3},{6,8},{7,5},{8,10},{9,7},{10,12},{11... | collective-permute-start | bytes 1572872 | tf_op jit(solution)/shard_map/ppermute | solution.py:35
  84.1 5.0 %collective-permute-start.11 = (bf16[2,1280,128]{2,1,0:T(8,128)(2,1)S(1)}, bf16[2,1280,128]{2,1,0:T(8,128)(2,1)S(1)}, u32[]{:S(2)}, u32[]{:S(2)}) collective-permute-start(bf16[2,1280,128]{2,1,0:T(8,128)(2,1)S(1)} %constant_dynamic-update-slice_fusion.refs_4_.refs_3_.refs_5_), channel_id=1, source_target_pairs={{0,1},{1,0},{2,3},{3,2},{4,5},{5,4},{6,7},{7,6},{8,9},{9,8},{10,11... | collective-permute-start | bytes 1966088 | tf_op jit(solution)/shard_map/ppermute | solution.py:29
  90.3 1.9 %collective-permute-start.14 = (bf16[2,1280,128]{2,1,0:T(8,128)(2,1)S(1)}, bf16[2,1280,128]{2,1,0:T(8,128)(2,1)S(1)}, u32[]{:S(2)}, u32[]{:S(2)}) collective-permute-start(bf16[2,1280,128]{2,1,0:T(8,128)(2,1)S(1)} %pad_maximum_fusion.1.refs_6_.refs_5_.refs_7_), channel_id=1, source_target_pairs={{0,1},{1,0},{2,3},{3,2},{4,5},{5,4},{6,7},{7,6},{8,9},{9,8},{10,11... | collective-permute-start | bytes 1966088 | tf_op jit(solution)/shard_map/ppermute | solution.py:29
  92.2 5.0 %collective-permute-done.9.refs_3_ = bf16[4,512,128]{2,1,0:T(8,128)(2,1)S(1)} collective-permute-done((bf16[4,512,128]{2,1,0:T(8,128)(2,1)S(1)}, bf16[4,512,128]{2,1,0:T(8,128)(2,1)S(1)}, u32[]{:S(2)}, u32[]{:S(2)}) %collective-permute-start.9) | collective-permute-done | bytes 524320 | tf_op jit(solution)/shard_map/ppermute | solution.py:35
  97.2 1.9 %collective-permute-start.10 = (bf16[4,512,128]{2,1,0:T(8,128)(2,1)S(1)}, bf16[4,512,128]{2,1,0:T(8,128)(2,1)S(1)}, u32[]{:S(2)}, u32[]{:S(2)}) collective-permute-start(bf16[4,512,128]{2,1,0:T(8,128)(2,1)S(1)} %collective-permute-done.9.refs_3_), channel_id=1, source_target_pairs={{0,2},{2,4},{3,1},{4,6},{5,3},{6,8},{7,5},{8,10},{9,7},{10,12},{11... | collective-permute-start | bytes 1572872 | tf_op jit(solution)/shard_map/ppermute | solution.py:35
  99.1 5.6 %near1.1 = (f32[512,512]{1,0:T(8,128)S(1)}, bf16[512,512]{1,0:T(8,128)(2,1)S(1)}) custom-call(s32[6]{0:T(128)S(1)} %stack.52.place_ref.refs_0_, s32[4,32]{1,0:T(4,128)S(1)} %get-tuple-element.18.refs_1_, bf16[4,512,128]{2,1,0:T(8,128)(2,1)S(1)} %node0.1.refs_2_.refs_1_, bf16[4,512,128]{2,1,0:T(8,128)(2,1)S(1)} %collective-permute-done.9.refs_3_, ...), custom_call_target="tpu_custom_call" | custom-call | tf_op jit(solution)/shard_map/near1/pallas_call | solution.py:210
  104.8 7.7 %collective-permute-done.10.refs_2_ = bf16[4,512,128]{2,1,0:T(8,128)(2,1)S(1)} collective-permute-done((bf16[4,512,128]{2,1,0:T(8,128)(2,1)S(1)}, bf16[4,512,128]{2,1,0:T(8,128)(2,1)S(1)}, u32[]{:S(2)}, u32[]{:S(2)}) %collective-permute-start.10) | collective-permute-done | bytes 524320 | tf_op jit(solution)/shard_map/ppermute | solution.py:35
  112.5 2.1 %far1.1.refs_2_ = bf16[512,512]{1,0:T(8,128)(2,1)S(1)} custom-call(s32[6]{0:T(128)S(1)} %stack.52.place_ref.refs_0_, s32[4,32]{1,0:T(4,128)S(1)} %get-tuple-element.18.refs_1_, bf16[4,512,128]{2,1,0:T(8,128)(2,1)S(1)} %collective-permute-done.10.refs_2_, bf16[2,1280,128]{2,1,0:T(8,128)(2,1)S(1)} %constant_dynamic-update-slice_fusion.refs_4_.refs_3_.refs_5_, ...), custom_call_target="tpu_custom_call" | custom-call | tf_op jit(solution)/shard_map/far1/pallas_call | solution.py:210
  114.6 1.9 %collective-permute-start.15 = (bf16[512,512]{1,0:T(8,128)(2,1)S(1)}, bf16[512,512]{1,0:T(8,128)(2,1)S(1)}, u32[]{:S(2)}, u32[]{:S(2)}) collective-permute-start(bf16[512,512]{1,0:T(8,128)(2,1)S(1)} %far1.1.refs_2_), channel_id=1, source_target_pairs={{0,1},{1,0},{2,3},{3,2},{4,5},{5,4},{6,7},{7,6},{8,9},{9,8},{10,11... | collective-permute-start | bytes 1572872 | tf_op jit(solution)/shard_map/ppermute | solution.py:29
  116.5 1.9 %collective-permute-done.15.refs_3_ = bf16[512,512]{1,0:T(8,128)(2,1)S(1)} collective-permute-done((bf16[512,512]{1,0:T(8,128)(2,1)S(1)}, bf16[512,512]{1,0:T(8,128)(2,1)S(1)}, u32[]{:S(2)}, u32[]{:S(2)}) %collective-permute-start.15) | collective-permute-done | bytes 524320 | tf_op jit(solution)/shard_map/ppermute | solution.py:29
  118.4 1.8 %node1.1 = (bf16[512,128]{1,0:T(8,128)(2,1)S(1)}, bf16[512,128]{1,0:T(8,128)(2,1)S(1)}) custom-call(s32[6]{0:T(128)S(1)} %stack.52.place_ref.refs_0_, bf16[4,512,128]{2,1,0:T(8,128)(2,1)S(1)} %node0.1.refs_2_.refs_1_, bf16[512,512]{1,0:T(8,128)(2,1)S(1)} %far1.1.refs_2_, bf16[512,512]{1,0:T(8,128)(2,1)S(1)} %collective-permute-done.15.refs_3_, ...), custom_call_target="tpu_custom_call" | custom-call | tf_op jit(solution)/shard_map/node1/pallas_call | solution.py:210
  120.2 1.9 %collective-permute-start.16 = (bf16[512,128]{1,0:T(8,128)(2,1)S(1)}, bf16[512,128]{1,0:T(8,128)(2,1)S(1)}, u32[]{:S(2)}, u32[]{:S(2)}) collective-permute-start(bf16[512,128]{1,0:T(8,128)(2,1)S(1)} %get-tuple-element.30), channel_id=1, source_target_pairs={{0,2},{1,3},{2,0},{3,1},{4,6},{5,7},{6,4},{7,5},{8,10},{9,11},{10,... | collective-permute-start | bytes 393224 | tf_op jit(solution)/shard_map/ppermute | solution.py:29
  122.1 5.5 %collective-permute-done.16.other_ref = bf16[512,128]{1,0:T(8,128)(2,1)S(1)} collective-permute-done((bf16[512,128]{1,0:T(8,128)(2,1)S(1)}, bf16[512,128]{1,0:T(8,128)(2,1)S(1)}, u32[]{:S(2)}, u32[]{:S(2)}) %collective-permute-start.16) | collective-permute-done | bytes 131104 | tf_op jit(solution)/shard_map/ppermute | solution.py:29
  (75 shorter events, 14.4 us)
Async XLA Ops:
  0.0 7.4 %copy-start.9 = (bf16[2,1024,128]{2,1,0:T(8,128)(2,1)S(1)}, bf16[2,1024,128]{2,1,0:T(8,128)(2,1)}, u32[]{:S(2)}) copy-start(bf16[2,1024,128]{2,1,0:T(8,128)(2,1)} %param.18) | copy-start | bytes 1572868
  0.0 8.2 %copy-start.13 = (bf16[2,512,128]{2,1,0:T(8,128)(2,1)S(1)}, bf16[2,512,128]{2,1,0:T(8,128)(2,1)}, u32[]{:S(2)}) copy-start(bf16[2,512,128]{2,1,0:T(8,128)(2,1)} %param.19) | copy-start | bytes 786436
  0.0 8.2 %copy-start.15 = (f32[2,4,128]{2,1,0:T(4,128)S(1)}, f32[2,4,128]{2,1,0:T(4,128)}, u32[]{:S(2)}) copy-start(f32[2,4,128]{2,1,0:T(4,128)} %param.22) | copy-start | bytes 12292
  0.0 8.2 %copy-start.16 = (f32[2,128]{1,0:T(2,128)S(1)}, f32[2,128]{1,0:T(2,128)}, u32[]{:S(2)}) copy-start(f32[2,128]{1,0:T(2,128)} %param.23) | copy-start | bytes 3076
  1.1 9.3 %collective-permute-start = (bf16[512,128]{1,0:T(8,128)(2,1)S(1)}, bf16[512,128]{1,0:T(8,128)(2,1)S(1)}, u32[]{:S(2)}, u32[]{:S(2)}) collective-permute-start(bf16[512,128]{1,0:T(8,128)(2,1)S(1)} %get-tuple-element.44), channel_id=1, source_target_pairs={{0,2},{1,3},{2,0},{3,1},{4,6},{5,7},{6,4},{7,5},{8,10},{9,11},{10,... | collective-permute-start | bytes 393224 | tf_op jit(solution)/shard_map/ppermute | solution.py:29
  8.3 18.2 %copy-start.11 = (bf16[1,512,128]{2,1,0:T(8,128)(2,1)S(1)}, bf16[1,512,128]{2,1,0:T(8,128)(2,1)}, u32[]{:S(2)}) copy-start(bf16[1,512,128]{2,1,0:T(8,128)(2,1)} %get-tuple-element.35) | copy-start | bytes 393220
  8.4 11.3 %collective-permute-start.5 = (bf16[1328,128]{1,0:T(8,128)(2,1)S(1)}, bf16[1328,128]{1,0:T(8,128)(2,1)S(1)}, u32[]{:S(2)}, u32[]{:S(2)}) collective-permute-start(bf16[1328,128]{1,0:T(8,128)(2,1)S(1)} %dynamic-slice_bitcast_fusion), channel_id=1, source_target_pairs={{0,2},{1,3},{2,0},{3,1},{4,6},{5,7},{6,4},{7,5},{8,10},{9,11},{10,... | collective-permute-start | bytes 1019912 | tf_op jit(solution)/shard_map/ppermute | solution.py:29
  10.4 4.5 %copy-start.12 = (bf16[512,128]{1,0:T(8,128)(2,1)}, bf16[512,128]{1,0:T(8,128)(2,1)S(1)}, u32[]{:S(2)}) copy-start(bf16[512,128]{1,0:T(8,128)(2,1)S(1)} %collective-permute-done) | copy-start | bytes 393220
  10.4 26.1 %copy-start.10 = (bf16[1,512,128]{2,1,0:T(8,128)(2,1)S(1)}, bf16[1,512,128]{2,1,0:T(8,128)(2,1)}, u32[]{:S(2)}) copy-start(bf16[1,512,128]{2,1,0:T(8,128)(2,1)} %get-tuple-element.34) | copy-start | bytes 393220
  10.4 12.8 %collective-permute-start.1 = (bf16[2,512,128]{2,1,0:T(8,128)(2,1)S(1)}, bf16[2,512,128]{2,1,0:T(8,128)(2,1)S(1)}, u32[]{:S(2)}, u32[]{:S(2)}) collective-permute-start(bf16[2,512,128]{2,1,0:T(8,128)(2,1)S(1)} %pad_maximum_fusion.3), channel_id=1, source_target_pairs={{0,1},{1,0},{2,3},{3,2},{4,5},{5,4},{6,7},{7,6},{8,9},{9,8},{10,11... | collective-permute-start | bytes 786440 | tf_op jit(solution)/shard_map/ppermute | solution.py:29
  12.5 41.3 %collective-permute-start.4 = (bf16[2,1328,128]{2,1,0:T(8,128)(2,1)S(1)}, bf16[2,1328,128]{2,1,0:T(8,128)(2,1)S(1)}, u32[]{:S(2)}, u32[]{:S(2)}) collective-permute-start(bf16[2,1328,128]{2,1,0:T(8,128)(2,1)S(1)} %constant_dynamic-update-slice_fusion.5.refs_4_.refs_3_.refs_5_), channel_id=1, source_target_pairs={{0,1},{1,0},{2,3},{3,2},{4,5},{5,4},{6,7},{7,6},{8,9},{9,8},{10,11... | collective-permute-start | bytes 2039816 | tf_op jit(solution)/shard_map/ppermute | solution.py:29
  14.9 30.6 %copy-start.14 = (s32[8,6,128]{2,0,1:T(8,128)S(1)}, s32[8,6,128]{2,0,1:T(8,128)}, u32[]{:S(2)}) copy-start(s32[8,6,128]{2,0,1:T(8,128)} %param.27) | copy-start | bytes 73732
  19.8 10.4 %collective-permute-start.6 = (bf16[1328,128]{1,0:T(8,128)(2,1)S(1)}, bf16[1328,128]{1,0:T(8,128)(2,1)S(1)}, u32[]{:S(2)}, u32[]{:S(2)}) collective-permute-start(bf16[1328,128]{1,0:T(8,128)(2,1)S(1)} %collective-permute-done.5), channel_id=1, source_target_pairs={{0,16},{1,17},{2,18},{3,19},{4,20},{5,21},{6,22},{7,23},{8,24},{9,... | collective-permute-start | bytes 1019912 | tf_op jit(solution)/shard_map/ppermute | solution.py:29
  24.2 21.3 %copy-start = (bf16[4,512,128]{2,1,0:T(8,128)(2,1)}, bf16[4,512,128]{2,1,0:T(8,128)(2,1)S(1)}, u32[]{:S(2)}) copy-start(bf16[4,512,128]{2,1,0:T(8,128)(2,1)S(1)} %pad_maximum_fusion.2.refs_2_.refs_1_) | copy-start | bytes 1572868
  24.2 19.3 %collective-permute-start.2 = (bf16[4,512,128]{2,1,0:T(8,128)(2,1)S(1)}, bf16[4,512,128]{2,1,0:T(8,128)(2,1)}, u32[]{:S(2)}, u32[]{:S(2)}) collective-permute-start(bf16[4,512,128]{2,1,0:T(8,128)(2,1)S(1)} %pad_maximum_fusion.2.refs_2_.refs_1_), channel_id=1, source_target_pairs={{0,2},{2,4},{3,1},{4,6},{5,3},{6,8},{7,5},{8,10},{9,7},{10,12},{11... | collective-permute-start | bytes 1572872 | tf_op jit(solution)/shard_map/ppermute | solution.py:35
  26.5 22.7 %copy-start.6 = (s32[8,6]{1,0:T(8,128)S(1)}, s32[8,6]{1,0:T(8,128)}, u32[]{:S(2)}) copy-start(s32[8,6]{1,0:T(8,128)} %nbr_ref.1) | copy-start | bytes 580
  26.5 22.7 %copy-start.7 = (s32[8,6]{1,0:T(8,128)S(1)}, s32[8,6]{1,0:T(8,128)}, u32[]{:S(2)}) copy-start(s32[8,6]{1,0:T(8,128)} %count_ref.1) | copy-start | bytes 580
  30.2 23.6 %collective-permute-start.7 = (bf16[2,1328,128]{2,1,0:T(8,128)(2,1)S(1)}, bf16[2,1328,128]{2,1,0:T(8,128)(2,1)S(1)}, u32[]{:S(2)}, u32[]{:S(2)}) collective-permute-start(bf16[2,1328,128]{2,1,0:T(8,128)(2,1)S(1)} %pad_maximum_fusion.refs_6_.refs_5_.refs_7_), channel_id=1, source_target_pairs={{0,1},{1,0},{2,3},{3,2},{4,5},{5,4},{6,7},{7,6},{8,9},{9,8},{10,11... | collective-permute-start | bytes 2039816 | tf_op jit(solution)/shard_map/ppermute | solution.py:29
  43.6 17.3 %collective-permute-start.3 = (bf16[4,512,128]{2,1,0:T(8,128)(2,1)}, bf16[4,512,128]{2,1,0:T(8,128)(2,1)}, u32[]{:S(2)}, u32[]{:S(2)}) collective-permute-start(bf16[4,512,128]{2,1,0:T(8,128)(2,1)} %collective-permute-done.2.refs_3_), channel_id=1, source_target_pairs={{0,2},{2,4},{3,1},{4,6},{5,3},{6,8},{7,5},{8,10},{9,7},{10,12},{11... | collective-permute-start | bytes 1572872 | tf_op jit(solution)/shard_map/ppermute | solution.py:35
  49.2 1.0 copy-start.2
  51.3 2.5 %copy-start.8 = (bf16[2,512,512]{2,1,0:T(8,128)(2,1)S(1)}, bf16[2,512,512]{2,1,0:T(8,128)(2,1)}, u32[]{:S(2)}) copy-start(bf16[2,512,512]{2,1,0:T(8,128)(2,1)} %param.17) | copy-start | bytes 3145732
  53.7 1.0 copy-start.1
  60.9 19.1 %copy-start.5 = (f32[2,512]{1,0:T(2,128)S(1)}, f32[2,512]{1,0:T(2,128)}, u32[]{:S(2)}) copy-start(f32[2,512]{1,0:T(2,128)} %refs_11_.3) | copy-start | bytes 12292
  63.5 16.5 %collective-permute-start.8 = (bf16[512,512]{1,0:T(8,128)(2,1)S(1)}, bf16[512,512]{1,0:T(8,128)(2,1)S(1)}, u32[]{:S(2)}, u32[]{:S(2)}) collective-permute-start(bf16[512,512]{1,0:T(8,128)(2,1)S(1)} %far0.1.refs_2_), channel_id=1, source_target_pairs={{0,1},{1,0},{2,3},{3,2},{4,5},{5,4},{6,7},{7,6},{8,9},{9,8},{10,11... | collective-permute-start | bytes 1572872 | tf_op jit(solution)/shard_map/ppermute | solution.py:29
  66.5 11.5 %collective-permute-start.12 = (bf16[1280,128]{1,0:T(8,128)(2,1)S(1)}, bf16[1280,128]{1,0:T(8,128)(2,1)S(1)}, u32[]{:S(2)}, u32[]{:S(2)}) collective-permute-start(bf16[1280,128]{1,0:T(8,128)(2,1)S(1)} %dynamic-slice_bitcast_fusion.1), channel_id=1, source_target_pairs={{0,2},{1,3},{2,0},{3,1},{4,6},{5,7},{6,4},{7,5},{8,10},{9,11},{10,... | collective-permute-start | bytes 983048 | tf_op jit(solution)/shard_map/ppermute | solution.py:29
  78.0 12.2 %collective-permute-start.13 = (bf16[1280,128]{1,0:T(8,128)(2,1)S(1)}, bf16[1280,128]{1,0:T(8,128)(2,1)S(1)}, u32[]{:S(2)}, u32[]{:S(2)}) collective-permute-start(bf16[1280,128]{1,0:T(8,128)(2,1)S(1)} %collective-permute-done.12), channel_id=1, source_target_pairs={{0,16},{1,17},{2,18},{3,19},{4,20},{5,21},{6,22},{7,23},{8,24},{9,... | collective-permute-start | bytes 983048 | tf_op jit(solution)/shard_map/ppermute | solution.py:29
  81.9 15.3 %collective-permute-start.9 = (bf16[4,512,128]{2,1,0:T(8,128)(2,1)S(1)}, bf16[4,512,128]{2,1,0:T(8,128)(2,1)S(1)}, u32[]{:S(2)}, u32[]{:S(2)}) collective-permute-start(bf16[4,512,128]{2,1,0:T(8,128)(2,1)S(1)} %node0.1.refs_2_.refs_1_), channel_id=1, source_target_pairs={{0,2},{2,4},{3,1},{4,6},{5,3},{6,8},{7,5},{8,10},{9,7},{10,12},{11... | collective-permute-start | bytes 1572872 | tf_op jit(solution)/shard_map/ppermute | solution.py:35
  84.1 15.0 %collective-permute-start.11 = (bf16[2,1280,128]{2,1,0:T(8,128)(2,1)S(1)}, bf16[2,1280,128]{2,1,0:T(8,128)(2,1)S(1)}, u32[]{:S(2)}, u32[]{:S(2)}) collective-permute-start(bf16[2,1280,128]{2,1,0:T(8,128)(2,1)S(1)} %constant_dynamic-update-slice_fusion.refs_4_.refs_3_.refs_5_), channel_id=1, source_target_pairs={{0,1},{1,0},{2,3},{3,2},{4,5},{5,4},{6,7},{7,6},{8,9},{9,8},{10,11... | collective-permute-start | bytes 1966088 | tf_op jit(solution)/shard_map/ppermute | solution.py:29
  90.3 8.9 %collective-permute-start.14 = (bf16[2,1280,128]{2,1,0:T(8,128)(2,1)S(1)}, bf16[2,1280,128]{2,1,0:T(8,128)(2,1)S(1)}, u32[]{:S(2)}, u32[]{:S(2)}) collective-permute-start(bf16[2,1280,128]{2,1,0:T(8,128)(2,1)S(1)} %pad_maximum_fusion.1.refs_6_.refs_5_.refs_7_), channel_id=1, source_target_pairs={{0,1},{1,0},{2,3},{3,2},{4,5},{5,4},{6,7},{7,6},{8,9},{9,8},{10,11... | collective-permute-start | bytes 1966088 | tf_op jit(solution)/shard_map/ppermute | solution.py:29
  97.2 15.3 %collective-permute-start.10 = (bf16[4,512,128]{2,1,0:T(8,128)(2,1)S(1)}, bf16[4,512,128]{2,1,0:T(8,128)(2,1)S(1)}, u32[]{:S(2)}, u32[]{:S(2)}) collective-permute-start(bf16[4,512,128]{2,1,0:T(8,128)(2,1)S(1)} %collective-permute-done.9.refs_3_), channel_id=1, source_target_pairs={{0,2},{2,4},{3,1},{4,6},{5,3},{6,8},{7,5},{8,10},{9,7},{10,12},{11... | collective-permute-start | bytes 1572872 | tf_op jit(solution)/shard_map/ppermute | solution.py:35
  114.6 3.8 %collective-permute-start.15 = (bf16[512,512]{1,0:T(8,128)(2,1)S(1)}, bf16[512,512]{1,0:T(8,128)(2,1)S(1)}, u32[]{:S(2)}, u32[]{:S(2)}) collective-permute-start(bf16[512,512]{1,0:T(8,128)(2,1)S(1)} %far1.1.refs_2_), channel_id=1, source_target_pairs={{0,1},{1,0},{2,3},{3,2},{4,5},{5,4},{6,7},{7,6},{8,9},{9,8},{10,11... | collective-permute-start | bytes 1572872 | tf_op jit(solution)/shard_map/ppermute | solution.py:29
  120.2 7.4 %collective-permute-start.16 = (bf16[512,128]{1,0:T(8,128)(2,1)S(1)}, bf16[512,128]{1,0:T(8,128)(2,1)S(1)}, u32[]{:S(2)}, u32[]{:S(2)}) collective-permute-start(bf16[512,128]{1,0:T(8,128)(2,1)S(1)} %get-tuple-element.30), channel_id=1, source_target_pairs={{0,2},{1,3},{2,0},{3,1},{4,6},{5,7},{6,4},{7,5},{8,10},{9,11},{10,... | collective-permute-start | bytes 393224 | tf_op jit(solution)/shard_map/ppermute | solution.py:29
  (2 other events, 2.1 us)

commit v3 on v2

--- a/solution.py
+++ b/solution.py
@@ -35,7 +35,18 @@
     return lax.ppermute(value, BOTH, [(i, t) for i, t in pairs if 0 <= t < total])
 
 
-def prepare_kernel(place_ref, nbr_ref, count_ref, src_ref, dst_ref, dst_row_ref, gather_ref, collect_ref, degree_ref, meta_ref):
+def from_other_side(value):
+    total = lax.axis_size(BOTH)
+    pairs = []
+    for i in range(total):
+        column, low = divmod(i, 16)
+        z, core = divmod(low, 2)
+        z = (z + (1 if z % 2 else -1)) % 8
+        pairs.append((i, column * 16 + z * 2 + core))
+    return lax.ppermute(value, BOTH, pairs)
+
+
+def prepare_kernel(place_ref, nbr_ref, count_ref, src_ref, dst_ref, gather_ref, collect_ref, degree_ref, meta_ref, turned):
     last, edges, _ = gather_ref.shape
     slots = nbr_ref.shape[1]
     blocks = last // slots
@@ -47,15 +58,17 @@
         meta_ref[1, i] = last - 1
         meta_ref[2, i] = 0
     near, far = jnp.int32(0), jnp.int32(0)
+    turned[...] = jnp.zeros_like(turned)
     for j in range(blocks):
-        to = dst_ref[first + j]
-        frm = src_ref[first + j]
-        to_row = dst_row_ref[first + j]
+        turned[0:slots, :] = src_ref[first + j].astype(F32)
+        turned[8 : 8 + slots, :] = dst_ref[first + j].astype(F32)
+        columns = turned[...].T.astype(jnp.int32)
+        to_row = dst_ref[first + j]
         degree = jnp.zeros((edges, edges), F32)
         for k in range(slots):
             s = j * slots + k
-            gather_ref[s, :, :edges] = (to[:, k : k + 1] == lanes).astype(F32).astype(BF16)
-            gather_ref[s, :, edges:] = (frm[:, k : k + 1] == lanes).astype(F32).astype(BF16)
+            gather_ref[s, :, :edges] = (columns[:, 8 + k : 9 + k] == lanes).astype(F32).astype(BF16)
+            gather_ref[s, :, edges:] = (columns[:, k : k + 1] == lanes).astype(F32).astype(BF16)
             live = ((to_row[k : k + 1, :] == rows) & (lanes < count_ref[first + j, k])).astype(F32)
             collect_ref[s] = live.astype(BF16)
             degree = degree + live
@@ -86,23 +99,43 @@
     collect_ref[last - 1] = jnp.zeros(collect_ref.shape[1:], BF16)
 
 
+def first_pack_kernel(src_ref, dst_ref, vec_ref, gain_ref, out_ref):
+    width = src_ref.shape[1]
+    out_ref[:width, :] = src_ref[0]
+    out_ref[width : 2 * width, :] = dst_ref[0]
+    rest = jnp.concatenate(
+        [part for layer in range(LAYERS) for part in (vec_ref[layer], gain_ref[layer : layer + 1, :])]
+        + [jnp.zeros((VECTOR_ROWS - 5 * LAYERS, src_ref.shape[2]), F32)],
+        axis=0,
+    )
+    for i in range(3):
+        at = 2 * width + i * VECTOR_ROWS
+        piece = rest.astype(BF16)
+        out_ref[at : at + VECTOR_ROWS, :] = piece
+        rest = rest - piece.astype(F32)
+
+
+def other_packs_kernel(src_ref, dst_ref, in_ref, out_w_ref, node_ref, next_ref):
+    width = src_ref.shape[1]
+    node_ref[: 2 * width, :] = in_ref[0]
+    node_ref[2 * width :, :] = out_w_ref[0]
+    next_ref[:width, :] = src_ref[1]
+    next_ref[width : 2 * width, :] = dst_ref[1]
+    next_ref[2 * width : 4 * width, :] = in_ref[1]
+    next_ref[4 * width :, :] = out_w_ref[1]
+
+
 def wide(ref, order=STRAIGHT):
     return jnp.concatenate([ref[i] for i in order], axis=1)
 
 
-def weight(shards, f, half, base, mixed):
-    part = shards[0].shape[-1]
+def weight(shards, f, base, mixed):
+    own, across, beside = shards
+    part = own.shape[-1]
     rows = []
     for i in range(4):
-        g = f ^ ORDER[i] if mixed else i
-        cols = []
-        for m, w in enumerate(shards):
-            at = g // 2 if m < 2 else (g // 2) ^ half
-            start = base + (g % 2) * part
-            if mixed:
-                start = pl.multiple_of(start, part)
-            cols.append(w[at, pl.ds(start, part), :])
-        rows.append(jnp.concatenate(cols, axis=1))
+        at = pl.ds(pl.multiple_of(base + (f ^ ORDER[i]) * part, part) if mixed else base + i * part, part)
+        rows.append(jnp.concatenate([own[at, :], beside[0, at, :], across[at, :], beside[1, at, :]], axis=1))
     return jnp.concatenate(rows, axis=0)
 
 
@@ -114,7 +147,7 @@
 def run_edges(which, shift, layer, f, meta_ref, receive, window, gather_ref, collect_ref, wmsg_ref, mvec_ref, hidden, normed, acc):
     slots = 6
     edges = gather_ref.shape[1]
-    w_msg = jnp.concatenate([wmsg_ref[f ^ m] for m in range(4)], axis=0)
+    w_msg = jnp.concatenate([wmsg_ref[4 * layer + (f ^ m)] for m in range(4)], axis=0)
     bias = mvec_ref[layer, 0:1, :]
 
     def body(step, carry):
@@ -142,50 +175,49 @@
     lax.fori_loop(0, (meta_ref[3, which] + UNROLL - 1) // UNROLL, body, 0)
 
 
-def near_kernel(layer, first, place_ref, meta_ref, h_ref, next_ref, w0, w1, w2, w3, *refs):
+def near_kernel(layer, first, place_ref, meta_ref, h_ref, next_ref, w_own, w_across, w_beside, *refs):
     if first:
         wmsg_ref, mvec_ref, gather_ref, collect_ref, acc, receive, vectors, window, hidden, normed = refs
     else:
         vectors, wmsg_ref, mvec_ref, gather_ref, collect_ref, acc, receive, window, hidden, normed = refs
-    f, half = place_ref[0], place_ref[4]
-    shards = (w0, w1, w2, w3)
-    edges = gather_ref.shape[1]
+    f = place_ref[0]
+    shards = (w_own, w_across, w_beside)
     if first:
-        end = w0.shape[1] - 3 * VECTOR_ROWS
-        for m, w in enumerate(shards):
-            rows = w[0, end : end + 3 * VECTOR_ROWS, :].astype(F32)
+        end = w_own.shape[0] - 3 * VECTOR_ROWS
+        for m, w in enumerate((w_own, w_beside.at[0], w_across, w_beside.at[1])):
+            rows = w[end : end + 3 * VECTOR_ROWS, :].astype(F32)
             vectors[m] = rows[:VECTOR_ROWS] + rows[VECTOR_ROWS : 2 * VECTOR_ROWS] + rows[2 * VECTOR_ROWS :]
-    w_src = weight(shards, f, half, 0, True)
+    w_src = weight(shards, f, 0, True)
     own = wide(h_ref)
-    block = own.shape[0]
+    block, width = own.shape
     window[:block, :] = dot(own, w_src).astype(BF16)
     window[block:, :] = dot(wide(next_ref, FLIPPED), w_src).astype(BF16)
-    receive[...] = (dot(own, weight(shards, f, half, 2 * edges, True)) + vector(vectors, layer, 0)).astype(BF16)
+    receive[...] = (dot(own, weight(shards, f, width, True)) + vector(vectors, layer, 0)).astype(BF16)
     acc[...] = jnp.zeros_like(acc)
     run_edges(0, 0, layer, f, meta_ref, receive, window, gather_ref, collect_ref, wmsg_ref, mvec_ref, hidden, normed, acc)
 
 
-def far_kernel(layer, place_ref, meta_ref, after_ref, w0, w1, w2, w3, wmsg_ref, mvec_ref, gather_ref, collect_ref, acc_in, receive, out_ref, window, hidden, normed, acc):
-    f, half = place_ref[0], place_ref[4]
-    edges = gather_ref.shape[1]
-    window[...] = dot(wide(after_ref), weight((w0, w1, w2, w3), f, half, 0, True)).astype(BF16)
+def far_kernel(layer, place_ref, meta_ref, after_ref, w_own, w_across, w_beside, wmsg_ref, mvec_ref, gather_ref, collect_ref, acc_in, receive, out_ref, window, hidden, normed, acc):
+    f = place_ref[0]
+    window[...] = dot(wide(after_ref), weight((w_own, w_across, w_beside), f, 0, True)).astype(BF16)
     acc[...] = acc_in[...]
     run_edges(1, 8, layer, f, meta_ref, receive, window, gather_ref, collect_ref, wmsg_ref, mvec_ref, hidden, normed, acc)
     out_ref[...] = acc[...].astype(BF16)
 
 
-def node_kernel(layer, final, place_ref, h_ref, part_a, part_b, degree_ref, w0, w1, w2, w3, vectors, mvec_ref, mgain_ref, *outs):
-    f, half = place_ref[0], place_ref[4]
-    shards = (w0, w1, w2, w3)
+def node_kernel(layer, final, place_ref, h_ref, part_a, part_b, degree_ref, w_own, w_across, w_beside, vectors, mvec_ref, mgain_ref, *outs):
+    f = place_ref[0]
+    shards = (w_own, w_across, w_beside)
     part = h_ref.shape[-1]
-    step = 2 * part
+    width = 4 * part
+    base = w_own.shape[0] - 3 * width
     total = part_a[...].astype(F32) + part_b[...].astype(F32)
     agg = total * mgain_ref[layer : layer + 1, :] + degree_ref[:, 0:1] * mvec_ref[layer, 1:2, :]
-    pre = dot(wide(h_ref), weight(shards, f, half, 2 * step, True))
-    pre = pre + dot(agg.astype(BF16), weight(shards, f, half, 3 * step, False)) + vector(vectors, layer, 1)
+    pre = dot(wide(h_ref), weight(shards, f, base, True))
+    pre = pre + dot(agg.astype(BF16), weight(shards, f, base + width, False)) + vector(vectors, layer, 1)
     inner = jnp.maximum(pre, 0.0).astype(BF16)
     inner = jnp.concatenate([inner[:, m * part : (m + 1) * part] for m in ORDER], axis=1)
-    node = dot(inner, weight(shards, f, half, 4 * step, True)) + vector(vectors, layer, 2)
+    node = dot(inner, weight(shards, f, base + 2 * width, True)) + vector(vectors, layer, 2)
     centred = node - jnp.mean(node, axis=1, keepdims=True)
     spread = jnp.mean(centred * centred, axis=1, keepdims=True)
     change = centred * lax.rsqrt(spread + EPSILON) * vector(vectors, layer, 4) + vector(vectors, layer, 3)
@@ -201,12 +233,12 @@
 
 def join_kernel(place_ref, own_ref, other_ref, out_ref):
     rows = own_ref.shape[0]
-    side = place_ref[5]
+    side = place_ref[4]
     out_ref[pl.ds(pl.multiple_of(side * rows, rows), rows), :] = own_ref[...]
     out_ref[pl.ds(pl.multiple_of((1 - side) * rows, rows), rows), :] = other_ref[...]
 
 
-def call(kernel, name, inputs, spaces, outs, out_spaces, scratch=()):
+def call(kernel, name, inputs, spaces, outs, out_spaces, scratch=(), us=2):
     return pl.pallas_call(
         kernel,
         out_shape=outs,
@@ -214,6 +246,7 @@
         out_specs=out_spaces,
         scratch_shapes=list(scratch),
         compiler_params=pltpu.CompilerParams(vmem_limit_bytes=32 * 1024 * 1024),
+        cost_estimate=pl.CostEstimate(flops=int(us * 1e9), bytes_accessed=1 << 20, transcendentals=0),
         name=name,
     )(*inputs)
 
@@ -243,51 +276,43 @@
     feat = lax.axis_index("feat")
     dom = lax.axis_index("dom")
     side = feat // 2
-    half = (dom // 4) % 2
-    place = jnp.stack(
-        [feat, feat % 2, side * mine, dom * block_count + side * mine, half, side]
-    ).astype(jnp.int32)
-
-    vec = jnp.concatenate([node_vectors, node_gain[:, None, :]], axis=1).reshape(LAYERS * 5, part)
-    vec = jnp.pad(vec, ((0, VECTOR_ROWS - LAYERS * 5), (0, 0)))
-    high = lax.reduce_precision(vec, 8, 7)
-    middle = lax.reduce_precision(vec - high, 8, 7)
-    low = vec - high - middle
-    thirds = jnp.concatenate([high, middle, low], axis=0).astype(BF16)
-    packs = []
-    for layer in range(LAYERS):
-        group = [
-            w.reshape(2, width // 2, part)
-            for w in (
-                w_src[layer], w_dst[layer], w_node_in[layer, :width], w_node_in[layer, width:], w_node_out[layer],
-            )
-        ]
-        if layer == 0:
-            group.append(jnp.broadcast_to(thirds[None], (2,) + thirds.shape))
-        packs.append(jnp.concatenate(group, axis=1))
-
-    def spread_weights(pack, share):
-        beside = exchange(pack, 1)
-        across = exchange(share, 2)
-        across = jnp.stack([across, exchange(across, 16)])
-        return pack, beside, across, exchange(across, 1)
-
-    def share_of(pack):
-        return lax.dynamic_index_in_dim(pack, half, 0, keepdims=False)
+    place = jnp.stack([feat, feat % 2, side * mine, dom * block_count + side * mine, side]).astype(jnp.int32)
+    barrier = lax.optimization_barrier
 
     halves = node_state.reshape(2, rows, part)
     own = lax.dynamic_index_in_dim(halves, side, 0, keepdims=False)
     other = lax.dynamic_index_in_dim(halves, 1 - side, 0, keepdims=False)
-    pair = jnp.stack([own, exchange(other, 2)])
+    across = exchange(other, 2)
+    first = call(
+        first_pack_kernel,
+        "first_pack",
+        (w_src, w_dst, node_vectors, node_gain),
+        [VMEM] * 4,
+        jax.ShapeDtypeStruct((2 * width + 3 * VECTOR_ROWS, part), BF16),
+        VMEM,
+        us=1,
+    )
+    first_across = exchange(first, 2)
+    node_pack, next_pack = call(
+        other_packs_kernel,
+        "other_packs",
+        (w_src, w_dst, w_node_in, w_node_out),
+        [VMEM] * 4,
+        (jax.ShapeDtypeStruct((3 * width, part), BF16), jax.ShapeDtypeStruct((5 * width, part), BF16)),
+        (VMEM, VMEM),
+        us=2,
+    )
+    pair = jnp.stack([own, across])
     latent = jnp.concatenate([pair, exchange(pair, 1)], axis=0)
-    weights = spread_weights(packs[0], share_of(packs[0]))
+    node_share, nbr_blocks = barrier((node_pack, nbr_blocks, latent))[:2]
+    node_across = exchange(node_share, 2)
 
     all_slots = mine * slots + 1
     gather, collect, degree, meta = call(
         prepare_kernel,
         "one_hots",
-        (place, nbr_blocks, edge_count, jnp.swapaxes(edge_src, 1, 2), jnp.swapaxes(edge_dst, 1, 2), edge_dst),
-        [SMEM] * 3 + [VMEM] * 3,
+        (place, nbr_blocks, edge_count, edge_src, edge_dst),
+        [SMEM] * 3 + [VMEM] * 2,
         (
             jax.ShapeDtypeStruct((all_slots, edges, 2 * edges), BF16),
             jax.ShapeDtypeStruct((all_slots, edges, edges), BF16),
@@ -295,18 +320,22 @@
             jax.ShapeDtypeStruct((4, LIST), jnp.int32),
         ),
         (VMEM, VMEM, VMEM, SMEM),
-    )
+        [pltpu.VMEM((edges, edges), F32)],
+        us=3,
+    )
+    edge_weights = (first, first_across, exchange(jnp.stack([first, first_across]), 1))
 
     vectors = None
+    messages = w_msg.reshape(LAYERS * 4, part, width)
     for layer in range(LAYERS):
         final = layer == LAYERS - 1
         after = pass_on(latent)
         beyond = pass_on(after)
-        if not final:
-            beyond, share = lax.optimization_barrier((beyond, share_of(packs[layer + 1])))
-        messages = w_msg[layer].reshape(4, part, width)
+        if layer == 0:
+            next_share = barrier((next_pack, after))[0]
+            next_across = from_other_side(next_share)
         outs = [jax.ShapeDtypeStruct((rows, width), F32), jax.ShapeDtypeStruct((rows, width), BF16)]
-        inputs = [place, meta, latent, after, *weights]
+        inputs = [place, meta, latent, after, *edge_weights]
         if layer == 0:
             outs.append(jax.ShapeDtypeStruct((4, VECTOR_ROWS, part), F32))
         else:
@@ -324,6 +353,7 @@
                 pltpu.VMEM((UNROLL * edges, width), BF16),
                 pltpu.VMEM((UNROLL * edges, width), BF16),
             ],
+            us=5,
         )
         acc, receive = result[0], result[1]
         if layer == 0:
@@ -331,8 +361,8 @@
         partial = call(
             lambda *refs, layer=layer: far_kernel(layer, *refs),
             f"far{layer}",
-            [place, meta, beyond, *weights, messages, msg_vectors, gather, collect, acc, receive],
-            [SMEM, SMEM] + [VMEM] * 11,
+            [place, meta, beyond, *edge_weights, messages, msg_vectors, gather, collect, acc, receive],
+            [SMEM, SMEM] + [VMEM] * 10,
             jax.ShapeDtypeStruct((rows, width), BF16),
             VMEM,
             [
@@ -341,8 +371,11 @@
                 pltpu.VMEM((UNROLL * edges, width), BF16),
                 pltpu.VMEM((rows, width), F32),
             ],
+            us=3,
         )
         theirs = exchange(partial, 1)
+        if layer == 0:
+            node_weights = (node_pack, node_across, exchange(jnp.stack([node_pack, node_across]), 1))
         if final:
             outs = [jax.ShapeDtypeStruct((rows, part), BF16)] * 2
         else:
@@ -350,8 +383,8 @@
         result = call(
             lambda *refs, layer=layer, final=final: node_kernel(layer, final, *refs),
             f"node{layer}",
-            [place, latent, partial, theirs, degree, *weights, vectors, msg_vectors, msg_gain],
-            [SMEM] + [VMEM] * 11,
+            [place, latent, partial, theirs, degree, *node_weights, vectors, msg_vectors, msg_gain],
+            [SMEM] + [VMEM] * 10,
             outs,
             [VMEM] * len(outs),
         )
@@ -365,7 +398,9 @@
                 VMEM,
             )
         latent = result[0]
-        weights = spread_weights(packs[layer + 1], share)
+        next_across = barrier((next_across, latent))[0]
+        edge_weights = (next_pack, next_across, exchange(jnp.stack([next_pack, next_across]), 1))
+        node_weights = edge_weights
 
 
 def solution(mesh):

time: 131 us -> 130 us (level); the launches traced: 129 us -> 129 us
  waiting for transfers between devices: 46.3 us -> 54 us
  local copies, waits for them, and re-layouts: 10.8 us -> 4.4 us
  Pallas kernels: 23.8 us -> 19.2 us
  starting transfers between devices: 46.2 us -> 50.1 us
    ppermute x0 -> x1, waiting for transfers between devices: none -> 16.4 us  [from_other_side(): return lax.ppermute(value, BOTH, pairs)]
    ppermute x13 -> x10, waiting for transfers between devices: 26.6 us -> 10.9 us  [exchange(): return lax.ppermute(value, BOTH, [(i, i ^ mask) for i in range(total)])]
    ppermute x4, waiting for transfers between devices: 19.8 us -> 26.7 us  [pass_on(): lax.ppermute(value, BOTH, [(i, t) for i, t in pairs if 0 <= t < total])]
    pallas_call x8 -> x10, Pallas kernels: 23.8 us -> 19.2 us  [call(): pl.pallas_call(kernel, out_shape=outs, in_specs=spaces, out_specs=out_spa...]
    unnamed x46 -> x28, local copies, waits for them, and re-layouts: 6.76 us -> 3.33 us
    slice x5 -> x0, local copies, waits for them, and re-layouts: 2.82 us -> none  [the longest x1 0.99 us: per_device(): w_src[layer]]
    ppermute x0 -> x1, starting transfers between devices: none -> 1.92 us  [from_other_side(): return lax.ppermute(value, BOTH, pairs)]
    ppermute x4, starting transfers between devices: 8.21 us -> 9.61 us  [pass_on(): lax.ppermute(value, BOTH, [(i, t) for i, t in pairs if 0 <= t < total])]
  transfers between devices with their start and end apart: 17 -> 15, of which waited for: 9 -> 8; matrix products, arithmetic and copies ran while one was open for 6% -> 1% of each run, Pallas kernels for 12% -> 11%
where the time goes in v3:
time: 130 us; the launch traced here: 129 us
  waiting for transfers between devices  54 us (42%)
  starting transfers between devices  50.1 us (39%)
  Pallas kernels  19.2 us (15%)
  local copies, waits for them, and re-layouts  4.4 us (3%)
    ppermute x10, starting transfers between devices, exchange(): return lax.ppermute(value, BOTH, [(i, i ^ mask) for i in range(total)])  38.6 us
    ppermute x4, waiting for transfers between devices, pass_on(): lax.ppermute(value, BOTH, [(i, t) for i, t in pairs if 0 <= t < total])  26.7 us
    pallas_call x10, Pallas kernels, call(): pl.pallas_call(kernel, out_shape=outs, in_specs=spaces, out_specs=out_spa...  19.2 us
    ppermute x1, waiting for transfers between devices, from_other_side(): return lax.ppermute(value, BOTH, pairs)  16.4 us
    ppermute x10, waiting for transfers between devices, exchange(): return lax.ppermute(value, BOTH, [(i, i ^ mask) for i in range(total)])  10.9 us
    ppermute x4, starting transfers between devices, pass_on(): lax.ppermute(value, BOTH, [(i, t) for i, t in pairs if 0 <= t < total])  9.61 us
    unnamed x28, local copies, waits for them, and re-layouts  3.33 us
  transfers between devices with their start and end apart: 15, of which 8 were waited for; matrix products, arithmetic and copies ran while one was open for 1% of the time, Pallas kernels for 11%

profile of v3, /device:TPU:6, one launch (start us, length us, event | category | flops | bytes accessed | tf_op | source)
XLA Modules:
  0.0 129.3 jit_solution(5677302265133419573)
XLA Ops:
  0.0 1.0 constant_dynamic-slice_fusion
  1.0 4.3 %collective-permute-start = (bf16[512,128]{1,0:T(8,128)(2,1)S(1)}, bf16[512,128]{1,0:T(8,128)(2,1)S(1)}, u32[]{:S(2)}, u32[]{:S(2)}) collective-permute-start(bf16[512,128]{1,0:T(8,128)(2,1)S(1)} %get-tuple-element.40), channel_id=1, source_target_pairs={{0,2},{1,3},{2,0},{3,1},{4,6},{5,7},{6,4},{7,5},{8,10},{9,11},{10,... | collective-permute-start | bytes 393224 | tf_op jit(solution)/shard_map/ppermute | solution.py:29
  5.3 3.5 %collective-permute-done = bf16[512,128]{1,0:T(8,128)(2,1)S(1)} collective-permute-done((bf16[512,128]{1,0:T(8,128)(2,1)S(1)}, bf16[512,128]{1,0:T(8,128)(2,1)S(1)}, u32[]{:S(2)}, u32[]{:S(2)}) %collective-permute-start) | collective-permute-done | bytes 131104 | tf_op jit(solution)/shard_map/ppermute | solution.py:29
  8.8 2.1 %collective-permute-start.1 = (bf16[2,512,128]{2,1,0:T(8,128)(2,1)S(1)}, bf16[2,512,128]{2,1,0:T(8,128)(2,1)S(1)}, u32[]{:S(2)}, u32[]{:S(2)}) collective-permute-start(bf16[2,512,128]{2,1,0:T(8,128)(2,1)S(1)} %pad_maximum_fusion.4), channel_id=1, source_target_pairs={{0,1},{1,0},{2,3},{3,2},{4,5},{5,4},{6,7},{7,6},{8,9},{9,8},{10,11... | collective-permute-start | bytes 786440 | tf_op jit(solution)/shard_map/ppermute | solution.py:29
  11.8 0.9 copy-done.3
  14.2 3.8 %collective-permute-start.4 = (bf16[1072,128]{1,0:T(8,128)(2,1)S(1)}, bf16[1072,128]{1,0:T(8,128)(2,1)S(1)}, u32[]{:S(2)}, u32[]{:S(2)}) collective-permute-start(bf16[1072,128]{1,0:T(8,128)(2,1)S(1)} %first_pack.1.refs_4_.refs_3_), channel_id=1, source_target_pairs={{0,2},{1,3},{2,0},{3,1},{4,6},{5,7},{6,4},{7,5},{8,10},{9,11},{10,... | collective-permute-start | bytes 823304 | tf_op jit(solution)/shard_map/ppermute | solution.py:29
  18.2 2.2 %collective-permute-start.2 = (bf16[4,512,128]{2,1,0:T(8,128)(2,1)S(1)}, bf16[4,512,128]{2,1,0:T(8,128)(2,1)}, u32[]{:S(2)}, u32[]{:S(2)}) collective-permute-start(bf16[4,512,128]{2,1,0:T(8,128)(2,1)S(1)} %pad_maximum_fusion.3.refs_2_.refs_1_), channel_id=1, source_target_pairs={{0,2},{2,4},{3,1},{4,6},{5,3},{6,8},{7,5},{8,10},{9,7},{10,12},{11... | collective-permute-start | bytes 1572872 | tf_op jit(solution)/shard_map/ppermute | solution.py:35
  20.4 6.4 %collective-permute-start.7 = (bf16[1536,128]{1,0:T(8,128)(2,1)S(1)}, bf16[1536,128]{1,0:T(8,128)(2,1)S(1)}, u32[]{:S(2)}, u32[]{:S(2)}) collective-permute-start(bf16[1536,128]{1,0:T(8,128)(2,1)S(1)} %get-tuple-element.30.refs_5_), channel_id=1, source_target_pairs={{0,2},{1,3},{2,0},{3,1},{4,6},{5,7},{6,4},{7,5},{8,10},{9,11},{10,... | collective-permute-start | bytes 1179656 | tf_op jit(solution)/shard_map/ppermute | solution.py:29
  27.6 7.5 %collective-permute-start.5 = (bf16[2,1072,128]{2,1,0:T(8,128)(2,1)}, bf16[2,1072,128]{2,1,0:T(8,128)(2,1)S(1)}, u32[]{:S(2)}, u32[]{:S(2)}) collective-permute-start(bf16[2,1072,128]{2,1,0:T(8,128)(2,1)} %pad_maximum_fusion.2), channel_id=1, source_target_pairs={{0,1},{1,0},{2,3},{3,2},{4,5},{5,4},{6,7},{7,6},{8,9},{9,8},{10,11... | collective-permute-start | bytes 1646600 | tf_op jit(solution)/shard_map/ppermute | solution.py:29
  35.3 2.2 %one_hots.1 = (bf16[25,128,256]{2,1,0:T(8,128)(2,1)S(1)}, bf16[25,128,128]{2,1,0:T(8,128)(2,1)S(1)}, f32[512,128]{1,0:T(8,128)S(1)}, s32[4,32]{1,0:T(4,128)S(1)}) custom-call(s32[5]{0:T(128)S(1)} %stack.57.place_ref.refs_0_, s32[8,6]{1,0:T(8,128)S(1)} %copy-done.7, s32[8,6]{1,0:T(8,128)S(1)} %copy-done.8, s32[8,6,128]{2,1,0:T(8,128)S(1)} %copy.15.src_ref, ...), custom_call_target="tpu_custom_call" | custom-call | flops 3000000000 | bytes 1048576 | tf_op jit(solution)/shard_map/one_hots/pallas_call | solution.py:242
  37.7 3.6 %collective-permute-start.3 = (bf16[4,512,128]{2,1,0:T(8,128)(2,1)}, bf16[4,512,128]{2,1,0:T(8,128)(2,1)S(1)}, u32[]{:S(2)}, u32[]{:S(2)}) collective-permute-start(bf16[4,512,128]{2,1,0:T(8,128)(2,1)} %collective-permute-done.2.refs_3_), channel_id=1, source_target_pairs={{0,2},{2,4},{3,1},{4,6},{5,3},{6,8},{7,5},{8,10},{9,7},{10,12},{11... | collective-permute-start | bytes 1572872 | tf_op jit(solution)/shard_map/ppermute | solution.py:35
  41.4 7.0 %collective-permute-start.8 = (bf16[2,1536,128]{2,1,0:T(8,128)(2,1)S(1)}, bf16[2,1536,128]{2,1,0:T(8,128)(2,1)S(1)}, u32[]{:S(2)}, u32[]{:S(2)}) collective-permute-start(bf16[2,1536,128]{2,1,0:T(8,128)(2,1)S(1)} %pad_maximum_fusion.1), channel_id=1, source_target_pairs={{0,1},{1,0},{2,3},{3,2},{4,5},{5,4},{6,7},{7,6},{8,9},{9,8},{10,11... | collective-permute-start | bytes 2359304 | tf_op jit(solution)/shard_map/ppermute | solution.py:29
  48.4 4.1 %near0.1 = (f32[512,512]{1,0:T(8,128)S(1)}, bf16[512,512]{1,0:T(8,128)(2,1)S(1)}, f32[4,16,128]{2,1,0:T(8,128)S(1)}) custom-call(s32[5]{0:T(128)S(1)} %stack.57.place_ref.refs_0_, s32[4,32]{1,0:T(4,128)S(1)} %get-tuple-element.24.refs_1_, bf16[4,512,128]{2,1,0:T(8,128)(2,1)S(1)} %pad_maximum_fusion.3.refs_2_.refs_1_, ...), custom_call_target="tpu_custom_call" | custom-call | flops 5000000000 | bytes 1048576 | tf_op jit(solution)/shard_map/near0/pallas_call | solution.py:242
  52.5 3.4 %collective-permute-done.3.refs_2_ = bf16[4,512,128]{2,1,0:T(8,128)(2,1)S(1)} collective-permute-done((bf16[4,512,128]{2,1,0:T(8,128)(2,1)}, bf16[4,512,128]{2,1,0:T(8,128)(2,1)S(1)}, u32[]{:S(2)}, u32[]{:S(2)}) %collective-permute-start.3) | collective-permute-done | bytes 524320 | tf_op jit(solution)/shard_map/ppermute | solution.py:35
  55.9 2.1 %far0.1.refs_2_ = bf16[512,512]{1,0:T(8,128)(2,1)S(1)} custom-call(s32[5]{0:T(128)S(1)} %stack.57.place_ref.refs_0_, s32[4,32]{1,0:T(4,128)S(1)} %get-tuple-element.24.refs_1_, bf16[4,512,128]{2,1,0:T(8,128)(2,1)S(1)} %collective-permute-done.3.refs_2_, bf16[1072,128]{1,0:T(8,128)(2,1)S(1)} %first_pack.1.refs_4_.refs_3_, ...), custom_call_target="tpu_custom_call" | custom-call | flops 3000000000 | bytes 1048576 | tf_op jit(solution)/shard_map/far0/pallas_call | solution.py:242
  58.0 1.9 %collective-permute-start.6 = (bf16[512,512]{1,0:T(8,128)(2,1)S(1)}, bf16[512,512]{1,0:T(8,128)(2,1)S(1)}, u32[]{:S(2)}, u32[]{:S(2)}) collective-permute-start(bf16[512,512]{1,0:T(8,128)(2,1)S(1)} %far0.1.refs_2_), channel_id=1, source_target_pairs={{0,1},{1,0},{2,3},{3,2},{4,5},{5,4},{6,7},{7,6},{8,9},{9,8},{10,11... | collective-permute-start | bytes 1572872 | tf_op jit(solution)/shard_map/ppermute | solution.py:29
  60.0 1.9 %collective-permute-start.11 = (bf16[2560,128]{1,0:T(8,128)(2,1)S(1)}, bf16[2560,128]{1,0:T(8,128)(2,1)S(1)}, u32[]{:S(2)}, u32[]{:S(2)}) collective-permute-start(bf16[2560,128]{1,0:T(8,128)(2,1)S(1)} %get-tuple-element.33.refs_4_.refs_3_.refs_5_), channel_id=1, source_target_pairs={{0,14},{1,15},{2,4},{3,5},{4,2},{5,3},{6,8},{7,9},{8,6},{9,7},{10,... | collective-permute-start | bytes 1966088 | tf_op jit(solution)/shard_map/ppermute | solution.py:46
  61.9 1.9 %node0.1.refs_2_.refs_1_ = bf16[4,512,128]{2,1,0:T(8,128)(2,1)S(1)} custom-call(s32[5]{0:T(128)S(1)} %stack.57.place_ref.refs_0_, bf16[4,512,128]{2,1,0:T(8,128)(2,1)S(1)} %pad_maximum_fusion.3.refs_2_.refs_1_, bf16[512,512]{1,0:T(8,128)(2,1)S(1)} %far0.1.refs_2_, bf16[512,512]{1,0:T(8,128)(2,1)S(1)} %collective-permute-done.6.refs_3_, ...), custom_call_target="tpu_custom_call" | custom-call | flops 2000000000 | bytes 1048576 | tf_op jit(solution)/shard_map/node0/pallas_call | solution.py:242
  63.8 16.4 %collective-permute-done.11.refs_5_.refs_4_.refs_6_ = bf16[2560,128]{1,0:T(8,128)(2,1)S(1)} collective-permute-done((bf16[2560,128]{1,0:T(8,128)(2,1)S(1)}, bf16[2560,128]{1,0:T(8,128)(2,1)S(1)}, u32[]{:S(2)}, u32[]{:S(2)}) %collective-permute-start.11) | collective-permute-done | bytes 655392 | tf_op jit(solution)/shard_map/ppermute | solution.py:46
  80.3 1.9 %collective-permute-start.12 = (bf16[2,2560,128]{2,1,0:T(8,128)(2,1)S(1)}, bf16[2,2560,128]{2,1,0:T(8,128)(2,1)S(1)}, u32[]{:S(2)}, u32[]{:S(2)}) collective-permute-start(bf16[2,2560,128]{2,1,0:T(8,128)(2,1)S(1)} %pad_maximum_fusion), channel_id=1, source_target_pairs={{0,1},{1,0},{2,3},{3,2},{4,5},{5,4},{6,7},{7,6},{8,9},{9,8},{10,11... | collective-permute-start | bytes 3932168 | tf_op jit(solution)/shard_map/ppermute | solution.py:29
  82.3 1.9 %collective-permute-start.9 = (bf16[4,512,128]{2,1,0:T(8,128)(2,1)S(1)}, bf16[4,512,128]{2,1,0:T(8,128)(2,1)S(1)}, u32[]{:S(2)}, u32[]{:S(2)}) collective-permute-start(bf16[4,512,128]{2,1,0:T(8,128)(2,1)S(1)} %node0.1.refs_2_.refs_1_), channel_id=1, source_target_pairs={{0,2},{2,4},{3,1},{4,6},{5,3},{6,8},{7,5},{8,10},{9,7},{10,12},{11... | collective-permute-start | bytes 1572872 | tf_op jit(solution)/shard_map/ppermute | solution.py:35
  84.2 13.4 %collective-permute-done.9.refs_3_ = bf16[4,512,128]{2,1,0:T(8,128)(2,1)S(1)} collective-permute-done((bf16[4,512,128]{2,1,0:T(8,128)(2,1)S(1)}, bf16[4,512,128]{2,1,0:T(8,128)(2,1)S(1)}, u32[]{:S(2)}, u32[]{:S(2)}) %collective-permute-start.9) | collective-permute-done | bytes 524320 | tf_op jit(solution)/shard_map/ppermute | solution.py:35
  97.6 1.9 %collective-permute-start.10 = (bf16[4,512,128]{2,1,0:T(8,128)(2,1)S(1)}, bf16[4,512,128]{2,1,0:T(8,128)(2,1)S(1)}, u32[]{:S(2)}, u32[]{:S(2)}) collective-permute-start(bf16[4,512,128]{2,1,0:T(8,128)(2,1)S(1)} %collective-permute-done.9.refs_3_), channel_id=1, source_target_pairs={{0,2},{2,4},{3,1},{4,6},{5,3},{6,8},{7,5},{8,10},{9,7},{10,12},{11... | collective-permute-start | bytes 1572872 | tf_op jit(solution)/shard_map/ppermute | solution.py:35
  99.5 3.6 %near1.1 = (f32[512,512]{1,0:T(8,128)S(1)}, bf16[512,512]{1,0:T(8,128)(2,1)S(1)}) custom-call(s32[5]{0:T(128)S(1)} %stack.57.place_ref.refs_0_, s32[4,32]{1,0:T(4,128)S(1)} %get-tuple-element.24.refs_1_, bf16[4,512,128]{2,1,0:T(8,128)(2,1)S(1)} %node0.1.refs_2_.refs_1_, bf16[4,512,128]{2,1,0:T(8,128)(2,1)S(1)} %collective-permute-done.9.refs_3_, ...), custom_call_target="tpu_custom_call" | custom-call | flops 5000000000 | bytes 1048576 | tf_op jit(solution)/shard_map/near1/pallas_call | solution.py:242
  103.1 9.7 %collective-permute-done.10.refs_2_ = bf16[4,512,128]{2,1,0:T(8,128)(2,1)S(1)} collective-permute-done((bf16[4,512,128]{2,1,0:T(8,128)(2,1)S(1)}, bf16[4,512,128]{2,1,0:T(8,128)(2,1)S(1)}, u32[]{:S(2)}, u32[]{:S(2)}) %collective-permute-start.10) | collective-permute-done | bytes 524320 | tf_op jit(solution)/shard_map/ppermute | solution.py:35
  112.8 2.1 %far1.1.refs_2_ = bf16[512,512]{1,0:T(8,128)(2,1)S(1)} custom-call(s32[5]{0:T(128)S(1)} %stack.57.place_ref.refs_0_, s32[4,32]{1,0:T(4,128)S(1)} %get-tuple-element.24.refs_1_, bf16[4,512,128]{2,1,0:T(8,128)(2,1)S(1)} %collective-permute-done.10.refs_2_, bf16[2560,128]{1,0:T(8,128)(2,1)S(1)} %get-tuple-element.33.refs_4_.refs_3_.refs_5_, ...), custom_call_target="tpu_custom_call" | custom-call | flops 3000000000 | bytes 1048576 | tf_op jit(solution)/shard_map/far1/pallas_call | solution.py:242
  114.9 1.9 %collective-permute-start.13 = (bf16[512,512]{1,0:T(8,128)(2,1)S(1)}, bf16[512,512]{1,0:T(8,128)(2,1)S(1)}, u32[]{:S(2)}, u32[]{:S(2)}) collective-permute-start(bf16[512,512]{1,0:T(8,128)(2,1)S(1)} %far1.1.refs_2_), channel_id=1, source_target_pairs={{0,1},{1,0},{2,3},{3,2},{4,5},{5,4},{6,7},{7,6},{8,9},{9,8},{10,11... | collective-permute-start | bytes 1572872 | tf_op jit(solution)/shard_map/ppermute | solution.py:29
  116.9 1.9 %collective-permute-done.13.refs_3_ = bf16[512,512]{1,0:T(8,128)(2,1)S(1)} collective-permute-done((bf16[512,512]{1,0:T(8,128)(2,1)S(1)}, bf16[512,512]{1,0:T(8,128)(2,1)S(1)}, u32[]{:S(2)}, u32[]{:S(2)}) %collective-permute-start.13) | collective-permute-done | bytes 524320 | tf_op jit(solution)/shard_map/ppermute | solution.py:29
  118.7 1.8 %node1.1 = (bf16[512,128]{1,0:T(8,128)(2,1)S(1)}, bf16[512,128]{1,0:T(8,128)(2,1)S(1)}) custom-call(s32[5]{0:T(128)S(1)} %stack.57.place_ref.refs_0_, bf16[4,512,128]{2,1,0:T(8,128)(2,1)S(1)} %node0.1.refs_2_.refs_1_, bf16[512,512]{1,0:T(8,128)(2,1)S(1)} %far1.1.refs_2_, bf16[512,512]{1,0:T(8,128)(2,1)S(1)} %collective-permute-done.13.refs_3_, ...), custom_call_target="tpu_custom_call" | custom-call | flops 2000000000 | bytes 1048576 | tf_op jit(solution)/shard_map/node1/pallas_call | solution.py:242
  120.5 1.9 %collective-permute-start.14 = (bf16[512,128]{1,0:T(8,128)(2,1)S(1)}, bf16[512,128]{1,0:T(8,128)(2,1)S(1)}, u32[]{:S(2)}, u32[]{:S(2)}) collective-permute-start(bf16[512,128]{1,0:T(8,128)(2,1)S(1)} %get-tuple-element.38), channel_id=1, source_target_pairs={{0,2},{1,3},{2,0},{3,1},{4,6},{5,7},{6,4},{7,5},{8,10},{9,11},{10,... | collective-permute-start | bytes 393224 | tf_op jit(solution)/shard_map/ppermute | solution.py:29
  122.5 5.5 %collective-permute-done.14.other_ref = bf16[512,128]{1,0:T(8,128)(2,1)S(1)} collective-permute-done((bf16[512,128]{1,0:T(8,128)(2,1)S(1)}, bf16[512,128]{1,0:T(8,128)(2,1)S(1)}, u32[]{:S(2)}, u32[]{:S(2)}) %collective-permute-start.14) | collective-permute-done | bytes 131104 | tf_op jit(solution)/shard_map/ppermute | solution.py:29
  128.0 1.3 join.1
  (43 shorter events, 3.9 us)
Async XLA Ops:
  1.0 7.8 %collective-permute-start = (bf16[512,128]{1,0:T(8,128)(2,1)S(1)}, bf16[512,128]{1,0:T(8,128)(2,1)S(1)}, u32[]{:S(2)}, u32[]{:S(2)}) collective-permute-start(bf16[512,128]{1,0:T(8,128)(2,1)S(1)} %get-tuple-element.40), channel_id=1, source_target_pairs={{0,2},{1,3},{2,0},{3,1},{4,6},{5,7},{6,4},{7,5},{8,10},{9,11},{10,... | collective-permute-start | bytes 393224 | tf_op jit(solution)/shard_map/ppermute | solution.py:29
  8.8 9.2 %copy-start.1 = (bf16[2,1024,128]{2,1,0:T(8,128)(2,1)S(1)}, bf16[2,1024,128]{2,1,0:T(8,128)(2,1)}, u32[]{:S(2)}) copy-start(bf16[2,1024,128]{2,1,0:T(8,128)(2,1)} %in_ref.1) | copy-start | bytes 1572868
  8.8 9.3 %collective-permute-start.1 = (bf16[2,512,128]{2,1,0:T(8,128)(2,1)S(1)}, bf16[2,512,128]{2,1,0:T(8,128)(2,1)S(1)}, u32[]{:S(2)}, u32[]{:S(2)}) collective-permute-start(bf16[2,512,128]{2,1,0:T(8,128)(2,1)S(1)} %pad_maximum_fusion.4), channel_id=1, source_target_pairs={{0,1},{1,0},{2,3},{3,2},{4,5},{5,4},{6,7},{7,6},{8,9},{9,8},{10,11... | collective-permute-start | bytes 786440 | tf_op jit(solution)/shard_map/ppermute | solution.py:29
  10.9 1.0 copy-start.2
  11.8 0.9 copy-start.3
  12.8 0.7 copy-start.6
  13.5 0.7 copy-start.10
  14.1 3.8 %copy-start.4 = (bf16[2,512,128]{2,1,0:T(8,128)(2,1)S(1)}, bf16[2,512,128]{2,1,0:T(8,128)(2,1)}, u32[]{:S(2)}) copy-start(bf16[2,512,128]{2,1,0:T(8,128)(2,1)} %out_w_ref.1) | copy-start | bytes 786436
  14.2 12.6 %collective-permute-start.4 = (bf16[1072,128]{1,0:T(8,128)(2,1)S(1)}, bf16[1072,128]{1,0:T(8,128)(2,1)S(1)}, u32[]{:S(2)}, u32[]{:S(2)}) collective-permute-start(bf16[1072,128]{1,0:T(8,128)(2,1)S(1)} %first_pack.1.refs_4_.refs_3_), channel_id=1, source_target_pairs={{0,2},{1,3},{2,0},{3,1},{4,6},{5,7},{6,4},{7,5},{8,10},{9,11},{10,... | collective-permute-start | bytes 823304 | tf_op jit(solution)/shard_map/ppermute | solution.py:29
  18.0 17.1 %copy-start.11 = (s32[8,6,128]{2,0,1:T(8,128)S(1)}, s32[8,6,128]{2,0,1:T(8,128)}, u32[]{:S(2)}) copy-start(s32[8,6,128]{2,0,1:T(8,128)} %param.26) | copy-start | bytes 73732
  18.1 17.1 %copy-start.12 = (s32[8,6,128]{2,0,1:T(8,128)S(1)}, s32[8,6,128]{2,0,1:T(8,128)}, u32[]{:S(2)}) copy-start(s32[8,6,128]{2,0,1:T(8,128)} %param.27) | copy-start | bytes 73732
  18.1 17.2 %copy-start.7 = (s32[8,6]{1,0:T(8,128)S(1)}, s32[8,6]{1,0:T(8,128)}, u32[]{:S(2)}) copy-start(s32[8,6]{1,0:T(8,128)} %nbr_ref) | copy-start | bytes 580
  18.1 17.2 %copy-start.8 = (s32[8,6]{1,0:T(8,128)S(1)}, s32[8,6]{1,0:T(8,128)}, u32[]{:S(2)}) copy-start(s32[8,6]{1,0:T(8,128)} %count_ref.1) | copy-start | bytes 580
  18.2 19.6 %collective-permute-start.2 = (bf16[4,512,128]{2,1,0:T(8,128)(2,1)S(1)}, bf16[4,512,128]{2,1,0:T(8,128)(2,1)}, u32[]{:S(2)}, u32[]{:S(2)}) collective-permute-start(bf16[4,512,128]{2,1,0:T(8,128)(2,1)S(1)} %pad_maximum_fusion.3.refs_2_.refs_1_), channel_id=1, source_target_pairs={{0,2},{2,4},{3,1},{4,6},{5,3},{6,8},{7,5},{8,10},{9,7},{10,12},{11... | collective-permute-start | bytes 1572872 | tf_op jit(solution)/shard_map/ppermute | solution.py:35
  20.4 20.9 %collective-permute-start.7 = (bf16[1536,128]{1,0:T(8,128)(2,1)S(1)}, bf16[1536,128]{1,0:T(8,128)(2,1)S(1)}, u32[]{:S(2)}, u32[]{:S(2)}) collective-permute-start(bf16[1536,128]{1,0:T(8,128)(2,1)S(1)} %get-tuple-element.30.refs_5_), channel_id=1, source_target_pairs={{0,2},{1,3},{2,0},{3,1},{4,6},{5,7},{6,4},{7,5},{8,10},{9,11},{10,... | collective-permute-start | bytes 1179656 | tf_op jit(solution)/shard_map/ppermute | solution.py:29
  27.6 20.8 %collective-permute-start.5 = (bf16[2,1072,128]{2,1,0:T(8,128)(2,1)}, bf16[2,1072,128]{2,1,0:T(8,128)(2,1)S(1)}, u32[]{:S(2)}, u32[]{:S(2)}) collective-permute-start(bf16[2,1072,128]{2,1,0:T(8,128)(2,1)} %pad_maximum_fusion.2), channel_id=1, source_target_pairs={{0,1},{1,0},{2,3},{3,2},{4,5},{5,4},{6,7},{7,6},{8,9},{9,8},{10,11... | collective-permute-start | bytes 1646600 | tf_op jit(solution)/shard_map/ppermute | solution.py:29
  37.5 10.9 %copy-start = (bf16[2,512,512]{2,1,0:T(8,128)(2,1)S(1)}, bf16[2,512,512]{2,1,0:T(8,128)(2,1)}, u32[]{:S(2)}) copy-start(bf16[2,512,512]{2,1,0:T(8,128)(2,1)} %param.17) | copy-start | bytes 3145732
  37.5 10.9 %copy-start.5 = (f32[2,2,512]{2,1,0:T(2,128)S(1)}, f32[2,2,512]{2,1,0:T(2,128)}, u32[]{:S(2)}) copy-start(f32[2,2,512]{2,1,0:T(2,128)} %refs_9_.5) | copy-start | bytes 24580
  37.7 18.2 %collective-permute-start.3 = (bf16[4,512,128]{2,1,0:T(8,128)(2,1)}, bf16[4,512,128]{2,1,0:T(8,128)(2,1)S(1)}, u32[]{:S(2)}, u32[]{:S(2)}) collective-permute-start(bf16[4,512,128]{2,1,0:T(8,128)(2,1)} %collective-permute-done.2.refs_3_), channel_id=1, source_target_pairs={{0,2},{2,4},{3,1},{4,6},{5,3},{6,8},{7,5},{8,10},{9,7},{10,12},{11... | collective-permute-start | bytes 1572872 | tf_op jit(solution)/shard_map/ppermute | solution.py:35
  41.4 20.5 %collective-permute-start.8 = (bf16[2,1536,128]{2,1,0:T(8,128)(2,1)S(1)}, bf16[2,1536,128]{2,1,0:T(8,128)(2,1)S(1)}, u32[]{:S(2)}, u32[]{:S(2)}) collective-permute-start(bf16[2,1536,128]{2,1,0:T(8,128)(2,1)S(1)} %pad_maximum_fusion.1), channel_id=1, source_target_pairs={{0,1},{1,0},{2,3},{3,2},{4,5},{5,4},{6,7},{7,6},{8,9},{9,8},{10,11... | collective-permute-start | bytes 2359304 | tf_op jit(solution)/shard_map/ppermute | solution.py:29
  55.9 6.0 %copy-start.9 = (f32[2,512]{1,0:T(2,128)S(1)}, f32[2,512]{1,0:T(2,128)}, u32[]{:S(2)}) copy-start(f32[2,512]{1,0:T(2,128)} %refs_10_.3) | copy-start | bytes 12292
  58.0 3.9 %collective-permute-start.6 = (bf16[512,512]{1,0:T(8,128)(2,1)S(1)}, bf16[512,512]{1,0:T(8,128)(2,1)S(1)}, u32[]{:S(2)}, u32[]{:S(2)}) collective-permute-start(bf16[512,512]{1,0:T(8,128)(2,1)S(1)} %far0.1.refs_2_), channel_id=1, source_target_pairs={{0,1},{1,0},{2,3},{3,2},{4,5},{5,4},{6,7},{7,6},{8,9},{9,8},{10,11... | collective-permute-start | bytes 1572872 | tf_op jit(solution)/shard_map/ppermute | solution.py:29
  60.0 20.2 %collective-permute-start.11 = (bf16[2560,128]{1,0:T(8,128)(2,1)S(1)}, bf16[2560,128]{1,0:T(8,128)(2,1)S(1)}, u32[]{:S(2)}, u32[]{:S(2)}) collective-permute-start(bf16[2560,128]{1,0:T(8,128)(2,1)S(1)} %get-tuple-element.33.refs_4_.refs_3_.refs_5_), channel_id=1, source_target_pairs={{0,14},{1,15},{2,4},{3,5},{4,2},{5,3},{6,8},{7,9},{8,6},{9,7},{10,... | collective-permute-start | bytes 1966088 | tf_op jit(solution)/shard_map/ppermute | solution.py:46
  80.3 19.1 %collective-permute-start.12 = (bf16[2,2560,128]{2,1,0:T(8,128)(2,1)S(1)}, bf16[2,2560,128]{2,1,0:T(8,128)(2,1)S(1)}, u32[]{:S(2)}, u32[]{:S(2)}) collective-permute-start(bf16[2,2560,128]{2,1,0:T(8,128)(2,1)S(1)} %pad_maximum_fusion), channel_id=1, source_target_pairs={{0,1},{1,0},{2,3},{3,2},{4,5},{5,4},{6,7},{7,6},{8,9},{9,8},{10,11... | collective-permute-start | bytes 3932168 | tf_op jit(solution)/shard_map/ppermute | solution.py:29
  82.3 15.3 %collective-permute-start.9 = (bf16[4,512,128]{2,1,0:T(8,128)(2,1)S(1)}, bf16[4,512,128]{2,1,0:T(8,128)(2,1)S(1)}, u32[]{:S(2)}, u32[]{:S(2)}) collective-permute-start(bf16[4,512,128]{2,1,0:T(8,128)(2,1)S(1)} %node0.1.refs_2_.refs_1_), channel_id=1, source_target_pairs={{0,2},{2,4},{3,1},{4,6},{5,3},{6,8},{7,5},{8,10},{9,7},{10,12},{11... | collective-permute-start | bytes 1572872 | tf_op jit(solution)/shard_map/ppermute | solution.py:35
  97.6 15.3 %collective-permute-start.10 = (bf16[4,512,128]{2,1,0:T(8,128)(2,1)S(1)}, bf16[4,512,128]{2,1,0:T(8,128)(2,1)S(1)}, u32[]{:S(2)}, u32[]{:S(2)}) collective-permute-start(bf16[4,512,128]{2,1,0:T(8,128)(2,1)S(1)} %collective-permute-done.9.refs_3_), channel_id=1, source_target_pairs={{0,2},{2,4},{3,1},{4,6},{5,3},{6,8},{7,5},{8,10},{9,7},{10,12},{11... | collective-permute-start | bytes 1572872 | tf_op jit(solution)/shard_map/ppermute | solution.py:35
  114.9 3.8 %collective-permute-start.13 = (bf16[512,512]{1,0:T(8,128)(2,1)S(1)}, bf16[512,512]{1,0:T(8,128)(2,1)S(1)}, u32[]{:S(2)}, u32[]{:S(2)}) collective-permute-start(bf16[512,512]{1,0:T(8,128)(2,1)S(1)} %far1.1.refs_2_), channel_id=1, source_target_pairs={{0,1},{1,0},{2,3},{3,2},{4,5},{5,4},{6,7},{7,6},{8,9},{9,8},{10,11... | collective-permute-start | bytes 1572872 | tf_op jit(solution)/shard_map/ppermute | solution.py:29
  120.5 7.4 %collective-permute-start.14 = (bf16[512,128]{1,0:T(8,128)(2,1)S(1)}, bf16[512,128]{1,0:T(8,128)(2,1)S(1)}, u32[]{:S(2)}, u32[]{:S(2)}) collective-permute-start(bf16[512,128]{1,0:T(8,128)(2,1)S(1)} %get-tuple-element.38), channel_id=1, source_target_pairs={{0,2},{1,3},{2,0},{3,1},{4,6},{5,7},{6,4},{7,5},{8,10},{9,11},{10,... | collective-permute-start | bytes 393224 | tf_op jit(solution)/shard_map/ppermute | solution.py:29

commit v4 on v3

--- a/solution.py
+++ b/solution.py
@@ -12,8 +12,9 @@
 BF16 = jnp.bfloat16
 VECTOR_ROWS = 16
 ORDER = (0, 2, 1, 3)
-FLIPPED = (1, 0, 3, 2)
 STRAIGHT = (0, 1, 2, 3)
+FROM_NEXT = (3, 2, 1, 0)
+FROM_BEYOND = (2, 3, 0, 1)
 UNROLL = 4
 LIST = 32
 VMEM = pl.BlockSpec(memory_space=pltpu.VMEM)
@@ -29,9 +30,10 @@
     return lax.ppermute(value, BOTH, [(i, i ^ mask) for i in range(total)])
 
 
-def pass_on(value):
+def swap_with(value, chips):
     total = lax.axis_size(BOTH)
-    pairs = [(i, i + (2 if i % 2 == 0 else -2)) for i in range(total)]
+    step = 2 * chips + 1
+    pairs = [(i, i + (step if i % 2 == 0 else -step)) for i in range(total)]
     return lax.ppermute(value, BOTH, [(i, t) for i, t in pairs if 0 <= t < total])
 
 
@@ -76,7 +78,7 @@
             step = (place + 2 * blocks) // blocks - 2
             hops = jnp.abs(step)
             meta_ref[2, s] = hops * blocks + place - step * blocks
-            mine = jnp.where(step == 0, core == j // (blocks // 2), (step > 0) == (core == 1))
+            mine = jnp.where(step == 0, core == j // (blocks // 2), (step > 0) == (core == 0))
             is_far = mine & (hops == 2)
             is_near = mine & (hops < 2)
 
@@ -99,42 +101,36 @@
     collect_ref[last - 1] = jnp.zeros(collect_ref.shape[1:], BF16)
 
 
-def first_pack_kernel(src_ref, dst_ref, vec_ref, gain_ref, out_ref):
+def pack_kernel(src_ref, dst_ref, in_ref, out_w_ref, vec_ref, gain_ref, first_ref, next_ref):
     width = src_ref.shape[1]
-    out_ref[:width, :] = src_ref[0]
-    out_ref[width : 2 * width, :] = dst_ref[0]
+    for layer, ref in enumerate((first_ref, next_ref)):
+        ref[: 2 * width, :] = in_ref[layer]
+        ref[2 * width : 3 * width, :] = out_w_ref[layer]
+        ref[3 * width : 4 * width, :] = src_ref[layer]
+        ref[4 * width : 5 * width, :] = dst_ref[layer]
     rest = jnp.concatenate(
         [part for layer in range(LAYERS) for part in (vec_ref[layer], gain_ref[layer : layer + 1, :])]
         + [jnp.zeros((VECTOR_ROWS - 5 * LAYERS, src_ref.shape[2]), F32)],
         axis=0,
     )
     for i in range(3):
-        at = 2 * width + i * VECTOR_ROWS
+        at = 5 * width + i * VECTOR_ROWS
         piece = rest.astype(BF16)
-        out_ref[at : at + VECTOR_ROWS, :] = piece
+        first_ref[at : at + VECTOR_ROWS, :] = piece
         rest = rest - piece.astype(F32)
-
-
-def other_packs_kernel(src_ref, dst_ref, in_ref, out_w_ref, node_ref, next_ref):
-    width = src_ref.shape[1]
-    node_ref[: 2 * width, :] = in_ref[0]
-    node_ref[2 * width :, :] = out_w_ref[0]
-    next_ref[:width, :] = src_ref[1]
-    next_ref[width : 2 * width, :] = dst_ref[1]
-    next_ref[2 * width : 4 * width, :] = in_ref[1]
-    next_ref[4 * width :, :] = out_w_ref[1]
+    first_ref[5 * width + 3 * VECTOR_ROWS :, :] = jnp.zeros((VECTOR_ROWS, src_ref.shape[2]), BF16)
 
 
 def wide(ref, order=STRAIGHT):
     return jnp.concatenate([ref[i] for i in order], axis=1)
 
 
-def weight(shards, f, base, mixed):
+def weight(shards, f, mixed):
     own, across, beside = shards
     part = own.shape[-1]
     rows = []
     for i in range(4):
-        at = pl.ds(pl.multiple_of(base + (f ^ ORDER[i]) * part, part) if mixed else base + i * part, part)
+        at = pl.ds(pl.multiple_of((f ^ ORDER[i]) * part, part) if mixed else i * part, part)
         rows.append(jnp.concatenate([own[at, :], beside[0, at, :], across[at, :], beside[1, at, :]], axis=1))
     return jnp.concatenate(rows, axis=0)
 
@@ -147,7 +143,7 @@
 def run_edges(which, shift, layer, f, meta_ref, receive, window, gather_ref, collect_ref, wmsg_ref, mvec_ref, hidden, normed, acc):
     slots = 6
     edges = gather_ref.shape[1]
-    w_msg = jnp.concatenate([wmsg_ref[4 * layer + (f ^ m)] for m in range(4)], axis=0)
+    w_msg = jnp.concatenate([wmsg_ref[f ^ m] for m in range(4)], axis=0)
     bias = mvec_ref[layer, 0:1, :]
 
     def body(step, carry):
@@ -175,49 +171,45 @@
     lax.fori_loop(0, (meta_ref[3, which] + UNROLL - 1) // UNROLL, body, 0)
 
 
-def near_kernel(layer, first, place_ref, meta_ref, h_ref, next_ref, w_own, w_across, w_beside, *refs):
+def near_kernel(layer, first, place_ref, meta_ref, h_ref, next_ref, wmsg_ref, mvec_ref, gather_ref, collect_ref, *refs):
+    source, target, refs = refs[:3], refs[3:6], refs[6:]
     if first:
-        wmsg_ref, mvec_ref, gather_ref, collect_ref, acc, receive, vectors, window, hidden, normed = refs
+        own_rows, across_rows, beside_rows, acc, receive, vectors, window, hidden, normed = refs
+        for m, w in enumerate((own_rows, beside_rows.at[0], across_rows, beside_rows.at[1])):
+            rows = w[...].astype(F32)
+            vectors[m] = rows[:VECTOR_ROWS] + rows[VECTOR_ROWS : 2 * VECTOR_ROWS] + rows[2 * VECTOR_ROWS : 3 * VECTOR_ROWS]
     else:
-        vectors, wmsg_ref, mvec_ref, gather_ref, collect_ref, acc, receive, window, hidden, normed = refs
+        vectors, acc, receive, window, hidden, normed = refs
     f = place_ref[0]
-    shards = (w_own, w_across, w_beside)
-    if first:
-        end = w_own.shape[0] - 3 * VECTOR_ROWS
-        for m, w in enumerate((w_own, w_beside.at[0], w_across, w_beside.at[1])):
-            rows = w[end : end + 3 * VECTOR_ROWS, :].astype(F32)
-            vectors[m] = rows[:VECTOR_ROWS] + rows[VECTOR_ROWS : 2 * VECTOR_ROWS] + rows[2 * VECTOR_ROWS :]
-    w_src = weight(shards, f, 0, True)
+    w_src = weight(source, f, True)
     own = wide(h_ref)
-    block, width = own.shape
+    block = own.shape[0]
     window[:block, :] = dot(own, w_src).astype(BF16)
-    window[block:, :] = dot(wide(next_ref, FLIPPED), w_src).astype(BF16)
-    receive[...] = (dot(own, weight(shards, f, width, True)) + vector(vectors, layer, 0)).astype(BF16)
+    window[block:, :] = dot(wide(next_ref, FROM_NEXT), w_src).astype(BF16)
+    receive[...] = (dot(own, weight(target, f, True)) + vector(vectors, layer, 0)).astype(BF16)
     acc[...] = jnp.zeros_like(acc)
     run_edges(0, 0, layer, f, meta_ref, receive, window, gather_ref, collect_ref, wmsg_ref, mvec_ref, hidden, normed, acc)
 
 
-def far_kernel(layer, place_ref, meta_ref, after_ref, w_own, w_across, w_beside, wmsg_ref, mvec_ref, gather_ref, collect_ref, acc_in, receive, out_ref, window, hidden, normed, acc):
+def far_kernel(layer, place_ref, meta_ref, after_ref, wmsg_ref, mvec_ref, gather_ref, collect_ref, acc_in, receive, w_own, w_across, w_beside, out_ref, window, hidden, normed, acc):
     f = place_ref[0]
-    window[...] = dot(wide(after_ref), weight((w_own, w_across, w_beside), f, 0, True)).astype(BF16)
+    window[...] = dot(wide(after_ref, FROM_BEYOND), weight((w_own, w_across, w_beside), f, True)).astype(BF16)
     acc[...] = acc_in[...]
     run_edges(1, 8, layer, f, meta_ref, receive, window, gather_ref, collect_ref, wmsg_ref, mvec_ref, hidden, normed, acc)
     out_ref[...] = acc[...].astype(BF16)
 
 
-def node_kernel(layer, final, place_ref, h_ref, part_a, part_b, degree_ref, w_own, w_across, w_beside, vectors, mvec_ref, mgain_ref, *outs):
+def node_kernel(layer, final, place_ref, h_ref, part_a, part_b, degree_ref, vectors, mvec_ref, mgain_ref, *refs):
     f = place_ref[0]
-    shards = (w_own, w_across, w_beside)
+    w_latent, w_sum, w_out, outs = refs[:3], refs[3:6], refs[6:9], refs[9:]
     part = h_ref.shape[-1]
-    width = 4 * part
-    base = w_own.shape[0] - 3 * width
     total = part_a[...].astype(F32) + part_b[...].astype(F32)
     agg = total * mgain_ref[layer : layer + 1, :] + degree_ref[:, 0:1] * mvec_ref[layer, 1:2, :]
-    pre = dot(wide(h_ref), weight(shards, f, base, True))
-    pre = pre + dot(agg.astype(BF16), weight(shards, f, base + width, False)) + vector(vectors, layer, 1)
+    pre = dot(wide(h_ref), weight(w_latent, f, True))
+    pre = pre + dot(agg.astype(BF16), weight(w_sum, f, False)) + vector(vectors, layer, 1)
     inner = jnp.maximum(pre, 0.0).astype(BF16)
     inner = jnp.concatenate([inner[:, m * part : (m + 1) * part] for m in ORDER], axis=1)
-    node = dot(inner, weight(shards, f, base + 2 * width, True)) + vector(vectors, layer, 2)
+    node = dot(inner, weight(w_out, f, True)) + vector(vectors, layer, 2)
     centred = node - jnp.mean(node, axis=1, keepdims=True)
     spread = jnp.mean(centred * centred, axis=1, keepdims=True)
     change = centred * lax.rsqrt(spread + EPSILON) * vector(vectors, layer, 4) + vector(vectors, layer, 3)
@@ -238,10 +230,16 @@
     out_ref[pl.ds(pl.multiple_of((1 - side) * rows, rows), rows), :] = other_ref[...]
 
 
+def rows_of(weights, at, count):
+    specs = [pl.BlockSpec((count, w.shape[-1]), lambda i: (at, 0)) for w in weights[:2]]
+    return weights, specs + [pl.BlockSpec((2, count, weights[2].shape[-1]), lambda i: (0, at, 0))]
+
+
 def call(kernel, name, inputs, spaces, outs, out_spaces, scratch=(), us=2):
     return pl.pallas_call(
         kernel,
         out_shape=outs,
+        grid=(1,),
         in_specs=spaces,
         out_specs=out_spaces,
         scratch_shapes=list(scratch),
@@ -283,31 +281,24 @@
     own = lax.dynamic_index_in_dim(halves, side, 0, keepdims=False)
     other = lax.dynamic_index_in_dim(halves, 1 - side, 0, keepdims=False)
     across = exchange(other, 2)
-    first = call(
-        first_pack_kernel,
-        "first_pack",
-        (w_src, w_dst, node_vectors, node_gain),
-        [VMEM] * 4,
-        jax.ShapeDtypeStruct((2 * width + 3 * VECTOR_ROWS, part), BF16),
-        VMEM,
-        us=1,
+    pack, next_pack = call(
+        pack_kernel,
+        "packs",
+        (w_src, w_dst, w_node_in, w_node_out, node_vectors, node_gain),
+        [VMEM] * 6,
+        (
+            jax.ShapeDtypeStruct((5 * width + 4 * VECTOR_ROWS, part), BF16),
+            jax.ShapeDtypeStruct((5 * width, part), BF16),
+        ),
+        (VMEM, VMEM),
     )
-    first_across = exchange(first, 2)
-    node_pack, next_pack = call(
-        other_packs_kernel,
-        "other_packs",
-        (w_src, w_dst, w_node_in, w_node_out),
-        [VMEM] * 4,
-        (jax.ShapeDtypeStruct((3 * width, part), BF16), jax.ShapeDtypeStruct((5 * width, part), BF16)),
-        (VMEM, VMEM),
-        us=2,
-    )
+    pack_across = exchange(pack, 2)
+    next_across = from_other_side(next_pack)
     pair = jnp.stack([own, across])
     latent = jnp.concatenate([pair, exchange(pair, 1)], axis=0)
-    node_share, nbr_blocks = barrier((node_pack, nbr_blocks, latent))[:2]
-    node_across = exchange(node_share, 2)
 
     all_slots = mine * slots + 1
+    nbr_blocks = barrier((nbr_blocks, latent))[0]
     gather, collect, degree, meta = call(
         prepare_kernel,
         "one_hots",
@@ -323,29 +314,31 @@
         [pltpu.VMEM((edges, edges), F32)],
         us=3,
     )
-    edge_weights = (first, first_across, exchange(jnp.stack([first, first_across]), 1))
-
     vectors = None
     messages = w_msg.reshape(LAYERS * 4, part, width)
     for layer in range(LAYERS):
         final = layer == LAYERS - 1
-        after = pass_on(latent)
-        beyond = pass_on(after)
+        after = swap_with(latent, 1)
+        beyond = swap_with(latent, 2)
         if layer == 0:
-            next_share = barrier((next_pack, after))[0]
-            next_across = from_other_side(next_share)
+            pack_across, next_across, after, meta = barrier((pack_across, next_across, after, meta))
+            weights = (pack, pack_across, exchange(jnp.stack([pack, pack_across]), 1))
+        message_spec = pl.BlockSpec((4, part, width), lambda i, layer=layer: (layer, 0, 0))
+        edge_inputs = [messages, msg_vectors, gather, collect]
+        edge_specs = [message_spec, VMEM, VMEM, VMEM]
+        source, source_specs = rows_of(weights, 3, width)
+        target, target_specs = rows_of(weights, 4, width)
         outs = [jax.ShapeDtypeStruct((rows, width), F32), jax.ShapeDtypeStruct((rows, width), BF16)]
-        inputs = [place, meta, latent, after, *edge_weights]
         if layer == 0:
             outs.append(jax.ShapeDtypeStruct((4, VECTOR_ROWS, part), F32))
+            extra, extra_specs = rows_of(weights, 5 * width // (4 * VECTOR_ROWS), 4 * VECTOR_ROWS)
         else:
-            inputs.append(vectors)
-        inputs += [messages, msg_vectors, gather, collect]
+            extra, extra_specs = (vectors,), [VMEM]
         result = call(
             lambda *refs, layer=layer: near_kernel(layer, layer == 0, *refs),
             f"near{layer}",
-            inputs,
-            [SMEM, SMEM] + [VMEM] * (len(inputs) - 2),
+            [place, meta, latent, after, *edge_inputs, *source, *target, *extra],
+            [SMEM, SMEM, VMEM, VMEM, *edge_specs, *source_specs, *target_specs, *extra_specs],
             outs,
             [VMEM] * len(outs),
             [
@@ -358,11 +351,17 @@
         acc, receive = result[0], result[1]
         if layer == 0:
             vectors = result[2]
+            acc, next_across = barrier((acc, next_across))
+            beside = exchange(jnp.stack([next_pack, next_across]), 1)
+            beyond, beside, acc = barrier((beyond, beside, acc))
+            next_weights = (next_pack, next_across, beside)
+        else:
+            beyond, acc = barrier((beyond, acc))
         partial = call(
             lambda *refs, layer=layer: far_kernel(layer, *refs),
             f"far{layer}",
-            [place, meta, beyond, *edge_weights, messages, msg_vectors, gather, collect, acc, receive],
-            [SMEM, SMEM] + [VMEM] * 10,
+            [place, meta, beyond, *edge_inputs, acc, receive, *source],
+            [SMEM, SMEM, VMEM, *edge_specs, VMEM, VMEM, *source_specs],
             jax.ShapeDtypeStruct((rows, width), BF16),
             VMEM,
             [
@@ -374,17 +373,16 @@
             us=3,
         )
         theirs = exchange(partial, 1)
-        if layer == 0:
-            node_weights = (node_pack, node_across, exchange(jnp.stack([node_pack, node_across]), 1))
         if final:
             outs = [jax.ShapeDtypeStruct((rows, part), BF16)] * 2
         else:
             outs = [jax.ShapeDtypeStruct((4, rows, part), BF16)]
+        matrices = [rows_of(weights, i, width) for i in range(3)]
         result = call(
             lambda *refs, layer=layer, final=final: node_kernel(layer, final, *refs),
             f"node{layer}",
-            [place, latent, partial, theirs, degree, *node_weights, vectors, msg_vectors, msg_gain],
-            [SMEM] + [VMEM] * 10,
+            [place, latent, partial, theirs, degree, vectors, msg_vectors, msg_gain] + [w for group, _ in matrices for w in group],
+            [SMEM] + [VMEM] * 7 + [spec for _, specs in matrices for spec in specs],
             outs,
             [VMEM] * len(outs),
         )
@@ -398,9 +396,7 @@
                 VMEM,
             )
         latent = result[0]
-        next_across = barrier((next_across, latent))[0]
-        edge_weights = (next_pack, next_across, exchange(jnp.stack([next_pack, next_across]), 1))
-        node_weights = edge_weights
+        weights = next_weights
 
 
 def solution(mesh):

time: 130 us -> 136 us (1.046)
  waiting for transfers between devices: 54 us -> 62.6 us
  starting transfers between devices: 50.1 us -> 44.3 us
  local copies, waits for them, and re-layouts: 4.4 us -> 6.36 us
  Pallas kernels: 19.2 us -> 21.1 us
    ppermute x10 -> x8, starting transfers between devices: 38.6 us -> 26.7 us  [exchange(): return lax.ppermute(value, BOTH, [(i, i ^ mask) for i in range(total)])]
    ppermute x1, starting transfers between devices: 1.92 us -> 9.13 us  [from_other_side(): return lax.ppermute(value, BOTH, pairs)]
    ppermute x4, waiting for transfers between devices: 26.7 us -> 31.8 us  [swap_with(): lax.ppermute(value, BOTH, [(i, t) for i, t in pairs if 0 <= t < total])]
    ppermute x10 -> x8, waiting for transfers between devices: 10.9 us -> 15.3 us  [exchange(): return lax.ppermute(value, BOTH, [(i, i ^ mask) for i in range(total)])]
    unnamed x28, local copies, waits for them, and re-layouts: 3.33 us -> 5.29 us
    pallas_call x10 -> x9, Pallas kernels: 19.2 us -> 21.1 us  [call(): pl.pallas_call(kernel, out_shape=outs, grid=(1,), in_specs=spaces, out_sp...]
  transfers between devices with their start and end apart: 15 -> 13, of which waited for: 8 -> 9; matrix products, arithmetic and copies ran while one was open for 1% -> 0% of each run, Pallas kernels for 11% -> 4%
where the time goes in v4:
time: 136 us; the launch traced here: 135 us
  waiting for transfers between devices  62.6 us (46%)
  starting transfers between devices  44.3 us (33%)
  Pallas kernels  21.1 us (16%)
  local copies, waits for them, and re-layouts  6.36 us (5%)
    ppermute x4, waiting for transfers between devices, swap_with(): lax.ppermute(value, BOTH, [(i, t) for i, t in pairs if 0 <= t < total])  31.8 us
    ppermute x8, starting transfers between devices, exchange(): return lax.ppermute(value, BOTH, [(i, i ^ mask) for i in range(total)])  26.7 us
    pallas_call x9, Pallas kernels, call(): pl.pallas_call(kernel, out_shape=outs, grid=(1,), in_specs=spaces, out_sp...  21.1 us
    ppermute x1, waiting for transfers between devices, from_other_side(): return lax.ppermute(value, BOTH, pairs)  15.6 us
    ppermute x8, waiting for transfers between devices, exchange(): return lax.ppermute(value, BOTH, [(i, i ^ mask) for i in range(total)])  15.3 us
    ppermute x1, starting transfers between devices, from_other_side(): return lax.ppermute(value, BOTH, pairs)  9.13 us
    ppermute x4, starting transfers between devices, swap_with(): lax.ppermute(value, BOTH, [(i, t) for i, t in pairs if 0 <= t < total])  8.43 us
    unnamed x28, local copies, waits for them, and re-layouts  5.29 us
  transfers between devices with their start and end apart: 13, of which 9 were waited for; matrix products, arithmetic and copies ran while one was open for 0% of the time, Pallas kernels for 4%

profile of v4, /device:TPU:6, one launch (start us, length us, event | category | flops | bytes accessed | tf_op | source)
XLA Modules:
  0.0 135.0 jit_solution(3787517680671891095)
XLA Ops:
  0.0 1.0 constant_dynamic-slice_fusion
  1.0 4.3 %collective-permute-start = (bf16[512,128]{1,0:T(8,128)(2,1)S(1)}, bf16[512,128]{1,0:T(8,128)(2,1)S(1)}, u32[]{:S(2)}, u32[]{:S(2)}) collective-permute-start(bf16[512,128]{1,0:T(8,128)(2,1)S(1)} %get-tuple-element.56), channel_id=1, source_target_pairs={{0,2},{1,3},{2,0},{3,1},{4,6},{5,7},{6,4},{7,5},{8,10},{9,11},{10,... | collective-permute-start | bytes 393224 | tf_op jit(solution)/shard_map/ppermute | solution.py:30
  5.3 3.5 %collective-permute-done = bf16[512,128]{1,0:T(8,128)(2,1)S(1)} collective-permute-done((bf16[512,128]{1,0:T(8,128)(2,1)S(1)}, bf16[512,128]{1,0:T(8,128)(2,1)S(1)}, u32[]{:S(2)}, u32[]{:S(2)}) %collective-permute-start) | collective-permute-done | bytes 131104 | tf_op jit(solution)/shard_map/ppermute | solution.py:30
  8.8 1.9 %collective-permute-start.1 = (bf16[2,512,128]{2,1,0:T(8,128)(2,1)S(1)}, bf16[2,512,128]{2,1,0:T(8,128)(2,1)S(1)}, u32[]{:S(2)}, u32[]{:S(2)}) collective-permute-start(bf16[2,512,128]{2,1,0:T(8,128)(2,1)S(1)} %pad_maximum_fusion.3), channel_id=1, source_target_pairs={{0,1},{1,0},{2,3},{3,2},{4,5},{5,4},{6,7},{7,6},{8,9},{9,8},{10,11... | collective-permute-start | bytes 786440 | tf_op jit(solution)/shard_map/ppermute | solution.py:30
  10.7 1.0 copy-done.3
  16.1 3.6 %collective-permute-start.2 = (bf16[2624,128]{1,0:T(8,128)(2,1)S(1)}, bf16[2624,128]{1,0:T(8,128)(2,1)S(1)}, u32[]{:S(2)}, u32[]{:S(2)}) collective-permute-start(bf16[2624,128]{1,0:T(8,128)(2,1)S(1)} %get-tuple-element.30.refs_8_.refs_11_.refs_14_.refs_9_), channel_id=1, source_target_pairs={{0,2},{1,3},{2,0},{3,1},{4,6},{5,7},{6,4},{7,5},{8,10},{9,11},{10,... | collective-permute-start | bytes 2015240 | tf_op jit(solution)/shard_map/ppermute | solution.py:30
  19.7 9.1 %collective-permute-start.3 = (bf16[2560,128]{1,0:T(8,128)(2,1)S(1)}, bf16[2560,128]{1,0:T(8,128)(2,1)S(1)}, u32[]{:S(2)}, u32[]{:S(2)}) collective-permute-start(bf16[2560,128]{1,0:T(8,128)(2,1)S(1)} %get-tuple-element.31.refs_8_.refs_11_.refs_9_.refs_14_), channel_id=1, source_target_pairs={{0,14},{1,15},{2,4},{3,5},{4,2},{5,3},{6,8},{7,9},{8,6},{9,7},{10,... | collective-permute-start | bytes 1966088 | tf_op jit(solution)/shard_map/ppermute | solution.py:48
  29.0 1.9 %collective-permute-start.4 = (bf16[4,512,128]{2,1,0:T(8,128)(2,1)S(1)}, bf16[4,512,128]{2,1,0:T(8,128)(2,1)}, u32[]{:S(2)}, u32[]{:S(2)}) collective-permute-start(bf16[4,512,128]{2,1,0:T(8,128)(2,1)S(1)} %pad_maximum_fusion.2.refs_2_.refs_1_), channel_id=1, source_target_pairs={{0,3},{2,5},{3,0},{4,7},{5,2},{6,9},{7,4},{8,11},{9,6},{10,13},{11... | collective-permute-start | bytes 1572872 | tf_op jit(solution)/shard_map/ppermute | solution.py:37
  31.1 2.2 %one_hots.1 = (bf16[25,128,256]{2,1,0:T(8,128)(2,1)S(1)}, bf16[25,128,128]{2,1,0:T(8,128)(2,1)S(1)}, f32[512,128]{1,0:T(8,128)S(1)}, s32[4,32]{1,0:T(4,128)S(1)}) custom-call(s32[5]{0:T(128)S(1)} %stack.48.place_ref.refs_0_, s32[8,6]{1,0:T(8,128)S(1)} %copy-done.8, s32[8,6]{1,0:T(8,128)S(1)} %copy-done.9, s32[8,6,128]{2,1,0:T(8,128)S(1)} %copy.15.src_ref, ...), custom_call_target="tpu_custom_call" | custom-call | flops 3000000000 | bytes 1048576 | tf_op jit(solution)/shard_map/one_hots/pallas_call | solution.py:239
  33.3 15.6 %collective-permute-done.3.refs_9_.refs_12_.refs_10_.refs_15_ = bf16[2560,128]{1,0:T(8,128)(2,1)S(1)} collective-permute-done((bf16[2560,128]{1,0:T(8,128)(2,1)S(1)}, bf16[2560,128]{1,0:T(8,128)(2,1)S(1)}, u32[]{:S(2)}, u32[]{:S(2)}) %collective-permute-start.3) | collective-permute-done | bytes 655392 | tf_op jit(solution)/shard_map/ppermute | solution.py:48
  49.0 2.1 %collective-permute-start.6 = (bf16[2,2624,128]{2,1,0:T(8,128)(2,1)S(1)}, bf16[2,2624,128]{2,1,0:T(8,128)(2,1)S(1)}, u32[]{:S(2)}, u32[]{:S(2)}) collective-permute-start(bf16[2,2624,128]{2,1,0:T(8,128)(2,1)S(1)} %pad_maximum_fusion), channel_id=1, source_target_pairs={{0,1},{1,0},{2,3},{3,2},{4,5},{5,4},{6,7},{7,6},{8,9},{9,8},{10,11... | collective-permute-start | bytes 4030472 | tf_op jit(solution)/shard_map/ppermute | solution.py:30
  51.1 3.0 %collective-permute-done.6.refs_10_.refs_13_.refs_16_.refs_11_ = bf16[2,2624,128]{2,1,0:T(8,128)(2,1)S(1)} collective-permute-done((bf16[2,2624,128]{2,1,0:T(8,128)(2,1)S(1)}, bf16[2,2624,128]{2,1,0:T(8,128)(2,1)S(1)}, u32[]{:S(2)}, u32[]{:S(2)}) %collective-permute-start.6) | collective-permute-done | bytes 1343520 | tf_op jit(solution)/shard_map/ppermute | solution.py:30
  54.1 4.1 %near0.1 = (f32[512,512]{1,0:T(8,128)S(1)}, bf16[512,512]{1,0:T(8,128)(2,1)S(1)}, f32[4,16,128]{2,1,0:T(8,128)S(1)}) custom-call(s32[5]{0:T(128)S(1)} %stack.48.place_ref.refs_0_, s32[4,32]{1,0:T(4,128)S(1)} %get-tuple-element.34.refs_1_, bf16[4,512,128]{2,1,0:T(8,128)(2,1)S(1)} %pad_maximum_fusion.2.refs_2_.refs_1_, ...), custom_call_target="tpu_custom_call" | custom-call | flops 5000000000 | bytes 1048576 | tf_op jit(solution)/shard_map/near0/pallas_call | solution.py:239
  58.3 2.0 %collective-permute-start.7 = (bf16[2,2560,128]{2,1,0:T(8,128)(2,1)S(1)}, bf16[2,2560,128]{2,1,0:T(8,128)(2,1)S(1)}, u32[]{:S(2)}, u32[]{:S(2)}) collective-permute-start(bf16[2,2560,128]{2,1,0:T(8,128)(2,1)S(1)} %pad_maximum_fusion.1), channel_id=1, source_target_pairs={{0,1},{1,0},{2,3},{3,2},{4,5},{5,4},{6,7},{7,6},{8,9},{9,8},{10,11... | collective-permute-start | bytes 3932168 | tf_op jit(solution)/shard_map/ppermute | solution.py:30
  60.4 1.9 %collective-permute-start.5 = (bf16[4,512,128]{2,1,0:T(8,128)(2,1)S(1)}, bf16[4,512,128]{2,1,0:T(8,128)(2,1)S(1)}, u32[]{:S(2)}, u32[]{:S(2)}) collective-permute-start(bf16[4,512,128]{2,1,0:T(8,128)(2,1)S(1)} %pad_maximum_fusion.2.refs_2_.refs_1_), channel_id=1, source_target_pairs={{0,5},{2,7},{4,9},{5,0},{6,11},{7,2},{8,13},{9,4},{10,15},{11,6},{... | collective-permute-start | bytes 1572872 | tf_op jit(solution)/shard_map/ppermute | solution.py:37
  62.3 17.9 %collective-permute-done.5.refs_2_ = bf16[4,512,128]{2,1,0:T(8,128)(2,1)S(1)} collective-permute-done((bf16[4,512,128]{2,1,0:T(8,128)(2,1)S(1)}, bf16[4,512,128]{2,1,0:T(8,128)(2,1)S(1)}, u32[]{:S(2)}, u32[]{:S(2)}) %collective-permute-start.5) | collective-permute-done | bytes 524320 | tf_op jit(solution)/shard_map/ppermute | solution.py:37
  80.2 3.1 %far0.1.refs_2_ = bf16[512,512]{1,0:T(8,128)(2,1)S(1)} custom-call(s32[5]{0:T(128)S(1)} %stack.48.place_ref.refs_0_, s32[4,32]{1,0:T(4,128)S(1)} %get-tuple-element.34.refs_1_, bf16[4,512,128]{2,1,0:T(8,128)(2,1)S(1)} %collective-permute-done.5.refs_2_, bf16[8,128,512]{2,1,0:T(8,128)(2,1)S(1)} %bitcast.19, f32[2,2,512]{2,1,0:T(2,128)S(1)} %copy-done, ...), custom_call_target="tpu_custom_call" | custom-call | flops 3000000000 | bytes 1048576 | tf_op jit(solution)/shard_map/far0/pallas_call | solution.py:239
  83.3 3.4 %collective-permute-start.8 = (bf16[512,512]{1,0:T(8,128)(2,1)S(1)}, bf16[512,512]{1,0:T(8,128)(2,1)S(1)}, u32[]{:S(2)}, u32[]{:S(2)}) collective-permute-start(bf16[512,512]{1,0:T(8,128)(2,1)S(1)} %far0.1.refs_2_), channel_id=1, source_target_pairs={{0,1},{1,0},{2,3},{3,2},{4,5},{5,4},{6,7},{7,6},{8,9},{9,8},{10,11... | collective-permute-start | bytes 1572872 | tf_op jit(solution)/shard_map/ppermute | solution.py:30
  86.7 1.5 %collective-permute-done.8.refs_3_ = bf16[512,512]{1,0:T(8,128)(2,1)S(1)} collective-permute-done((bf16[512,512]{1,0:T(8,128)(2,1)S(1)}, bf16[512,512]{1,0:T(8,128)(2,1)S(1)}, u32[]{:S(2)}, u32[]{:S(2)}) %collective-permute-start.8) | collective-permute-done | bytes 524320 | tf_op jit(solution)/shard_map/ppermute | solution.py:30
  88.3 1.9 %node0.1.refs_2_.refs_1_ = bf16[4,512,128]{2,1,0:T(8,128)(2,1)S(1)} custom-call(s32[5]{0:T(128)S(1)} %stack.48.place_ref.refs_0_, bf16[4,512,128]{2,1,0:T(8,128)(2,1)S(1)} %pad_maximum_fusion.2.refs_2_.refs_1_, bf16[512,512]{1,0:T(8,128)(2,1)S(1)} %far0.1.refs_2_, bf16[512,512]{1,0:T(8,128)(2,1)S(1)} %collective-permute-done.8.refs_3_, ...), custom_call_target="tpu_custom_call" | custom-call | flops 2000000000 | bytes 1048576 | tf_op jit(solution)/shard_map/node0/pallas_call | solution.py:239
  90.2 1.9 %collective-permute-start.10 = (bf16[4,512,128]{2,1,0:T(8,128)(2,1)S(1)}, bf16[4,512,128]{2,1,0:T(8,128)(2,1)S(1)}, u32[]{:S(2)}, u32[]{:S(2)}) collective-permute-start(bf16[4,512,128]{2,1,0:T(8,128)(2,1)S(1)} %node0.1.refs_2_.refs_1_), channel_id=1, source_target_pairs={{0,3},{2,5},{3,0},{4,7},{5,2},{6,9},{7,4},{8,11},{9,6},{10,13},{11... | collective-permute-start | bytes 1572872 | tf_op jit(solution)/shard_map/ppermute | solution.py:37
  92.1 2.7 %collective-permute-start.9 = (bf16[4,512,128]{2,1,0:T(8,128)(2,1)S(1)}, bf16[4,512,128]{2,1,0:T(8,128)(2,1)S(1)}, u32[]{:S(2)}, u32[]{:S(2)}) collective-permute-start(bf16[4,512,128]{2,1,0:T(8,128)(2,1)S(1)} %node0.1.refs_2_.refs_1_), channel_id=1, source_target_pairs={{0,5},{2,7},{4,9},{5,0},{6,11},{7,2},{8,13},{9,4},{10,15},{11,6},{... | collective-permute-start | bytes 1572872 | tf_op jit(solution)/shard_map/ppermute | solution.py:37
  94.8 11.5 %collective-permute-done.10.refs_3_ = bf16[4,512,128]{2,1,0:T(8,128)(2,1)S(1)} collective-permute-done((bf16[4,512,128]{2,1,0:T(8,128)(2,1)S(1)}, bf16[4,512,128]{2,1,0:T(8,128)(2,1)S(1)}, u32[]{:S(2)}, u32[]{:S(2)}) %collective-permute-start.10) | collective-permute-done | bytes 524320 | tf_op jit(solution)/shard_map/ppermute | solution.py:37
  106.2 3.6 %near1.1 = (f32[512,512]{1,0:T(8,128)S(1)}, bf16[512,512]{1,0:T(8,128)(2,1)S(1)}) custom-call(s32[5]{0:T(128)S(1)} %stack.48.place_ref.refs_0_, s32[4,32]{1,0:T(4,128)S(1)} %get-tuple-element.34.refs_1_, bf16[4,512,128]{2,1,0:T(8,128)(2,1)S(1)} %node0.1.refs_2_.refs_1_, bf16[4,512,128]{2,1,0:T(8,128)(2,1)S(1)} %collective-permute-done.10.refs_3_, ...), custom_call_target="tpu_custom_call" | custom-call | flops 5000000000 | bytes 1048576 | tf_op jit(solution)/shard_map/near1/pallas_call | solution.py:239
  109.8 2.4 %collective-permute-done.9.refs_2_ = bf16[4,512,128]{2,1,0:T(8,128)(2,1)S(1)} collective-permute-done((bf16[4,512,128]{2,1,0:T(8,128)(2,1)S(1)}, bf16[4,512,128]{2,1,0:T(8,128)(2,1)S(1)}, u32[]{:S(2)}, u32[]{:S(2)}) %collective-permute-start.9) | collective-permute-done | bytes 524320 | tf_op jit(solution)/shard_map/ppermute | solution.py:37
  112.2 3.1 %far1.1.refs_2_ = bf16[512,512]{1,0:T(8,128)(2,1)S(1)} custom-call(s32[5]{0:T(128)S(1)} %stack.48.place_ref.refs_0_, s32[4,32]{1,0:T(4,128)S(1)} %get-tuple-element.34.refs_1_, bf16[4,512,128]{2,1,0:T(8,128)(2,1)S(1)} %collective-permute-done.9.refs_2_, bf16[8,128,512]{2,1,0:T(8,128)(2,1)S(1)} %bitcast.21, f32[2,2,512]{2,1,0:T(2,128)S(1)} %copy-done, ...), custom_call_target="tpu_custom_call" | custom-call | flops 3000000000 | bytes 1048576 | tf_op jit(solution)/shard_map/far1/pallas_call | solution.py:239
  115.3 7.5 %collective-permute-start.11 = (bf16[512,512]{1,0:T(8,128)(2,1)S(1)}, bf16[512,512]{1,0:T(8,128)(2,1)S(1)}, u32[]{:S(2)}, u32[]{:S(2)}) collective-permute-start(bf16[512,512]{1,0:T(8,128)(2,1)S(1)} %far1.1.refs_2_), channel_id=1, source_target_pairs={{0,1},{1,0},{2,3},{3,2},{4,5},{5,4},{6,7},{7,6},{8,9},{9,8},{10,11... | collective-permute-start | bytes 1572872 | tf_op jit(solution)/shard_map/ppermute | solution.py:30
  122.7 1.5 %collective-permute-done.11.refs_3_ = bf16[512,512]{1,0:T(8,128)(2,1)S(1)} collective-permute-done((bf16[512,512]{1,0:T(8,128)(2,1)S(1)}, bf16[512,512]{1,0:T(8,128)(2,1)S(1)}, u32[]{:S(2)}, u32[]{:S(2)}) %collective-permute-start.11) | collective-permute-done | bytes 524320 | tf_op jit(solution)/shard_map/ppermute | solution.py:30
  124.3 1.8 %node1.1 = (bf16[512,128]{1,0:T(8,128)(2,1)S(1)}, bf16[512,128]{1,0:T(8,128)(2,1)S(1)}) custom-call(s32[5]{0:T(128)S(1)} %stack.48.place_ref.refs_0_, bf16[4,512,128]{2,1,0:T(8,128)(2,1)S(1)} %node0.1.refs_2_.refs_1_, bf16[512,512]{1,0:T(8,128)(2,1)S(1)} %far1.1.refs_2_, bf16[512,512]{1,0:T(8,128)(2,1)S(1)} %collective-permute-done.11.refs_3_, ...), custom_call_target="tpu_custom_call" | custom-call | flops 2000000000 | bytes 1048576 | tf_op jit(solution)/shard_map/node1/pallas_call | solution.py:239
  126.1 1.9 %collective-permute-start.12 = (bf16[512,128]{1,0:T(8,128)(2,1)S(1)}, bf16[512,128]{1,0:T(8,128)(2,1)S(1)}, u32[]{:S(2)}, u32[]{:S(2)}) collective-permute-start(bf16[512,128]{1,0:T(8,128)(2,1)S(1)} %get-tuple-element.54), channel_id=1, source_target_pairs={{0,2},{1,3},{2,0},{3,1},{4,6},{5,7},{6,4},{7,5},{8,10},{9,11},{10,... | collective-permute-start | bytes 393224 | tf_op jit(solution)/shard_map/ppermute | solution.py:30
  128.0 5.7 %collective-permute-done.12.other_ref = bf16[512,128]{1,0:T(8,128)(2,1)S(1)} collective-permute-done((bf16[512,128]{1,0:T(8,128)(2,1)S(1)}, bf16[512,128]{1,0:T(8,128)(2,1)S(1)}, u32[]{:S(2)}, u32[]{:S(2)}) %collective-permute-start.12) | collective-permute-done | bytes 131104 | tf_op jit(solution)/shard_map/ppermute | solution.py:30
  133.7 1.3 join.1
  (37 shorter events, 4.8 us)
Async XLA Ops:
  1.0 7.8 %collective-permute-start = (bf16[512,128]{1,0:T(8,128)(2,1)S(1)}, bf16[512,128]{1,0:T(8,128)(2,1)S(1)}, u32[]{:S(2)}, u32[]{:S(2)}) collective-permute-start(bf16[512,128]{1,0:T(8,128)(2,1)S(1)} %get-tuple-element.56), channel_id=1, source_target_pairs={{0,2},{1,3},{2,0},{3,1},{4,6},{5,7},{6,4},{7,5},{8,10},{9,11},{10,... | collective-permute-start | bytes 393224 | tf_op jit(solution)/shard_map/ppermute | solution.py:30
  8.8 20.1 %collective-permute-start.1 = (bf16[2,512,128]{2,1,0:T(8,128)(2,1)S(1)}, bf16[2,512,128]{2,1,0:T(8,128)(2,1)S(1)}, u32[]{:S(2)}, u32[]{:S(2)}) collective-permute-start(bf16[2,512,128]{2,1,0:T(8,128)(2,1)S(1)} %pad_maximum_fusion.3), channel_id=1, source_target_pairs={{0,1},{1,0},{2,3},{3,2},{4,5},{5,4},{6,7},{7,6},{8,9},{9,8},{10,11... | collective-permute-start | bytes 786440 | tf_op jit(solution)/shard_map/ppermute | solution.py:30
  10.7 1.0 copy-start.3
  11.8 0.9 copy-start.4
  12.7 0.9 copy-start.5
  13.7 0.9 copy-start.6
  14.6 0.7 copy-start.7
  15.3 0.7 copy-start.10
  16.0 14.9 %copy-start.11 = (s32[8,6,128]{2,0,1:T(8,128)S(1)}, s32[8,6,128]{2,0,1:T(8,128)}, u32[]{:S(2)}) copy-start(s32[8,6,128]{2,0,1:T(8,128)} %param.26) | copy-start | bytes 73732
  16.0 14.9 %copy-start.12 = (s32[8,6,128]{2,0,1:T(8,128)S(1)}, s32[8,6,128]{2,0,1:T(8,128)}, u32[]{:S(2)}) copy-start(s32[8,6,128]{2,0,1:T(8,128)} %param.27) | copy-start | bytes 73732
  16.0 15.1 %copy-start.8 = (s32[8,6]{1,0:T(8,128)S(1)}, s32[8,6]{1,0:T(8,128)}, u32[]{:S(2)}) copy-start(s32[8,6]{1,0:T(8,128)} %nbr_ref) | copy-start | bytes 580
  16.0 15.1 %copy-start.9 = (s32[8,6]{1,0:T(8,128)S(1)}, s32[8,6]{1,0:T(8,128)}, u32[]{:S(2)}) copy-start(s32[8,6]{1,0:T(8,128)} %count_ref.1) | copy-start | bytes 580
  16.1 32.8 %collective-permute-start.2 = (bf16[2624,128]{1,0:T(8,128)(2,1)S(1)}, bf16[2624,128]{1,0:T(8,128)(2,1)S(1)}, u32[]{:S(2)}, u32[]{:S(2)}) collective-permute-start(bf16[2624,128]{1,0:T(8,128)(2,1)S(1)} %get-tuple-element.30.refs_8_.refs_11_.refs_14_.refs_9_), channel_id=1, source_target_pairs={{0,2},{1,3},{2,0},{3,1},{4,6},{5,7},{6,4},{7,5},{8,10},{9,11},{10,... | collective-permute-start | bytes 2015240 | tf_op jit(solution)/shard_map/ppermute | solution.py:30
  19.7 29.1 %collective-permute-start.3 = (bf16[2560,128]{1,0:T(8,128)(2,1)S(1)}, bf16[2560,128]{1,0:T(8,128)(2,1)S(1)}, u32[]{:S(2)}, u32[]{:S(2)}) collective-permute-start(bf16[2560,128]{1,0:T(8,128)(2,1)S(1)} %get-tuple-element.31.refs_8_.refs_11_.refs_9_.refs_14_), channel_id=1, source_target_pairs={{0,14},{1,15},{2,4},{3,5},{4,2},{5,3},{6,8},{7,9},{8,6},{9,7},{10,... | collective-permute-start | bytes 1966088 | tf_op jit(solution)/shard_map/ppermute | solution.py:48
  29.0 19.9 %collective-permute-start.4 = (bf16[4,512,128]{2,1,0:T(8,128)(2,1)S(1)}, bf16[4,512,128]{2,1,0:T(8,128)(2,1)}, u32[]{:S(2)}, u32[]{:S(2)}) collective-permute-start(bf16[4,512,128]{2,1,0:T(8,128)(2,1)S(1)} %pad_maximum_fusion.2.refs_2_.refs_1_), channel_id=1, source_target_pairs={{0,3},{2,5},{3,0},{4,7},{5,2},{6,9},{7,4},{8,11},{9,6},{10,13},{11... | collective-permute-start | bytes 1572872 | tf_op jit(solution)/shard_map/ppermute | solution.py:37
  48.9 5.3 %copy-start = (f32[2,2,512]{2,1,0:T(2,128)S(1)}, f32[2,2,512]{2,1,0:T(2,128)}, u32[]{:S(2)}) copy-start(f32[2,2,512]{2,1,0:T(2,128)} %refs_6_.3) | copy-start | bytes 24580
  48.9 5.3 %copy-start.2 = (bf16[2,512,512]{2,1,0:T(8,128)(2,1)S(1)}, bf16[2,512,512]{2,1,0:T(8,128)(2,1)}, u32[]{:S(2)}) copy-start(bf16[2,512,512]{2,1,0:T(8,128)(2,1)} %param.17) | copy-start | bytes 3145732
  49.0 5.1 %collective-permute-start.6 = (bf16[2,2624,128]{2,1,0:T(8,128)(2,1)S(1)}, bf16[2,2624,128]{2,1,0:T(8,128)(2,1)S(1)}, u32[]{:S(2)}, u32[]{:S(2)}) collective-permute-start(bf16[2,2624,128]{2,1,0:T(8,128)(2,1)S(1)} %pad_maximum_fusion), channel_id=1, source_target_pairs={{0,1},{1,0},{2,3},{3,2},{4,5},{5,4},{6,7},{7,6},{8,9},{9,8},{10,11... | collective-permute-start | bytes 4030472 | tf_op jit(solution)/shard_map/ppermute | solution.py:30
  58.3 21.9 %collective-permute-start.7 = (bf16[2,2560,128]{2,1,0:T(8,128)(2,1)S(1)}, bf16[2,2560,128]{2,1,0:T(8,128)(2,1)S(1)}, u32[]{:S(2)}, u32[]{:S(2)}) collective-permute-start(bf16[2,2560,128]{2,1,0:T(8,128)(2,1)S(1)} %pad_maximum_fusion.1), channel_id=1, source_target_pairs={{0,1},{1,0},{2,3},{3,2},{4,5},{5,4},{6,7},{7,6},{8,9},{9,8},{10,11... | collective-permute-start | bytes 3932168 | tf_op jit(solution)/shard_map/ppermute | solution.py:30
  60.4 19.9 %collective-permute-start.5 = (bf16[4,512,128]{2,1,0:T(8,128)(2,1)S(1)}, bf16[4,512,128]{2,1,0:T(8,128)(2,1)S(1)}, u32[]{:S(2)}, u32[]{:S(2)}) collective-permute-start(bf16[4,512,128]{2,1,0:T(8,128)(2,1)S(1)} %pad_maximum_fusion.2.refs_2_.refs_1_), channel_id=1, source_target_pairs={{0,5},{2,7},{4,9},{5,0},{6,11},{7,2},{8,13},{9,4},{10,15},{11,6},{... | collective-permute-start | bytes 1572872 | tf_op jit(solution)/shard_map/ppermute | solution.py:37
  80.2 8.0 %copy-start.1 = (f32[2,512]{1,0:T(2,128)S(1)}, f32[2,512]{1,0:T(2,128)}, u32[]{:S(2)}) copy-start(f32[2,512]{1,0:T(2,128)} %refs_7_.3) | copy-start | bytes 12292
  83.3 4.9 %collective-permute-start.8 = (bf16[512,512]{1,0:T(8,128)(2,1)S(1)}, bf16[512,512]{1,0:T(8,128)(2,1)S(1)}, u32[]{:S(2)}, u32[]{:S(2)}) collective-permute-start(bf16[512,512]{1,0:T(8,128)(2,1)S(1)} %far0.1.refs_2_), channel_id=1, source_target_pairs={{0,1},{1,0},{2,3},{3,2},{4,5},{5,4},{6,7},{7,6},{8,9},{9,8},{10,11... | collective-permute-start | bytes 1572872 | tf_op jit(solution)/shard_map/ppermute | solution.py:30
  90.2 16.1 %collective-permute-start.10 = (bf16[4,512,128]{2,1,0:T(8,128)(2,1)S(1)}, bf16[4,512,128]{2,1,0:T(8,128)(2,1)S(1)}, u32[]{:S(2)}, u32[]{:S(2)}) collective-permute-start(bf16[4,512,128]{2,1,0:T(8,128)(2,1)S(1)} %node0.1.refs_2_.refs_1_), channel_id=1, source_target_pairs={{0,3},{2,5},{3,0},{4,7},{5,2},{6,9},{7,4},{8,11},{9,6},{10,13},{11... | collective-permute-start | bytes 1572872 | tf_op jit(solution)/shard_map/ppermute | solution.py:37
  92.1 20.1 %collective-permute-start.9 = (bf16[4,512,128]{2,1,0:T(8,128)(2,1)S(1)}, bf16[4,512,128]{2,1,0:T(8,128)(2,1)S(1)}, u32[]{:S(2)}, u32[]{:S(2)}) collective-permute-start(bf16[4,512,128]{2,1,0:T(8,128)(2,1)S(1)} %node0.1.refs_2_.refs_1_), channel_id=1, source_target_pairs={{0,5},{2,7},{4,9},{5,0},{6,11},{7,2},{8,13},{9,4},{10,15},{11,6},{... | collective-permute-start | bytes 1572872 | tf_op jit(solution)/shard_map/ppermute | solution.py:37
  115.3 9.0 %collective-permute-start.11 = (bf16[512,512]{1,0:T(8,128)(2,1)S(1)}, bf16[512,512]{1,0:T(8,128)(2,1)S(1)}, u32[]{:S(2)}, u32[]{:S(2)}) collective-permute-start(bf16[512,512]{1,0:T(8,128)(2,1)S(1)} %far1.1.refs_2_), channel_id=1, source_target_pairs={{0,1},{1,0},{2,3},{3,2},{4,5},{5,4},{6,7},{7,6},{8,9},{9,8},{10,11... | collective-permute-start | bytes 1572872 | tf_op jit(solution)/shard_map/ppermute | solution.py:30
  126.1 7.7 %collective-permute-start.12 = (bf16[512,128]{1,0:T(8,128)(2,1)S(1)}, bf16[512,128]{1,0:T(8,128)(2,1)S(1)}, u32[]{:S(2)}, u32[]{:S(2)}) collective-permute-start(bf16[512,128]{1,0:T(8,128)(2,1)S(1)} %get-tuple-element.54), channel_id=1, source_target_pairs={{0,2},{1,3},{2,0},{3,1},{4,6},{5,7},{6,4},{7,5},{8,10},{9,11},{10,... | collective-permute-start | bytes 393224 | tf_op jit(solution)/shard_map/ppermute | solution.py:30

commit v5 on v4

--- a/solution.py
+++ b/solution.py
@@ -19,6 +19,7 @@
 LIST = 32
 VMEM = pl.BlockSpec(memory_space=pltpu.VMEM)
 SMEM = pl.BlockSpec(memory_space=pltpu.SMEM)
+ANY = pl.BlockSpec(memory_space=pl.ANY)
 
 
 def dot(a, b):
@@ -101,24 +102,36 @@
     collect_ref[last - 1] = jnp.zeros(collect_ref.shape[1:], BF16)
 
 
-def pack_kernel(src_ref, dst_ref, in_ref, out_w_ref, vec_ref, gain_ref, first_ref, next_ref):
+def pack_kernel(src_ref, dst_ref, in_ref, out_w_ref, vec_ref, gain_ref, first_ref, next_ref, rows, sems):
     width = src_ref.shape[1]
+    copies = []
     for layer, ref in enumerate((first_ref, next_ref)):
-        ref[: 2 * width, :] = in_ref[layer]
-        ref[2 * width : 3 * width, :] = out_w_ref[layer]
-        ref[3 * width : 4 * width, :] = src_ref[layer]
-        ref[4 * width : 5 * width, :] = dst_ref[layer]
+        for source, at in ((in_ref, 0), (out_w_ref, 2), (src_ref, 3), (dst_ref, 4)):
+            count = source.shape[1]
+            copies.append(
+                pltpu.make_async_copy(
+                    source.at[layer], ref.at[pl.ds(at * width, count), :], sems.at[len(copies)]
+                )
+            )
+    for copy in copies:
+        copy.start()
     rest = jnp.concatenate(
         [part for layer in range(LAYERS) for part in (vec_ref[layer], gain_ref[layer : layer + 1, :])]
         + [jnp.zeros((VECTOR_ROWS - 5 * LAYERS, src_ref.shape[2]), F32)],
         axis=0,
     )
     for i in range(3):
-        at = 5 * width + i * VECTOR_ROWS
         piece = rest.astype(BF16)
-        first_ref[at : at + VECTOR_ROWS, :] = piece
+        rows[i * VECTOR_ROWS : (i + 1) * VECTOR_ROWS, :] = piece
         rest = rest - piece.astype(F32)
-    first_ref[5 * width + 3 * VECTOR_ROWS :, :] = jnp.zeros((VECTOR_ROWS, src_ref.shape[2]), BF16)
+    rows[3 * VECTOR_ROWS :, :] = jnp.zeros((VECTOR_ROWS, src_ref.shape[2]), BF16)
+    last = pltpu.make_async_copy(
+        rows, first_ref.at[pl.ds(5 * width, 4 * VECTOR_ROWS), :], sems.at[len(copies)]
+    )
+    last.start()
+    for copy in copies:
+        copy.wait()
+    last.wait()
 
 
 def wide(ref, order=STRAIGHT):
@@ -126,12 +139,11 @@
 
 
 def weight(shards, f, mixed):
-    own, across, beside = shards
-    part = own.shape[-1]
+    part = shards[0].shape[-1]
     rows = []
     for i in range(4):
         at = pl.ds(pl.multiple_of((f ^ ORDER[i]) * part, part) if mixed else i * part, part)
-        rows.append(jnp.concatenate([own[at, :], beside[0, at, :], across[at, :], beside[1, at, :]], axis=1))
+        rows.append(jnp.concatenate([w[at, :] for w in shards], axis=1))
     return jnp.concatenate(rows, axis=0)
 
 
@@ -172,10 +184,10 @@
 
 
 def near_kernel(layer, first, place_ref, meta_ref, h_ref, next_ref, wmsg_ref, mvec_ref, gather_ref, collect_ref, *refs):
-    source, target, refs = refs[:3], refs[3:6], refs[6:]
+    source, target, refs = refs[:4], refs[4:8], refs[8:]
     if first:
-        own_rows, across_rows, beside_rows, acc, receive, vectors, window, hidden, normed = refs
-        for m, w in enumerate((own_rows, beside_rows.at[0], across_rows, beside_rows.at[1])):
+        shards, (acc, receive, vectors, window, hidden, normed) = refs[:4], refs[4:]
+        for m, w in enumerate(shards):
             rows = w[...].astype(F32)
             vectors[m] = rows[:VECTOR_ROWS] + rows[VECTOR_ROWS : 2 * VECTOR_ROWS] + rows[2 * VECTOR_ROWS : 3 * VECTOR_ROWS]
     else:
@@ -191,9 +203,9 @@
     run_edges(0, 0, layer, f, meta_ref, receive, window, gather_ref, collect_ref, wmsg_ref, mvec_ref, hidden, normed, acc)
 
 
-def far_kernel(layer, place_ref, meta_ref, after_ref, wmsg_ref, mvec_ref, gather_ref, collect_ref, acc_in, receive, w_own, w_across, w_beside, out_ref, window, hidden, normed, acc):
+def far_kernel(layer, place_ref, meta_ref, after_ref, wmsg_ref, mvec_ref, gather_ref, collect_ref, acc_in, receive, w0, w1, w2, w3, out_ref, window, hidden, normed, acc):
     f = place_ref[0]
-    window[...] = dot(wide(after_ref, FROM_BEYOND), weight((w_own, w_across, w_beside), f, True)).astype(BF16)
+    window[...] = dot(wide(after_ref, FROM_BEYOND), weight((w0, w1, w2, w3), f, True)).astype(BF16)
     acc[...] = acc_in[...]
     run_edges(1, 8, layer, f, meta_ref, receive, window, gather_ref, collect_ref, wmsg_ref, mvec_ref, hidden, normed, acc)
     out_ref[...] = acc[...].astype(BF16)
@@ -201,7 +213,7 @@
 
 def node_kernel(layer, final, place_ref, h_ref, part_a, part_b, degree_ref, vectors, mvec_ref, mgain_ref, *refs):
     f = place_ref[0]
-    w_latent, w_sum, w_out, outs = refs[:3], refs[3:6], refs[6:9], refs[9:]
+    w_latent, w_sum, w_out, outs = refs[:4], refs[4:8], refs[8:12], refs[12:]
     part = h_ref.shape[-1]
     total = part_a[...].astype(F32) + part_b[...].astype(F32)
     agg = total * mgain_ref[layer : layer + 1, :] + degree_ref[:, 0:1] * mvec_ref[layer, 1:2, :]
@@ -231,8 +243,7 @@
 
 
 def rows_of(weights, at, count):
-    specs = [pl.BlockSpec((count, w.shape[-1]), lambda i: (at, 0)) for w in weights[:2]]
-    return weights, specs + [pl.BlockSpec((2, count, weights[2].shape[-1]), lambda i: (0, at, 0))]
+    return weights, [pl.BlockSpec((count, w.shape[-1]), lambda i: (at, 0)) for w in weights]
 
 
 def call(kernel, name, inputs, spaces, outs, out_spaces, scratch=(), us=2):
@@ -280,21 +291,26 @@
     halves = node_state.reshape(2, rows, part)
     own = lax.dynamic_index_in_dim(halves, side, 0, keepdims=False)
     other = lax.dynamic_index_in_dim(halves, 1 - side, 0, keepdims=False)
-    across = exchange(other, 2)
     pack, next_pack = call(
         pack_kernel,
         "packs",
         (w_src, w_dst, w_node_in, w_node_out, node_vectors, node_gain),
-        [VMEM] * 6,
+        [ANY] * 4 + [VMEM] * 2,
         (
             jax.ShapeDtypeStruct((5 * width + 4 * VECTOR_ROWS, part), BF16),
             jax.ShapeDtypeStruct((5 * width, part), BF16),
         ),
-        (VMEM, VMEM),
-    )
+        (ANY, ANY),
+        [pltpu.VMEM((4 * VECTOR_ROWS, part), BF16), pltpu.SemaphoreType.DMA((9,))],
+    )
+    across = exchange(other, 2)
     pack_across = exchange(pack, 2)
-    next_across = from_other_side(next_pack)
-    pair = jnp.stack([own, across])
+    next_share, across = barrier((next_pack, across))
+    next_across = from_other_side(next_share)
+    beside = exchange(pack, 1)
+    next_share, beside = barrier((next_pack, beside))
+    next_beside = exchange(next_share, 1)
+    pair = barrier((jnp.stack([own, across]), pack))[0]
     latent = jnp.concatenate([pair, exchange(pair, 1)], axis=0)
 
     all_slots = mine * slots + 1
@@ -321,8 +337,10 @@
         after = swap_with(latent, 1)
         beyond = swap_with(latent, 2)
         if layer == 0:
-            pack_across, next_across, after, meta = barrier((pack_across, next_across, after, meta))
-            weights = (pack, pack_across, exchange(jnp.stack([pack, pack_across]), 1))
+            pack_across, next_across, next_beside, after, beyond, meta = barrier(
+                (pack_across, next_across, next_beside, after, beyond, meta)
+            )
+            weights = (pack, beside, pack_across, exchange(pack_across, 1))
         message_spec = pl.BlockSpec((4, part, width), lambda i, layer=layer: (layer, 0, 0))
         edge_inputs = [messages, msg_vectors, gather, collect]
         edge_specs = [message_spec, VMEM, VMEM, VMEM]
@@ -351,10 +369,7 @@
         acc, receive = result[0], result[1]
         if layer == 0:
             vectors = result[2]
-            acc, next_across = barrier((acc, next_across))
-            beside = exchange(jnp.stack([next_pack, next_across]), 1)
-            beyond, beside, acc = barrier((beyond, beside, acc))
-            next_weights = (next_pack, next_across, beside)
+            next_weights = (next_pack, next_beside, next_across, exchange(next_across, 1))
         else:
             beyond, acc = barrier((beyond, acc))
         partial = call(

time: 136 us -> 132 us (0.971)
  the two profiles are of different devices: /device:TPU:6 before, /device:TPU:1 now
where the time goes in v5:
time: 132 us; the launch traced here: 131 us
  starting transfers between devices  69.4 us (53%)
  waiting for transfers between devices  35.5 us (27%)
  Pallas kernels  18.6 us (14%)
  local copies, waits for them, and re-layouts  6.87 us (5%)
    ppermute x10, starting transfers between devices, exchange(): return lax.ppermute(value, BOTH, [(i, i ^ mask) for i in range(total)])  59.5 us
    ppermute x1, waiting for transfers between devices, from_other_side(): return lax.ppermute(value, BOTH, pairs)  20.6 us
    pallas_call x9, Pallas kernels, call(): pl.pallas_call(kernel, out_shape=outs, grid=(1,), in_specs=spaces, out_sp...  18.6 us
    ppermute x10, waiting for transfers between devices, exchange(): return lax.ppermute(value, BOTH, [(i, i ^ mask) for i in range(total)])  14.8 us
    unnamed x31, local copies, waits for them, and re-layouts  6.03 us
    ppermute x1, starting transfers between devices, from_other_side(): return lax.ppermute(value, BOTH, pairs)  5.55 us
    ppermute x4, starting transfers between devices, swap_with(): lax.ppermute(value, BOTH, [(i, t) for i, t in pairs if 0 <= t < total])  4.34 us
  transfers between devices with their start and end apart: 15, of which 6 were waited for; matrix products, arithmetic and copies ran while one was open for 1% of the time, Pallas kernels for 6%

profile of v5, /device:TPU:1, one launch (start us, length us, event | category | flops | bytes accessed | tf_op | source)
XLA Modules:
  0.0 130.7 jit_solution(7733818019339233488)
XLA Ops:
  0.0 1.0 copy-done.3
  1.0 0.9 copy-done.4
  2.0 0.9 copy-done.5
  2.9 0.9 copy-done.6
  5.3 1.2 packs.1
  6.5 8.9 %collective-permute-start.4 = (bf16[2624,128]{1,0:T(8,128)(2,1)S(1)}, bf16[2624,128]{1,0:T(8,128)(2,1)S(1)}, u32[]{:S(2)}, u32[]{:S(2)}) collective-permute-start(bf16[2624,128]{1,0:T(8,128)(2,1)S(1)} %get-tuple-element.34.refs_8_.refs_12_.refs_16_.refs_9_), channel_id=1, source_target_pairs={{0,1},{1,0},{2,3},{3,2},{4,5},{5,4},{6,7},{7,6},{8,9},{9,8},{10,11... | collective-permute-start | bytes 2015240 | tf_op jit(solution)/shard_map/ppermute | solution.py:31
  15.5 1.9 %collective-permute-start = (bf16[512,128]{1,0:T(8,128)(2,1)S(1)}, bf16[512,128]{1,0:T(8,128)(2,1)S(1)}, u32[]{:S(2)}, u32[]{:S(2)}) collective-permute-start(bf16[512,128]{1,0:T(8,128)(2,1)S(1)} %get-tuple-element.60), channel_id=1, source_target_pairs={{0,2},{1,3},{2,0},{3,1},{4,6},{5,7},{6,4},{7,5},{8,10},{9,11},{10,... | collective-permute-start | bytes 393224 | tf_op jit(solution)/shard_map/ppermute | solution.py:31
  17.4 5.1 %collective-permute-done = bf16[512,128]{1,0:T(8,128)(2,1)S(1)} collective-permute-done((bf16[512,128]{1,0:T(8,128)(2,1)S(1)}, bf16[512,128]{1,0:T(8,128)(2,1)S(1)}, u32[]{:S(2)}, u32[]{:S(2)}) %collective-permute-start) | collective-permute-done | bytes 131104 | tf_op jit(solution)/shard_map/ppermute | solution.py:31
  22.5 2.7 %collective-permute-start.1 = (bf16[2,512,128]{2,1,0:T(8,128)(2,1)S(1)}, bf16[2,512,128]{2,1,0:T(8,128)(2,1)S(1)}, u32[]{:S(2)}, u32[]{:S(2)}) collective-permute-start(bf16[2,512,128]{2,1,0:T(8,128)(2,1)S(1)} %pad_maximum_fusion), channel_id=1, source_target_pairs={{0,1},{1,0},{2,3},{3,2},{4,5},{5,4},{6,7},{7,6},{8,9},{9,8},{10,11... | collective-permute-start | bytes 786440 | tf_op jit(solution)/shard_map/ppermute | solution.py:31
  25.2 1.9 %collective-permute-start.2 = (bf16[2624,128]{1,0:T(8,128)(2,1)S(1)}, bf16[2624,128]{1,0:T(8,128)(2,1)S(1)}, u32[]{:S(2)}, u32[]{:S(2)}) collective-permute-start(bf16[2624,128]{1,0:T(8,128)(2,1)S(1)} %get-tuple-element.34.refs_8_.refs_12_.refs_16_.refs_9_), channel_id=1, source_target_pairs={{0,2},{1,3},{2,0},{3,1},{4,6},{5,7},{6,4},{7,5},{8,10},{9,11},{10,... | collective-permute-start | bytes 2015240 | tf_op jit(solution)/shard_map/ppermute | solution.py:31
  27.2 5.6 %collective-permute-start.3 = (bf16[2560,128]{1,0:T(8,128)(2,1)S(1)}, bf16[2560,128]{1,0:T(8,128)(2,1)S(1)}, u32[]{:S(2)}, u32[]{:S(2)}) collective-permute-start(bf16[2560,128]{1,0:T(8,128)(2,1)S(1)} %get-tuple-element.37.refs_8_.refs_12_.refs_9_.refs_16_), channel_id=1, source_target_pairs={{0,14},{1,15},{2,4},{3,5},{4,2},{5,3},{6,8},{7,9},{8,6},{9,7},{10,... | collective-permute-start | bytes 1966088 | tf_op jit(solution)/shard_map/ppermute | solution.py:49
  32.7 2.5 %collective-permute-start.5 = (bf16[2560,128]{1,0:T(8,128)(2,1)S(1)}, bf16[2560,128]{1,0:T(8,128)(2,1)}, u32[]{:S(2)}, u32[]{:S(2)}) collective-permute-start(bf16[2560,128]{1,0:T(8,128)(2,1)S(1)} %get-tuple-element.37.refs_8_.refs_12_.refs_9_.refs_16_), channel_id=1, source_target_pairs={{0,1},{1,0},{2,3},{3,2},{4,5},{5,4},{6,7},{7,6},{8,9},{9,8},{10,11... | collective-permute-start | bytes 1966088 | tf_op jit(solution)/shard_map/ppermute | solution.py:31
  36.7 1.5 %collective-permute-start.6 = (bf16[4,512,128]{2,1,0:T(8,128)(2,1)}, bf16[4,512,128]{2,1,0:T(8,128)(2,1)}, u32[]{:S(2)}, u32[]{:S(2)}) collective-permute-start(bf16[4,512,128]{2,1,0:T(8,128)(2,1)} %constant_dynamic-update-slice_fusion.refs_2_.refs_1_), channel_id=1, source_target_pairs={{0,3},{2,5},{3,0},{4,7},{5,2},{6,9},{7,4},{8,11},{9,6},{10,13},{11... | collective-permute-start | bytes 1572872 | tf_op jit(solution)/shard_map/ppermute | solution.py:38
  38.1 1.5 %collective-permute-start.7 = (bf16[4,512,128]{2,1,0:T(8,128)(2,1)}, bf16[4,512,128]{2,1,0:T(8,128)(2,1)}, u32[]{:S(2)}, u32[]{:S(2)}) collective-permute-start(bf16[4,512,128]{2,1,0:T(8,128)(2,1)} %constant_dynamic-update-slice_fusion.refs_2_.refs_1_), channel_id=1, source_target_pairs={{0,5},{2,7},{4,9},{5,0},{6,11},{7,2},{8,13},{9,4},{10,15},{11,6},{... | collective-permute-start | bytes 1572872 | tf_op jit(solution)/shard_map/ppermute | solution.py:38
  39.8 2.2 %one_hots.1 = (bf16[25,128,256]{2,1,0:T(8,128)(2,1)S(1)}, bf16[25,128,128]{2,1,0:T(8,128)(2,1)S(1)}, f32[512,128]{1,0:T(8,128)S(1)}, s32[4,32]{1,0:T(4,128)S(1)}) custom-call(s32[5]{0:T(128)S(1)} %stack.30.place_ref.refs_0_, s32[8,6]{1,0:T(8,128)S(1)} %copy-done.8, s32[8,6]{1,0:T(8,128)S(1)} %copy-done.9, s32[8,6,128]{2,1,0:T(8,128)S(1)} %copy.15.src_ref, ...), custom_call_target="tpu_custom_call" | custom-call | flops 3000000000 | bytes 1048576 | tf_op jit(solution)/shard_map/one_hots/pallas_call | solution.py:250
  42.0 1.8 %collective-permute-done.2.refs_10_.refs_14_.refs_18_.refs_11_ = bf16[2624,128]{1,0:T(8,128)(2,1)S(1)} collective-permute-done((bf16[2624,128]{1,0:T(8,128)(2,1)S(1)}, bf16[2624,128]{1,0:T(8,128)(2,1)S(1)}, u32[]{:S(2)}, u32[]{:S(2)}) %collective-permute-start.2) | collective-permute-done | bytes 671776 | tf_op jit(solution)/shard_map/ppermute | solution.py:31
  43.8 20.6 %collective-permute-done.3.refs_10_.refs_14_.refs_11_.refs_18_ = bf16[2560,128]{1,0:T(8,128)(2,1)S(1)} collective-permute-done((bf16[2560,128]{1,0:T(8,128)(2,1)S(1)}, bf16[2560,128]{1,0:T(8,128)(2,1)S(1)}, u32[]{:S(2)}, u32[]{:S(2)}) %collective-permute-start.3) | collective-permute-done | bytes 655392 | tf_op jit(solution)/shard_map/ppermute | solution.py:49
  64.5 2.7 %collective-permute-start.8 = (bf16[2624,128]{1,0:T(8,128)(2,1)S(1)}, bf16[2624,128]{1,0:T(8,128)(2,1)S(1)}, u32[]{:S(2)}, u32[]{:S(2)}) collective-permute-start(bf16[2624,128]{1,0:T(8,128)(2,1)S(1)} %collective-permute-done.2.refs_10_.refs_14_.refs_18_.refs_11_), channel_id=1, source_target_pairs={{0,1},{1,0},{2,3},{3,2},{4,5},{5,4},{6,7},{7,6},{8,9},{9,8},{10,11... | collective-permute-start | bytes 2015240 | tf_op jit(solution)/shard_map/ppermute | solution.py:31
  67.2 1.7 %collective-permute-done.8.refs_11_.refs_15_.refs_19_.refs_12_ = bf16[2624,128]{1,0:T(8,128)(2,1)S(1)} collective-permute-done((bf16[2624,128]{1,0:T(8,128)(2,1)S(1)}, bf16[2624,128]{1,0:T(8,128)(2,1)S(1)}, u32[]{:S(2)}, u32[]{:S(2)}) %collective-permute-start.8) | collective-permute-done | bytes 671776 | tf_op jit(solution)/shard_map/ppermute | solution.py:31
  68.9 3.2 %near0.1 = (f32[512,512]{1,0:T(8,128)S(1)}, bf16[512,512]{1,0:T(8,128)(2,1)S(1)}, f32[4,16,128]{2,1,0:T(8,128)S(1)}) custom-call(s32[5]{0:T(128)S(1)} %stack.30.place_ref.refs_0_, s32[4,32]{1,0:T(4,128)S(1)} %get-tuple-element.40.refs_1_, bf16[4,512,128]{2,1,0:T(8,128)(2,1)} %constant_dynamic-update-slice_fusion.refs_2_.refs_1_, ...), custom_call_target="tpu_custom_call" | custom-call | flops 5000000000 | bytes 1048576 | tf_op jit(solution)/shard_map/near0/pallas_call | solution.py:250
  72.2 1.6 %far0.1.refs_2_ = bf16[512,512]{1,0:T(8,128)(2,1)S(1)} custom-call(s32[5]{0:T(128)S(1)} %stack.30.place_ref.refs_0_, s32[4,32]{1,0:T(4,128)S(1)} %get-tuple-element.40.refs_1_, bf16[4,512,128]{2,1,0:T(8,128)(2,1)} %collective-permute-done.7.refs_2_, bf16[8,128,512]{2,1,0:T(8,128)(2,1)S(1)} %bitcast.11, f32[2,2,512]{2,1,0:T(2,128)S(1)} %copy-done, ...), custom_call_target="tpu_custom_call" | custom-call | flops 3000000000 | bytes 1048576 | tf_op jit(solution)/shard_map/far0/pallas_call | solution.py:250
  73.8 7.3 %collective-permute-start.9 = (bf16[512,512]{1,0:T(8,128)(2,1)S(1)}, bf16[512,512]{1,0:T(8,128)(2,1)S(1)}, u32[]{:S(2)}, u32[]{:S(2)}) collective-permute-start(bf16[512,512]{1,0:T(8,128)(2,1)S(1)} %far0.1.refs_2_), channel_id=1, source_target_pairs={{0,1},{1,0},{2,3},{3,2},{4,5},{5,4},{6,7},{7,6},{8,9},{9,8},{10,11... | collective-permute-start | bytes 1572872 | tf_op jit(solution)/shard_map/ppermute | solution.py:31
  81.0 1.9 %collective-permute-start.12 = (bf16[2560,128]{1,0:T(8,128)(2,1)S(1)}, bf16[2560,128]{1,0:T(8,128)(2,1)S(1)}, u32[]{:S(2)}, u32[]{:S(2)}) collective-permute-start(bf16[2560,128]{1,0:T(8,128)(2,1)S(1)} %collective-permute-done.3.refs_10_.refs_14_.refs_11_.refs_18_), channel_id=1, source_target_pairs={{0,1},{1,0},{2,3},{3,2},{4,5},{5,4},{6,7},{7,6},{8,9},{9,8},{10,11... | collective-permute-start | bytes 1966088 | tf_op jit(solution)/shard_map/ppermute | solution.py:31
  83.0 2.4 %node0.1.refs_2_.refs_1_ = bf16[4,512,128]{2,1,0:T(8,128)(2,1)S(1)} custom-call(s32[5]{0:T(128)S(1)} %stack.30.place_ref.refs_0_, bf16[4,512,128]{2,1,0:T(8,128)(2,1)} %constant_dynamic-update-slice_fusion.refs_2_.refs_1_, bf16[512,512]{1,0:T(8,128)(2,1)S(1)} %far0.1.refs_2_, bf16[512,512]{1,0:T(8,128)(2,1)S(1)} %collective-permute-done.9.refs_3_, ...), custom_call_target="tpu_custom_call" | custom-call | flops 2000000000 | bytes 1048576 | tf_op jit(solution)/shard_map/node0/pallas_call | solution.py:250
  86.8 3.0 %near1.1 = (f32[512,512]{1,0:T(8,128)S(1)}, bf16[512,512]{1,0:T(8,128)(2,1)S(1)}) custom-call(s32[5]{0:T(128)S(1)} %stack.30.place_ref.refs_0_, s32[4,32]{1,0:T(4,128)S(1)} %get-tuple-element.40.refs_1_, bf16[4,512,128]{2,1,0:T(8,128)(2,1)S(1)} %node0.1.refs_2_.refs_1_, bf16[4,512,128]{2,1,0:T(8,128)(2,1)S(1)} %collective-permute-done.11.refs_3_, ...), custom_call_target="tpu_custom_call" | custom-call | flops 5000000000 | bytes 1048576 | tf_op jit(solution)/shard_map/near1/pallas_call | solution.py:250
  89.9 1.4 %far1.1.refs_2_ = bf16[512,512]{1,0:T(8,128)(2,1)S(1)} custom-call(s32[5]{0:T(128)S(1)} %stack.30.place_ref.refs_0_, s32[4,32]{1,0:T(4,128)S(1)} %get-tuple-element.40.refs_1_, bf16[4,512,128]{2,1,0:T(8,128)(2,1)S(1)} %collective-permute-done.10.refs_2_, bf16[8,128,512]{2,1,0:T(8,128)(2,1)S(1)} %bitcast.13, f32[2,2,512]{2,1,0:T(2,128)S(1)} %copy-done, ...), custom_call_target="tpu_custom_call" | custom-call | flops 3000000000 | bytes 1048576 | tf_op jit(solution)/shard_map/far1/pallas_call | solution.py:250
  91.3 27.7 %collective-permute-start.13 = (bf16[512,512]{1,0:T(8,128)(2,1)S(1)}, bf16[512,512]{1,0:T(8,128)(2,1)S(1)}, u32[]{:S(2)}, u32[]{:S(2)}) collective-permute-start(bf16[512,512]{1,0:T(8,128)(2,1)S(1)} %far1.1.refs_2_), channel_id=1, source_target_pairs={{0,1},{1,0},{2,3},{3,2},{4,5},{5,4},{6,7},{7,6},{8,9},{9,8},{10,11... | collective-permute-start | bytes 1572872 | tf_op jit(solution)/shard_map/ppermute | solution.py:31
  119.0 1.5 %collective-permute-done.13.refs_3_ = bf16[512,512]{1,0:T(8,128)(2,1)S(1)} collective-permute-done((bf16[512,512]{1,0:T(8,128)(2,1)S(1)}, bf16[512,512]{1,0:T(8,128)(2,1)S(1)}, u32[]{:S(2)}, u32[]{:S(2)}) %collective-permute-start.13) | collective-permute-done | bytes 524320 | tf_op jit(solution)/shard_map/ppermute | solution.py:31
  120.5 2.3 %node1.1 = (bf16[512,128]{1,0:T(8,128)(2,1)S(1)}, bf16[512,128]{1,0:T(8,128)(2,1)S(1)}) custom-call(s32[5]{0:T(128)S(1)} %stack.30.place_ref.refs_0_, bf16[4,512,128]{2,1,0:T(8,128)(2,1)S(1)} %node0.1.refs_2_.refs_1_, bf16[512,512]{1,0:T(8,128)(2,1)S(1)} %far1.1.refs_2_, bf16[512,512]{1,0:T(8,128)(2,1)S(1)} %collective-permute-done.13.refs_3_, ...), custom_call_target="tpu_custom_call" | custom-call | flops 2000000000 | bytes 1048576 | tf_op jit(solution)/shard_map/node1/pallas_call | solution.py:250
  122.9 1.9 %collective-permute-start.14 = (bf16[512,128]{1,0:T(8,128)(2,1)S(1)}, bf16[512,128]{1,0:T(8,128)(2,1)S(1)}, u32[]{:S(2)}, u32[]{:S(2)}) collective-permute-start(bf16[512,128]{1,0:T(8,128)(2,1)S(1)} %get-tuple-element.58), channel_id=1, source_target_pairs={{0,2},{1,3},{2,0},{3,1},{4,6},{5,7},{6,4},{7,5},{8,10},{9,11},{10,... | collective-permute-start | bytes 393224 | tf_op jit(solution)/shard_map/ppermute | solution.py:31
  124.8 4.7 %collective-permute-done.14.other_ref = bf16[512,128]{1,0:T(8,128)(2,1)S(1)} collective-permute-done((bf16[512,128]{1,0:T(8,128)(2,1)S(1)}, bf16[512,128]{1,0:T(8,128)(2,1)S(1)}, u32[]{:S(2)}, u32[]{:S(2)}) %collective-permute-start.14) | collective-permute-done | bytes 131104 | tf_op jit(solution)/shard_map/ppermute | solution.py:31
  129.5 1.3 join.1
  (42 shorter events, 4.4 us)
Async XLA Ops:
  0.0 1.0 copy-start.3
  1.0 0.9 copy-start.4
  2.0 0.9 copy-start.5
  2.9 0.9 copy-start.6
  3.9 0.7 copy-start.7
  4.6 0.7 copy-start.10
  5.3 10.2 %copy-start.11 = (bf16[1024,128]{1,0:T(8,128)(2,1)S(1)}, bf16[1024,128]{1,0:T(8,128)(2,1)}, u32[]{:S(2)}) copy-start(bf16[1024,128]{1,0:T(8,128)(2,1)} %param.14) | copy-start | bytes 786436
  6.4 33.2 %copy-start.12 = (s32[8,6,128]{2,0,1:T(8,128)S(1)}, s32[8,6,128]{2,0,1:T(8,128)}, u32[]{:S(2)}) copy-start(s32[8,6,128]{2,0,1:T(8,128)} %param.26) | copy-start | bytes 73732
  6.5 33.2 %copy-start.13 = (s32[8,6,128]{2,0,1:T(8,128)S(1)}, s32[8,6,128]{2,0,1:T(8,128)}, u32[]{:S(2)}) copy-start(s32[8,6,128]{2,0,1:T(8,128)} %param.27) | copy-start | bytes 73732
  6.5 33.3 %copy-start.8 = (s32[8,6]{1,0:T(8,128)S(1)}, s32[8,6]{1,0:T(8,128)}, u32[]{:S(2)}) copy-start(s32[8,6]{1,0:T(8,128)} %nbr_ref) | copy-start | bytes 580
  6.5 33.3 %copy-start.9 = (s32[8,6]{1,0:T(8,128)S(1)}, s32[8,6]{1,0:T(8,128)}, u32[]{:S(2)}) copy-start(s32[8,6]{1,0:T(8,128)} %count_ref.1) | copy-start | bytes 580
  6.5 26.2 %collective-permute-start.4 = (bf16[2624,128]{1,0:T(8,128)(2,1)S(1)}, bf16[2624,128]{1,0:T(8,128)(2,1)S(1)}, u32[]{:S(2)}, u32[]{:S(2)}) collective-permute-start(bf16[2624,128]{1,0:T(8,128)(2,1)S(1)} %get-tuple-element.34.refs_8_.refs_12_.refs_16_.refs_9_), channel_id=1, source_target_pairs={{0,1},{1,0},{2,3},{3,2},{4,5},{5,4},{6,7},{7,6},{8,9},{9,8},{10,11... | collective-permute-start | bytes 2015240 | tf_op jit(solution)/shard_map/ppermute | solution.py:31
  15.5 7.0 %collective-permute-start = (bf16[512,128]{1,0:T(8,128)(2,1)S(1)}, bf16[512,128]{1,0:T(8,128)(2,1)S(1)}, u32[]{:S(2)}, u32[]{:S(2)}) collective-permute-start(bf16[512,128]{1,0:T(8,128)(2,1)S(1)} %get-tuple-element.60), channel_id=1, source_target_pairs={{0,2},{1,3},{2,0},{3,1},{4,6},{5,7},{6,4},{7,5},{8,10},{9,11},{10,... | collective-permute-start | bytes 393224 | tf_op jit(solution)/shard_map/ppermute | solution.py:31
  22.5 13.4 %collective-permute-start.1 = (bf16[2,512,128]{2,1,0:T(8,128)(2,1)S(1)}, bf16[2,512,128]{2,1,0:T(8,128)(2,1)S(1)}, u32[]{:S(2)}, u32[]{:S(2)}) collective-permute-start(bf16[2,512,128]{2,1,0:T(8,128)(2,1)S(1)} %pad_maximum_fusion), channel_id=1, source_target_pairs={{0,1},{1,0},{2,3},{3,2},{4,5},{5,4},{6,7},{7,6},{8,9},{9,8},{10,11... | collective-permute-start | bytes 786440 | tf_op jit(solution)/shard_map/ppermute | solution.py:31
  25.2 18.6 %collective-permute-start.2 = (bf16[2624,128]{1,0:T(8,128)(2,1)S(1)}, bf16[2624,128]{1,0:T(8,128)(2,1)S(1)}, u32[]{:S(2)}, u32[]{:S(2)}) collective-permute-start(bf16[2624,128]{1,0:T(8,128)(2,1)S(1)} %get-tuple-element.34.refs_8_.refs_12_.refs_16_.refs_9_), channel_id=1, source_target_pairs={{0,2},{1,3},{2,0},{3,1},{4,6},{5,7},{6,4},{7,5},{8,10},{9,11},{10,... | collective-permute-start | bytes 2015240 | tf_op jit(solution)/shard_map/ppermute | solution.py:31
  27.2 37.3 %collective-permute-start.3 = (bf16[2560,128]{1,0:T(8,128)(2,1)S(1)}, bf16[2560,128]{1,0:T(8,128)(2,1)S(1)}, u32[]{:S(2)}, u32[]{:S(2)}) collective-permute-start(bf16[2560,128]{1,0:T(8,128)(2,1)S(1)} %get-tuple-element.37.refs_8_.refs_12_.refs_9_.refs_16_), channel_id=1, source_target_pairs={{0,14},{1,15},{2,4},{3,5},{4,2},{5,3},{6,8},{7,9},{8,6},{9,7},{10,... | collective-permute-start | bytes 1966088 | tf_op jit(solution)/shard_map/ppermute | solution.py:49
  32.7 31.7 %collective-permute-start.5 = (bf16[2560,128]{1,0:T(8,128)(2,1)S(1)}, bf16[2560,128]{1,0:T(8,128)(2,1)}, u32[]{:S(2)}, u32[]{:S(2)}) collective-permute-start(bf16[2560,128]{1,0:T(8,128)(2,1)S(1)} %get-tuple-element.37.refs_8_.refs_12_.refs_9_.refs_16_), channel_id=1, source_target_pairs={{0,1},{1,0},{2,3},{3,2},{4,5},{5,4},{6,7},{7,6},{8,9},{9,8},{10,11... | collective-permute-start | bytes 1966088 | tf_op jit(solution)/shard_map/ppermute | solution.py:31
  36.7 27.8 %collective-permute-start.6 = (bf16[4,512,128]{2,1,0:T(8,128)(2,1)}, bf16[4,512,128]{2,1,0:T(8,128)(2,1)}, u32[]{:S(2)}, u32[]{:S(2)}) collective-permute-start(bf16[4,512,128]{2,1,0:T(8,128)(2,1)} %constant_dynamic-update-slice_fusion.refs_2_.refs_1_), channel_id=1, source_target_pairs={{0,3},{2,5},{3,0},{4,7},{5,2},{6,9},{7,4},{8,11},{9,6},{10,13},{11... | collective-permute-start | bytes 1572872 | tf_op jit(solution)/shard_map/ppermute | solution.py:38
  38.1 26.3 %collective-permute-start.7 = (bf16[4,512,128]{2,1,0:T(8,128)(2,1)}, bf16[4,512,128]{2,1,0:T(8,128)(2,1)}, u32[]{:S(2)}, u32[]{:S(2)}) collective-permute-start(bf16[4,512,128]{2,1,0:T(8,128)(2,1)} %constant_dynamic-update-slice_fusion.refs_2_.refs_1_), channel_id=1, source_target_pairs={{0,5},{2,7},{4,9},{5,0},{6,11},{7,2},{8,13},{9,4},{10,15},{11,6},{... | collective-permute-start | bytes 1572872 | tf_op jit(solution)/shard_map/ppermute | solution.py:38
  39.8 29.1 %copy-start = (f32[2,2,512]{2,1,0:T(2,128)S(1)}, f32[2,2,512]{2,1,0:T(2,128)}, u32[]{:S(2)}) copy-start(f32[2,2,512]{2,1,0:T(2,128)} %refs_6_.3) | copy-start | bytes 24580
  39.8 29.1 %copy-start.2 = (bf16[2,512,512]{2,1,0:T(8,128)(2,1)S(1)}, bf16[2,512,512]{2,1,0:T(8,128)(2,1)}, u32[]{:S(2)}) copy-start(bf16[2,512,512]{2,1,0:T(8,128)(2,1)} %param.17) | copy-start | bytes 3145732
  64.5 4.4 %collective-permute-start.8 = (bf16[2624,128]{1,0:T(8,128)(2,1)S(1)}, bf16[2624,128]{1,0:T(8,128)(2,1)S(1)}, u32[]{:S(2)}, u32[]{:S(2)}) collective-permute-start(bf16[2624,128]{1,0:T(8,128)(2,1)S(1)} %collective-permute-done.2.refs_10_.refs_14_.refs_18_.refs_11_), channel_id=1, source_target_pairs={{0,1},{1,0},{2,3},{3,2},{4,5},{5,4},{6,7},{7,6},{8,9},{9,8},{10,11... | collective-permute-start | bytes 2015240 | tf_op jit(solution)/shard_map/ppermute | solution.py:31
  72.2 10.8 %copy-start.1 = (f32[2,512]{1,0:T(2,128)S(1)}, f32[2,512]{1,0:T(2,128)}, u32[]{:S(2)}) copy-start(f32[2,512]{1,0:T(2,128)} %refs_7_.3) | copy-start | bytes 12292
  73.8 9.2 %collective-permute-start.9 = (bf16[512,512]{1,0:T(8,128)(2,1)S(1)}, bf16[512,512]{1,0:T(8,128)(2,1)S(1)}, u32[]{:S(2)}, u32[]{:S(2)}) collective-permute-start(bf16[512,512]{1,0:T(8,128)(2,1)S(1)} %far0.1.refs_2_), channel_id=1, source_target_pairs={{0,1},{1,0},{2,3},{3,2},{4,5},{5,4},{6,7},{7,6},{8,9},{9,8},{10,11... | collective-permute-start | bytes 1572872 | tf_op jit(solution)/shard_map/ppermute | solution.py:31
  81.0 5.8 %collective-permute-start.12 = (bf16[2560,128]{1,0:T(8,128)(2,1)S(1)}, bf16[2560,128]{1,0:T(8,128)(2,1)S(1)}, u32[]{:S(2)}, u32[]{:S(2)}) collective-permute-start(bf16[2560,128]{1,0:T(8,128)(2,1)S(1)} %collective-permute-done.3.refs_10_.refs_14_.refs_11_.refs_18_), channel_id=1, source_target_pairs={{0,1},{1,0},{2,3},{3,2},{4,5},{5,4},{6,7},{7,6},{8,9},{9,8},{10,11... | collective-permute-start | bytes 1966088 | tf_op jit(solution)/shard_map/ppermute | solution.py:31
  85.4 1.4 %collective-permute-start.11 = (bf16[4,512,128]{2,1,0:T(8,128)(2,1)S(1)}, bf16[4,512,128]{2,1,0:T(8,128)(2,1)S(1)}, u32[]{:S(2)}, u32[]{:S(2)}) collective-permute-start(bf16[4,512,128]{2,1,0:T(8,128)(2,1)S(1)} %node0.1.refs_2_.refs_1_), channel_id=1, source_target_pairs={{0,3},{2,5},{3,0},{4,7},{5,2},{6,9},{7,4},{8,11},{9,6},{10,13},{11... | collective-permute-start | bytes 1572872 | tf_op jit(solution)/shard_map/ppermute | solution.py:38
  86.1 3.8 %collective-permute-start.10 = (bf16[4,512,128]{2,1,0:T(8,128)(2,1)S(1)}, bf16[4,512,128]{2,1,0:T(8,128)(2,1)S(1)}, u32[]{:S(2)}, u32[]{:S(2)}) collective-permute-start(bf16[4,512,128]{2,1,0:T(8,128)(2,1)S(1)} %node0.1.refs_2_.refs_1_), channel_id=1, source_target_pairs={{0,5},{2,7},{4,9},{5,0},{6,11},{7,2},{8,13},{9,4},{10,15},{11,6},{... | collective-permute-start | bytes 1572872 | tf_op jit(solution)/shard_map/ppermute | solution.py:38
  91.3 29.2 %collective-permute-start.13 = (bf16[512,512]{1,0:T(8,128)(2,1)S(1)}, bf16[512,512]{1,0:T(8,128)(2,1)S(1)}, u32[]{:S(2)}, u32[]{:S(2)}) collective-permute-start(bf16[512,512]{1,0:T(8,128)(2,1)S(1)} %far1.1.refs_2_), channel_id=1, source_target_pairs={{0,1},{1,0},{2,3},{3,2},{4,5},{5,4},{6,7},{7,6},{8,9},{9,8},{10,11... | collective-permute-start | bytes 1572872 | tf_op jit(solution)/shard_map/ppermute | solution.py:31
  122.9 6.6 %collective-permute-start.14 = (bf16[512,128]{1,0:T(8,128)(2,1)S(1)}, bf16[512,128]{1,0:T(8,128)(2,1)S(1)}, u32[]{:S(2)}, u32[]{:S(2)}) collective-permute-start(bf16[512,128]{1,0:T(8,128)(2,1)S(1)} %get-tuple-element.58), channel_id=1, source_target_pairs={{0,2},{1,3},{2,0},{3,1},{4,6},{5,7},{6,4},{7,5},{8,10},{9,11},{10,... | collective-permute-start | bytes 393224 | tf_op jit(solution)/shard_map/ppermute | solution.py:31

commit v6 on v5

--- a/solution.py
+++ b/solution.py
@@ -19,7 +19,7 @@
 LIST = 32
 VMEM = pl.BlockSpec(memory_space=pltpu.VMEM)
 SMEM = pl.BlockSpec(memory_space=pltpu.SMEM)
-ANY = pl.BlockSpec(memory_space=pl.ANY)
+HBM = pl.BlockSpec(memory_space=pltpu.HBM)
 
 
 def dot(a, b):
@@ -246,7 +246,7 @@
     return weights, [pl.BlockSpec((count, w.shape[-1]), lambda i: (at, 0)) for w in weights]
 
 
-def call(kernel, name, inputs, spaces, outs, out_spaces, scratch=(), us=2):
+def call(kernel, name, inputs, spaces, outs, out_spaces, scratch=(), us=2, mib=32):
     return pl.pallas_call(
         kernel,
         out_shape=outs,
@@ -254,7 +254,7 @@
         in_specs=spaces,
         out_specs=out_spaces,
         scratch_shapes=list(scratch),
-        compiler_params=pltpu.CompilerParams(vmem_limit_bytes=32 * 1024 * 1024),
+        compiler_params=pltpu.CompilerParams(vmem_limit_bytes=mib * 1024 * 1024),
         cost_estimate=pl.CostEstimate(flops=int(us * 1e9), bytes_accessed=1 << 20, transcendentals=0),
         name=name,
     )(*inputs)
@@ -295,26 +295,23 @@
         pack_kernel,
         "packs",
         (w_src, w_dst, w_node_in, w_node_out, node_vectors, node_gain),
-        [ANY] * 4 + [VMEM] * 2,
+        [HBM] * 4 + [VMEM] * 2,
         (
             jax.ShapeDtypeStruct((5 * width + 4 * VECTOR_ROWS, part), BF16),
             jax.ShapeDtypeStruct((5 * width, part), BF16),
         ),
-        (ANY, ANY),
+        (HBM, HBM),
         [pltpu.VMEM((4 * VECTOR_ROWS, part), BF16), pltpu.SemaphoreType.DMA((9,))],
-    )
+        mib=60,
+    )
+    other = barrier((other, pack))[0]
     across = exchange(other, 2)
     pack_across = exchange(pack, 2)
-    next_share, across = barrier((next_pack, across))
-    next_across = from_other_side(next_share)
+    next_across = from_other_side(next_pack)
     beside = exchange(pack, 1)
-    next_share, beside = barrier((next_pack, beside))
-    next_beside = exchange(next_share, 1)
-    pair = barrier((jnp.stack([own, across]), pack))[0]
-    latent = jnp.concatenate([pair, exchange(pair, 1)], axis=0)
+    next_beside = exchange(next_pack, 1)
 
     all_slots = mine * slots + 1
-    nbr_blocks = barrier((nbr_blocks, latent))[0]
     gather, collect, degree, meta = call(
         prepare_kernel,
         "one_hots",
@@ -330,17 +327,20 @@
         [pltpu.VMEM((edges, edges), F32)],
         us=3,
     )
+    pair = jnp.stack([own, across])
+    pair, pack_across, next_across, beside, next_beside, meta = barrier(
+        (pair, pack_across, next_across, beside, next_beside, meta)
+    )
+    latent = jnp.concatenate([pair, exchange(pair, 1)], axis=0)
+    pack_across = barrier((pack_across, latent))[0]
+    weights = (pack, beside, pack_across, exchange(pack_across, 1))
+
     vectors = None
     messages = w_msg.reshape(LAYERS * 4, part, width)
     for layer in range(LAYERS):
         final = layer == LAYERS - 1
         after = swap_with(latent, 1)
         beyond = swap_with(latent, 2)
-        if layer == 0:
-            pack_across, next_across, next_beside, after, beyond, meta = barrier(
-                (pack_across, next_across, next_beside, after, beyond, meta)
-            )
-            weights = (pack, beside, pack_across, exchange(pack_across, 1))
         message_spec = pl.BlockSpec((4, part, width), lambda i, layer=layer: (layer, 0, 0))
         edge_inputs = [messages, msg_vectors, gather, collect]
         edge_specs = [message_spec, VMEM, VMEM, VMEM]
@@ -369,9 +369,9 @@
         acc, receive = result[0], result[1]
         if layer == 0:
             vectors = result[2]
+            next_across = barrier((next_across, acc))[0]
             next_weights = (next_pack, next_beside, next_across, exchange(next_across, 1))
-        else:
-            beyond, acc = barrier((beyond, acc))
+        beyond, acc = barrier((beyond, acc))
         partial = call(
             lambda *refs, layer=layer: far_kernel(layer, *refs),
             f"far{layer}",

time: 132 us -> 159 us (1.20)
  the two profiles are of different devices: /device:TPU:1 before, /device:TPU:6 now
where the time goes in v6:
time: 159 us; the launch traced here: 158 us
  Pallas kernels  62.2 us (39%)
  waiting for transfers between devices  50.5 us (32%)
  starting transfers between devices  44.9 us (28%)
    pallas_call x9, Pallas kernels, call(): pl.pallas_call(kernel, out_shape=outs, grid=(1,), in_specs=spaces, out_sp...  62.2 us
    ppermute x4, waiting for transfers between devices, swap_with(): lax.ppermute(value, BOTH, [(i, t) for i, t in pairs if 0 <= t < total])  31.3 us
    ppermute x10, starting transfers between devices, exchange(): return lax.ppermute(value, BOTH, [(i, i ^ mask) for i in range(total)])  27.5 us
    ppermute x10, waiting for transfers between devices, exchange(): return lax.ppermute(value, BOTH, [(i, i ^ mask) for i in range(total)])  11.3 us
    ppermute x1, starting transfers between devices, from_other_side(): return lax.ppermute(value, BOTH, pairs)  9.13 us
    ppermute x4, starting transfers between devices, swap_with(): lax.ppermute(value, BOTH, [(i, t) for i, t in pairs if 0 <= t < total])  8.26 us
    ppermute x1, waiting for transfers between devices, from_other_side(): return lax.ppermute(value, BOTH, pairs)  7.86 us
  transfers between devices with their start and end apart: 15, of which 8 were waited for; matrix products, arithmetic and copies ran while one was open for 0% of the time, Pallas kernels for 8%

profile of v6, /device:TPU:6, one launch (start us, length us, event | category | flops | bytes accessed | tf_op | source)
XLA Modules:
  0.0 158.3 jit_solution(362022914470292397)
XLA Ops:
  0.0 41.6 %packs.1 = (bf16[2624,128]{1,0:T(8,128)(2,1)}, bf16[2560,128]{1,0:T(8,128)(2,1)}) custom-call(bf16[2,512,128]{2,1,0:T(8,128)(2,1)} %src_ref.2, bf16[2,512,128]{2,1,0:T(8,128)(2,1)} %dst_ref.2, bf16[2,1024,128]{2,1,0:T(8,128)(2,1)} %in_ref.1, bf16[2,512,128]{2,1,0:T(8,128)(2,1)} %out_w_ref.1, f32[2,4,128]{2,1,0:T(4,128)} %vec_ref.1, f32[2,128]{1,0:T(2,128)} %gain_ref.1), custom_call_target="tpu_custom_call" | custom-call | flops 2000000000 | bytes 1048576 | tf_op jit(solution)/shard_map/packs/pallas_call | solution.py:250
  41.7 1.9 %collective-permute-start.3 = (bf16[2624,128]{1,0:T(8,128)(2,1)}, bf16[2624,128]{1,0:T(8,128)(2,1)S(1)}, u32[]{:S(2)}, u32[]{:S(2)}) collective-permute-start(bf16[2624,128]{1,0:T(8,128)(2,1)} %get-tuple-element.31.refs_8_.refs_12_.refs_16_.refs_9_), channel_id=1, source_target_pairs={{0,1},{1,0},{2,3},{3,2},{4,5},{5,4},{6,7},{7,6},{8,9},{9,8},{10,11... | collective-permute-start | bytes 2015240 | tf_op jit(solution)/shard_map/ppermute | solution.py:31
  43.6 4.3 %collective-permute-start.1 = (bf16[2624,128]{1,0:T(8,128)(2,1)}, bf16[2624,128]{1,0:T(8,128)(2,1)S(1)}, u32[]{:S(2)}, u32[]{:S(2)}) collective-permute-start(bf16[2624,128]{1,0:T(8,128)(2,1)} %get-tuple-element.31.refs_8_.refs_12_.refs_16_.refs_9_), channel_id=1, source_target_pairs={{0,2},{1,3},{2,0},{3,1},{4,6},{5,7},{6,4},{7,5},{8,10},{9,11},{10,... | collective-permute-start | bytes 2015240 | tf_op jit(solution)/shard_map/ppermute | solution.py:31
  47.9 2.1 %collective-permute-start.4 = (bf16[2560,128]{1,0:T(8,128)(2,1)}, bf16[2560,128]{1,0:T(8,128)(2,1)S(1)}, u32[]{:S(2)}, u32[]{:S(2)}) collective-permute-start(bf16[2560,128]{1,0:T(8,128)(2,1)} %get-tuple-element.33.refs_8_.refs_12_.refs_9_.refs_16_), channel_id=1, source_target_pairs={{0,1},{1,0},{2,3},{3,2},{4,5},{5,4},{6,7},{7,6},{8,9},{9,8},{10,11... | collective-permute-start | bytes 1966088 | tf_op jit(solution)/shard_map/ppermute | solution.py:31
  50.0 9.1 %collective-permute-start.2 = (bf16[2560,128]{1,0:T(8,128)(2,1)}, bf16[2560,128]{1,0:T(8,128)(2,1)S(1)}, u32[]{:S(2)}, u32[]{:S(2)}) collective-permute-start(bf16[2560,128]{1,0:T(8,128)(2,1)} %get-tuple-element.33.refs_8_.refs_12_.refs_9_.refs_16_), channel_id=1, source_target_pairs={{0,14},{1,15},{2,4},{3,5},{4,2},{5,3},{6,8},{7,9},{8,6},{9,7},{10,... | collective-permute-start | bytes 1966088 | tf_op jit(solution)/shard_map/ppermute | solution.py:49
  59.2 1.9 %collective-permute-start = (bf16[512,128]{1,0:T(8,128)(2,1)S(1)}, bf16[512,128]{1,0:T(8,128)(2,1)S(1)}, u32[]{:S(2)}, u32[]{:S(2)}) collective-permute-start(bf16[512,128]{1,0:T(8,128)(2,1)S(1)} %get-tuple-element.32), channel_id=1, source_target_pairs={{0,2},{1,3},{2,0},{3,1},{4,6},{5,7},{6,4},{7,5},{8,10},{9,11},{10,... | collective-permute-start | bytes 393224 | tf_op jit(solution)/shard_map/ppermute | solution.py:31
  61.3 2.2 %one_hots.1 = (bf16[25,128,256]{2,1,0:T(8,128)(2,1)S(1)}, bf16[25,128,128]{2,1,0:T(8,128)(2,1)S(1)}, f32[512,128]{1,0:T(8,128)S(1)}, s32[4,32]{1,0:T(4,128)S(1)}) custom-call(s32[5]{0:T(128)S(1)} %stack.30.place_ref.refs_0_, s32[8,6]{1,0:T(8,128)S(1)} %copy-done.5, s32[8,6]{1,0:T(8,128)S(1)} %copy-done.6, s32[8,6,128]{2,1,0:T(8,128)S(1)} %copy.15.src_ref, ...), custom_call_target="tpu_custom_call" | custom-call | flops 3000000000 | bytes 1048576 | tf_op jit(solution)/shard_map/one_hots/pallas_call | solution.py:250
  63.6 3.1 %collective-permute-done = bf16[512,128]{1,0:T(8,128)(2,1)S(1)} collective-permute-done((bf16[512,128]{1,0:T(8,128)(2,1)S(1)}, bf16[512,128]{1,0:T(8,128)(2,1)S(1)}, u32[]{:S(2)}, u32[]{:S(2)}) %collective-permute-start) | collective-permute-done | bytes 131104 | tf_op jit(solution)/shard_map/ppermute | solution.py:31
  66.7 7.9 %collective-permute-done.2.refs_10_.refs_14_.refs_11_.refs_18_ = bf16[2560,128]{1,0:T(8,128)(2,1)S(1)} collective-permute-done((bf16[2560,128]{1,0:T(8,128)(2,1)}, bf16[2560,128]{1,0:T(8,128)(2,1)S(1)}, u32[]{:S(2)}, u32[]{:S(2)}) %collective-permute-start.2) | collective-permute-done | bytes 655392 | tf_op jit(solution)/shard_map/ppermute | solution.py:49
  74.5 1.9 %collective-permute-start.5 = (bf16[2,512,128]{2,1,0:T(8,128)(2,1)S(1)}, bf16[2,512,128]{2,1,0:T(8,128)(2,1)S(1)}, u32[]{:S(2)}, u32[]{:S(2)}) collective-permute-start(bf16[2,512,128]{2,1,0:T(8,128)(2,1)S(1)} %pad_maximum_fusion), channel_id=1, source_target_pairs={{0,1},{1,0},{2,3},{3,2},{4,5},{5,4},{6,7},{7,6},{8,9},{9,8},{10,11... | collective-permute-start | bytes 786440 | tf_op jit(solution)/shard_map/ppermute | solution.py:31
  76.5 1.5 collective-permute-done.5
  78.0 2.0 %collective-permute-start.8 = (bf16[2624,128]{1,0:T(8,128)(2,1)S(1)}, bf16[2624,128]{1,0:T(8,128)(2,1)S(1)}, u32[]{:S(2)}, u32[]{:S(2)}) collective-permute-start(bf16[2624,128]{1,0:T(8,128)(2,1)S(1)} %collective-permute-done.1.refs_10_.refs_14_.refs_18_.refs_11_), channel_id=1, source_target_pairs={{0,1},{1,0},{2,3},{3,2},{4,5},{5,4},{6,7},{7,6},{8,9},{9,8},{10,11... | collective-permute-start | bytes 2015240 | tf_op jit(solution)/shard_map/ppermute | solution.py:31
  80.0 1.9 %collective-permute-start.7 = (bf16[4,512,128]{2,1,0:T(8,128)(2,1)S(1)}, bf16[4,512,128]{2,1,0:T(8,128)(2,1)S(1)}, u32[]{:S(2)}, u32[]{:S(2)}) collective-permute-start(bf16[4,512,128]{2,1,0:T(8,128)(2,1)S(1)} %constant_dynamic-update-slice_fusion.refs_2_.refs_1_), channel_id=1, source_target_pairs={{0,3},{2,5},{3,0},{4,7},{5,2},{6,9},{7,4},{8,11},{9,6},{10,13},{11... | collective-permute-start | bytes 1572872 | tf_op jit(solution)/shard_map/ppermute | solution.py:38
  82.0 1.9 %collective-permute-start.6 = (bf16[4,512,128]{2,1,0:T(8,128)(2,1)S(1)}, bf16[4,512,128]{2,1,0:T(8,128)(2,1)S(1)}, u32[]{:S(2)}, u32[]{:S(2)}) collective-permute-start(bf16[4,512,128]{2,1,0:T(8,128)(2,1)S(1)} %constant_dynamic-update-slice_fusion.refs_2_.refs_1_), channel_id=1, source_target_pairs={{0,5},{2,7},{4,9},{5,0},{6,11},{7,2},{8,13},{9,4},{10,15},{11,6},{... | collective-permute-start | bytes 1572872 | tf_op jit(solution)/shard_map/ppermute | solution.py:38
  83.9 17.9 %collective-permute-done.7.refs_3_ = bf16[4,512,128]{2,1,0:T(8,128)(2,1)S(1)} collective-permute-done((bf16[4,512,128]{2,1,0:T(8,128)(2,1)S(1)}, bf16[4,512,128]{2,1,0:T(8,128)(2,1)S(1)}, u32[]{:S(2)}, u32[]{:S(2)}) %collective-permute-start.7) | collective-permute-done | bytes 524320 | tf_op jit(solution)/shard_map/ppermute | solution.py:38
  101.8 4.6 %near0.1 = (f32[512,512]{1,0:T(8,128)S(1)}, bf16[512,512]{1,0:T(8,128)(2,1)S(1)}, f32[4,16,128]{2,1,0:T(8,128)S(1)}) custom-call(s32[5]{0:T(128)S(1)} %stack.30.place_ref.refs_0_, s32[4,32]{1,0:T(4,128)S(1)} %get-tuple-element.36.refs_1_, bf16[4,512,128]{2,1,0:T(8,128)(2,1)S(1)} %constant_dynamic-update-slice_fusion.refs_2_.refs_1_, ...), custom_call_target="tpu_custom_call" | custom-call | flops 5000000000 | bytes 1048576 | tf_op jit(solution)/shard_map/near0/pallas_call | solution.py:250
  106.5 2.1 %far0.1.refs_2_ = bf16[512,512]{1,0:T(8,128)(2,1)S(1)} custom-call(s32[5]{0:T(128)S(1)} %stack.30.place_ref.refs_0_, s32[4,32]{1,0:T(4,128)S(1)} %get-tuple-element.36.refs_1_, bf16[4,512,128]{2,1,0:T(8,128)(2,1)S(1)} %collective-permute-done.6.refs_2_, bf16[8,128,512]{2,1,0:T(8,128)(2,1)S(1)} %bitcast.11, f32[2,2,512]{2,1,0:T(2,128)S(1)} %copy-done.2, ...), custom_call_target="tpu_custom_call" | custom-call | flops 3000000000 | bytes 1048576 | tf_op jit(solution)/shard_map/far0/pallas_call | solution.py:250
  108.5 3.1 %collective-permute-start.9 = (bf16[512,512]{1,0:T(8,128)(2,1)S(1)}, bf16[512,512]{1,0:T(8,128)(2,1)S(1)}, u32[]{:S(2)}, u32[]{:S(2)}) collective-permute-start(bf16[512,512]{1,0:T(8,128)(2,1)S(1)} %far0.1.refs_2_), channel_id=1, source_target_pairs={{0,1},{1,0},{2,3},{3,2},{4,5},{5,4},{6,7},{7,6},{8,9},{9,8},{10,11... | collective-permute-start | bytes 1572872 | tf_op jit(solution)/shard_map/ppermute | solution.py:31
  111.7 1.9 %collective-permute-start.12 = (bf16[2560,128]{1,0:T(8,128)(2,1)S(1)}, bf16[2560,128]{1,0:T(8,128)(2,1)S(1)}, u32[]{:S(2)}, u32[]{:S(2)}) collective-permute-start(bf16[2560,128]{1,0:T(8,128)(2,1)S(1)} %collective-permute-done.2.refs_10_.refs_14_.refs_11_.refs_18_), channel_id=1, source_target_pairs={{0,1},{1,0},{2,3},{3,2},{4,5},{5,4},{6,7},{7,6},{8,9},{9,8},{10,11... | collective-permute-start | bytes 1966088 | tf_op jit(solution)/shard_map/ppermute | solution.py:31
  113.7 1.9 %node0.1.refs_2_.refs_1_ = bf16[4,512,128]{2,1,0:T(8,128)(2,1)S(1)} custom-call(s32[5]{0:T(128)S(1)} %stack.30.place_ref.refs_0_, bf16[4,512,128]{2,1,0:T(8,128)(2,1)S(1)} %constant_dynamic-update-slice_fusion.refs_2_.refs_1_, bf16[512,512]{1,0:T(8,128)(2,1)S(1)} %far0.1.refs_2_, bf16[512,512]{1,0:T(8,128)(2,1)S(1)} %collective-permute-done.9.refs_3_, ...), custom_call_target="tpu_custom_call" | custom-call | flops 2000000000 | bytes 1048576 | tf_op jit(solution)/shard_map/node0/pallas_call | solution.py:250
  115.6 1.9 %collective-permute-start.11 = (bf16[4,512,128]{2,1,0:T(8,128)(2,1)S(1)}, bf16[4,512,128]{2,1,0:T(8,128)(2,1)S(1)}, u32[]{:S(2)}, u32[]{:S(2)}) collective-permute-start(bf16[4,512,128]{2,1,0:T(8,128)(2,1)S(1)} %node0.1.refs_2_.refs_1_), channel_id=1, source_target_pairs={{0,3},{2,5},{3,0},{4,7},{5,2},{6,9},{7,4},{8,11},{9,6},{10,13},{11... | collective-permute-start | bytes 1572872 | tf_op jit(solution)/shard_map/ppermute | solution.py:38
  117.5 2.5 %collective-permute-start.10 = (bf16[4,512,128]{2,1,0:T(8,128)(2,1)S(1)}, bf16[4,512,128]{2,1,0:T(8,128)(2,1)S(1)}, u32[]{:S(2)}, u32[]{:S(2)}) collective-permute-start(bf16[4,512,128]{2,1,0:T(8,128)(2,1)S(1)} %node0.1.refs_2_.refs_1_), channel_id=1, source_target_pairs={{0,5},{2,7},{4,9},{5,0},{6,11},{7,2},{8,13},{9,4},{10,15},{11,6},{... | collective-permute-start | bytes 1572872 | tf_op jit(solution)/shard_map/ppermute | solution.py:38
  120.0 8.3 %collective-permute-done.11.refs_3_ = bf16[4,512,128]{2,1,0:T(8,128)(2,1)S(1)} collective-permute-done((bf16[4,512,128]{2,1,0:T(8,128)(2,1)S(1)}, bf16[4,512,128]{2,1,0:T(8,128)(2,1)S(1)}, u32[]{:S(2)}, u32[]{:S(2)}) %collective-permute-start.11) | collective-permute-done | bytes 524320 | tf_op jit(solution)/shard_map/ppermute | solution.py:38
  128.4 4.6 %near1.1 = (f32[512,512]{1,0:T(8,128)S(1)}, bf16[512,512]{1,0:T(8,128)(2,1)S(1)}) custom-call(s32[5]{0:T(128)S(1)} %stack.30.place_ref.refs_0_, s32[4,32]{1,0:T(4,128)S(1)} %get-tuple-element.36.refs_1_, bf16[4,512,128]{2,1,0:T(8,128)(2,1)S(1)} %node0.1.refs_2_.refs_1_, bf16[4,512,128]{2,1,0:T(8,128)(2,1)S(1)} %collective-permute-done.11.refs_3_, ...), custom_call_target="tpu_custom_call" | custom-call | flops 5000000000 | bytes 1048576 | tf_op jit(solution)/shard_map/near1/pallas_call | solution.py:250
  133.0 5.1 %collective-permute-done.10.refs_2_ = bf16[4,512,128]{2,1,0:T(8,128)(2,1)S(1)} collective-permute-done((bf16[4,512,128]{2,1,0:T(8,128)(2,1)S(1)}, bf16[4,512,128]{2,1,0:T(8,128)(2,1)S(1)}, u32[]{:S(2)}, u32[]{:S(2)}) %collective-permute-start.10) | collective-permute-done | bytes 524320 | tf_op jit(solution)/shard_map/ppermute | solution.py:38
  138.1 2.1 %far1.1.refs_2_ = bf16[512,512]{1,0:T(8,128)(2,1)S(1)} custom-call(s32[5]{0:T(128)S(1)} %stack.30.place_ref.refs_0_, s32[4,32]{1,0:T(4,128)S(1)} %get-tuple-element.36.refs_1_, bf16[4,512,128]{2,1,0:T(8,128)(2,1)S(1)} %collective-permute-done.10.refs_2_, bf16[8,128,512]{2,1,0:T(8,128)(2,1)S(1)} %bitcast.13, f32[2,2,512]{2,1,0:T(2,128)S(1)} %copy-done.2, ...), custom_call_target="tpu_custom_call" | custom-call | flops 3000000000 | bytes 1048576 | tf_op jit(solution)/shard_map/far1/pallas_call | solution.py:250
  140.2 5.8 %collective-permute-start.13 = (bf16[512,512]{1,0:T(8,128)(2,1)S(1)}, bf16[512,512]{1,0:T(8,128)(2,1)S(1)}, u32[]{:S(2)}, u32[]{:S(2)}) collective-permute-start(bf16[512,512]{1,0:T(8,128)(2,1)S(1)} %far1.1.refs_2_), channel_id=1, source_target_pairs={{0,1},{1,0},{2,3},{3,2},{4,5},{5,4},{6,7},{7,6},{8,9},{9,8},{10,11... | collective-permute-start | bytes 1572872 | tf_op jit(solution)/shard_map/ppermute | solution.py:31
  146.0 1.5 collective-permute-done.13.refs_3_
  147.5 1.8 %node1.1 = (bf16[512,128]{1,0:T(8,128)(2,1)S(1)}, bf16[512,128]{1,0:T(8,128)(2,1)S(1)}) custom-call(s32[5]{0:T(128)S(1)} %stack.30.place_ref.refs_0_, bf16[4,512,128]{2,1,0:T(8,128)(2,1)S(1)} %node0.1.refs_2_.refs_1_, bf16[512,512]{1,0:T(8,128)(2,1)S(1)} %far1.1.refs_2_, bf16[512,512]{1,0:T(8,128)(2,1)S(1)} %collective-permute-done.13.refs_3_, ...), custom_call_target="tpu_custom_call" | custom-call | flops 2000000000 | bytes 1048576 | tf_op jit(solution)/shard_map/node1/pallas_call | solution.py:250
  149.3 2.4 %collective-permute-start.14 = (bf16[512,128]{1,0:T(8,128)(2,1)S(1)}, bf16[512,128]{1,0:T(8,128)(2,1)S(1)}, u32[]{:S(2)}, u32[]{:S(2)}) collective-permute-start(bf16[512,128]{1,0:T(8,128)(2,1)S(1)} %get-tuple-element.56), channel_id=1, source_target_pairs={{0,2},{1,3},{2,0},{3,1},{4,6},{5,7},{6,4},{7,5},{8,10},{9,11},{10,... | collective-permute-start | bytes 393224 | tf_op jit(solution)/shard_map/ppermute | solution.py:31
  151.8 5.3 %collective-permute-done.14.other_ref = bf16[512,128]{1,0:T(8,128)(2,1)S(1)} collective-permute-done((bf16[512,128]{1,0:T(8,128)(2,1)S(1)}, bf16[512,128]{1,0:T(8,128)(2,1)S(1)}, u32[]{:S(2)}, u32[]{:S(2)}) %collective-permute-start.14) | collective-permute-done | bytes 131104 | tf_op jit(solution)/shard_map/ppermute | solution.py:31
  157.0 1.3 join.1
  (34 shorter events, 0.3 us)
Async XLA Ops:
  0.0 59.2 %copy-start.7 = (bf16[1024,128]{1,0:T(8,128)(2,1)S(1)}, bf16[1024,128]{1,0:T(8,128)(2,1)}, u32[]{:S(2)}) copy-start(bf16[1024,128]{1,0:T(8,128)(2,1)} %param.14) | copy-start | bytes 786436
  0.0 61.2 %copy-start.8 = (s32[8,6,128]{2,0,1:T(8,128)S(1)}, s32[8,6,128]{2,0,1:T(8,128)}, u32[]{:S(2)}) copy-start(s32[8,6,128]{2,0,1:T(8,128)} %param.26) | copy-start | bytes 73732
  0.0 61.2 %copy-start.9 = (s32[8,6,128]{2,0,1:T(8,128)S(1)}, s32[8,6,128]{2,0,1:T(8,128)}, u32[]{:S(2)}) copy-start(s32[8,6,128]{2,0,1:T(8,128)} %param.27) | copy-start | bytes 73732
  0.0 61.3 %copy-start.6 = (s32[8,6]{1,0:T(8,128)S(1)}, s32[8,6]{1,0:T(8,128)}, u32[]{:S(2)}) copy-start(s32[8,6]{1,0:T(8,128)} %count_ref.1) | copy-start | bytes 580
  0.0 61.3 %copy-start.5 = (s32[8,6]{1,0:T(8,128)S(1)}, s32[8,6]{1,0:T(8,128)}, u32[]{:S(2)}) copy-start(s32[8,6]{1,0:T(8,128)} %nbr_ref.1) | copy-start | bytes 580
  41.7 32.9 %collective-permute-start.3 = (bf16[2624,128]{1,0:T(8,128)(2,1)}, bf16[2624,128]{1,0:T(8,128)(2,1)S(1)}, u32[]{:S(2)}, u32[]{:S(2)}) collective-permute-start(bf16[2624,128]{1,0:T(8,128)(2,1)} %get-tuple-element.31.refs_8_.refs_12_.refs_16_.refs_9_), channel_id=1, source_target_pairs={{0,1},{1,0},{2,3},{3,2},{4,5},{5,4},{6,7},{7,6},{8,9},{9,8},{10,11... | collective-permute-start | bytes 2015240 | tf_op jit(solution)/shard_map/ppermute | solution.py:31
  43.6 30.9 %collective-permute-start.1 = (bf16[2624,128]{1,0:T(8,128)(2,1)}, bf16[2624,128]{1,0:T(8,128)(2,1)S(1)}, u32[]{:S(2)}, u32[]{:S(2)}) collective-permute-start(bf16[2624,128]{1,0:T(8,128)(2,1)} %get-tuple-element.31.refs_8_.refs_12_.refs_16_.refs_9_), channel_id=1, source_target_pairs={{0,2},{1,3},{2,0},{3,1},{4,6},{5,7},{6,4},{7,5},{8,10},{9,11},{10,... | collective-permute-start | bytes 2015240 | tf_op jit(solution)/shard_map/ppermute | solution.py:31
  47.9 18.8 %collective-permute-start.4 = (bf16[2560,128]{1,0:T(8,128)(2,1)}, bf16[2560,128]{1,0:T(8,128)(2,1)S(1)}, u32[]{:S(2)}, u32[]{:S(2)}) collective-permute-start(bf16[2560,128]{1,0:T(8,128)(2,1)} %get-tuple-element.33.refs_8_.refs_12_.refs_9_.refs_16_), channel_id=1, source_target_pairs={{0,1},{1,0},{2,3},{3,2},{4,5},{5,4},{6,7},{7,6},{8,9},{9,8},{10,11... | collective-permute-start | bytes 1966088 | tf_op jit(solution)/shard_map/ppermute | solution.py:31
  50.0 24.5 %collective-permute-start.2 = (bf16[2560,128]{1,0:T(8,128)(2,1)}, bf16[2560,128]{1,0:T(8,128)(2,1)S(1)}, u32[]{:S(2)}, u32[]{:S(2)}) collective-permute-start(bf16[2560,128]{1,0:T(8,128)(2,1)} %get-tuple-element.33.refs_8_.refs_12_.refs_9_.refs_16_), channel_id=1, source_target_pairs={{0,14},{1,15},{2,4},{3,5},{4,2},{5,3},{6,8},{7,9},{8,6},{9,7},{10,... | collective-permute-start | bytes 1966088 | tf_op jit(solution)/shard_map/ppermute | solution.py:49
  59.2 7.4 %collective-permute-start = (bf16[512,128]{1,0:T(8,128)(2,1)S(1)}, bf16[512,128]{1,0:T(8,128)(2,1)S(1)}, u32[]{:S(2)}, u32[]{:S(2)}) collective-permute-start(bf16[512,128]{1,0:T(8,128)(2,1)S(1)} %get-tuple-element.32), channel_id=1, source_target_pairs={{0,2},{1,3},{2,0},{3,1},{4,6},{5,7},{6,4},{7,5},{8,10},{9,11},{10,... | collective-permute-start | bytes 393224 | tf_op jit(solution)/shard_map/ppermute | solution.py:31
  61.3 40.5 %copy-start = (bf16[2624,128]{1,0:T(8,128)(2,1)S(1)}, bf16[2624,128]{1,0:T(8,128)(2,1)}, u32[]{:S(2)}) copy-start(bf16[2624,128]{1,0:T(8,128)(2,1)} %get-tuple-element.31.refs_8_.refs_12_.refs_16_.refs_9_) | copy-start | bytes 2015236
  61.3 40.5 %copy-start.2 = (f32[2,2,512]{2,1,0:T(2,128)S(1)}, f32[2,2,512]{2,1,0:T(2,128)}, u32[]{:S(2)}) copy-start(f32[2,2,512]{2,1,0:T(2,128)} %refs_6_.3) | copy-start | bytes 24580
  61.3 40.5 %copy-start.4 = (bf16[2,512,512]{2,1,0:T(8,128)(2,1)S(1)}, bf16[2,512,512]{2,1,0:T(8,128)(2,1)}, u32[]{:S(2)}) copy-start(bf16[2,512,512]{2,1,0:T(8,128)(2,1)} %param.17) | copy-start | bytes 3145732
  74.5 3.4 %collective-permute-start.5 = (bf16[2,512,128]{2,1,0:T(8,128)(2,1)S(1)}, bf16[2,512,128]{2,1,0:T(8,128)(2,1)S(1)}, u32[]{:S(2)}, u32[]{:S(2)}) collective-permute-start(bf16[2,512,128]{2,1,0:T(8,128)(2,1)S(1)} %pad_maximum_fusion), channel_id=1, source_target_pairs={{0,1},{1,0},{2,3},{3,2},{4,5},{5,4},{6,7},{7,6},{8,9},{9,8},{10,11... | collective-permute-start | bytes 786440 | tf_op jit(solution)/shard_map/ppermute | solution.py:31
  78.0 23.8 %collective-permute-start.8 = (bf16[2624,128]{1,0:T(8,128)(2,1)S(1)}, bf16[2624,128]{1,0:T(8,128)(2,1)S(1)}, u32[]{:S(2)}, u32[]{:S(2)}) collective-permute-start(bf16[2624,128]{1,0:T(8,128)(2,1)S(1)} %collective-permute-done.1.refs_10_.refs_14_.refs_18_.refs_11_), channel_id=1, source_target_pairs={{0,1},{1,0},{2,3},{3,2},{4,5},{5,4},{6,7},{7,6},{8,9},{9,8},{10,11... | collective-permute-start | bytes 2015240 | tf_op jit(solution)/shard_map/ppermute | solution.py:31
  80.0 21.7 %collective-permute-start.7 = (bf16[4,512,128]{2,1,0:T(8,128)(2,1)S(1)}, bf16[4,512,128]{2,1,0:T(8,128)(2,1)S(1)}, u32[]{:S(2)}, u32[]{:S(2)}) collective-permute-start(bf16[4,512,128]{2,1,0:T(8,128)(2,1)S(1)} %constant_dynamic-update-slice_fusion.refs_2_.refs_1_), channel_id=1, source_target_pairs={{0,3},{2,5},{3,0},{4,7},{5,2},{6,9},{7,4},{8,11},{9,6},{10,13},{11... | collective-permute-start | bytes 1572872 | tf_op jit(solution)/shard_map/ppermute | solution.py:38
  82.0 24.5 %collective-permute-start.6 = (bf16[4,512,128]{2,1,0:T(8,128)(2,1)S(1)}, bf16[4,512,128]{2,1,0:T(8,128)(2,1)S(1)}, u32[]{:S(2)}, u32[]{:S(2)}) collective-permute-start(bf16[4,512,128]{2,1,0:T(8,128)(2,1)S(1)} %constant_dynamic-update-slice_fusion.refs_2_.refs_1_), channel_id=1, source_target_pairs={{0,5},{2,7},{4,9},{5,0},{6,11},{7,2},{8,13},{9,4},{10,15},{11,6},{... | collective-permute-start | bytes 1572872 | tf_op jit(solution)/shard_map/ppermute | solution.py:38
  106.4 7.2 %copy-start.3 = (f32[2,512]{1,0:T(2,128)S(1)}, f32[2,512]{1,0:T(2,128)}, u32[]{:S(2)}) copy-start(f32[2,512]{1,0:T(2,128)} %refs_7_.3) | copy-start | bytes 12292
  108.5 5.1 %collective-permute-start.9 = (bf16[512,512]{1,0:T(8,128)(2,1)S(1)}, bf16[512,512]{1,0:T(8,128)(2,1)S(1)}, u32[]{:S(2)}, u32[]{:S(2)}) collective-permute-start(bf16[512,512]{1,0:T(8,128)(2,1)S(1)} %far0.1.refs_2_), channel_id=1, source_target_pairs={{0,1},{1,0},{2,3},{3,2},{4,5},{5,4},{6,7},{7,6},{8,9},{9,8},{10,11... | collective-permute-start | bytes 1572872 | tf_op jit(solution)/shard_map/ppermute | solution.py:31
  111.7 8.3 %collective-permute-start.12 = (bf16[2560,128]{1,0:T(8,128)(2,1)S(1)}, bf16[2560,128]{1,0:T(8,128)(2,1)S(1)}, u32[]{:S(2)}, u32[]{:S(2)}) collective-permute-start(bf16[2560,128]{1,0:T(8,128)(2,1)S(1)} %collective-permute-done.2.refs_10_.refs_14_.refs_11_.refs_18_), channel_id=1, source_target_pairs={{0,1},{1,0},{2,3},{3,2},{4,5},{5,4},{6,7},{7,6},{8,9},{9,8},{10,11... | collective-permute-start | bytes 1966088 | tf_op jit(solution)/shard_map/ppermute | solution.py:31
  113.6 14.7 %copy-start.1 = (bf16[2560,128]{1,0:T(8,128)(2,1)S(1)}, bf16[2560,128]{1,0:T(8,128)(2,1)}, u32[]{:S(2)}) copy-start(bf16[2560,128]{1,0:T(8,128)(2,1)} %get-tuple-element.33.refs_8_.refs_12_.refs_9_.refs_16_) | copy-start | bytes 1966084
  115.6 12.8 %collective-permute-start.11 = (bf16[4,512,128]{2,1,0:T(8,128)(2,1)S(1)}, bf16[4,512,128]{2,1,0:T(8,128)(2,1)S(1)}, u32[]{:S(2)}, u32[]{:S(2)}) collective-permute-start(bf16[4,512,128]{2,1,0:T(8,128)(2,1)S(1)} %node0.1.refs_2_.refs_1_), channel_id=1, source_target_pairs={{0,3},{2,5},{3,0},{4,7},{5,2},{6,9},{7,4},{8,11},{9,6},{10,13},{11... | collective-permute-start | bytes 1572872 | tf_op jit(solution)/shard_map/ppermute | solution.py:38
  117.5 20.6 %collective-permute-start.10 = (bf16[4,512,128]{2,1,0:T(8,128)(2,1)S(1)}, bf16[4,512,128]{2,1,0:T(8,128)(2,1)S(1)}, u32[]{:S(2)}, u32[]{:S(2)}) collective-permute-start(bf16[4,512,128]{2,1,0:T(8,128)(2,1)S(1)} %node0.1.refs_2_.refs_1_), channel_id=1, source_target_pairs={{0,5},{2,7},{4,9},{5,0},{6,11},{7,2},{8,13},{9,4},{10,15},{11,6},{... | collective-permute-start | bytes 1572872 | tf_op jit(solution)/shard_map/ppermute | solution.py:38
  140.2 7.4 %collective-permute-start.13 = (bf16[512,512]{1,0:T(8,128)(2,1)S(1)}, bf16[512,512]{1,0:T(8,128)(2,1)S(1)}, u32[]{:S(2)}, u32[]{:S(2)}) collective-permute-start(bf16[512,512]{1,0:T(8,128)(2,1)S(1)} %far1.1.refs_2_), channel_id=1, source_target_pairs={{0,1},{1,0},{2,3},{3,2},{4,5},{5,4},{6,7},{7,6},{8,9},{9,8},{10,11... | collective-permute-start | bytes 1572872 | tf_op jit(solution)/shard_map/ppermute | solution.py:31
  149.3 7.7 %collective-permute-start.14 = (bf16[512,128]{1,0:T(8,128)(2,1)S(1)}, bf16[512,128]{1,0:T(8,128)(2,1)S(1)}, u32[]{:S(2)}, u32[]{:S(2)}) collective-permute-start(bf16[512,128]{1,0:T(8,128)(2,1)S(1)} %get-tuple-element.56), channel_id=1, source_target_pairs={{0,2},{1,3},{2,0},{3,1},{4,6},{5,7},{6,4},{7,5},{8,10},{9,11},{10,... | collective-permute-start | bytes 393224 | tf_op jit(solution)/shard_map/ppermute | solution.py:31

commit v7 on v6

--- a/solution.py
+++ b/solution.py
@@ -295,7 +295,7 @@
         pack_kernel,
         "packs",
         (w_src, w_dst, w_node_in, w_node_out, node_vectors, node_gain),
-        [HBM] * 4 + [VMEM] * 2,
+        [VMEM] * 6,
         (
             jax.ShapeDtypeStruct((5 * width + 4 * VECTOR_ROWS, part), BF16),
             jax.ShapeDtypeStruct((5 * width, part), BF16),
@@ -304,12 +304,12 @@
         [pltpu.VMEM((4 * VECTOR_ROWS, part), BF16), pltpu.SemaphoreType.DMA((9,))],
         mib=60,
     )
-    other = barrier((other, pack))[0]
     across = exchange(other, 2)
     pack_across = exchange(pack, 2)
-    next_across = from_other_side(next_pack)
     beside = exchange(pack, 1)
-    next_beside = exchange(next_pack, 1)
+    next_share, beside = barrier((next_pack, beside))
+    next_across = from_other_side(next_share)
+    next_beside = exchange(next_share, 1)
 
     all_slots = mine * slots + 1
     gather, collect, degree, meta = call(

time: 159 us -> 120 us (0.75)
  Pallas kernels: 62.2 us -> 23.1 us
  waiting for transfers between devices: 50.5 us -> 55.1 us
  starting transfers between devices: 44.9 us -> 40.4 us
    pallas_call x9, Pallas kernels: 62.2 us -> 23.1 us  [call(): pl.pallas_call(kernel, out_shape=outs, grid=(1,), in_specs=spaces, out_sp...]
    ppermute x4, waiting for transfers between devices: 31.3 us -> 35.8 us  [swap_with(): lax.ppermute(value, BOTH, [(i, t) for i, t in pairs if 0 <= t < total])]
    ppermute x10, starting transfers between devices: 27.5 us -> 23.6 us  [exchange(): return lax.ppermute(value, BOTH, [(i, i ^ mask) for i in range(total)])]
  transfers between devices with their start and end apart: 15 -> 15, of which waited for: 8 -> 7; matrix products, arithmetic and copies ran while one was open for 0% -> 0% of each run, Pallas kernels for 8% -> 11%
where the time goes in v7:
time: 120 us; the launch traced here: 119 us
  waiting for transfers between devices  55.1 us (46%)
  starting transfers between devices  40.4 us (34%)
  Pallas kernels  23.1 us (19%)
    ppermute x4, waiting for transfers between devices, swap_with(): lax.ppermute(value, BOTH, [(i, t) for i, t in pairs if 0 <= t < total])  35.8 us
    ppermute x10, starting transfers between devices, exchange(): return lax.ppermute(value, BOTH, [(i, i ^ mask) for i in range(total)])  23.6 us
    pallas_call x9, Pallas kernels, call(): pl.pallas_call(kernel, out_shape=outs, grid=(1,), in_specs=spaces, out_sp...  23.1 us
    ppermute x10, waiting for transfers between devices, exchange(): return lax.ppermute(value, BOTH, [(i, i ^ mask) for i in range(total)])  11.4 us
    ppermute x1, starting transfers between devices, from_other_side(): return lax.ppermute(value, BOTH, pairs)  9.13 us
    ppermute x1, waiting for transfers between devices, from_other_side(): return lax.ppermute(value, BOTH, pairs)  7.86 us
    ppermute x4, starting transfers between devices, swap_with(): lax.ppermute(value, BOTH, [(i, t) for i, t in pairs if 0 <= t < total])  7.68 us
  transfers between devices with their start and end apart: 15, of which 7 were waited for; matrix products, arithmetic and copies ran while one was open for 0% of the time, Pallas kernels for 11%

profile of v7, /device:TPU:6, one launch (start us, length us, event | category | flops | bytes accessed | tf_op | source)
XLA Modules:
  0.0 119.2 jit_solution(1540350191854297385)
XLA Ops:
  0.0 2.5 %packs.1 = (bf16[2624,128]{1,0:T(8,128)(2,1)}, bf16[2560,128]{1,0:T(8,128)(2,1)}) custom-call(bf16[2,512,128]{2,1,0:T(8,128)(2,1)} %src_ref.2, bf16[2,512,128]{2,1,0:T(8,128)(2,1)} %dst_ref.2, bf16[2,1024,128]{2,1,0:T(8,128)(2,1)} %in_ref.1, bf16[2,512,128]{2,1,0:T(8,128)(2,1)} %out_w_ref.1, f32[2,4,128]{2,1,0:T(4,128)} %vec_ref.1, f32[2,128]{1,0:T(2,128)} %gain_ref.1), custom_call_target="tpu_custom_call" | custom-call | flops 2000000000 | bytes 1048576 | tf_op jit(solution)/shard_map/packs/pallas_call | solution.py:250
  2.5 1.9 %collective-permute-start.2 = (bf16[2624,128]{1,0:T(8,128)(2,1)}, bf16[2624,128]{1,0:T(8,128)(2,1)S(1)}, u32[]{:S(2)}, u32[]{:S(2)}) collective-permute-start(bf16[2624,128]{1,0:T(8,128)(2,1)} %get-tuple-element.32.refs_8_.refs_12_.refs_16_.refs_9_), channel_id=1, source_target_pairs={{0,1},{1,0},{2,3},{3,2},{4,5},{5,4},{6,7},{7,6},{8,9},{9,8},{10,11... | collective-permute-start | bytes 2015240 | tf_op jit(solution)/shard_map/ppermute | solution.py:31
  4.5 4.3 %collective-permute-start.1 = (bf16[2624,128]{1,0:T(8,128)(2,1)}, bf16[2624,128]{1,0:T(8,128)(2,1)S(1)}, u32[]{:S(2)}, u32[]{:S(2)}) collective-permute-start(bf16[2624,128]{1,0:T(8,128)(2,1)} %get-tuple-element.32.refs_8_.refs_12_.refs_16_.refs_9_), channel_id=1, source_target_pairs={{0,2},{1,3},{2,0},{3,1},{4,6},{5,7},{6,4},{7,5},{8,10},{9,11},{10,... | collective-permute-start | bytes 2015240 | tf_op jit(solution)/shard_map/ppermute | solution.py:31
  8.8 2.1 %collective-permute-start.4 = (bf16[2560,128]{1,0:T(8,128)(2,1)}, bf16[2560,128]{1,0:T(8,128)(2,1)S(1)}, u32[]{:S(2)}, u32[]{:S(2)}) collective-permute-start(bf16[2560,128]{1,0:T(8,128)(2,1)} %get-tuple-element.34.refs_8_.refs_12_.refs_9_.refs_16_), channel_id=1, source_target_pairs={{0,1},{1,0},{2,3},{3,2},{4,5},{5,4},{6,7},{7,6},{8,9},{9,8},{10,11... | collective-permute-start | bytes 1966088 | tf_op jit(solution)/shard_map/ppermute | solution.py:31
  10.9 9.1 %collective-permute-start.3 = (bf16[2560,128]{1,0:T(8,128)(2,1)}, bf16[2560,128]{1,0:T(8,128)(2,1)S(1)}, u32[]{:S(2)}, u32[]{:S(2)}) collective-permute-start(bf16[2560,128]{1,0:T(8,128)(2,1)} %get-tuple-element.34.refs_8_.refs_12_.refs_9_.refs_16_), channel_id=1, source_target_pairs={{0,14},{1,15},{2,4},{3,5},{4,2},{5,3},{6,8},{7,9},{8,6},{9,7},{10,... | collective-permute-start | bytes 1966088 | tf_op jit(solution)/shard_map/ppermute | solution.py:49
  20.1 1.9 %collective-permute-start = (bf16[512,128]{1,0:T(8,128)(2,1)S(1)}, bf16[512,128]{1,0:T(8,128)(2,1)S(1)}, u32[]{:S(2)}, u32[]{:S(2)}) collective-permute-start(bf16[512,128]{1,0:T(8,128)(2,1)S(1)} %get-tuple-element.60), channel_id=1, source_target_pairs={{0,2},{1,3},{2,0},{3,1},{4,6},{5,7},{6,4},{7,5},{8,10},{9,11},{10,... | collective-permute-start | bytes 393224 | tf_op jit(solution)/shard_map/ppermute | solution.py:31
  22.1 0.1 stack.30.place_ref.refs_0_
  22.2 2.2 %one_hots.1 = (bf16[25,128,256]{2,1,0:T(8,128)(2,1)S(1)}, bf16[25,128,128]{2,1,0:T(8,128)(2,1)S(1)}, f32[512,128]{1,0:T(8,128)S(1)}, s32[4,32]{1,0:T(4,128)S(1)}) custom-call(s32[5]{0:T(128)S(1)} %stack.30.place_ref.refs_0_, s32[8,6]{1,0:T(8,128)S(1)} %copy-done.5, s32[8,6]{1,0:T(8,128)S(1)} %copy-done.6, s32[8,6,128]{2,1,0:T(8,128)S(1)} %copy.15.src_ref, ...), custom_call_target="tpu_custom_call" | custom-call | flops 3000000000 | bytes 1048576 | tf_op jit(solution)/shard_map/one_hots/pallas_call | solution.py:250
  24.5 3.0 %collective-permute-done = bf16[512,128]{1,0:T(8,128)(2,1)S(1)} collective-permute-done((bf16[512,128]{1,0:T(8,128)(2,1)S(1)}, bf16[512,128]{1,0:T(8,128)(2,1)S(1)}, u32[]{:S(2)}, u32[]{:S(2)}) %collective-permute-start) | collective-permute-done | bytes 131104 | tf_op jit(solution)/shard_map/ppermute | solution.py:31
  27.6 7.9 %collective-permute-done.3.refs_10_.refs_14_.refs_11_.refs_18_ = bf16[2560,128]{1,0:T(8,128)(2,1)S(1)} collective-permute-done((bf16[2560,128]{1,0:T(8,128)(2,1)}, bf16[2560,128]{1,0:T(8,128)(2,1)S(1)}, u32[]{:S(2)}, u32[]{:S(2)}) %collective-permute-start.3) | collective-permute-done | bytes 655392 | tf_op jit(solution)/shard_map/ppermute | solution.py:49
  35.4 1.9 %collective-permute-start.5 = (bf16[2,512,128]{2,1,0:T(8,128)(2,1)S(1)}, bf16[2,512,128]{2,1,0:T(8,128)(2,1)S(1)}, u32[]{:S(2)}, u32[]{:S(2)}) collective-permute-start(bf16[2,512,128]{2,1,0:T(8,128)(2,1)S(1)} %pad_maximum_fusion), channel_id=1, source_target_pairs={{0,1},{1,0},{2,3},{3,2},{4,5},{5,4},{6,7},{7,6},{8,9},{9,8},{10,11... | collective-permute-start | bytes 786440 | tf_op jit(solution)/shard_map/ppermute | solution.py:31
  37.4 1.5 %collective-permute-done.5 = bf16[2,512,128]{2,1,0:T(8,128)(2,1)S(1)} collective-permute-done((bf16[2,512,128]{2,1,0:T(8,128)(2,1)S(1)}, bf16[2,512,128]{2,1,0:T(8,128)(2,1)S(1)}, u32[]{:S(2)}, u32[]{:S(2)}) %collective-permute-start.5) | collective-permute-done | bytes 262176 | tf_op jit(solution)/shard_map/ppermute | solution.py:31
  38.9 2.0 %collective-permute-start.8 = (bf16[2624,128]{1,0:T(8,128)(2,1)S(1)}, bf16[2624,128]{1,0:T(8,128)(2,1)S(1)}, u32[]{:S(2)}, u32[]{:S(2)}) collective-permute-start(bf16[2624,128]{1,0:T(8,128)(2,1)S(1)} %collective-permute-done.1.refs_10_.refs_14_.refs_18_.refs_11_), channel_id=1, source_target_pairs={{0,1},{1,0},{2,3},{3,2},{4,5},{5,4},{6,7},{7,6},{8,9},{9,8},{10,11... | collective-permute-start | bytes 2015240 | tf_op jit(solution)/shard_map/ppermute | solution.py:31
  40.9 1.9 %collective-permute-start.7 = (bf16[4,512,128]{2,1,0:T(8,128)(2,1)S(1)}, bf16[4,512,128]{2,1,0:T(8,128)(2,1)S(1)}, u32[]{:S(2)}, u32[]{:S(2)}) collective-permute-start(bf16[4,512,128]{2,1,0:T(8,128)(2,1)S(1)} %constant_dynamic-update-slice_fusion.refs_2_.refs_1_), channel_id=1, source_target_pairs={{0,3},{2,5},{3,0},{4,7},{5,2},{6,9},{7,4},{8,11},{9,6},{10,13},{11... | collective-permute-start | bytes 1572872 | tf_op jit(solution)/shard_map/ppermute | solution.py:38
  42.9 1.9 %collective-permute-start.6 = (bf16[4,512,128]{2,1,0:T(8,128)(2,1)S(1)}, bf16[4,512,128]{2,1,0:T(8,128)(2,1)S(1)}, u32[]{:S(2)}, u32[]{:S(2)}) collective-permute-start(bf16[4,512,128]{2,1,0:T(8,128)(2,1)S(1)} %constant_dynamic-update-slice_fusion.refs_2_.refs_1_), channel_id=1, source_target_pairs={{0,5},{2,7},{4,9},{5,0},{6,11},{7,2},{8,13},{9,4},{10,15},{11,6},{... | collective-permute-start | bytes 1572872 | tf_op jit(solution)/shard_map/ppermute | solution.py:38
  44.8 17.9 %collective-permute-done.7.refs_3_ = bf16[4,512,128]{2,1,0:T(8,128)(2,1)S(1)} collective-permute-done((bf16[4,512,128]{2,1,0:T(8,128)(2,1)S(1)}, bf16[4,512,128]{2,1,0:T(8,128)(2,1)S(1)}, u32[]{:S(2)}, u32[]{:S(2)}) %collective-permute-start.7) | collective-permute-done | bytes 524320 | tf_op jit(solution)/shard_map/ppermute | solution.py:38
  62.7 4.6 %near0.1 = (f32[512,512]{1,0:T(8,128)S(1)}, bf16[512,512]{1,0:T(8,128)(2,1)S(1)}, f32[4,16,128]{2,1,0:T(8,128)S(1)}) custom-call(s32[5]{0:T(128)S(1)} %stack.30.place_ref.refs_0_, s32[4,32]{1,0:T(4,128)S(1)} %get-tuple-element.38.refs_1_, bf16[4,512,128]{2,1,0:T(8,128)(2,1)S(1)} %constant_dynamic-update-slice_fusion.refs_2_.refs_1_, ...), custom_call_target="tpu_custom_call" | custom-call | flops 5000000000 | bytes 1048576 | tf_op jit(solution)/shard_map/near0/pallas_call | solution.py:250
  67.3 2.1 %far0.1.refs_2_ = bf16[512,512]{1,0:T(8,128)(2,1)S(1)} custom-call(s32[5]{0:T(128)S(1)} %stack.30.place_ref.refs_0_, s32[4,32]{1,0:T(4,128)S(1)} %get-tuple-element.38.refs_1_, bf16[4,512,128]{2,1,0:T(8,128)(2,1)S(1)} %collective-permute-done.6.refs_2_, bf16[8,128,512]{2,1,0:T(8,128)(2,1)S(1)} %bitcast.11, f32[2,2,512]{2,1,0:T(2,128)S(1)} %copy-done.2, ...), custom_call_target="tpu_custom_call" | custom-call | flops 3000000000 | bytes 1048576 | tf_op jit(solution)/shard_map/far0/pallas_call | solution.py:250
  69.4 3.1 %collective-permute-start.9 = (bf16[512,512]{1,0:T(8,128)(2,1)S(1)}, bf16[512,512]{1,0:T(8,128)(2,1)S(1)}, u32[]{:S(2)}, u32[]{:S(2)}) collective-permute-start(bf16[512,512]{1,0:T(8,128)(2,1)S(1)} %far0.1.refs_2_), channel_id=1, source_target_pairs={{0,1},{1,0},{2,3},{3,2},{4,5},{5,4},{6,7},{7,6},{8,9},{9,8},{10,11... | collective-permute-start | bytes 1572872 | tf_op jit(solution)/shard_map/ppermute | solution.py:31
  72.6 1.9 %collective-permute-start.12 = (bf16[2560,128]{1,0:T(8,128)(2,1)S(1)}, bf16[2560,128]{1,0:T(8,128)(2,1)S(1)}, u32[]{:S(2)}, u32[]{:S(2)}) collective-permute-start(bf16[2560,128]{1,0:T(8,128)(2,1)S(1)} %collective-permute-done.3.refs_10_.refs_14_.refs_11_.refs_18_), channel_id=1, source_target_pairs={{0,1},{1,0},{2,3},{3,2},{4,5},{5,4},{6,7},{7,6},{8,9},{9,8},{10,11... | collective-permute-start | bytes 1966088 | tf_op jit(solution)/shard_map/ppermute | solution.py:31
  74.5 1.9 %node0.1.refs_2_.refs_1_ = bf16[4,512,128]{2,1,0:T(8,128)(2,1)S(1)} custom-call(s32[5]{0:T(128)S(1)} %stack.30.place_ref.refs_0_, bf16[4,512,128]{2,1,0:T(8,128)(2,1)S(1)} %constant_dynamic-update-slice_fusion.refs_2_.refs_1_, bf16[512,512]{1,0:T(8,128)(2,1)S(1)} %far0.1.refs_2_, bf16[512,512]{1,0:T(8,128)(2,1)S(1)} %collective-permute-done.9.refs_3_, ...), custom_call_target="tpu_custom_call" | custom-call | flops 2000000000 | bytes 1048576 | tf_op jit(solution)/shard_map/node0/pallas_call | solution.py:250
  76.4 1.9 %collective-permute-start.11 = (bf16[4,512,128]{2,1,0:T(8,128)(2,1)S(1)}, bf16[4,512,128]{2,1,0:T(8,128)(2,1)S(1)}, u32[]{:S(2)}, u32[]{:S(2)}) collective-permute-start(bf16[4,512,128]{2,1,0:T(8,128)(2,1)S(1)} %node0.1.refs_2_.refs_1_), channel_id=1, source_target_pairs={{0,3},{2,5},{3,0},{4,7},{5,2},{6,9},{7,4},{8,11},{9,6},{10,13},{11... | collective-permute-start | bytes 1572872 | tf_op jit(solution)/shard_map/ppermute | solution.py:38
  78.4 1.9 %collective-permute-start.10 = (bf16[4,512,128]{2,1,0:T(8,128)(2,1)S(1)}, bf16[4,512,128]{2,1,0:T(8,128)(2,1)S(1)}, u32[]{:S(2)}, u32[]{:S(2)}) collective-permute-start(bf16[4,512,128]{2,1,0:T(8,128)(2,1)S(1)} %node0.1.refs_2_.refs_1_), channel_id=1, source_target_pairs={{0,5},{2,7},{4,9},{5,0},{6,11},{7,2},{8,13},{9,4},{10,15},{11,6},{... | collective-permute-start | bytes 1572872 | tf_op jit(solution)/shard_map/ppermute | solution.py:38
  80.3 17.9 %collective-permute-done.11.refs_3_ = bf16[4,512,128]{2,1,0:T(8,128)(2,1)S(1)} collective-permute-done((bf16[4,512,128]{2,1,0:T(8,128)(2,1)S(1)}, bf16[4,512,128]{2,1,0:T(8,128)(2,1)S(1)}, u32[]{:S(2)}, u32[]{:S(2)}) %collective-permute-start.11) | collective-permute-done | bytes 524320 | tf_op jit(solution)/shard_map/ppermute | solution.py:38
  98.2 4.6 %near1.1 = (f32[512,512]{1,0:T(8,128)S(1)}, bf16[512,512]{1,0:T(8,128)(2,1)S(1)}) custom-call(s32[5]{0:T(128)S(1)} %stack.30.place_ref.refs_0_, s32[4,32]{1,0:T(4,128)S(1)} %get-tuple-element.38.refs_1_, bf16[4,512,128]{2,1,0:T(8,128)(2,1)S(1)} %node0.1.refs_2_.refs_1_, bf16[4,512,128]{2,1,0:T(8,128)(2,1)S(1)} %collective-permute-done.11.refs_3_, ...), custom_call_target="tpu_custom_call" | custom-call | flops 5000000000 | bytes 1048576 | tf_op jit(solution)/shard_map/near1/pallas_call | solution.py:250
  102.8 2.1 %far1.1.refs_2_ = bf16[512,512]{1,0:T(8,128)(2,1)S(1)} custom-call(s32[5]{0:T(128)S(1)} %stack.30.place_ref.refs_0_, s32[4,32]{1,0:T(4,128)S(1)} %get-tuple-element.38.refs_1_, bf16[4,512,128]{2,1,0:T(8,128)(2,1)S(1)} %collective-permute-done.10.refs_2_, bf16[8,128,512]{2,1,0:T(8,128)(2,1)S(1)} %bitcast.13, f32[2,2,512]{2,1,0:T(2,128)S(1)} %copy-done.2, ...), custom_call_target="tpu_custom_call" | custom-call | flops 3000000000 | bytes 1048576 | tf_op jit(solution)/shard_map/far1/pallas_call | solution.py:250
  104.9 2.0 %collective-permute-start.13 = (bf16[512,512]{1,0:T(8,128)(2,1)S(1)}, bf16[512,512]{1,0:T(8,128)(2,1)S(1)}, u32[]{:S(2)}, u32[]{:S(2)}) collective-permute-start(bf16[512,512]{1,0:T(8,128)(2,1)S(1)} %far1.1.refs_2_), channel_id=1, source_target_pairs={{0,1},{1,0},{2,3},{3,2},{4,5},{5,4},{6,7},{7,6},{8,9},{9,8},{10,11... | collective-permute-start | bytes 1572872 | tf_op jit(solution)/shard_map/ppermute | solution.py:31
  106.9 1.8 %collective-permute-done.13.refs_3_ = bf16[512,512]{1,0:T(8,128)(2,1)S(1)} collective-permute-done((bf16[512,512]{1,0:T(8,128)(2,1)S(1)}, bf16[512,512]{1,0:T(8,128)(2,1)S(1)}, u32[]{:S(2)}, u32[]{:S(2)}) %collective-permute-start.13) | collective-permute-done | bytes 524320 | tf_op jit(solution)/shard_map/ppermute | solution.py:31
  108.7 1.8 %node1.1 = (bf16[512,128]{1,0:T(8,128)(2,1)S(1)}, bf16[512,128]{1,0:T(8,128)(2,1)S(1)}) custom-call(s32[5]{0:T(128)S(1)} %stack.30.place_ref.refs_0_, bf16[4,512,128]{2,1,0:T(8,128)(2,1)S(1)} %node0.1.refs_2_.refs_1_, bf16[512,512]{1,0:T(8,128)(2,1)S(1)} %far1.1.refs_2_, bf16[512,512]{1,0:T(8,128)(2,1)S(1)} %collective-permute-done.13.refs_3_, ...), custom_call_target="tpu_custom_call" | custom-call | flops 2000000000 | bytes 1048576 | tf_op jit(solution)/shard_map/node1/pallas_call | solution.py:250
  110.5 2.3 %collective-permute-start.14 = (bf16[512,128]{1,0:T(8,128)(2,1)S(1)}, bf16[512,128]{1,0:T(8,128)(2,1)S(1)}, u32[]{:S(2)}, u32[]{:S(2)}) collective-permute-start(bf16[512,128]{1,0:T(8,128)(2,1)S(1)} %get-tuple-element.58), channel_id=1, source_target_pairs={{0,2},{1,3},{2,0},{3,1},{4,6},{5,7},{6,4},{7,5},{8,10},{9,11},{10,... | collective-permute-start | bytes 393224 | tf_op jit(solution)/shard_map/ppermute | solution.py:31
  112.8 5.1 %collective-permute-done.14.other_ref = bf16[512,128]{1,0:T(8,128)(2,1)S(1)} collective-permute-done((bf16[512,128]{1,0:T(8,128)(2,1)S(1)}, bf16[512,128]{1,0:T(8,128)(2,1)S(1)}, u32[]{:S(2)}, u32[]{:S(2)}) %collective-permute-start.14) | collective-permute-done | bytes 131104 | tf_op jit(solution)/shard_map/ppermute | solution.py:31
  117.9 1.3 %join.1 = bf16[1024,128]{1,0:T(8,128)(2,1)} custom-call(s32[5]{0:T(128)S(1)} %stack.30.place_ref.refs_0_, bf16[512,128]{1,0:T(8,128)(2,1)S(1)} %get-tuple-element.57.own_ref, bf16[512,128]{1,0:T(8,128)(2,1)S(1)} %collective-permute-done.14.other_ref), custom_call_target="tpu_custom_call" | custom-call | flops 2000000000 | bytes 1048576 | tf_op jit(solution)/shard_map/join/pallas_call | solution.py:250
  (34 shorter events, 0.2 us)
Async XLA Ops:
  0.0 20.1 %copy-start.7 = (bf16[1024,128]{1,0:T(8,128)(2,1)S(1)}, bf16[1024,128]{1,0:T(8,128)(2,1)}, u32[]{:S(2)}) copy-start(bf16[1024,128]{1,0:T(8,128)(2,1)} %param.14) | copy-start | bytes 786436
  0.0 22.0 %copy-start.8 = (s32[8,6,128]{2,0,1:T(8,128)S(1)}, s32[8,6,128]{2,0,1:T(8,128)}, u32[]{:S(2)}) copy-start(s32[8,6,128]{2,0,1:T(8,128)} %param.26) | copy-start | bytes 73732
  0.0 22.1 %copy-start.9 = (s32[8,6,128]{2,0,1:T(8,128)S(1)}, s32[8,6,128]{2,0,1:T(8,128)}, u32[]{:S(2)}) copy-start(s32[8,6,128]{2,0,1:T(8,128)} %param.27) | copy-start | bytes 73732
  0.0 22.2 %copy-start.6 = (s32[8,6]{1,0:T(8,128)S(1)}, s32[8,6]{1,0:T(8,128)}, u32[]{:S(2)}) copy-start(s32[8,6]{1,0:T(8,128)} %count_ref.1) | copy-start | bytes 580
  0.0 22.2 %copy-start.5 = (s32[8,6]{1,0:T(8,128)S(1)}, s32[8,6]{1,0:T(8,128)}, u32[]{:S(2)}) copy-start(s32[8,6]{1,0:T(8,128)} %nbr_ref.1) | copy-start | bytes 580
  2.5 6.2 %collective-permute-start.2 = (bf16[2624,128]{1,0:T(8,128)(2,1)}, bf16[2624,128]{1,0:T(8,128)(2,1)S(1)}, u32[]{:S(2)}, u32[]{:S(2)}) collective-permute-start(bf16[2624,128]{1,0:T(8,128)(2,1)} %get-tuple-element.32.refs_8_.refs_12_.refs_16_.refs_9_), channel_id=1, source_target_pairs={{0,1},{1,0},{2,3},{3,2},{4,5},{5,4},{6,7},{7,6},{8,9},{9,8},{10,11... | collective-permute-start | bytes 2015240 | tf_op jit(solution)/shard_map/ppermute | solution.py:31
  4.5 23.1 %collective-permute-start.1 = (bf16[2624,128]{1,0:T(8,128)(2,1)}, bf16[2624,128]{1,0:T(8,128)(2,1)S(1)}, u32[]{:S(2)}, u32[]{:S(2)}) collective-permute-start(bf16[2624,128]{1,0:T(8,128)(2,1)} %get-tuple-element.32.refs_8_.refs_12_.refs_16_.refs_9_), channel_id=1, source_target_pairs={{0,2},{1,3},{2,0},{3,1},{4,6},{5,7},{6,4},{7,5},{8,10},{9,11},{10,... | collective-permute-start | bytes 2015240 | tf_op jit(solution)/shard_map/ppermute | solution.py:31
  8.8 18.8 %collective-permute-start.4 = (bf16[2560,128]{1,0:T(8,128)(2,1)}, bf16[2560,128]{1,0:T(8,128)(2,1)S(1)}, u32[]{:S(2)}, u32[]{:S(2)}) collective-permute-start(bf16[2560,128]{1,0:T(8,128)(2,1)} %get-tuple-element.34.refs_8_.refs_12_.refs_9_.refs_16_), channel_id=1, source_target_pairs={{0,1},{1,0},{2,3},{3,2},{4,5},{5,4},{6,7},{7,6},{8,9},{9,8},{10,11... | collective-permute-start | bytes 1966088 | tf_op jit(solution)/shard_map/ppermute | solution.py:31
  10.9 24.5 %collective-permute-start.3 = (bf16[2560,128]{1,0:T(8,128)(2,1)}, bf16[2560,128]{1,0:T(8,128)(2,1)S(1)}, u32[]{:S(2)}, u32[]{:S(2)}) collective-permute-start(bf16[2560,128]{1,0:T(8,128)(2,1)} %get-tuple-element.34.refs_8_.refs_12_.refs_9_.refs_16_), channel_id=1, source_target_pairs={{0,14},{1,15},{2,4},{3,5},{4,2},{5,3},{6,8},{7,9},{8,6},{9,7},{10,... | collective-permute-start | bytes 1966088 | tf_op jit(solution)/shard_map/ppermute | solution.py:49
  20.1 7.4 %collective-permute-start = (bf16[512,128]{1,0:T(8,128)(2,1)S(1)}, bf16[512,128]{1,0:T(8,128)(2,1)S(1)}, u32[]{:S(2)}, u32[]{:S(2)}) collective-permute-start(bf16[512,128]{1,0:T(8,128)(2,1)S(1)} %get-tuple-element.60), channel_id=1, source_target_pairs={{0,2},{1,3},{2,0},{3,1},{4,6},{5,7},{6,4},{7,5},{8,10},{9,11},{10,... | collective-permute-start | bytes 393224 | tf_op jit(solution)/shard_map/ppermute | solution.py:31
  22.2 40.5 %copy-start = (bf16[2624,128]{1,0:T(8,128)(2,1)S(1)}, bf16[2624,128]{1,0:T(8,128)(2,1)}, u32[]{:S(2)}) copy-start(bf16[2624,128]{1,0:T(8,128)(2,1)} %get-tuple-element.32.refs_8_.refs_12_.refs_16_.refs_9_) | copy-start | bytes 2015236
  22.2 40.5 %copy-start.2 = (f32[2,2,512]{2,1,0:T(2,128)S(1)}, f32[2,2,512]{2,1,0:T(2,128)}, u32[]{:S(2)}) copy-start(f32[2,2,512]{2,1,0:T(2,128)} %refs_6_.3) | copy-start | bytes 24580
  22.2 40.5 %copy-start.4 = (bf16[2,512,512]{2,1,0:T(8,128)(2,1)S(1)}, bf16[2,512,512]{2,1,0:T(8,128)(2,1)}, u32[]{:S(2)}) copy-start(bf16[2,512,512]{2,1,0:T(8,128)(2,1)} %param.17) | copy-start | bytes 3145732
  35.4 3.4 %collective-permute-start.5 = (bf16[2,512,128]{2,1,0:T(8,128)(2,1)S(1)}, bf16[2,512,128]{2,1,0:T(8,128)(2,1)S(1)}, u32[]{:S(2)}, u32[]{:S(2)}) collective-permute-start(bf16[2,512,128]{2,1,0:T(8,128)(2,1)S(1)} %pad_maximum_fusion), channel_id=1, source_target_pairs={{0,1},{1,0},{2,3},{3,2},{4,5},{5,4},{6,7},{7,6},{8,9},{9,8},{10,11... | collective-permute-start | bytes 786440 | tf_op jit(solution)/shard_map/ppermute | solution.py:31
  38.9 23.8 %collective-permute-start.8 = (bf16[2624,128]{1,0:T(8,128)(2,1)S(1)}, bf16[2624,128]{1,0:T(8,128)(2,1)S(1)}, u32[]{:S(2)}, u32[]{:S(2)}) collective-permute-start(bf16[2624,128]{1,0:T(8,128)(2,1)S(1)} %collective-permute-done.1.refs_10_.refs_14_.refs_18_.refs_11_), channel_id=1, source_target_pairs={{0,1},{1,0},{2,3},{3,2},{4,5},{5,4},{6,7},{7,6},{8,9},{9,8},{10,11... | collective-permute-start | bytes 2015240 | tf_op jit(solution)/shard_map/ppermute | solution.py:31
  40.9 21.7 %collective-permute-start.7 = (bf16[4,512,128]{2,1,0:T(8,128)(2,1)S(1)}, bf16[4,512,128]{2,1,0:T(8,128)(2,1)S(1)}, u32[]{:S(2)}, u32[]{:S(2)}) collective-permute-start(bf16[4,512,128]{2,1,0:T(8,128)(2,1)S(1)} %constant_dynamic-update-slice_fusion.refs_2_.refs_1_), channel_id=1, source_target_pairs={{0,3},{2,5},{3,0},{4,7},{5,2},{6,9},{7,4},{8,11},{9,6},{10,13},{11... | collective-permute-start | bytes 1572872 | tf_op jit(solution)/shard_map/ppermute | solution.py:38
  42.9 24.5 %collective-permute-start.6 = (bf16[4,512,128]{2,1,0:T(8,128)(2,1)S(1)}, bf16[4,512,128]{2,1,0:T(8,128)(2,1)S(1)}, u32[]{:S(2)}, u32[]{:S(2)}) collective-permute-start(bf16[4,512,128]{2,1,0:T(8,128)(2,1)S(1)} %constant_dynamic-update-slice_fusion.refs_2_.refs_1_), channel_id=1, source_target_pairs={{0,5},{2,7},{4,9},{5,0},{6,11},{7,2},{8,13},{9,4},{10,15},{11,6},{... | collective-permute-start | bytes 1572872 | tf_op jit(solution)/shard_map/ppermute | solution.py:38
  67.3 7.2 %copy-start.3 = (f32[2,512]{1,0:T(2,128)S(1)}, f32[2,512]{1,0:T(2,128)}, u32[]{:S(2)}) copy-start(f32[2,512]{1,0:T(2,128)} %refs_7_.3) | copy-start | bytes 12292
  69.4 5.1 %collective-permute-start.9 = (bf16[512,512]{1,0:T(8,128)(2,1)S(1)}, bf16[512,512]{1,0:T(8,128)(2,1)S(1)}, u32[]{:S(2)}, u32[]{:S(2)}) collective-permute-start(bf16[512,512]{1,0:T(8,128)(2,1)S(1)} %far0.1.refs_2_), channel_id=1, source_target_pairs={{0,1},{1,0},{2,3},{3,2},{4,5},{5,4},{6,7},{7,6},{8,9},{9,8},{10,11... | collective-permute-start | bytes 1572872 | tf_op jit(solution)/shard_map/ppermute | solution.py:31
  72.6 7.7 %collective-permute-start.12 = (bf16[2560,128]{1,0:T(8,128)(2,1)S(1)}, bf16[2560,128]{1,0:T(8,128)(2,1)S(1)}, u32[]{:S(2)}, u32[]{:S(2)}) collective-permute-start(bf16[2560,128]{1,0:T(8,128)(2,1)S(1)} %collective-permute-done.3.refs_10_.refs_14_.refs_11_.refs_18_), channel_id=1, source_target_pairs={{0,1},{1,0},{2,3},{3,2},{4,5},{5,4},{6,7},{7,6},{8,9},{9,8},{10,11... | collective-permute-start | bytes 1966088 | tf_op jit(solution)/shard_map/ppermute | solution.py:31
  74.5 23.7 %copy-start.1 = (bf16[2560,128]{1,0:T(8,128)(2,1)S(1)}, bf16[2560,128]{1,0:T(8,128)(2,1)}, u32[]{:S(2)}) copy-start(bf16[2560,128]{1,0:T(8,128)(2,1)} %get-tuple-element.34.refs_8_.refs_12_.refs_9_.refs_16_) | copy-start | bytes 1966084
  76.4 21.7 %collective-permute-start.11 = (bf16[4,512,128]{2,1,0:T(8,128)(2,1)S(1)}, bf16[4,512,128]{2,1,0:T(8,128)(2,1)S(1)}, u32[]{:S(2)}, u32[]{:S(2)}) collective-permute-start(bf16[4,512,128]{2,1,0:T(8,128)(2,1)S(1)} %node0.1.refs_2_.refs_1_), channel_id=1, source_target_pairs={{0,3},{2,5},{3,0},{4,7},{5,2},{6,9},{7,4},{8,11},{9,6},{10,13},{11... | collective-permute-start | bytes 1572872 | tf_op jit(solution)/shard_map/ppermute | solution.py:38
  78.4 24.4 %collective-permute-start.10 = (bf16[4,512,128]{2,1,0:T(8,128)(2,1)S(1)}, bf16[4,512,128]{2,1,0:T(8,128)(2,1)S(1)}, u32[]{:S(2)}, u32[]{:S(2)}) collective-permute-start(bf16[4,512,128]{2,1,0:T(8,128)(2,1)S(1)} %node0.1.refs_2_.refs_1_), channel_id=1, source_target_pairs={{0,5},{2,7},{4,9},{5,0},{6,11},{7,2},{8,13},{9,4},{10,15},{11,6},{... | collective-permute-start | bytes 1572872 | tf_op jit(solution)/shard_map/ppermute | solution.py:38
  104.9 3.8 %collective-permute-start.13 = (bf16[512,512]{1,0:T(8,128)(2,1)S(1)}, bf16[512,512]{1,0:T(8,128)(2,1)S(1)}, u32[]{:S(2)}, u32[]{:S(2)}) collective-permute-start(bf16[512,512]{1,0:T(8,128)(2,1)S(1)} %far1.1.refs_2_), channel_id=1, source_target_pairs={{0,1},{1,0},{2,3},{3,2},{4,5},{5,4},{6,7},{7,6},{8,9},{9,8},{10,11... | collective-permute-start | bytes 1572872 | tf_op jit(solution)/shard_map/ppermute | solution.py:31
  110.5 7.4 %collective-permute-start.14 = (bf16[512,128]{1,0:T(8,128)(2,1)S(1)}, bf16[512,128]{1,0:T(8,128)(2,1)S(1)}, u32[]{:S(2)}, u32[]{:S(2)}) collective-permute-start(bf16[512,128]{1,0:T(8,128)(2,1)S(1)} %get-tuple-element.58), channel_id=1, source_target_pairs={{0,2},{1,3},{2,0},{3,1},{4,6},{5,7},{6,4},{7,5},{8,10},{9,11},{10,... | collective-permute-start | bytes 393224 | tf_op jit(solution)/shard_map/ppermute | solution.py:31

commit v8 on v7

--- a/solution.py
+++ b/solution.py
@@ -102,19 +102,26 @@
     collect_ref[last - 1] = jnp.zeros(collect_ref.shape[1:], BF16)
 
 
-def pack_kernel(src_ref, dst_ref, in_ref, out_w_ref, vec_ref, gain_ref, first_ref, next_ref, rows, sems):
+def pack_kernel(src_ref, dst_ref, in_ref, out_w_ref, vec_ref, gain_ref, *refs):
+    outs, (rows, sems) = refs[:6], refs[6:]
     width = src_ref.shape[1]
     copies = []
-    for layer, ref in enumerate((first_ref, next_ref)):
-        for source, at in ((in_ref, 0), (out_w_ref, 2), (src_ref, 3), (dst_ref, 4)):
-            count = source.shape[1]
-            copies.append(
-                pltpu.make_async_copy(
-                    source.at[layer], ref.at[pl.ds(at * width, count), :], sems.at[len(copies)]
-                )
-            )
-    for copy in copies:
-        copy.start()
+
+    def copy(source, ref, at):
+        copies.append(
+            pltpu.make_async_copy(source, ref.at[pl.ds(at, source.shape[0]), :], sems.at[len(copies)])
+        )
+        copies[-1].start()
+
+    for layer in range(LAYERS):
+        pack, edge, node = outs[3 * layer : 3 * layer + 3]
+        copy(src_ref.at[layer], edge, 0)
+        copy(dst_ref.at[layer], edge, width)
+        copy(src_ref.at[layer], pack, 3 * width)
+        copy(dst_ref.at[layer], pack, 4 * width)
+        for ref in (pack, node):
+            copy(in_ref.at[layer], ref, 0)
+            copy(out_w_ref.at[layer], ref, 2 * width)
     rest = jnp.concatenate(
         [part for layer in range(LAYERS) for part in (vec_ref[layer], gain_ref[layer : layer + 1, :])]
         + [jnp.zeros((VECTOR_ROWS - 5 * LAYERS, src_ref.shape[2]), F32)],
@@ -125,13 +132,10 @@
         rows[i * VECTOR_ROWS : (i + 1) * VECTOR_ROWS, :] = piece
         rest = rest - piece.astype(F32)
     rows[3 * VECTOR_ROWS :, :] = jnp.zeros((VECTOR_ROWS, src_ref.shape[2]), BF16)
-    last = pltpu.make_async_copy(
-        rows, first_ref.at[pl.ds(5 * width, 4 * VECTOR_ROWS), :], sems.at[len(copies)]
-    )
-    last.start()
-    for copy in copies:
-        copy.wait()
-    last.wait()
+    copy(rows, outs[0], 5 * width)
+    copy(rows, outs[1], 2 * width)
+    for each in copies:
+        each.wait()
 
 
 def wide(ref, order=STRAIGHT):
@@ -242,8 +246,23 @@
     out_ref[pl.ds(pl.multiple_of((1 - side) * rows, rows), rows), :] = other_ref[...]
 
 
-def rows_of(weights, at, count):
-    return weights, [pl.BlockSpec((count, w.shape[-1]), lambda i: (at, 0)) for w in weights]
+def rows_of(weights, matrix, width):
+    inputs, specs = [], []
+    for w in weights:
+        at = matrix
+        if isinstance(w, tuple):
+            w, at = (w[0], matrix - 3) if matrix > 2 else (w[1], matrix)
+        inputs.append(w)
+        specs.append(pl.BlockSpec((width, w.shape[-1]), lambda i, at=at: (at, 0)))
+    return inputs, specs
+
+
+def vectors_of(weights):
+    count = 4 * VECTOR_ROWS
+    inputs = [w[0] if isinstance(w, tuple) else w for w in weights]
+    return inputs, [
+        pl.BlockSpec((count, w.shape[-1]), lambda i, at=w.shape[0] // count - 1: (at, 0)) for w in inputs
+    ]
 
 
 def call(kernel, name, inputs, spaces, outs, out_spaces, scratch=(), us=2, mib=32):
@@ -291,24 +310,26 @@
     halves = node_state.reshape(2, rows, part)
     own = lax.dynamic_index_in_dim(halves, side, 0, keepdims=False)
     other = lax.dynamic_index_in_dim(halves, 1 - side, 0, keepdims=False)
-    pack, next_pack = call(
+    extra_rows = 4 * VECTOR_ROWS
+    pack, edge, node, next_pack, next_edge, next_node = call(
         pack_kernel,
         "packs",
         (w_src, w_dst, w_node_in, w_node_out, node_vectors, node_gain),
         [VMEM] * 6,
-        (
-            jax.ShapeDtypeStruct((5 * width + 4 * VECTOR_ROWS, part), BF16),
-            jax.ShapeDtypeStruct((5 * width, part), BF16),
-        ),
-        (HBM, HBM),
-        [pltpu.VMEM((4 * VECTOR_ROWS, part), BF16), pltpu.SemaphoreType.DMA((9,))],
+        [
+            jax.ShapeDtypeStruct((count, part), BF16)
+            for count in (
+                5 * width + extra_rows, 2 * width + extra_rows, 3 * width, 5 * width, 2 * width, 3 * width,
+            )
+        ],
+        [HBM] * 6,
+        [pltpu.VMEM((extra_rows, part), BF16), pltpu.SemaphoreType.DMA((18,))],
         mib=60,
     )
     across = exchange(other, 2)
-    pack_across = exchange(pack, 2)
+    edge_across = exchange(edge, 2)
     beside = exchange(pack, 1)
     next_share, beside = barrier((next_pack, beside))
-    next_across = from_other_side(next_share)
     next_beside = exchange(next_share, 1)
 
     all_slots = mine * slots + 1
@@ -328,12 +349,12 @@
         us=3,
     )
     pair = jnp.stack([own, across])
-    pair, pack_across, next_across, beside, next_beside, meta = barrier(
-        (pair, pack_across, next_across, beside, next_beside, meta)
-    )
+    pair, edge_across, beside, next_beside, meta = barrier((pair, edge_across, beside, next_beside, meta))
     latent = jnp.concatenate([pair, exchange(pair, 1)], axis=0)
-    pack_across = barrier((pack_across, latent))[0]
-    weights = (pack, beside, pack_across, exchange(pack_across, 1))
+    edge_across, node_share = barrier((edge_across, node, latent))[:2]
+    edge_beyond = exchange(edge_across, 1)
+    node_across = from_other_side(node_share)
+    weights = (pack, beside, (edge_across, None), (edge_beyond, None))
 
     vectors = None
     messages = w_msg.reshape(LAYERS * 4, part, width)
@@ -349,7 +370,7 @@
         outs = [jax.ShapeDtypeStruct((rows, width), F32), jax.ShapeDtypeStruct((rows, width), BF16)]
         if layer == 0:
             outs.append(jax.ShapeDtypeStruct((4, VECTOR_ROWS, part), F32))
-            extra, extra_specs = rows_of(weights, 5 * width // (4 * VECTOR_ROWS), 4 * VECTOR_ROWS)
+            extra, extra_specs = vectors_of(weights)
         else:
             extra, extra_specs = (vectors,), [VMEM]
         result = call(
@@ -369,8 +390,17 @@
         acc, receive = result[0], result[1]
         if layer == 0:
             vectors = result[2]
-            next_across = barrier((next_across, acc))[0]
-            next_weights = (next_pack, next_beside, next_across, exchange(next_across, 1))
+            node_across, next_edge, next_node, acc = barrier((node_across, next_edge, next_node, acc))
+            next_edge = exchange(next_edge, 2)
+            next_node = from_other_side(next_node)
+            node_beyond = exchange(node_across, 1)
+            beyond, node_beyond = barrier((beyond, node_beyond))
+            weights = (pack, beside, (edge_across, node_across), (edge_beyond, node_beyond))
+        else:
+            next_node, acc = barrier((next_node, acc))
+            node_beyond = exchange(next_node, 1)
+            beyond, node_beyond = barrier((beyond, node_beyond))
+            weights = (next_pack, next_beside, (next_edge, next_node), (edge_beyond, node_beyond))
         beyond, acc = barrier((beyond, acc))
         partial = call(
             lambda *refs, layer=layer: far_kernel(layer, *refs),
@@ -387,7 +417,12 @@
             ],
             us=3,
         )
+        if layer == 0:
+            next_edge, next_node, partial = barrier((next_edge, next_node, partial))
+            edge_beyond = exchange(next_edge, 1)
         theirs = exchange(partial, 1)
+        if layer == 0:
+            theirs, edge_beyond = barrier((theirs, edge_beyond))
         if final:
             outs = [jax.ShapeDtypeStruct((rows, part), BF16)] * 2
         else:
@@ -411,7 +446,7 @@
                 VMEM,
             )
         latent = result[0]
-        weights = next_weights
+        weights = (next_pack, next_beside, (next_edge, None), (edge_beyond, None))
 
 
 def solution(mesh):

time: 120 us -> 134 us (1.12)
  starting transfers between devices: 40.4 us -> 64.5 us
  waiting for transfers between devices: 55.1 us -> 44.9 us
    ppermute x4, waiting for transfers between devices: 35.8 us -> 7.42 us  [swap_with(): lax.ppermute(value, BOTH, [(i, t) for i, t in pairs if 0 <= t < total])]
    ppermute x10 -> x13, starting transfers between devices: 23.6 us -> 47.2 us  [exchange(): return lax.ppermute(value, BOTH, [(i, i ^ mask) for i in range(total)])]
    ppermute x10 -> x13, waiting for transfers between devices: 11.4 us -> 24.6 us  [exchange(): return lax.ppermute(value, BOTH, [(i, i ^ mask) for i in range(total)])]
    ppermute x1 -> x2, waiting for transfers between devices: 7.86 us -> 12.8 us  [from_other_side(): return lax.ppermute(value, BOTH, pairs)]
    ppermute x4, starting transfers between devices: 7.68 us -> 9.82 us  [swap_with(): lax.ppermute(value, BOTH, [(i, t) for i, t in pairs if 0 <= t < total])]
    ppermute x1 -> x2, starting transfers between devices: 9.13 us -> 7.46 us  [from_other_side(): return lax.ppermute(value, BOTH, pairs)]
  transfers between devices with their start and end apart: 15 -> 19, of which waited for: 7 -> 10; matrix products, arithmetic and copies ran while one was open for 0% -> 0% of each run, Pallas kernels for 11% -> 10%
where the time goes in v8:
time: 134 us
  starting transfers between devices  64.5 us (48%)
  waiting for transfers between devices  44.9 us (34%)
  Pallas kernels  23.6 us (18%)
    ppermute x13, starting transfers between devices, exchange(): return lax.ppermute(value, BOTH, [(i, i ^ mask) for i in range(total)])  47.2 us
    ppermute x13, waiting for transfers between devices, exchange(): return lax.ppermute(value, BOTH, [(i, i ^ mask) for i in range(total)])  24.6 us
    pallas_call x9, Pallas kernels, call(): pl.pallas_call(kernel, out_shape=outs, grid=(1,), in_specs=spaces, out_sp...  23.6 us
    ppermute x2, waiting for transfers between devices, from_other_side(): return lax.ppermute(value, BOTH, pairs)  12.8 us
    ppermute x4, starting transfers between devices, swap_with(): lax.ppermute(value, BOTH, [(i, t) for i, t in pairs if 0 <= t < total])  9.82 us
    ppermute x2, starting transfers between devices, from_other_side(): return lax.ppermute(value, BOTH, pairs)  7.46 us
    ppermute x4, waiting for transfers between devices, swap_with(): lax.ppermute(value, BOTH, [(i, t) for i, t in pairs if 0 <= t < total])  7.42 us
  transfers between devices with their start and end apart: 19, of which 10 were waited for; matrix products, arithmetic and copies ran while one was open for 0% of the time, Pallas kernels for 10%

profile of v8, /device:TPU:6, one launch (start us, length us, event | category | flops | bytes accessed | tf_op | source)
XLA Modules:
  0.0 133.7 jit_solution(8654961320395018721)
XLA Ops:
  0.0 2.9 %packs.1 = (bf16[2624,128]{1,0:T(8,128)(2,1)}, bf16[1088,128]{1,0:T(8,128)(2,1)}, bf16[1536,128]{1,0:T(8,128)(2,1)}, bf16[2560,128]{1,0:T(8,128)(2,1)}, bf16[102...) custom-call(bf16[2,512,128]{2,1,0:T(8,128)(2,1)} %src_ref.2, bf16[2,512,128]{2,1,0:T(8,128)(2,1)} %dst_ref.2, ...), custom_call_target="tpu_custom_call" | custom-call | flops 2000000000 | bytes 1048576 | tf_op jit(solution)/shard_map/packs/pallas_call | solution.py:269
  3.0 1.9 %collective-permute-start.2 = (bf16[2624,128]{1,0:T(8,128)(2,1)}, bf16[2624,128]{1,0:T(8,128)(2,1)S(1)}, u32[]{:S(2)}, u32[]{:S(2)}) collective-permute-start(bf16[2624,128]{1,0:T(8,128)(2,1)} %get-tuple-element.52.refs_8_.refs_12_.refs_16_.refs_9_), channel_id=1, source_target_pairs={{0,1},{1,0},{2,3},{3,2},{4,5},{5,4},{6,7},{7,6},{8,9},{9,8},{10,11... | collective-permute-start | bytes 2015240 | tf_op jit(solution)/shard_map/ppermute | solution.py:31
  4.9 2.3 %collective-permute-done.2.refs_9_.refs_13_.refs_17_.refs_10_ = bf16[2624,128]{1,0:T(8,128)(2,1)S(1)} collective-permute-done((bf16[2624,128]{1,0:T(8,128)(2,1)}, bf16[2624,128]{1,0:T(8,128)(2,1)S(1)}, u32[]{:S(2)}, u32[]{:S(2)}) %collective-permute-start.2) | collective-permute-done | bytes 671776 | tf_op jit(solution)/shard_map/ppermute | solution.py:31
  7.2 2.0 %collective-permute-start.3 = (bf16[2560,128]{1,0:T(8,128)(2,1)}, bf16[2560,128]{1,0:T(8,128)(2,1)S(1)}, u32[]{:S(2)}, u32[]{:S(2)}) collective-permute-start(bf16[2560,128]{1,0:T(8,128)(2,1)} %get-tuple-element.54.refs_8_.refs_12_.refs_9_.refs_16_), channel_id=1, source_target_pairs={{0,1},{1,0},{2,3},{3,2},{4,5},{5,4},{6,7},{7,6},{8,9},{9,8},{10,11... | collective-permute-start | bytes 1966088 | tf_op jit(solution)/shard_map/ppermute | solution.py:31
  9.3 4.3 %collective-permute-start = (bf16[512,128]{1,0:T(8,128)(2,1)S(1)}, bf16[512,128]{1,0:T(8,128)(2,1)S(1)}, u32[]{:S(2)}, u32[]{:S(2)}) collective-permute-start(bf16[512,128]{1,0:T(8,128)(2,1)S(1)} %get-tuple-element.96), channel_id=1, source_target_pairs={{0,2},{1,3},{2,0},{3,1},{4,6},{5,7},{6,4},{7,5},{8,10},{9,11},{10,... | collective-permute-start | bytes 393224 | tf_op jit(solution)/shard_map/ppermute | solution.py:31
  13.6 1.9 %collective-permute-start.1 = (bf16[1088,128]{1,0:T(8,128)(2,1)}, bf16[1088,128]{1,0:T(8,128)(2,1)S(1)}, u32[]{:S(2)}, u32[]{:S(2)}) collective-permute-start(bf16[1088,128]{1,0:T(8,128)(2,1)} %get-tuple-element.50), channel_id=1, source_target_pairs={{0,2},{1,3},{2,0},{3,1},{4,6},{5,7},{6,4},{7,5},{8,10},{9,11},{10,... | collective-permute-start | bytes 835592 | tf_op jit(solution)/shard_map/ppermute | solution.py:31
  15.8 2.2 %one_hots.1 = (bf16[25,128,256]{2,1,0:T(8,128)(2,1)S(1)}, bf16[25,128,128]{2,1,0:T(8,128)(2,1)S(1)}, f32[512,128]{1,0:T(8,128)S(1)}, s32[4,32]{1,0:T(4,128)S(1)}) custom-call(s32[5]{0:T(128)S(1)} %stack.30.place_ref.refs_0_, s32[8,6]{1,0:T(8,128)S(1)} %copy-done.5, s32[8,6]{1,0:T(8,128)S(1)} %copy-done.6, s32[8,6,128]{2,1,0:T(8,128)S(1)} %copy.15.src_ref, ...), custom_call_target="tpu_custom_call" | custom-call | flops 3000000000 | bytes 1048576 | tf_op jit(solution)/shard_map/one_hots/pallas_call | solution.py:269
  18.0 6.3 %collective-permute-done.1.refs_10_.refs_14_.refs_18_.refs_11_ = bf16[1088,128]{1,0:T(8,128)(2,1)S(1)} collective-permute-done((bf16[1088,128]{1,0:T(8,128)(2,1)}, bf16[1088,128]{1,0:T(8,128)(2,1)S(1)}, u32[]{:S(2)}, u32[]{:S(2)}) %collective-permute-start.1) | collective-permute-done | bytes 278560 | tf_op jit(solution)/shard_map/ppermute | solution.py:31
  24.4 1.9 %collective-permute-start.4 = (bf16[2,512,128]{2,1,0:T(8,128)(2,1)S(1)}, bf16[2,512,128]{2,1,0:T(8,128)(2,1)S(1)}, u32[]{:S(2)}, u32[]{:S(2)}) collective-permute-start(bf16[2,512,128]{2,1,0:T(8,128)(2,1)S(1)} %pad_maximum_fusion), channel_id=1, source_target_pairs={{0,1},{1,0},{2,3},{3,2},{4,5},{5,4},{6,7},{7,6},{8,9},{9,8},{10,11... | collective-permute-start | bytes 786440 | tf_op jit(solution)/shard_map/ppermute | solution.py:31
  27.8 2.6 %collective-permute-start.6 = (bf16[4,512,128]{2,1,0:T(8,128)(2,1)S(1)}, bf16[4,512,128]{2,1,0:T(8,128)(2,1)S(1)}, u32[]{:S(2)}, u32[]{:S(2)}) collective-permute-start(bf16[4,512,128]{2,1,0:T(8,128)(2,1)S(1)} %constant_dynamic-update-slice_fusion.refs_2_.refs_1_), channel_id=1, source_target_pairs={{0,3},{2,5},{3,0},{4,7},{5,2},{6,9},{7,4},{8,11},{9,6},{10,13},{11... | collective-permute-start | bytes 1572872 | tf_op jit(solution)/shard_map/ppermute | solution.py:38
  30.4 12.1 %collective-permute-start.7 = (bf16[1088,128]{1,0:T(8,128)(2,1)S(1)}, bf16[1088,128]{1,0:T(8,128)(2,1)S(1)}, u32[]{:S(2)}, u32[]{:S(2)}) collective-permute-start(bf16[1088,128]{1,0:T(8,128)(2,1)S(1)} %collective-permute-done.1.refs_10_.refs_14_.refs_18_.refs_11_), channel_id=1, source_target_pairs={{0,1},{1,0},{2,3},{3,2},{4,5},{5,4},{6,7},{7,6},{8,9},{9,8},{10,11... | collective-permute-start | bytes 835592 | tf_op jit(solution)/shard_map/ppermute | solution.py:31
  42.6 1.9 %collective-permute-start.10 = (bf16[4,512,128]{2,1,0:T(8,128)(2,1)S(1)}, bf16[4,512,128]{2,1,0:T(8,128)(2,1)S(1)}, u32[]{:S(2)}, u32[]{:S(2)}) collective-permute-start(bf16[4,512,128]{2,1,0:T(8,128)(2,1)S(1)} %constant_dynamic-update-slice_fusion.refs_2_.refs_1_), channel_id=1, source_target_pairs={{0,5},{2,7},{4,9},{5,0},{6,11},{7,2},{8,13},{9,4},{10,15},{11,6},{... | collective-permute-start | bytes 1572872 | tf_op jit(solution)/shard_map/ppermute | solution.py:38
  44.5 1.9 %collective-permute-start.5 = (bf16[1536,128]{1,0:T(8,128)(2,1)S(1)}, bf16[1536,128]{1,0:T(8,128)(2,1)S(1)}, u32[]{:S(2)}, u32[]{:S(2)}) collective-permute-start(bf16[1536,128]{1,0:T(8,128)(2,1)S(1)} %copy-done.11), channel_id=1, source_target_pairs={{0,14},{1,15},{2,4},{3,5},{4,2},{5,3},{6,8},{7,9},{8,6},{9,7},{10,... | collective-permute-start | bytes 1179656 | tf_op jit(solution)/shard_map/ppermute | solution.py:49
  46.5 4.6 %near0.1 = (f32[512,512]{1,0:T(8,128)S(1)}, bf16[512,512]{1,0:T(8,128)(2,1)S(1)}, f32[4,16,128]{2,1,0:T(8,128)S(1)}) custom-call(s32[5]{0:T(128)S(1)} %stack.30.place_ref.refs_0_, s32[4,32]{1,0:T(4,128)S(1)} %get-tuple-element.62.refs_1_, bf16[4,512,128]{2,1,0:T(8,128)(2,1)S(1)} %constant_dynamic-update-slice_fusion.refs_2_.refs_1_, ...), custom_call_target="tpu_custom_call" | custom-call | flops 5000000000 | bytes 1048576 | tf_op jit(solution)/shard_map/near0/pallas_call | solution.py:269
  51.2 12.8 %collective-permute-done.5.refs_10_.refs_14_.refs_18_ = bf16[1536,128]{1,0:T(8,128)(2,1)S(1)} collective-permute-done((bf16[1536,128]{1,0:T(8,128)(2,1)S(1)}, bf16[1536,128]{1,0:T(8,128)(2,1)S(1)}, u32[]{:S(2)}, u32[]{:S(2)}) %collective-permute-start.5) | collective-permute-done | bytes 393248 | tf_op jit(solution)/shard_map/ppermute | solution.py:49
  64.0 2.1 %collective-permute-start.11 = (bf16[1536,128]{1,0:T(8,128)(2,1)S(1)}, bf16[1536,128]{1,0:T(8,128)(2,1)S(1)}, u32[]{:S(2)}, u32[]{:S(2)}) collective-permute-start(bf16[1536,128]{1,0:T(8,128)(2,1)S(1)} %collective-permute-done.5.refs_10_.refs_14_.refs_18_), channel_id=1, source_target_pairs={{0,1},{1,0},{2,3},{3,2},{4,5},{5,4},{6,7},{7,6},{8,9},{9,8},{10,11... | collective-permute-start | bytes 1179656 | tf_op jit(solution)/shard_map/ppermute | solution.py:31
  66.1 5.5 %collective-permute-start.9 = (bf16[1536,128]{1,0:T(8,128)(2,1)S(1)}, bf16[1536,128]{1,0:T(8,128)(2,1)S(1)}, u32[]{:S(2)}, u32[]{:S(2)}) collective-permute-start(bf16[1536,128]{1,0:T(8,128)(2,1)S(1)} %copy-done.10), channel_id=1, source_target_pairs={{0,14},{1,15},{2,4},{3,5},{4,2},{5,3},{6,8},{7,9},{8,6},{9,7},{10,... | collective-permute-start | bytes 1179656 | tf_op jit(solution)/shard_map/ppermute | solution.py:49
  71.7 1.9 %collective-permute-start.8 = (bf16[1024,128]{1,0:T(8,128)(2,1)S(1)}, bf16[1024,128]{1,0:T(8,128)(2,1)S(1)}, u32[]{:S(2)}, u32[]{:S(2)}) collective-permute-start(bf16[1024,128]{1,0:T(8,128)(2,1)S(1)} %copy-done.12), channel_id=1, source_target_pairs={{0,2},{1,3},{2,0},{3,1},{4,6},{5,7},{6,4},{7,5},{8,10},{9,11},{10,... | collective-permute-start | bytes 786440 | tf_op jit(solution)/shard_map/ppermute | solution.py:31
  73.6 2.1 %far0.1.refs_2_ = bf16[512,512]{1,0:T(8,128)(2,1)S(1)} custom-call(s32[5]{0:T(128)S(1)} %stack.30.place_ref.refs_0_, s32[4,32]{1,0:T(4,128)S(1)} %get-tuple-element.62.refs_1_, bf16[4,512,128]{2,1,0:T(8,128)(2,1)S(1)} %collective-permute-done.10.refs_2_, bf16[8,128,512]{2,1,0:T(8,128)(2,1)S(1)} %bitcast.11, f32[2,2,512]{2,1,0:T(2,128)S(1)} %copy-done.2, ...), custom_call_target="tpu_custom_call" | custom-call | flops 3000000000 | bytes 1048576 | tf_op jit(solution)/shard_map/far0/pallas_call | solution.py:269
  75.7 6.1 %collective-permute-done.8.refs_10_.refs_14_.refs_11_ = bf16[1024,128]{1,0:T(8,128)(2,1)S(1)} collective-permute-done((bf16[1024,128]{1,0:T(8,128)(2,1)S(1)}, bf16[1024,128]{1,0:T(8,128)(2,1)S(1)}, u32[]{:S(2)}, u32[]{:S(2)}) %collective-permute-start.8) | collective-permute-done | bytes 262176 | tf_op jit(solution)/shard_map/ppermute | solution.py:31
  81.9 1.9 %collective-permute-start.12 = (bf16[512,512]{1,0:T(8,128)(2,1)S(1)}, bf16[512,512]{1,0:T(8,128)(2,1)S(1)}, u32[]{:S(2)}, u32[]{:S(2)}) collective-permute-start(bf16[512,512]{1,0:T(8,128)(2,1)S(1)} %far0.1.refs_2_), channel_id=1, source_target_pairs={{0,1},{1,0},{2,3},{3,2},{4,5},{5,4},{6,7},{7,6},{8,9},{9,8},{10,11... | collective-permute-start | bytes 1572872 | tf_op jit(solution)/shard_map/ppermute | solution.py:31
  83.8 2.4 %collective-permute-start.13 = (bf16[1024,128]{1,0:T(8,128)(2,1)S(1)}, bf16[1024,128]{1,0:T(8,128)(2,1)S(1)}, u32[]{:S(2)}, u32[]{:S(2)}) collective-permute-start(bf16[1024,128]{1,0:T(8,128)(2,1)S(1)} %collective-permute-done.8.refs_10_.refs_14_.refs_11_), channel_id=1, source_target_pairs={{0,1},{1,0},{2,3},{3,2},{4,5},{5,4},{6,7},{7,6},{8,9},{9,8},{10,11... | collective-permute-start | bytes 786440 | tf_op jit(solution)/shard_map/ppermute | solution.py:31
  89.2 2.2 %collective-permute-start.15 = (bf16[4,512,128]{2,1,0:T(8,128)(2,1)S(1)}, bf16[4,512,128]{2,1,0:T(8,128)(2,1)S(1)}, u32[]{:S(2)}, u32[]{:S(2)}) collective-permute-start(bf16[4,512,128]{2,1,0:T(8,128)(2,1)S(1)} %node0.1.refs_2_.refs_1_), channel_id=1, source_target_pairs={{0,3},{2,5},{3,0},{4,7},{5,2},{6,9},{7,4},{8,11},{9,6},{10,13},{11... | collective-permute-start | bytes 1572872 | tf_op jit(solution)/shard_map/ppermute | solution.py:38
  91.4 3.1 %collective-permute-start.14 = (bf16[4,512,128]{2,1,0:T(8,128)(2,1)S(1)}, bf16[4,512,128]{2,1,0:T(8,128)(2,1)S(1)}, u32[]{:S(2)}, u32[]{:S(2)}) collective-permute-start(bf16[4,512,128]{2,1,0:T(8,128)(2,1)S(1)} %node0.1.refs_2_.refs_1_), channel_id=1, source_target_pairs={{0,5},{2,7},{4,9},{5,0},{6,11},{7,2},{8,13},{9,4},{10,15},{11,6},{... | collective-permute-start | bytes 1572872 | tf_op jit(solution)/shard_map/ppermute | solution.py:38
  94.5 5.2 %collective-permute-done.15.refs_3_ = bf16[4,512,128]{2,1,0:T(8,128)(2,1)S(1)} collective-permute-done((bf16[4,512,128]{2,1,0:T(8,128)(2,1)S(1)}, bf16[4,512,128]{2,1,0:T(8,128)(2,1)S(1)}, u32[]{:S(2)}, u32[]{:S(2)}) %collective-permute-start.15) | collective-permute-done | bytes 524320 | tf_op jit(solution)/shard_map/ppermute | solution.py:38
  99.7 4.6 %near1.1 = (f32[512,512]{1,0:T(8,128)S(1)}, bf16[512,512]{1,0:T(8,128)(2,1)S(1)}) custom-call(s32[5]{0:T(128)S(1)} %stack.30.place_ref.refs_0_, s32[4,32]{1,0:T(4,128)S(1)} %get-tuple-element.62.refs_1_, bf16[4,512,128]{2,1,0:T(8,128)(2,1)S(1)} %node0.1.refs_2_.refs_1_, bf16[4,512,128]{2,1,0:T(8,128)(2,1)S(1)} %collective-permute-done.15.refs_3_, ...), custom_call_target="tpu_custom_call" | custom-call | flops 5000000000 | bytes 1048576 | tf_op jit(solution)/shard_map/near1/pallas_call | solution.py:269
  104.4 6.0 %collective-permute-start.16 = (bf16[1536,128]{1,0:T(8,128)(2,1)S(1)}, bf16[1536,128]{1,0:T(8,128)(2,1)S(1)}, u32[]{:S(2)}, u32[]{:S(2)}) collective-permute-start(bf16[1536,128]{1,0:T(8,128)(2,1)S(1)} %collective-permute-done.9.refs_10_.refs_14_.refs_18_), channel_id=1, source_target_pairs={{0,1},{1,0},{2,3},{3,2},{4,5},{5,4},{6,7},{7,6},{8,9},{9,8},{10,11... | collective-permute-start | bytes 1179656 | tf_op jit(solution)/shard_map/ppermute | solution.py:31
  110.4 2.2 %collective-permute-done.14.refs_2_ = bf16[4,512,128]{2,1,0:T(8,128)(2,1)S(1)} collective-permute-done((bf16[4,512,128]{2,1,0:T(8,128)(2,1)S(1)}, bf16[4,512,128]{2,1,0:T(8,128)(2,1)S(1)}, u32[]{:S(2)}, u32[]{:S(2)}) %collective-permute-start.14) | collective-permute-done | bytes 524320 | tf_op jit(solution)/shard_map/ppermute | solution.py:38
  112.6 2.1 %far1.1.refs_2_ = bf16[512,512]{1,0:T(8,128)(2,1)S(1)} custom-call(s32[5]{0:T(128)S(1)} %stack.30.place_ref.refs_0_, s32[4,32]{1,0:T(4,128)S(1)} %get-tuple-element.62.refs_1_, bf16[4,512,128]{2,1,0:T(8,128)(2,1)S(1)} %collective-permute-done.14.refs_2_, bf16[8,128,512]{2,1,0:T(8,128)(2,1)S(1)} %bitcast.13, f32[2,2,512]{2,1,0:T(2,128)S(1)} %copy-done.2, ...), custom_call_target="tpu_custom_call" | custom-call | flops 3000000000 | bytes 1048576 | tf_op jit(solution)/shard_map/far1/pallas_call | solution.py:269
  114.7 6.7 %collective-permute-start.17 = (bf16[512,512]{1,0:T(8,128)(2,1)S(1)}, bf16[512,512]{1,0:T(8,128)(2,1)S(1)}, u32[]{:S(2)}, u32[]{:S(2)}) collective-permute-start(bf16[512,512]{1,0:T(8,128)(2,1)S(1)} %far1.1.refs_2_), channel_id=1, source_target_pairs={{0,1},{1,0},{2,3},{3,2},{4,5},{5,4},{6,7},{7,6},{8,9},{9,8},{10,11... | collective-permute-start | bytes 1572872 | tf_op jit(solution)/shard_map/ppermute | solution.py:31
  124.8 1.9 %collective-permute-start.18 = (bf16[512,128]{1,0:T(8,128)(2,1)S(1)}, bf16[512,128]{1,0:T(8,128)(2,1)S(1)}, u32[]{:S(2)}, u32[]{:S(2)}) collective-permute-start(bf16[512,128]{1,0:T(8,128)(2,1)S(1)} %get-tuple-element.94), channel_id=1, source_target_pairs={{0,2},{1,3},{2,0},{3,1},{4,6},{5,7},{6,4},{7,5},{8,10},{9,11},{10,... | collective-permute-start | bytes 393224 | tf_op jit(solution)/shard_map/ppermute | solution.py:31
  126.7 5.8 %collective-permute-done.18.other_ref = bf16[512,128]{1,0:T(8,128)(2,1)S(1)} collective-permute-done((bf16[512,128]{1,0:T(8,128)(2,1)S(1)}, bf16[512,128]{1,0:T(8,128)(2,1)S(1)}, u32[]{:S(2)}, u32[]{:S(2)}) %collective-permute-start.18) | collective-permute-done | bytes 131104 | tf_op jit(solution)/shard_map/ppermute | solution.py:31
  (48 shorter events, 9.4 us)
Async XLA Ops:
  0.0 9.3 %copy-start.7 = (bf16[1024,128]{1,0:T(8,128)(2,1)S(1)}, bf16[1024,128]{1,0:T(8,128)(2,1)}, u32[]{:S(2)}) copy-start(bf16[1024,128]{1,0:T(8,128)(2,1)} %param.14) | copy-start | bytes 786436
  0.0 15.6 %copy-start.8 = (s32[8,6,128]{2,0,1:T(8,128)S(1)}, s32[8,6,128]{2,0,1:T(8,128)}, u32[]{:S(2)}) copy-start(s32[8,6,128]{2,0,1:T(8,128)} %param.26) | copy-start | bytes 73732
  0.0 15.6 %copy-start.9 = (s32[8,6,128]{2,0,1:T(8,128)S(1)}, s32[8,6,128]{2,0,1:T(8,128)}, u32[]{:S(2)}) copy-start(s32[8,6,128]{2,0,1:T(8,128)} %param.27) | copy-start | bytes 73732
  0.0 15.7 %copy-start.6 = (s32[8,6]{1,0:T(8,128)S(1)}, s32[8,6]{1,0:T(8,128)}, u32[]{:S(2)}) copy-start(s32[8,6]{1,0:T(8,128)} %count_ref.1) | copy-start | bytes 580
  0.0 15.7 %copy-start.5 = (s32[8,6]{1,0:T(8,128)S(1)}, s32[8,6]{1,0:T(8,128)}, u32[]{:S(2)}) copy-start(s32[8,6]{1,0:T(8,128)} %nbr_ref.1) | copy-start | bytes 580
  3.0 4.2 %collective-permute-start.2 = (bf16[2624,128]{1,0:T(8,128)(2,1)}, bf16[2624,128]{1,0:T(8,128)(2,1)S(1)}, u32[]{:S(2)}, u32[]{:S(2)}) collective-permute-start(bf16[2624,128]{1,0:T(8,128)(2,1)} %get-tuple-element.52.refs_8_.refs_12_.refs_16_.refs_9_), channel_id=1, source_target_pairs={{0,1},{1,0},{2,3},{3,2},{4,5},{5,4},{6,7},{7,6},{8,9},{9,8},{10,11... | collective-permute-start | bytes 2015240 | tf_op jit(solution)/shard_map/ppermute | solution.py:31
  7.2 17.2 %collective-permute-start.3 = (bf16[2560,128]{1,0:T(8,128)(2,1)}, bf16[2560,128]{1,0:T(8,128)(2,1)S(1)}, u32[]{:S(2)}, u32[]{:S(2)}) collective-permute-start(bf16[2560,128]{1,0:T(8,128)(2,1)} %get-tuple-element.54.refs_8_.refs_12_.refs_9_.refs_16_), channel_id=1, source_target_pairs={{0,1},{1,0},{2,3},{3,2},{4,5},{5,4},{6,7},{7,6},{8,9},{9,8},{10,11... | collective-permute-start | bytes 1966088 | tf_op jit(solution)/shard_map/ppermute | solution.py:31
  9.3 8.7 %collective-permute-start = (bf16[512,128]{1,0:T(8,128)(2,1)S(1)}, bf16[512,128]{1,0:T(8,128)(2,1)S(1)}, u32[]{:S(2)}, u32[]{:S(2)}) collective-permute-start(bf16[512,128]{1,0:T(8,128)(2,1)S(1)} %get-tuple-element.96), channel_id=1, source_target_pairs={{0,2},{1,3},{2,0},{3,1},{4,6},{5,7},{6,4},{7,5},{8,10},{9,11},{10,... | collective-permute-start | bytes 393224 | tf_op jit(solution)/shard_map/ppermute | solution.py:31
  13.6 10.7 %collective-permute-start.1 = (bf16[1088,128]{1,0:T(8,128)(2,1)}, bf16[1088,128]{1,0:T(8,128)(2,1)S(1)}, u32[]{:S(2)}, u32[]{:S(2)}) collective-permute-start(bf16[1088,128]{1,0:T(8,128)(2,1)} %get-tuple-element.50), channel_id=1, source_target_pairs={{0,2},{1,3},{2,0},{3,1},{4,6},{5,7},{6,4},{7,5},{8,10},{9,11},{10,... | collective-permute-start | bytes 835592 | tf_op jit(solution)/shard_map/ppermute | solution.py:31
  15.7 28.8 %copy-start.11 = (bf16[1536,128]{1,0:T(8,128)(2,1)S(1)}, bf16[1536,128]{1,0:T(8,128)(2,1)}, u32[]{:S(2)}) copy-start(bf16[1536,128]{1,0:T(8,128)(2,1)} %get-tuple-element.59) | copy-start | bytes 1179652
  15.7 30.7 %copy-start = (bf16[2624,128]{1,0:T(8,128)(2,1)S(1)}, bf16[2624,128]{1,0:T(8,128)(2,1)}, u32[]{:S(2)}) copy-start(bf16[2624,128]{1,0:T(8,128)(2,1)} %get-tuple-element.52.refs_8_.refs_12_.refs_16_.refs_9_) | copy-start | bytes 2015236
  15.7 30.7 %copy-start.2 = (f32[2,2,512]{2,1,0:T(2,128)S(1)}, f32[2,2,512]{2,1,0:T(2,128)}, u32[]{:S(2)}) copy-start(f32[2,2,512]{2,1,0:T(2,128)} %refs_6_.3) | copy-start | bytes 24580
  15.7 30.7 %copy-start.4 = (bf16[2,512,512]{2,1,0:T(8,128)(2,1)S(1)}, bf16[2,512,512]{2,1,0:T(8,128)(2,1)}, u32[]{:S(2)}) copy-start(bf16[2,512,512]{2,1,0:T(8,128)(2,1)} %param.17) | copy-start | bytes 3145732
  24.4 3.4 %collective-permute-start.4 = (bf16[2,512,128]{2,1,0:T(8,128)(2,1)S(1)}, bf16[2,512,128]{2,1,0:T(8,128)(2,1)S(1)}, u32[]{:S(2)}, u32[]{:S(2)}) collective-permute-start(bf16[2,512,128]{2,1,0:T(8,128)(2,1)S(1)} %pad_maximum_fusion), channel_id=1, source_target_pairs={{0,1},{1,0},{2,3},{3,2},{4,5},{5,4},{6,7},{7,6},{8,9},{9,8},{10,11... | collective-permute-start | bytes 786440 | tf_op jit(solution)/shard_map/ppermute | solution.py:31
  27.8 18.6 %collective-permute-start.6 = (bf16[4,512,128]{2,1,0:T(8,128)(2,1)S(1)}, bf16[4,512,128]{2,1,0:T(8,128)(2,1)S(1)}, u32[]{:S(2)}, u32[]{:S(2)}) collective-permute-start(bf16[4,512,128]{2,1,0:T(8,128)(2,1)S(1)} %constant_dynamic-update-slice_fusion.refs_2_.refs_1_), channel_id=1, source_target_pairs={{0,3},{2,5},{3,0},{4,7},{5,2},{6,9},{7,4},{8,11},{9,6},{10,13},{11... | collective-permute-start | bytes 1572872 | tf_op jit(solution)/shard_map/ppermute | solution.py:38
  30.4 16.0 %collective-permute-start.7 = (bf16[1088,128]{1,0:T(8,128)(2,1)S(1)}, bf16[1088,128]{1,0:T(8,128)(2,1)S(1)}, u32[]{:S(2)}, u32[]{:S(2)}) collective-permute-start(bf16[1088,128]{1,0:T(8,128)(2,1)S(1)} %collective-permute-done.1.refs_10_.refs_14_.refs_18_.refs_11_), channel_id=1, source_target_pairs={{0,1},{1,0},{2,3},{3,2},{4,5},{5,4},{6,7},{7,6},{8,9},{9,8},{10,11... | collective-permute-start | bytes 835592 | tf_op jit(solution)/shard_map/ppermute | solution.py:31
  42.6 31.0 %collective-permute-start.10 = (bf16[4,512,128]{2,1,0:T(8,128)(2,1)S(1)}, bf16[4,512,128]{2,1,0:T(8,128)(2,1)S(1)}, u32[]{:S(2)}, u32[]{:S(2)}) collective-permute-start(bf16[4,512,128]{2,1,0:T(8,128)(2,1)S(1)} %constant_dynamic-update-slice_fusion.refs_2_.refs_1_), channel_id=1, source_target_pairs={{0,5},{2,7},{4,9},{5,0},{6,11},{7,2},{8,13},{9,4},{10,15},{11,6},{... | collective-permute-start | bytes 1572872 | tf_op jit(solution)/shard_map/ppermute | solution.py:38
  44.5 19.5 %collective-permute-start.5 = (bf16[1536,128]{1,0:T(8,128)(2,1)S(1)}, bf16[1536,128]{1,0:T(8,128)(2,1)S(1)}, u32[]{:S(2)}, u32[]{:S(2)}) collective-permute-start(bf16[1536,128]{1,0:T(8,128)(2,1)S(1)} %copy-done.11), channel_id=1, source_target_pairs={{0,14},{1,15},{2,4},{3,5},{4,2},{5,3},{6,8},{7,9},{8,6},{9,7},{10,... | collective-permute-start | bytes 1179656 | tf_op jit(solution)/shard_map/ppermute | solution.py:49
  46.5 19.6 %copy-start.10 = (bf16[1536,128]{1,0:T(8,128)(2,1)S(1)}, bf16[1536,128]{1,0:T(8,128)(2,1)}, u32[]{:S(2)}) copy-start(bf16[1536,128]{1,0:T(8,128)(2,1)} %get-tuple-element.69) | copy-start | bytes 1179652
  46.5 25.2 %copy-start.12 = (bf16[1024,128]{1,0:T(8,128)(2,1)S(1)}, bf16[1024,128]{1,0:T(8,128)(2,1)}, u32[]{:S(2)}) copy-start(bf16[1024,128]{1,0:T(8,128)(2,1)} %get-tuple-element.68) | copy-start | bytes 786436
  64.0 9.6 %collective-permute-start.11 = (bf16[1536,128]{1,0:T(8,128)(2,1)S(1)}, bf16[1536,128]{1,0:T(8,128)(2,1)S(1)}, u32[]{:S(2)}, u32[]{:S(2)}) collective-permute-start(bf16[1536,128]{1,0:T(8,128)(2,1)S(1)} %collective-permute-done.5.refs_10_.refs_14_.refs_18_), channel_id=1, source_target_pairs={{0,1},{1,0},{2,3},{3,2},{4,5},{5,4},{6,7},{7,6},{8,9},{9,8},{10,11... | collective-permute-start | bytes 1179656 | tf_op jit(solution)/shard_map/ppermute | solution.py:31
  66.1 15.7 %collective-permute-start.9 = (bf16[1536,128]{1,0:T(8,128)(2,1)S(1)}, bf16[1536,128]{1,0:T(8,128)(2,1)S(1)}, u32[]{:S(2)}, u32[]{:S(2)}) collective-permute-start(bf16[1536,128]{1,0:T(8,128)(2,1)S(1)} %copy-done.10), channel_id=1, source_target_pairs={{0,14},{1,15},{2,4},{3,5},{4,2},{5,3},{6,8},{7,9},{8,6},{9,7},{10,... | collective-permute-start | bytes 1179656 | tf_op jit(solution)/shard_map/ppermute | solution.py:49
  71.7 10.2 %collective-permute-start.8 = (bf16[1024,128]{1,0:T(8,128)(2,1)S(1)}, bf16[1024,128]{1,0:T(8,128)(2,1)S(1)}, u32[]{:S(2)}, u32[]{:S(2)}) collective-permute-start(bf16[1024,128]{1,0:T(8,128)(2,1)S(1)} %copy-done.12), channel_id=1, source_target_pairs={{0,2},{1,3},{2,0},{3,1},{4,6},{5,7},{6,4},{7,5},{8,10},{9,11},{10,... | collective-permute-start | bytes 786440 | tf_op jit(solution)/shard_map/ppermute | solution.py:31
  73.6 13.7 %copy-start.3 = (f32[2,512]{1,0:T(2,128)S(1)}, f32[2,512]{1,0:T(2,128)}, u32[]{:S(2)}) copy-start(f32[2,512]{1,0:T(2,128)} %refs_7_.3) | copy-start | bytes 12292
  81.9 5.5 %collective-permute-start.12 = (bf16[512,512]{1,0:T(8,128)(2,1)S(1)}, bf16[512,512]{1,0:T(8,128)(2,1)S(1)}, u32[]{:S(2)}, u32[]{:S(2)}) collective-permute-start(bf16[512,512]{1,0:T(8,128)(2,1)S(1)} %far0.1.refs_2_), channel_id=1, source_target_pairs={{0,1},{1,0},{2,3},{3,2},{4,5},{5,4},{6,7},{7,6},{8,9},{9,8},{10,11... | collective-permute-start | bytes 1572872 | tf_op jit(solution)/shard_map/ppermute | solution.py:31
  83.8 3.6 %collective-permute-start.13 = (bf16[1024,128]{1,0:T(8,128)(2,1)S(1)}, bf16[1024,128]{1,0:T(8,128)(2,1)S(1)}, u32[]{:S(2)}, u32[]{:S(2)}) collective-permute-start(bf16[1024,128]{1,0:T(8,128)(2,1)S(1)} %collective-permute-done.8.refs_10_.refs_14_.refs_11_), channel_id=1, source_target_pairs={{0,1},{1,0},{2,3},{3,2},{4,5},{5,4},{6,7},{7,6},{8,9},{9,8},{10,11... | collective-permute-start | bytes 786440 | tf_op jit(solution)/shard_map/ppermute | solution.py:31
  87.3 12.4 %copy-start.1 = (bf16[2560,128]{1,0:T(8,128)(2,1)S(1)}, bf16[2560,128]{1,0:T(8,128)(2,1)}, u32[]{:S(2)}) copy-start(bf16[2560,128]{1,0:T(8,128)(2,1)} %get-tuple-element.54.refs_8_.refs_12_.refs_9_.refs_16_) | copy-start | bytes 1966084
  89.2 10.5 %collective-permute-start.15 = (bf16[4,512,128]{2,1,0:T(8,128)(2,1)S(1)}, bf16[4,512,128]{2,1,0:T(8,128)(2,1)S(1)}, u32[]{:S(2)}, u32[]{:S(2)}) collective-permute-start(bf16[4,512,128]{2,1,0:T(8,128)(2,1)S(1)} %node0.1.refs_2_.refs_1_), channel_id=1, source_target_pairs={{0,3},{2,5},{3,0},{4,7},{5,2},{6,9},{7,4},{8,11},{9,6},{10,13},{11... | collective-permute-start | bytes 1572872 | tf_op jit(solution)/shard_map/ppermute | solution.py:38
  91.4 21.2 %collective-permute-start.14 = (bf16[4,512,128]{2,1,0:T(8,128)(2,1)S(1)}, bf16[4,512,128]{2,1,0:T(8,128)(2,1)S(1)}, u32[]{:S(2)}, u32[]{:S(2)}) collective-permute-start(bf16[4,512,128]{2,1,0:T(8,128)(2,1)S(1)} %node0.1.refs_2_.refs_1_), channel_id=1, source_target_pairs={{0,5},{2,7},{4,9},{5,0},{6,11},{7,2},{8,13},{9,4},{10,15},{11,6},{... | collective-permute-start | bytes 1572872 | tf_op jit(solution)/shard_map/ppermute | solution.py:38
  104.4 8.3 %collective-permute-start.16 = (bf16[1536,128]{1,0:T(8,128)(2,1)S(1)}, bf16[1536,128]{1,0:T(8,128)(2,1)S(1)}, u32[]{:S(2)}, u32[]{:S(2)}) collective-permute-start(bf16[1536,128]{1,0:T(8,128)(2,1)S(1)} %collective-permute-done.9.refs_10_.refs_14_.refs_18_), channel_id=1, source_target_pairs={{0,1},{1,0},{2,3},{3,2},{4,5},{5,4},{6,7},{7,6},{8,9},{9,8},{10,11... | collective-permute-start | bytes 1179656 | tf_op jit(solution)/shard_map/ppermute | solution.py:31
  114.7 8.3 %collective-permute-start.17 = (bf16[512,512]{1,0:T(8,128)(2,1)S(1)}, bf16[512,512]{1,0:T(8,128)(2,1)S(1)}, u32[]{:S(2)}, u32[]{:S(2)}) collective-permute-start(bf16[512,512]{1,0:T(8,128)(2,1)S(1)} %far1.1.refs_2_), channel_id=1, source_target_pairs={{0,1},{1,0},{2,3},{3,2},{4,5},{5,4},{6,7},{7,6},{8,9},{9,8},{10,11... | collective-permute-start | bytes 1572872 | tf_op jit(solution)/shard_map/ppermute | solution.py:31
  124.8 7.7 %collective-permute-start.18 = (bf16[512,128]{1,0:T(8,128)(2,1)S(1)}, bf16[512,128]{1,0:T(8,128)(2,1)S(1)}, u32[]{:S(2)}, u32[]{:S(2)}) collective-permute-start(bf16[512,128]{1,0:T(8,128)(2,1)S(1)} %get-tuple-element.94), channel_id=1, source_target_pairs={{0,2},{1,3},{2,0},{3,1},{4,6},{5,7},{6,4},{7,5},{8,10},{9,11},{10,... | collective-permute-start | bytes 393224 | tf_op jit(solution)/shard_map/ppermute | solution.py:31

commit v9 on v7

--- a/solution.py
+++ b/solution.py
@@ -328,11 +328,10 @@
         us=3,
     )
     pair = jnp.stack([own, across])
-    pair, pack_across, next_across, beside, next_beside, meta = barrier(
-        (pair, pack_across, next_across, beside, next_beside, meta)
-    )
     latent = jnp.concatenate([pair, exchange(pair, 1)], axis=0)
-    pack_across = barrier((pack_across, latent))[0]
+    latent, pack_across, next_across, beside, next_beside, meta = barrier(
+        (latent, pack_across, next_across, beside, next_beside, meta)
+    )
     weights = (pack, beside, pack_across, exchange(pack_across, 1))
 
     vectors = None

time: 120 us -> 121 us (level)
  starting transfers between devices: 40.4 us -> 48.2 us
  waiting for transfers between devices: 55.1 us -> 49.1 us
  Pallas kernels: 23.1 us -> 21.1 us
    ppermute x10, starting transfers between devices: 23.6 us -> 30.2 us  [exchange(): return lax.ppermute(value, BOTH, [(i, i ^ mask) for i in range(total)])]
    ppermute x4, waiting for transfers between devices: 35.8 us -> 32.2 us  [swap_with(): lax.ppermute(value, BOTH, [(i, t) for i, t in pairs if 0 <= t < total])]
    pallas_call x9, Pallas kernels: 23.1 us -> 21.1 us  [call(): pl.pallas_call(kernel, out_shape=outs, grid=(1,), in_specs=spaces, out_sp...]
    ppermute x10, waiting for transfers between devices: 11.4 us -> 10 us  [exchange(): return lax.ppermute(value, BOTH, [(i, i ^ mask) for i in range(total)])]
    ppermute x1, starting transfers between devices: 9.13 us -> 10.4 us  [from_other_side(): return lax.ppermute(value, BOTH, pairs)]
  transfers between devices with their start and end apart: 15 -> 15, of which waited for: 7 -> 7; matrix products, arithmetic and copies ran while one was open for 0% -> 0% of each run, Pallas kernels for 11% -> 10%
where the time goes in v9:
time: 121 us; the launch traced here: 119 us
  waiting for transfers between devices  49.1 us (41%)
  starting transfers between devices  48.2 us (40%)
  Pallas kernels  21.1 us (17%)
    ppermute x4, waiting for transfers between devices, swap_with(): lax.ppermute(value, BOTH, [(i, t) for i, t in pairs if 0 <= t < total])  32.2 us
    ppermute x10, starting transfers between devices, exchange(): return lax.ppermute(value, BOTH, [(i, i ^ mask) for i in range(total)])  30.2 us
    pallas_call x9, Pallas kernels, call(): pl.pallas_call(kernel, out_shape=outs, grid=(1,), in_specs=spaces, out_sp...  21.1 us
    ppermute x1, starting transfers between devices, from_other_side(): return lax.ppermute(value, BOTH, pairs)  10.4 us
    ppermute x10, waiting for transfers between devices, exchange(): return lax.ppermute(value, BOTH, [(i, i ^ mask) for i in range(total)])  10 us
    ppermute x4, starting transfers between devices, swap_with(): lax.ppermute(value, BOTH, [(i, t) for i, t in pairs if 0 <= t < total])  7.68 us
    ppermute x1, waiting for transfers between devices, from_other_side(): return lax.ppermute(value, BOTH, pairs)  6.9 us
  transfers between devices with their start and end apart: 15, of which 7 were waited for; matrix products, arithmetic and copies ran while one was open for 0% of the time, Pallas kernels for 10%

profile of v9, /device:TPU:6, one launch (start us, length us, event | category | flops | bytes accessed | tf_op | source)
XLA Modules:
  0.0 119.1 jit_solution(16083434834146977491)
XLA Ops:
  0.0 2.5 %packs.1 = (bf16[2624,128]{1,0:T(8,128)(2,1)}, bf16[2560,128]{1,0:T(8,128)(2,1)}) custom-call(bf16[2,512,128]{2,1,0:T(8,128)(2,1)} %src_ref.2, bf16[2,512,128]{2,1,0:T(8,128)(2,1)} %dst_ref.2, bf16[2,1024,128]{2,1,0:T(8,128)(2,1)} %in_ref.1, bf16[2,512,128]{2,1,0:T(8,128)(2,1)} %out_w_ref.1, f32[2,4,128]{2,1,0:T(4,128)} %vec_ref.1, f32[2,128]{1,0:T(2,128)} %gain_ref.1), custom_call_target="tpu_custom_call" | custom-call | flops 2000000000 | bytes 1048576 | tf_op jit(solution)/shard_map/packs/pallas_call | solution.py:250
  2.5 1.9 %collective-permute-start.3 = (bf16[2624,128]{1,0:T(8,128)(2,1)}, bf16[2624,128]{1,0:T(8,128)(2,1)S(1)}, u32[]{:S(2)}, u32[]{:S(2)}) collective-permute-start(bf16[2624,128]{1,0:T(8,128)(2,1)} %get-tuple-element.31.refs_8_.refs_12_.refs_16_.refs_9_), channel_id=1, source_target_pairs={{0,1},{1,0},{2,3},{3,2},{4,5},{5,4},{6,7},{7,6},{8,9},{9,8},{10,11... | collective-permute-start | bytes 2015240 | tf_op jit(solution)/shard_map/ppermute | solution.py:31
  4.5 4.3 %collective-permute-start.2 = (bf16[2624,128]{1,0:T(8,128)(2,1)}, bf16[2624,128]{1,0:T(8,128)(2,1)S(1)}, u32[]{:S(2)}, u32[]{:S(2)}) collective-permute-start(bf16[2624,128]{1,0:T(8,128)(2,1)} %get-tuple-element.31.refs_8_.refs_12_.refs_16_.refs_9_), channel_id=1, source_target_pairs={{0,2},{1,3},{2,0},{3,1},{4,6},{5,7},{6,4},{7,5},{8,10},{9,11},{10,... | collective-permute-start | bytes 2015240 | tf_op jit(solution)/shard_map/ppermute | solution.py:31
  8.8 1.9 %collective-permute-start = (bf16[512,128]{1,0:T(8,128)(2,1)S(1)}, bf16[512,128]{1,0:T(8,128)(2,1)S(1)}, u32[]{:S(2)}, u32[]{:S(2)}) collective-permute-start(bf16[512,128]{1,0:T(8,128)(2,1)S(1)} %get-tuple-element.58), channel_id=1, source_target_pairs={{0,2},{1,3},{2,0},{3,1},{4,6},{5,7},{6,4},{7,5},{8,10},{9,11},{10,... | collective-permute-start | bytes 393224 | tf_op jit(solution)/shard_map/ppermute | solution.py:31
  10.8 2.1 %collective-permute-start.5 = (bf16[2560,128]{1,0:T(8,128)(2,1)}, bf16[2560,128]{1,0:T(8,128)(2,1)S(1)}, u32[]{:S(2)}, u32[]{:S(2)}) collective-permute-start(bf16[2560,128]{1,0:T(8,128)(2,1)} %get-tuple-element.33.refs_8_.refs_12_.refs_9_.refs_16_), channel_id=1, source_target_pairs={{0,1},{1,0},{2,3},{3,2},{4,5},{5,4},{6,7},{7,6},{8,9},{9,8},{10,11... | collective-permute-start | bytes 1966088 | tf_op jit(solution)/shard_map/ppermute | solution.py:31
  12.9 10.4 %collective-permute-start.4 = (bf16[2560,128]{1,0:T(8,128)(2,1)}, bf16[2560,128]{1,0:T(8,128)(2,1)S(1)}, u32[]{:S(2)}, u32[]{:S(2)}) collective-permute-start(bf16[2560,128]{1,0:T(8,128)(2,1)} %get-tuple-element.33.refs_8_.refs_12_.refs_9_.refs_16_), channel_id=1, source_target_pairs={{0,14},{1,15},{2,4},{3,5},{4,2},{5,3},{6,8},{7,9},{8,6},{9,7},{10,... | collective-permute-start | bytes 1966088 | tf_op jit(solution)/shard_map/ppermute | solution.py:49
  23.4 0.1 stack.30.place_ref.refs_0_
  23.5 4.1 %collective-permute-done = bf16[512,128]{1,0:T(8,128)(2,1)S(1)} collective-permute-done((bf16[512,128]{1,0:T(8,128)(2,1)S(1)}, bf16[512,128]{1,0:T(8,128)(2,1)S(1)}, u32[]{:S(2)}, u32[]{:S(2)}) %collective-permute-start) | collective-permute-done | bytes 131104 | tf_op jit(solution)/shard_map/ppermute | solution.py:31
  27.6 2.1 %collective-permute-start.1 = (bf16[2,512,128]{2,1,0:T(8,128)(2,1)S(1)}, bf16[2,512,128]{2,1,0:T(8,128)(2,1)S(1)}, u32[]{:S(2)}, u32[]{:S(2)}) collective-permute-start(bf16[2,512,128]{2,1,0:T(8,128)(2,1)S(1)} %pad_maximum_fusion.1), channel_id=1, source_target_pairs={{0,1},{1,0},{2,3},{3,2},{4,5},{5,4},{6,7},{7,6},{8,9},{9,8},{10,11... | collective-permute-start | bytes 786440 | tf_op jit(solution)/shard_map/ppermute | solution.py:31
  29.6 2.2 %one_hots.1 = (bf16[25,128,256]{2,1,0:T(8,128)(2,1)S(1)}, bf16[25,128,128]{2,1,0:T(8,128)(2,1)S(1)}, f32[512,128]{1,0:T(8,128)S(1)}, s32[4,32]{1,0:T(4,128)S(1)}) custom-call(s32[5]{0:T(128)S(1)} %stack.30.place_ref.refs_0_, s32[8,6]{1,0:T(8,128)S(1)} %copy-done.5, s32[8,6]{1,0:T(8,128)S(1)} %copy-done.6, s32[8,6,128]{2,1,0:T(8,128)S(1)} %copy.15.src_ref, ...), custom_call_target="tpu_custom_call" | custom-call | flops 3000000000 | bytes 1048576 | tf_op jit(solution)/shard_map/one_hots/pallas_call | solution.py:250
  32.0 6.9 %collective-permute-done.4.refs_10_.refs_14_.refs_11_.refs_18_ = bf16[2560,128]{1,0:T(8,128)(2,1)S(1)} collective-permute-done((bf16[2560,128]{1,0:T(8,128)(2,1)}, bf16[2560,128]{1,0:T(8,128)(2,1)S(1)}, u32[]{:S(2)}, u32[]{:S(2)}) %collective-permute-start.4) | collective-permute-done | bytes 655392 | tf_op jit(solution)/shard_map/ppermute | solution.py:49
  38.9 1.9 %collective-permute-start.8 = (bf16[2624,128]{1,0:T(8,128)(2,1)S(1)}, bf16[2624,128]{1,0:T(8,128)(2,1)S(1)}, u32[]{:S(2)}, u32[]{:S(2)}) collective-permute-start(bf16[2624,128]{1,0:T(8,128)(2,1)S(1)} %collective-permute-done.2.refs_10_.refs_14_.refs_18_.refs_11_), channel_id=1, source_target_pairs={{0,1},{1,0},{2,3},{3,2},{4,5},{5,4},{6,7},{7,6},{8,9},{9,8},{10,11... | collective-permute-start | bytes 2015240 | tf_op jit(solution)/shard_map/ppermute | solution.py:31
  40.8 1.9 %collective-permute-start.7 = (bf16[4,512,128]{2,1,0:T(8,128)(2,1)S(1)}, bf16[4,512,128]{2,1,0:T(8,128)(2,1)S(1)}, u32[]{:S(2)}, u32[]{:S(2)}) collective-permute-start(bf16[4,512,128]{2,1,0:T(8,128)(2,1)S(1)} %pad_maximum_fusion.refs_2_.refs_1_), channel_id=1, source_target_pairs={{0,3},{2,5},{3,0},{4,7},{5,2},{6,9},{7,4},{8,11},{9,6},{10,13},{11... | collective-permute-start | bytes 1572872 | tf_op jit(solution)/shard_map/ppermute | solution.py:38
  42.7 1.9 %collective-permute-start.6 = (bf16[4,512,128]{2,1,0:T(8,128)(2,1)S(1)}, bf16[4,512,128]{2,1,0:T(8,128)(2,1)S(1)}, u32[]{:S(2)}, u32[]{:S(2)}) collective-permute-start(bf16[4,512,128]{2,1,0:T(8,128)(2,1)S(1)} %pad_maximum_fusion.refs_2_.refs_1_), channel_id=1, source_target_pairs={{0,5},{2,7},{4,9},{5,0},{6,11},{7,2},{8,13},{9,4},{10,15},{11,6},{... | collective-permute-start | bytes 1572872 | tf_op jit(solution)/shard_map/ppermute | solution.py:38
  44.6 14.1 %collective-permute-done.7.refs_3_ = bf16[4,512,128]{2,1,0:T(8,128)(2,1)S(1)} collective-permute-done((bf16[4,512,128]{2,1,0:T(8,128)(2,1)S(1)}, bf16[4,512,128]{2,1,0:T(8,128)(2,1)S(1)}, u32[]{:S(2)}, u32[]{:S(2)}) %collective-permute-start.7) | collective-permute-done | bytes 524320 | tf_op jit(solution)/shard_map/ppermute | solution.py:38
  58.7 3.6 %near0.1 = (f32[512,512]{1,0:T(8,128)S(1)}, bf16[512,512]{1,0:T(8,128)(2,1)S(1)}, f32[4,16,128]{2,1,0:T(8,128)S(1)}) custom-call(s32[5]{0:T(128)S(1)} %stack.30.place_ref.refs_0_, s32[4,32]{1,0:T(4,128)S(1)} %get-tuple-element.37.refs_1_, bf16[4,512,128]{2,1,0:T(8,128)(2,1)S(1)} %pad_maximum_fusion.refs_2_.refs_1_, ...), custom_call_target="tpu_custom_call" | custom-call | flops 5000000000 | bytes 1048576 | tf_op jit(solution)/shard_map/near0/pallas_call | solution.py:250
  62.4 0.2 collective-permute-done.6.refs_2_
  62.6 2.1 %far0.1.refs_2_ = bf16[512,512]{1,0:T(8,128)(2,1)S(1)} custom-call(s32[5]{0:T(128)S(1)} %stack.30.place_ref.refs_0_, s32[4,32]{1,0:T(4,128)S(1)} %get-tuple-element.37.refs_1_, bf16[4,512,128]{2,1,0:T(8,128)(2,1)S(1)} %collective-permute-done.6.refs_2_, bf16[8,128,512]{2,1,0:T(8,128)(2,1)S(1)} %bitcast.11, f32[2,2,512]{2,1,0:T(2,128)S(1)} %copy-done.2, ...), custom_call_target="tpu_custom_call" | custom-call | flops 3000000000 | bytes 1048576 | tf_op jit(solution)/shard_map/far0/pallas_call | solution.py:250
  64.7 7.8 %collective-permute-start.9 = (bf16[512,512]{1,0:T(8,128)(2,1)S(1)}, bf16[512,512]{1,0:T(8,128)(2,1)S(1)}, u32[]{:S(2)}, u32[]{:S(2)}) collective-permute-start(bf16[512,512]{1,0:T(8,128)(2,1)S(1)} %far0.1.refs_2_), channel_id=1, source_target_pairs={{0,1},{1,0},{2,3},{3,2},{4,5},{5,4},{6,7},{7,6},{8,9},{9,8},{10,11... | collective-permute-start | bytes 1572872 | tf_op jit(solution)/shard_map/ppermute | solution.py:31
  72.5 1.9 %collective-permute-start.12 = (bf16[2560,128]{1,0:T(8,128)(2,1)S(1)}, bf16[2560,128]{1,0:T(8,128)(2,1)S(1)}, u32[]{:S(2)}, u32[]{:S(2)}) collective-permute-start(bf16[2560,128]{1,0:T(8,128)(2,1)S(1)} %collective-permute-done.4.refs_10_.refs_14_.refs_11_.refs_18_), channel_id=1, source_target_pairs={{0,1},{1,0},{2,3},{3,2},{4,5},{5,4},{6,7},{7,6},{8,9},{9,8},{10,11... | collective-permute-start | bytes 1966088 | tf_op jit(solution)/shard_map/ppermute | solution.py:31
  74.4 1.9 %node0.1.refs_2_.refs_1_ = bf16[4,512,128]{2,1,0:T(8,128)(2,1)S(1)} custom-call(s32[5]{0:T(128)S(1)} %stack.30.place_ref.refs_0_, bf16[4,512,128]{2,1,0:T(8,128)(2,1)S(1)} %pad_maximum_fusion.refs_2_.refs_1_, bf16[512,512]{1,0:T(8,128)(2,1)S(1)} %far0.1.refs_2_, bf16[512,512]{1,0:T(8,128)(2,1)S(1)} %collective-permute-done.9.refs_3_, ...), custom_call_target="tpu_custom_call" | custom-call | flops 2000000000 | bytes 1048576 | tf_op jit(solution)/shard_map/node0/pallas_call | solution.py:250
  76.4 1.9 %collective-permute-start.11 = (bf16[4,512,128]{2,1,0:T(8,128)(2,1)S(1)}, bf16[4,512,128]{2,1,0:T(8,128)(2,1)S(1)}, u32[]{:S(2)}, u32[]{:S(2)}) collective-permute-start(bf16[4,512,128]{2,1,0:T(8,128)(2,1)S(1)} %node0.1.refs_2_.refs_1_), channel_id=1, source_target_pairs={{0,3},{2,5},{3,0},{4,7},{5,2},{6,9},{7,4},{8,11},{9,6},{10,13},{11... | collective-permute-start | bytes 1572872 | tf_op jit(solution)/shard_map/ppermute | solution.py:38
  78.3 1.9 %collective-permute-start.10 = (bf16[4,512,128]{2,1,0:T(8,128)(2,1)S(1)}, bf16[4,512,128]{2,1,0:T(8,128)(2,1)S(1)}, u32[]{:S(2)}, u32[]{:S(2)}) collective-permute-start(bf16[4,512,128]{2,1,0:T(8,128)(2,1)S(1)} %node0.1.refs_2_.refs_1_), channel_id=1, source_target_pairs={{0,5},{2,7},{4,9},{5,0},{6,11},{7,2},{8,13},{9,4},{10,15},{11,6},{... | collective-permute-start | bytes 1572872 | tf_op jit(solution)/shard_map/ppermute | solution.py:38
  80.2 17.9 %collective-permute-done.11.refs_3_ = bf16[4,512,128]{2,1,0:T(8,128)(2,1)S(1)} collective-permute-done((bf16[4,512,128]{2,1,0:T(8,128)(2,1)S(1)}, bf16[4,512,128]{2,1,0:T(8,128)(2,1)S(1)}, u32[]{:S(2)}, u32[]{:S(2)}) %collective-permute-start.11) | collective-permute-done | bytes 524320 | tf_op jit(solution)/shard_map/ppermute | solution.py:38
  98.1 3.6 %near1.1 = (f32[512,512]{1,0:T(8,128)S(1)}, bf16[512,512]{1,0:T(8,128)(2,1)S(1)}) custom-call(s32[5]{0:T(128)S(1)} %stack.30.place_ref.refs_0_, s32[4,32]{1,0:T(4,128)S(1)} %get-tuple-element.37.refs_1_, bf16[4,512,128]{2,1,0:T(8,128)(2,1)S(1)} %node0.1.refs_2_.refs_1_, bf16[4,512,128]{2,1,0:T(8,128)(2,1)S(1)} %collective-permute-done.11.refs_3_, ...), custom_call_target="tpu_custom_call" | custom-call | flops 5000000000 | bytes 1048576 | tf_op jit(solution)/shard_map/near1/pallas_call | solution.py:250
  101.7 2.1 %far1.1.refs_2_ = bf16[512,512]{1,0:T(8,128)(2,1)S(1)} custom-call(s32[5]{0:T(128)S(1)} %stack.30.place_ref.refs_0_, s32[4,32]{1,0:T(4,128)S(1)} %get-tuple-element.37.refs_1_, bf16[4,512,128]{2,1,0:T(8,128)(2,1)S(1)} %collective-permute-done.10.refs_2_, bf16[8,128,512]{2,1,0:T(8,128)(2,1)S(1)} %bitcast.13, f32[2,2,512]{2,1,0:T(2,128)S(1)} %copy-done.2, ...), custom_call_target="tpu_custom_call" | custom-call | flops 3000000000 | bytes 1048576 | tf_op jit(solution)/shard_map/far1/pallas_call | solution.py:250
  103.8 3.0 %collective-permute-start.13 = (bf16[512,512]{1,0:T(8,128)(2,1)S(1)}, bf16[512,512]{1,0:T(8,128)(2,1)S(1)}, u32[]{:S(2)}, u32[]{:S(2)}) collective-permute-start(bf16[512,512]{1,0:T(8,128)(2,1)S(1)} %far1.1.refs_2_), channel_id=1, source_target_pairs={{0,1},{1,0},{2,3},{3,2},{4,5},{5,4},{6,7},{7,6},{8,9},{9,8},{10,11... | collective-permute-start | bytes 1572872 | tf_op jit(solution)/shard_map/ppermute | solution.py:31
  106.8 1.5 %collective-permute-done.13.refs_3_ = bf16[512,512]{1,0:T(8,128)(2,1)S(1)} collective-permute-done((bf16[512,512]{1,0:T(8,128)(2,1)S(1)}, bf16[512,512]{1,0:T(8,128)(2,1)S(1)}, u32[]{:S(2)}, u32[]{:S(2)}) %collective-permute-start.13) | collective-permute-done | bytes 524320 | tf_op jit(solution)/shard_map/ppermute | solution.py:31
  108.3 1.8 %node1.1 = (bf16[512,128]{1,0:T(8,128)(2,1)S(1)}, bf16[512,128]{1,0:T(8,128)(2,1)S(1)}) custom-call(s32[5]{0:T(128)S(1)} %stack.30.place_ref.refs_0_, bf16[4,512,128]{2,1,0:T(8,128)(2,1)S(1)} %node0.1.refs_2_.refs_1_, bf16[512,512]{1,0:T(8,128)(2,1)S(1)} %far1.1.refs_2_, bf16[512,512]{1,0:T(8,128)(2,1)S(1)} %collective-permute-done.13.refs_3_, ...), custom_call_target="tpu_custom_call" | custom-call | flops 2000000000 | bytes 1048576 | tf_op jit(solution)/shard_map/node1/pallas_call | solution.py:250
  110.1 3.2 %collective-permute-start.14 = (bf16[512,128]{1,0:T(8,128)(2,1)S(1)}, bf16[512,128]{1,0:T(8,128)(2,1)S(1)}, u32[]{:S(2)}, u32[]{:S(2)}) collective-permute-start(bf16[512,128]{1,0:T(8,128)(2,1)S(1)} %get-tuple-element.56), channel_id=1, source_target_pairs={{0,2},{1,3},{2,0},{3,1},{4,6},{5,7},{6,4},{7,5},{8,10},{9,11},{10,... | collective-permute-start | bytes 393224 | tf_op jit(solution)/shard_map/ppermute | solution.py:31
  113.4 4.4 %collective-permute-done.14.other_ref = bf16[512,128]{1,0:T(8,128)(2,1)S(1)} collective-permute-done((bf16[512,128]{1,0:T(8,128)(2,1)S(1)}, bf16[512,128]{1,0:T(8,128)(2,1)S(1)}, u32[]{:S(2)}, u32[]{:S(2)}) %collective-permute-start.14) | collective-permute-done | bytes 131104 | tf_op jit(solution)/shard_map/ppermute | solution.py:31
  117.8 1.3 %join.1 = bf16[1024,128]{1,0:T(8,128)(2,1)} custom-call(s32[5]{0:T(128)S(1)} %stack.30.place_ref.refs_0_, bf16[512,128]{1,0:T(8,128)(2,1)S(1)} %get-tuple-element.55.own_ref, bf16[512,128]{1,0:T(8,128)(2,1)S(1)} %collective-permute-done.14.other_ref), custom_call_target="tpu_custom_call" | custom-call | flops 2000000000 | bytes 1048576 | tf_op jit(solution)/shard_map/join/pallas_call | solution.py:250
  (33 shorter events, 0.2 us)
Async XLA Ops:
  0.0 8.8 %copy-start.7 = (bf16[1024,128]{1,0:T(8,128)(2,1)S(1)}, bf16[1024,128]{1,0:T(8,128)(2,1)}, u32[]{:S(2)}) copy-start(bf16[1024,128]{1,0:T(8,128)(2,1)} %param.14) | copy-start | bytes 786436
  0.0 23.3 %copy-start.8 = (s32[8,6,128]{2,0,1:T(8,128)S(1)}, s32[8,6,128]{2,0,1:T(8,128)}, u32[]{:S(2)}) copy-start(s32[8,6,128]{2,0,1:T(8,128)} %param.26) | copy-start | bytes 73732
  0.0 23.3 %copy-start.9 = (s32[8,6,128]{2,0,1:T(8,128)S(1)}, s32[8,6,128]{2,0,1:T(8,128)}, u32[]{:S(2)}) copy-start(s32[8,6,128]{2,0,1:T(8,128)} %param.27) | copy-start | bytes 73732
  0.0 29.6 %copy-start.6 = (s32[8,6]{1,0:T(8,128)S(1)}, s32[8,6]{1,0:T(8,128)}, u32[]{:S(2)}) copy-start(s32[8,6]{1,0:T(8,128)} %count_ref.1) | copy-start | bytes 580
  0.0 29.6 %copy-start.5 = (s32[8,6]{1,0:T(8,128)S(1)}, s32[8,6]{1,0:T(8,128)}, u32[]{:S(2)}) copy-start(s32[8,6]{1,0:T(8,128)} %nbr_ref.1) | copy-start | bytes 580
  2.5 8.2 %collective-permute-start.3 = (bf16[2624,128]{1,0:T(8,128)(2,1)}, bf16[2624,128]{1,0:T(8,128)(2,1)S(1)}, u32[]{:S(2)}, u32[]{:S(2)}) collective-permute-start(bf16[2624,128]{1,0:T(8,128)(2,1)} %get-tuple-element.31.refs_8_.refs_12_.refs_16_.refs_9_), channel_id=1, source_target_pairs={{0,1},{1,0},{2,3},{3,2},{4,5},{5,4},{6,7},{7,6},{8,9},{9,8},{10,11... | collective-permute-start | bytes 2015240 | tf_op jit(solution)/shard_map/ppermute | solution.py:31
  4.5 27.5 %collective-permute-start.2 = (bf16[2624,128]{1,0:T(8,128)(2,1)}, bf16[2624,128]{1,0:T(8,128)(2,1)S(1)}, u32[]{:S(2)}, u32[]{:S(2)}) collective-permute-start(bf16[2624,128]{1,0:T(8,128)(2,1)} %get-tuple-element.31.refs_8_.refs_12_.refs_16_.refs_9_), channel_id=1, source_target_pairs={{0,2},{1,3},{2,0},{3,1},{4,6},{5,7},{6,4},{7,5},{8,10},{9,11},{10,... | collective-permute-start | bytes 2015240 | tf_op jit(solution)/shard_map/ppermute | solution.py:31
  8.8 18.7 %collective-permute-start = (bf16[512,128]{1,0:T(8,128)(2,1)S(1)}, bf16[512,128]{1,0:T(8,128)(2,1)S(1)}, u32[]{:S(2)}, u32[]{:S(2)}) collective-permute-start(bf16[512,128]{1,0:T(8,128)(2,1)S(1)} %get-tuple-element.58), channel_id=1, source_target_pairs={{0,2},{1,3},{2,0},{3,1},{4,6},{5,7},{6,4},{7,5},{8,10},{9,11},{10,... | collective-permute-start | bytes 393224 | tf_op jit(solution)/shard_map/ppermute | solution.py:31
  10.8 21.2 %collective-permute-start.5 = (bf16[2560,128]{1,0:T(8,128)(2,1)}, bf16[2560,128]{1,0:T(8,128)(2,1)S(1)}, u32[]{:S(2)}, u32[]{:S(2)}) collective-permute-start(bf16[2560,128]{1,0:T(8,128)(2,1)} %get-tuple-element.33.refs_8_.refs_12_.refs_9_.refs_16_), channel_id=1, source_target_pairs={{0,1},{1,0},{2,3},{3,2},{4,5},{5,4},{6,7},{7,6},{8,9},{9,8},{10,11... | collective-permute-start | bytes 1966088 | tf_op jit(solution)/shard_map/ppermute | solution.py:31
  12.9 26.0 %collective-permute-start.4 = (bf16[2560,128]{1,0:T(8,128)(2,1)}, bf16[2560,128]{1,0:T(8,128)(2,1)S(1)}, u32[]{:S(2)}, u32[]{:S(2)}) collective-permute-start(bf16[2560,128]{1,0:T(8,128)(2,1)} %get-tuple-element.33.refs_8_.refs_12_.refs_9_.refs_16_), channel_id=1, source_target_pairs={{0,14},{1,15},{2,4},{3,5},{4,2},{5,3},{6,8},{7,9},{8,6},{9,7},{10,... | collective-permute-start | bytes 1966088 | tf_op jit(solution)/shard_map/ppermute | solution.py:49
  27.5 31.2 %copy-start = (bf16[2624,128]{1,0:T(8,128)(2,1)S(1)}, bf16[2624,128]{1,0:T(8,128)(2,1)}, u32[]{:S(2)}) copy-start(bf16[2624,128]{1,0:T(8,128)(2,1)} %get-tuple-element.31.refs_8_.refs_12_.refs_16_.refs_9_) | copy-start | bytes 2015236
  27.5 31.2 %copy-start.2 = (f32[2,2,512]{2,1,0:T(2,128)S(1)}, f32[2,2,512]{2,1,0:T(2,128)}, u32[]{:S(2)}) copy-start(f32[2,2,512]{2,1,0:T(2,128)} %refs_6_.3) | copy-start | bytes 24580
  27.6 31.2 %copy-start.4 = (bf16[2,512,512]{2,1,0:T(8,128)(2,1)S(1)}, bf16[2,512,512]{2,1,0:T(8,128)(2,1)}, u32[]{:S(2)}) copy-start(bf16[2,512,512]{2,1,0:T(8,128)(2,1)} %param.17) | copy-start | bytes 3145732
  27.6 4.3 %collective-permute-start.1 = (bf16[2,512,128]{2,1,0:T(8,128)(2,1)S(1)}, bf16[2,512,128]{2,1,0:T(8,128)(2,1)S(1)}, u32[]{:S(2)}, u32[]{:S(2)}) collective-permute-start(bf16[2,512,128]{2,1,0:T(8,128)(2,1)S(1)} %pad_maximum_fusion.1), channel_id=1, source_target_pairs={{0,1},{1,0},{2,3},{3,2},{4,5},{5,4},{6,7},{7,6},{8,9},{9,8},{10,11... | collective-permute-start | bytes 786440 | tf_op jit(solution)/shard_map/ppermute | solution.py:31
  38.9 19.8 %collective-permute-start.8 = (bf16[2624,128]{1,0:T(8,128)(2,1)S(1)}, bf16[2624,128]{1,0:T(8,128)(2,1)S(1)}, u32[]{:S(2)}, u32[]{:S(2)}) collective-permute-start(bf16[2624,128]{1,0:T(8,128)(2,1)S(1)} %collective-permute-done.2.refs_10_.refs_14_.refs_18_.refs_11_), channel_id=1, source_target_pairs={{0,1},{1,0},{2,3},{3,2},{4,5},{5,4},{6,7},{7,6},{8,9},{9,8},{10,11... | collective-permute-start | bytes 2015240 | tf_op jit(solution)/shard_map/ppermute | solution.py:31
  40.8 17.9 %collective-permute-start.7 = (bf16[4,512,128]{2,1,0:T(8,128)(2,1)S(1)}, bf16[4,512,128]{2,1,0:T(8,128)(2,1)S(1)}, u32[]{:S(2)}, u32[]{:S(2)}) collective-permute-start(bf16[4,512,128]{2,1,0:T(8,128)(2,1)S(1)} %pad_maximum_fusion.refs_2_.refs_1_), channel_id=1, source_target_pairs={{0,3},{2,5},{3,0},{4,7},{5,2},{6,9},{7,4},{8,11},{9,6},{10,13},{11... | collective-permute-start | bytes 1572872 | tf_op jit(solution)/shard_map/ppermute | solution.py:38
  42.7 19.9 %collective-permute-start.6 = (bf16[4,512,128]{2,1,0:T(8,128)(2,1)S(1)}, bf16[4,512,128]{2,1,0:T(8,128)(2,1)S(1)}, u32[]{:S(2)}, u32[]{:S(2)}) collective-permute-start(bf16[4,512,128]{2,1,0:T(8,128)(2,1)S(1)} %pad_maximum_fusion.refs_2_.refs_1_), channel_id=1, source_target_pairs={{0,5},{2,7},{4,9},{5,0},{6,11},{7,2},{8,13},{9,4},{10,15},{11,6},{... | collective-permute-start | bytes 1572872 | tf_op jit(solution)/shard_map/ppermute | solution.py:38
  62.6 11.8 %copy-start.3 = (f32[2,512]{1,0:T(2,128)S(1)}, f32[2,512]{1,0:T(2,128)}, u32[]{:S(2)}) copy-start(f32[2,512]{1,0:T(2,128)} %refs_7_.3) | copy-start | bytes 12292
  64.7 9.7 %collective-permute-start.9 = (bf16[512,512]{1,0:T(8,128)(2,1)S(1)}, bf16[512,512]{1,0:T(8,128)(2,1)S(1)}, u32[]{:S(2)}, u32[]{:S(2)}) collective-permute-start(bf16[512,512]{1,0:T(8,128)(2,1)S(1)} %far0.1.refs_2_), channel_id=1, source_target_pairs={{0,1},{1,0},{2,3},{3,2},{4,5},{5,4},{6,7},{7,6},{8,9},{9,8},{10,11... | collective-permute-start | bytes 1572872 | tf_op jit(solution)/shard_map/ppermute | solution.py:31
  72.5 7.7 %collective-permute-start.12 = (bf16[2560,128]{1,0:T(8,128)(2,1)S(1)}, bf16[2560,128]{1,0:T(8,128)(2,1)S(1)}, u32[]{:S(2)}, u32[]{:S(2)}) collective-permute-start(bf16[2560,128]{1,0:T(8,128)(2,1)S(1)} %collective-permute-done.4.refs_10_.refs_14_.refs_11_.refs_18_), channel_id=1, source_target_pairs={{0,1},{1,0},{2,3},{3,2},{4,5},{5,4},{6,7},{7,6},{8,9},{9,8},{10,11... | collective-permute-start | bytes 1966088 | tf_op jit(solution)/shard_map/ppermute | solution.py:31
  74.4 23.7 %copy-start.1 = (bf16[2560,128]{1,0:T(8,128)(2,1)S(1)}, bf16[2560,128]{1,0:T(8,128)(2,1)}, u32[]{:S(2)}) copy-start(bf16[2560,128]{1,0:T(8,128)(2,1)} %get-tuple-element.33.refs_8_.refs_12_.refs_9_.refs_16_) | copy-start | bytes 1966084
  76.4 21.7 %collective-permute-start.11 = (bf16[4,512,128]{2,1,0:T(8,128)(2,1)S(1)}, bf16[4,512,128]{2,1,0:T(8,128)(2,1)S(1)}, u32[]{:S(2)}, u32[]{:S(2)}) collective-permute-start(bf16[4,512,128]{2,1,0:T(8,128)(2,1)S(1)} %node0.1.refs_2_.refs_1_), channel_id=1, source_target_pairs={{0,3},{2,5},{3,0},{4,7},{5,2},{6,9},{7,4},{8,11},{9,6},{10,13},{11... | collective-permute-start | bytes 1572872 | tf_op jit(solution)/shard_map/ppermute | solution.py:38
  78.3 23.4 %collective-permute-start.10 = (bf16[4,512,128]{2,1,0:T(8,128)(2,1)S(1)}, bf16[4,512,128]{2,1,0:T(8,128)(2,1)S(1)}, u32[]{:S(2)}, u32[]{:S(2)}) collective-permute-start(bf16[4,512,128]{2,1,0:T(8,128)(2,1)S(1)} %node0.1.refs_2_.refs_1_), channel_id=1, source_target_pairs={{0,5},{2,7},{4,9},{5,0},{6,11},{7,2},{8,13},{9,4},{10,15},{11,6},{... | collective-permute-start | bytes 1572872 | tf_op jit(solution)/shard_map/ppermute | solution.py:38
  103.8 4.5 %collective-permute-start.13 = (bf16[512,512]{1,0:T(8,128)(2,1)S(1)}, bf16[512,512]{1,0:T(8,128)(2,1)S(1)}, u32[]{:S(2)}, u32[]{:S(2)}) collective-permute-start(bf16[512,512]{1,0:T(8,128)(2,1)S(1)} %far1.1.refs_2_), channel_id=1, source_target_pairs={{0,1},{1,0},{2,3},{3,2},{4,5},{5,4},{6,7},{7,6},{8,9},{9,8},{10,11... | collective-permute-start | bytes 1572872 | tf_op jit(solution)/shard_map/ppermute | solution.py:31
  110.1 7.7 %collective-permute-start.14 = (bf16[512,128]{1,0:T(8,128)(2,1)S(1)}, bf16[512,128]{1,0:T(8,128)(2,1)S(1)}, u32[]{:S(2)}, u32[]{:S(2)}) collective-permute-start(bf16[512,128]{1,0:T(8,128)(2,1)S(1)} %get-tuple-element.56), channel_id=1, source_target_pairs={{0,2},{1,3},{2,0},{3,1},{4,6},{5,7},{6,4},{7,5},{8,10},{9,11},{10,... | collective-permute-start | bytes 393224 | tf_op jit(solution)/shard_map/ppermute | solution.py:31

commit v10 on v9

--- a/solution.py
+++ b/solution.py
@@ -329,17 +329,17 @@
     )
     pair = jnp.stack([own, across])
     latent = jnp.concatenate([pair, exchange(pair, 1)], axis=0)
-    latent, pack_across, next_across, beside, next_beside, meta = barrier(
-        (latent, pack_across, next_across, beside, next_beside, meta)
-    )
-    weights = (pack, beside, pack_across, exchange(pack_across, 1))
-
     vectors = None
     messages = w_msg.reshape(LAYERS * 4, part, width)
     for layer in range(LAYERS):
         final = layer == LAYERS - 1
         after = swap_with(latent, 1)
         beyond = swap_with(latent, 2)
+        if layer == 0:
+            after, beyond, pack_across, next_across, beside, next_beside, meta = barrier(
+                (after, beyond, pack_across, next_across, beside, next_beside, meta)
+            )
+            weights = (pack, beside, pack_across, exchange(pack_across, 1))
         message_spec = pl.BlockSpec((4, part, width), lambda i, layer=layer: (layer, 0, 0))
         edge_inputs = [messages, msg_vectors, gather, collect]
         edge_specs = [message_spec, VMEM, VMEM, VMEM]

time: 121 us -> 128 us (1.058)
  the two profiles are of different devices: /device:TPU:6 before, /device:TPU:1 now
where the time goes in v10:
time: 128 us; the launch traced here: 127 us
  starting transfers between devices  67 us (52%)
  waiting for transfers between devices  39.6 us (31%)
  Pallas kernels  20 us (16%)
    ppermute x10, starting transfers between devices, exchange(): return lax.ppermute(value, BOTH, [(i, i ^ mask) for i in range(total)])  57.1 us
    ppermute x10, waiting for transfers between devices, exchange(): return lax.ppermute(value, BOTH, [(i, i ^ mask) for i in range(total)])  21.9 us
    pallas_call x9, Pallas kernels, call(): pl.pallas_call(kernel, out_shape=outs, grid=(1,), in_specs=spaces, out_sp...  20 us
    ppermute x1, waiting for transfers between devices, from_other_side(): return lax.ppermute(value, BOTH, pairs)  17.7 us
    ppermute x1, starting transfers between devices, from_other_side(): return lax.ppermute(value, BOTH, pairs)  5.55 us
    ppermute x4, starting transfers between devices, swap_with(): lax.ppermute(value, BOTH, [(i, t) for i, t in pairs if 0 <= t < total])  4.33 us
  transfers between devices with their start and end apart: 15, of which 6 were waited for; matrix products, arithmetic and copies ran while one was open for 0% of the time, Pallas kernels for 6%

profile of v10, /device:TPU:1, one launch (start us, length us, event | category | flops | bytes accessed | tf_op | source)
XLA Modules:
  0.0 127.3 jit_solution(5933692758782191919)
XLA Ops:
  0.0 2.5 %packs.1 = (bf16[2624,128]{1,0:T(8,128)(2,1)}, bf16[2560,128]{1,0:T(8,128)(2,1)}) custom-call(bf16[2,512,128]{2,1,0:T(8,128)(2,1)} %src_ref.2, bf16[2,512,128]{2,1,0:T(8,128)(2,1)} %dst_ref.2, bf16[2,1024,128]{2,1,0:T(8,128)(2,1)} %in_ref.1, bf16[2,512,128]{2,1,0:T(8,128)(2,1)} %out_w_ref.1, f32[2,4,128]{2,1,0:T(4,128)} %vec_ref.1, f32[2,128]{1,0:T(2,128)} %gain_ref.1), custom_call_target="tpu_custom_call" | custom-call | flops 2000000000 | bytes 1048576 | tf_op jit(solution)/shard_map/packs/pallas_call | solution.py:250
  2.6 8.9 %collective-permute-start.5 = (bf16[2624,128]{1,0:T(8,128)(2,1)}, bf16[2624,128]{1,0:T(8,128)(2,1)S(1)}, u32[]{:S(2)}, u32[]{:S(2)}) collective-permute-start(bf16[2624,128]{1,0:T(8,128)(2,1)} %get-tuple-element.32.refs_8_.refs_12_.refs_16_.refs_9_), channel_id=1, source_target_pairs={{0,1},{1,0},{2,3},{3,2},{4,5},{5,4},{6,7},{7,6},{8,9},{9,8},{10,11... | collective-permute-start | bytes 2015240 | tf_op jit(solution)/shard_map/ppermute | solution.py:31
  11.6 1.9 %collective-permute-start = (bf16[512,128]{1,0:T(8,128)(2,1)S(1)}, bf16[512,128]{1,0:T(8,128)(2,1)S(1)}, u32[]{:S(2)}, u32[]{:S(2)}) collective-permute-start(bf16[512,128]{1,0:T(8,128)(2,1)S(1)} %get-tuple-element.60), channel_id=1, source_target_pairs={{0,2},{1,3},{2,0},{3,1},{4,6},{5,7},{6,4},{7,5},{8,10},{9,11},{10,... | collective-permute-start | bytes 393224 | tf_op jit(solution)/shard_map/ppermute | solution.py:31
  13.5 5.1 %collective-permute-done = bf16[512,128]{1,0:T(8,128)(2,1)S(1)} collective-permute-done((bf16[512,128]{1,0:T(8,128)(2,1)S(1)}, bf16[512,128]{1,0:T(8,128)(2,1)S(1)}, u32[]{:S(2)}, u32[]{:S(2)}) %collective-permute-start) | collective-permute-done | bytes 131104 | tf_op jit(solution)/shard_map/ppermute | solution.py:31
  18.6 2.7 %collective-permute-start.1 = (bf16[2,512,128]{2,1,0:T(8,128)(2,1)S(1)}, bf16[2,512,128]{2,1,0:T(8,128)(2,1)S(1)}, u32[]{:S(2)}, u32[]{:S(2)}) collective-permute-start(bf16[2,512,128]{2,1,0:T(8,128)(2,1)S(1)} %pad_maximum_fusion.1), channel_id=1, source_target_pairs={{0,1},{1,0},{2,3},{3,2},{4,5},{5,4},{6,7},{7,6},{8,9},{9,8},{10,11... | collective-permute-start | bytes 786440 | tf_op jit(solution)/shard_map/ppermute | solution.py:31
  21.3 1.9 %collective-permute-start.4 = (bf16[2624,128]{1,0:T(8,128)(2,1)}, bf16[2624,128]{1,0:T(8,128)(2,1)S(1)}, u32[]{:S(2)}, u32[]{:S(2)}) collective-permute-start(bf16[2624,128]{1,0:T(8,128)(2,1)} %get-tuple-element.32.refs_8_.refs_12_.refs_16_.refs_9_), channel_id=1, source_target_pairs={{0,2},{1,3},{2,0},{3,1},{4,6},{5,7},{6,4},{7,5},{8,10},{9,11},{10,... | collective-permute-start | bytes 2015240 | tf_op jit(solution)/shard_map/ppermute | solution.py:31
  23.2 2.2 %collective-permute-start.7 = (bf16[2560,128]{1,0:T(8,128)(2,1)}, bf16[2560,128]{1,0:T(8,128)(2,1)S(1)}, u32[]{:S(2)}, u32[]{:S(2)}) collective-permute-start(bf16[2560,128]{1,0:T(8,128)(2,1)} %get-tuple-element.34.refs_8_.refs_12_.refs_9_.refs_16_), channel_id=1, source_target_pairs={{0,1},{1,0},{2,3},{3,2},{4,5},{5,4},{6,7},{7,6},{8,9},{9,8},{10,11... | collective-permute-start | bytes 1966088 | tf_op jit(solution)/shard_map/ppermute | solution.py:31
  25.5 5.6 %collective-permute-start.6 = (bf16[2560,128]{1,0:T(8,128)(2,1)}, bf16[2560,128]{1,0:T(8,128)(2,1)S(1)}, u32[]{:S(2)}, u32[]{:S(2)}) collective-permute-start(bf16[2560,128]{1,0:T(8,128)(2,1)} %get-tuple-element.34.refs_8_.refs_12_.refs_9_.refs_16_), channel_id=1, source_target_pairs={{0,14},{1,15},{2,4},{3,5},{4,2},{5,3},{6,8},{7,9},{8,6},{9,7},{10,... | collective-permute-start | bytes 1966088 | tf_op jit(solution)/shard_map/ppermute | solution.py:49
  31.0 0.1 pad_maximum_fusion.refs_2_.refs_1_
  31.1 1.5 %collective-permute-start.3 = (bf16[4,512,128]{2,1,0:T(8,128)(2,1)S(1)}, bf16[4,512,128]{2,1,0:T(8,128)(2,1)}, u32[]{:S(2)}, u32[]{:S(2)}) collective-permute-start(bf16[4,512,128]{2,1,0:T(8,128)(2,1)S(1)} %pad_maximum_fusion.refs_2_.refs_1_), channel_id=1, source_target_pairs={{0,5},{2,7},{4,9},{5,0},{6,11},{7,2},{8,13},{9,4},{10,15},{11,6},{... | collective-permute-start | bytes 1572872 | tf_op jit(solution)/shard_map/ppermute | solution.py:38
  32.6 1.5 %collective-permute-start.2 = (bf16[4,512,128]{2,1,0:T(8,128)(2,1)S(1)}, bf16[4,512,128]{2,1,0:T(8,128)(2,1)}, u32[]{:S(2)}, u32[]{:S(2)}) collective-permute-start(bf16[4,512,128]{2,1,0:T(8,128)(2,1)S(1)} %pad_maximum_fusion.refs_2_.refs_1_), channel_id=1, source_target_pairs={{0,3},{2,5},{3,0},{4,7},{5,2},{6,9},{7,4},{8,11},{9,6},{10,13},{11... | collective-permute-start | bytes 1572872 | tf_op jit(solution)/shard_map/ppermute | solution.py:38
  34.1 0.1 stack.30.place_ref.refs_0_
  34.2 2.2 %one_hots.1 = (bf16[25,128,256]{2,1,0:T(8,128)(2,1)S(1)}, bf16[25,128,128]{2,1,0:T(8,128)(2,1)S(1)}, f32[512,128]{1,0:T(8,128)S(1)}, s32[4,32]{1,0:T(4,128)S(1)}) custom-call(s32[5]{0:T(128)S(1)} %stack.30.place_ref.refs_0_, s32[8,6]{1,0:T(8,128)S(1)} %copy-done.5, s32[8,6]{1,0:T(8,128)S(1)} %copy-done.6, s32[8,6,128]{2,1,0:T(8,128)S(1)} %copy.15.src_ref, ...), custom_call_target="tpu_custom_call" | custom-call | flops 3000000000 | bytes 1048576 | tf_op jit(solution)/shard_map/one_hots/pallas_call | solution.py:250
  36.4 8.9 %collective-permute-done.4.refs_10_.refs_14_.refs_18_.refs_11_ = bf16[2624,128]{1,0:T(8,128)(2,1)S(1)} collective-permute-done((bf16[2624,128]{1,0:T(8,128)(2,1)}, bf16[2624,128]{1,0:T(8,128)(2,1)S(1)}, u32[]{:S(2)}, u32[]{:S(2)}) %collective-permute-start.4) | collective-permute-done | bytes 671776 | tf_op jit(solution)/shard_map/ppermute | solution.py:31
  45.4 17.7 %collective-permute-done.6.refs_10_.refs_14_.refs_11_.refs_18_ = bf16[2560,128]{1,0:T(8,128)(2,1)S(1)} collective-permute-done((bf16[2560,128]{1,0:T(8,128)(2,1)}, bf16[2560,128]{1,0:T(8,128)(2,1)S(1)}, u32[]{:S(2)}, u32[]{:S(2)}) %collective-permute-start.6) | collective-permute-done | bytes 655392 | tf_op jit(solution)/shard_map/ppermute | solution.py:49
  63.0 2.6 %collective-permute-start.8 = (bf16[2624,128]{1,0:T(8,128)(2,1)S(1)}, bf16[2624,128]{1,0:T(8,128)(2,1)S(1)}, u32[]{:S(2)}, u32[]{:S(2)}) collective-permute-start(bf16[2624,128]{1,0:T(8,128)(2,1)S(1)} %collective-permute-done.4.refs_10_.refs_14_.refs_18_.refs_11_), channel_id=1, source_target_pairs={{0,1},{1,0},{2,3},{3,2},{4,5},{5,4},{6,7},{7,6},{8,9},{9,8},{10,11... | collective-permute-start | bytes 2015240 | tf_op jit(solution)/shard_map/ppermute | solution.py:31
  65.7 1.7 %collective-permute-done.8.refs_11_.refs_15_.refs_19_.refs_12_ = bf16[2624,128]{1,0:T(8,128)(2,1)S(1)} collective-permute-done((bf16[2624,128]{1,0:T(8,128)(2,1)S(1)}, bf16[2624,128]{1,0:T(8,128)(2,1)S(1)}, u32[]{:S(2)}, u32[]{:S(2)}) %collective-permute-start.8) | collective-permute-done | bytes 671776 | tf_op jit(solution)/shard_map/ppermute | solution.py:31
  67.4 4.1 %near0.1 = (f32[512,512]{1,0:T(8,128)S(1)}, bf16[512,512]{1,0:T(8,128)(2,1)S(1)}, f32[4,16,128]{2,1,0:T(8,128)S(1)}) custom-call(s32[5]{0:T(128)S(1)} %stack.30.place_ref.refs_0_, s32[4,32]{1,0:T(4,128)S(1)} %get-tuple-element.37.refs_1_, bf16[4,512,128]{2,1,0:T(8,128)(2,1)S(1)} %pad_maximum_fusion.refs_2_.refs_1_, ...), custom_call_target="tpu_custom_call" | custom-call | flops 5000000000 | bytes 1048576 | tf_op jit(solution)/shard_map/near0/pallas_call | solution.py:250
  71.5 1.6 %far0.1.refs_2_ = bf16[512,512]{1,0:T(8,128)(2,1)S(1)} custom-call(s32[5]{0:T(128)S(1)} %stack.30.place_ref.refs_0_, s32[4,32]{1,0:T(4,128)S(1)} %get-tuple-element.37.refs_1_, bf16[4,512,128]{2,1,0:T(8,128)(2,1)} %collective-permute-done.3.refs_2_, bf16[8,128,512]{2,1,0:T(8,128)(2,1)S(1)} %bitcast.11, f32[2,2,512]{2,1,0:T(2,128)S(1)} %copy-done.2, ...), custom_call_target="tpu_custom_call" | custom-call | flops 3000000000 | bytes 1048576 | tf_op jit(solution)/shard_map/far0/pallas_call | solution.py:250
  73.1 6.3 %collective-permute-start.9 = (bf16[512,512]{1,0:T(8,128)(2,1)S(1)}, bf16[512,512]{1,0:T(8,128)(2,1)S(1)}, u32[]{:S(2)}, u32[]{:S(2)}) collective-permute-start(bf16[512,512]{1,0:T(8,128)(2,1)S(1)} %far0.1.refs_2_), channel_id=1, source_target_pairs={{0,1},{1,0},{2,3},{3,2},{4,5},{5,4},{6,7},{7,6},{8,9},{9,8},{10,11... | collective-permute-start | bytes 1572872 | tf_op jit(solution)/shard_map/ppermute | solution.py:31
  79.4 1.9 %collective-permute-start.12 = (bf16[2560,128]{1,0:T(8,128)(2,1)S(1)}, bf16[2560,128]{1,0:T(8,128)(2,1)S(1)}, u32[]{:S(2)}, u32[]{:S(2)}) collective-permute-start(bf16[2560,128]{1,0:T(8,128)(2,1)S(1)} %collective-permute-done.6.refs_10_.refs_14_.refs_11_.refs_18_), channel_id=1, source_target_pairs={{0,1},{1,0},{2,3},{3,2},{4,5},{5,4},{6,7},{7,6},{8,9},{9,8},{10,11... | collective-permute-start | bytes 1966088 | tf_op jit(solution)/shard_map/ppermute | solution.py:31
  81.3 1.9 %node0.1.refs_2_.refs_1_ = bf16[4,512,128]{2,1,0:T(8,128)(2,1)S(1)} custom-call(s32[5]{0:T(128)S(1)} %stack.30.place_ref.refs_0_, bf16[4,512,128]{2,1,0:T(8,128)(2,1)S(1)} %pad_maximum_fusion.refs_2_.refs_1_, bf16[512,512]{1,0:T(8,128)(2,1)S(1)} %far0.1.refs_2_, bf16[512,512]{1,0:T(8,128)(2,1)S(1)} %collective-permute-done.9.refs_3_, ...), custom_call_target="tpu_custom_call" | custom-call | flops 2000000000 | bytes 1048576 | tf_op jit(solution)/shard_map/node0/pallas_call | solution.py:250
  83.3 0.7 collective-permute-start.11
  84.0 0.7 collective-permute-start.10
  84.7 3.6 %near1.1 = (f32[512,512]{1,0:T(8,128)S(1)}, bf16[512,512]{1,0:T(8,128)(2,1)S(1)}) custom-call(s32[5]{0:T(128)S(1)} %stack.30.place_ref.refs_0_, s32[4,32]{1,0:T(4,128)S(1)} %get-tuple-element.37.refs_1_, bf16[4,512,128]{2,1,0:T(8,128)(2,1)S(1)} %node0.1.refs_2_.refs_1_, bf16[4,512,128]{2,1,0:T(8,128)(2,1)S(1)} %collective-permute-done.11.refs_3_, ...), custom_call_target="tpu_custom_call" | custom-call | flops 5000000000 | bytes 1048576 | tf_op jit(solution)/shard_map/near1/pallas_call | solution.py:250
  88.3 1.1 far1.1.refs_2_
  89.4 26.7 %collective-permute-start.13 = (bf16[512,512]{1,0:T(8,128)(2,1)S(1)}, bf16[512,512]{1,0:T(8,128)(2,1)S(1)}, u32[]{:S(2)}, u32[]{:S(2)}) collective-permute-start(bf16[512,512]{1,0:T(8,128)(2,1)S(1)} %far1.1.refs_2_), channel_id=1, source_target_pairs={{0,1},{1,0},{2,3},{3,2},{4,5},{5,4},{6,7},{7,6},{8,9},{9,8},{10,11... | collective-permute-start | bytes 1572872 | tf_op jit(solution)/shard_map/ppermute | solution.py:31
  116.1 1.5 %collective-permute-done.13.refs_3_ = bf16[512,512]{1,0:T(8,128)(2,1)S(1)} collective-permute-done((bf16[512,512]{1,0:T(8,128)(2,1)S(1)}, bf16[512,512]{1,0:T(8,128)(2,1)S(1)}, u32[]{:S(2)}, u32[]{:S(2)}) %collective-permute-start.13) | collective-permute-done | bytes 524320 | tf_op jit(solution)/shard_map/ppermute | solution.py:31
  117.6 1.8 %node1.1 = (bf16[512,128]{1,0:T(8,128)(2,1)S(1)}, bf16[512,128]{1,0:T(8,128)(2,1)S(1)}) custom-call(s32[5]{0:T(128)S(1)} %stack.30.place_ref.refs_0_, bf16[4,512,128]{2,1,0:T(8,128)(2,1)S(1)} %node0.1.refs_2_.refs_1_, bf16[512,512]{1,0:T(8,128)(2,1)S(1)} %far1.1.refs_2_, bf16[512,512]{1,0:T(8,128)(2,1)S(1)} %collective-permute-done.13.refs_3_, ...), custom_call_target="tpu_custom_call" | custom-call | flops 2000000000 | bytes 1048576 | tf_op jit(solution)/shard_map/node1/pallas_call | solution.py:250
  119.4 1.9 %collective-permute-start.14 = (bf16[512,128]{1,0:T(8,128)(2,1)S(1)}, bf16[512,128]{1,0:T(8,128)(2,1)S(1)}, u32[]{:S(2)}, u32[]{:S(2)}) collective-permute-start(bf16[512,128]{1,0:T(8,128)(2,1)S(1)} %get-tuple-element.58), channel_id=1, source_target_pairs={{0,2},{1,3},{2,0},{3,1},{4,6},{5,7},{6,4},{7,5},{8,10},{9,11},{10,... | collective-permute-start | bytes 393224 | tf_op jit(solution)/shard_map/ppermute | solution.py:31
  121.4 4.6 %collective-permute-done.14.other_ref = bf16[512,128]{1,0:T(8,128)(2,1)S(1)} collective-permute-done((bf16[512,128]{1,0:T(8,128)(2,1)S(1)}, bf16[512,128]{1,0:T(8,128)(2,1)S(1)}, u32[]{:S(2)}, u32[]{:S(2)}) %collective-permute-start.14) | collective-permute-done | bytes 131104 | tf_op jit(solution)/shard_map/ppermute | solution.py:31
  126.0 1.3 join.1
  (33 shorter events, 0.1 us)
Async XLA Ops:
  0.0 11.5 %copy-start.7 = (bf16[1024,128]{1,0:T(8,128)(2,1)S(1)}, bf16[1024,128]{1,0:T(8,128)(2,1)}, u32[]{:S(2)}) copy-start(bf16[1024,128]{1,0:T(8,128)(2,1)} %param.14) | copy-start | bytes 786436
  2.5 31.5 %copy-start.8 = (s32[8,6,128]{2,0,1:T(8,128)S(1)}, s32[8,6,128]{2,0,1:T(8,128)}, u32[]{:S(2)}) copy-start(s32[8,6,128]{2,0,1:T(8,128)} %param.26) | copy-start | bytes 73732
  2.5 31.5 %copy-start.9 = (s32[8,6,128]{2,0,1:T(8,128)S(1)}, s32[8,6,128]{2,0,1:T(8,128)}, u32[]{:S(2)}) copy-start(s32[8,6,128]{2,0,1:T(8,128)} %param.27) | copy-start | bytes 73732
  2.5 31.6 %copy-start.5 = (s32[8,6]{1,0:T(8,128)S(1)}, s32[8,6]{1,0:T(8,128)}, u32[]{:S(2)}) copy-start(s32[8,6]{1,0:T(8,128)} %nbr_ref.1) | copy-start | bytes 580
  2.6 31.6 %copy-start.6 = (s32[8,6]{1,0:T(8,128)S(1)}, s32[8,6]{1,0:T(8,128)}, u32[]{:S(2)}) copy-start(s32[8,6]{1,0:T(8,128)} %count_ref.1) | copy-start | bytes 580
  2.6 20.7 %collective-permute-start.5 = (bf16[2624,128]{1,0:T(8,128)(2,1)}, bf16[2624,128]{1,0:T(8,128)(2,1)S(1)}, u32[]{:S(2)}, u32[]{:S(2)}) collective-permute-start(bf16[2624,128]{1,0:T(8,128)(2,1)} %get-tuple-element.32.refs_8_.refs_12_.refs_16_.refs_9_), channel_id=1, source_target_pairs={{0,1},{1,0},{2,3},{3,2},{4,5},{5,4},{6,7},{7,6},{8,9},{9,8},{10,11... | collective-permute-start | bytes 2015240 | tf_op jit(solution)/shard_map/ppermute | solution.py:31
  11.6 7.0 %collective-permute-start = (bf16[512,128]{1,0:T(8,128)(2,1)S(1)}, bf16[512,128]{1,0:T(8,128)(2,1)S(1)}, u32[]{:S(2)}, u32[]{:S(2)}) collective-permute-start(bf16[512,128]{1,0:T(8,128)(2,1)S(1)} %get-tuple-element.60), channel_id=1, source_target_pairs={{0,2},{1,3},{2,0},{3,1},{4,6},{5,7},{6,4},{7,5},{8,10},{9,11},{10,... | collective-permute-start | bytes 393224 | tf_op jit(solution)/shard_map/ppermute | solution.py:31
  18.6 12.4 %collective-permute-start.1 = (bf16[2,512,128]{2,1,0:T(8,128)(2,1)S(1)}, bf16[2,512,128]{2,1,0:T(8,128)(2,1)S(1)}, u32[]{:S(2)}, u32[]{:S(2)}) collective-permute-start(bf16[2,512,128]{2,1,0:T(8,128)(2,1)S(1)} %pad_maximum_fusion.1), channel_id=1, source_target_pairs={{0,1},{1,0},{2,3},{3,2},{4,5},{5,4},{6,7},{7,6},{8,9},{9,8},{10,11... | collective-permute-start | bytes 786440 | tf_op jit(solution)/shard_map/ppermute | solution.py:31
  21.3 24.1 %collective-permute-start.4 = (bf16[2624,128]{1,0:T(8,128)(2,1)}, bf16[2624,128]{1,0:T(8,128)(2,1)S(1)}, u32[]{:S(2)}, u32[]{:S(2)}) collective-permute-start(bf16[2624,128]{1,0:T(8,128)(2,1)} %get-tuple-element.32.refs_8_.refs_12_.refs_16_.refs_9_), channel_id=1, source_target_pairs={{0,2},{1,3},{2,0},{3,1},{4,6},{5,7},{6,4},{7,5},{8,10},{9,11},{10,... | collective-permute-start | bytes 2015240 | tf_op jit(solution)/shard_map/ppermute | solution.py:31
  23.2 22.1 %collective-permute-start.7 = (bf16[2560,128]{1,0:T(8,128)(2,1)}, bf16[2560,128]{1,0:T(8,128)(2,1)S(1)}, u32[]{:S(2)}, u32[]{:S(2)}) collective-permute-start(bf16[2560,128]{1,0:T(8,128)(2,1)} %get-tuple-element.34.refs_8_.refs_12_.refs_9_.refs_16_), channel_id=1, source_target_pairs={{0,1},{1,0},{2,3},{3,2},{4,5},{5,4},{6,7},{7,6},{8,9},{9,8},{10,11... | collective-permute-start | bytes 1966088 | tf_op jit(solution)/shard_map/ppermute | solution.py:31
  25.5 37.6 %collective-permute-start.6 = (bf16[2560,128]{1,0:T(8,128)(2,1)}, bf16[2560,128]{1,0:T(8,128)(2,1)S(1)}, u32[]{:S(2)}, u32[]{:S(2)}) collective-permute-start(bf16[2560,128]{1,0:T(8,128)(2,1)} %get-tuple-element.34.refs_8_.refs_12_.refs_9_.refs_16_), channel_id=1, source_target_pairs={{0,14},{1,15},{2,4},{3,5},{4,2},{5,3},{6,8},{7,9},{8,6},{9,7},{10,... | collective-permute-start | bytes 1966088 | tf_op jit(solution)/shard_map/ppermute | solution.py:49
  31.1 14.3 %collective-permute-start.3 = (bf16[4,512,128]{2,1,0:T(8,128)(2,1)S(1)}, bf16[4,512,128]{2,1,0:T(8,128)(2,1)}, u32[]{:S(2)}, u32[]{:S(2)}) collective-permute-start(bf16[4,512,128]{2,1,0:T(8,128)(2,1)S(1)} %pad_maximum_fusion.refs_2_.refs_1_), channel_id=1, source_target_pairs={{0,5},{2,7},{4,9},{5,0},{6,11},{7,2},{8,13},{9,4},{10,15},{11,6},{... | collective-permute-start | bytes 1572872 | tf_op jit(solution)/shard_map/ppermute | solution.py:38
  32.6 12.8 %collective-permute-start.2 = (bf16[4,512,128]{2,1,0:T(8,128)(2,1)S(1)}, bf16[4,512,128]{2,1,0:T(8,128)(2,1)}, u32[]{:S(2)}, u32[]{:S(2)}) collective-permute-start(bf16[4,512,128]{2,1,0:T(8,128)(2,1)S(1)} %pad_maximum_fusion.refs_2_.refs_1_), channel_id=1, source_target_pairs={{0,3},{2,5},{3,0},{4,7},{5,2},{6,9},{7,4},{8,11},{9,6},{10,13},{11... | collective-permute-start | bytes 1572872 | tf_op jit(solution)/shard_map/ppermute | solution.py:38
  34.2 33.2 %copy-start = (bf16[2624,128]{1,0:T(8,128)(2,1)S(1)}, bf16[2624,128]{1,0:T(8,128)(2,1)}, u32[]{:S(2)}) copy-start(bf16[2624,128]{1,0:T(8,128)(2,1)} %get-tuple-element.32.refs_8_.refs_12_.refs_16_.refs_9_) | copy-start | bytes 2015236
  34.2 33.2 %copy-start.2 = (f32[2,2,512]{2,1,0:T(2,128)S(1)}, f32[2,2,512]{2,1,0:T(2,128)}, u32[]{:S(2)}) copy-start(f32[2,2,512]{2,1,0:T(2,128)} %refs_6_.3) | copy-start | bytes 24580
  34.2 33.2 %copy-start.4 = (bf16[2,512,512]{2,1,0:T(8,128)(2,1)S(1)}, bf16[2,512,512]{2,1,0:T(8,128)(2,1)}, u32[]{:S(2)}) copy-start(bf16[2,512,512]{2,1,0:T(8,128)(2,1)} %param.17) | copy-start | bytes 3145732
  63.0 4.3 %collective-permute-start.8 = (bf16[2624,128]{1,0:T(8,128)(2,1)S(1)}, bf16[2624,128]{1,0:T(8,128)(2,1)S(1)}, u32[]{:S(2)}, u32[]{:S(2)}) collective-permute-start(bf16[2624,128]{1,0:T(8,128)(2,1)S(1)} %collective-permute-done.4.refs_10_.refs_14_.refs_18_.refs_11_), channel_id=1, source_target_pairs={{0,1},{1,0},{2,3},{3,2},{4,5},{5,4},{6,7},{7,6},{8,9},{9,8},{10,11... | collective-permute-start | bytes 2015240 | tf_op jit(solution)/shard_map/ppermute | solution.py:31
  71.5 9.8 %copy-start.3 = (f32[2,512]{1,0:T(2,128)S(1)}, f32[2,512]{1,0:T(2,128)}, u32[]{:S(2)}) copy-start(f32[2,512]{1,0:T(2,128)} %refs_7_.3) | copy-start | bytes 12292
  73.1 8.2 %collective-permute-start.9 = (bf16[512,512]{1,0:T(8,128)(2,1)S(1)}, bf16[512,512]{1,0:T(8,128)(2,1)S(1)}, u32[]{:S(2)}, u32[]{:S(2)}) collective-permute-start(bf16[512,512]{1,0:T(8,128)(2,1)S(1)} %far0.1.refs_2_), channel_id=1, source_target_pairs={{0,1},{1,0},{2,3},{3,2},{4,5},{5,4},{6,7},{7,6},{8,9},{9,8},{10,11... | collective-permute-start | bytes 1572872 | tf_op jit(solution)/shard_map/ppermute | solution.py:31
  79.4 5.3 %collective-permute-start.12 = (bf16[2560,128]{1,0:T(8,128)(2,1)S(1)}, bf16[2560,128]{1,0:T(8,128)(2,1)S(1)}, u32[]{:S(2)}, u32[]{:S(2)}) collective-permute-start(bf16[2560,128]{1,0:T(8,128)(2,1)S(1)} %collective-permute-done.6.refs_10_.refs_14_.refs_11_.refs_18_), channel_id=1, source_target_pairs={{0,1},{1,0},{2,3},{3,2},{4,5},{5,4},{6,7},{7,6},{8,9},{9,8},{10,11... | collective-permute-start | bytes 1966088 | tf_op jit(solution)/shard_map/ppermute | solution.py:31
  81.3 3.3 %copy-start.1 = (bf16[2560,128]{1,0:T(8,128)(2,1)S(1)}, bf16[2560,128]{1,0:T(8,128)(2,1)}, u32[]{:S(2)}) copy-start(bf16[2560,128]{1,0:T(8,128)(2,1)} %get-tuple-element.34.refs_8_.refs_12_.refs_9_.refs_16_) | copy-start | bytes 1966084
  83.3 1.4 %collective-permute-start.11 = (bf16[4,512,128]{2,1,0:T(8,128)(2,1)S(1)}, bf16[4,512,128]{2,1,0:T(8,128)(2,1)S(1)}, u32[]{:S(2)}, u32[]{:S(2)}) collective-permute-start(bf16[4,512,128]{2,1,0:T(8,128)(2,1)S(1)} %node0.1.refs_2_.refs_1_), channel_id=1, source_target_pairs={{0,3},{2,5},{3,0},{4,7},{5,2},{6,9},{7,4},{8,11},{9,6},{10,13},{11... | collective-permute-start | bytes 1572872 | tf_op jit(solution)/shard_map/ppermute | solution.py:38
  84.0 4.4 %collective-permute-start.10 = (bf16[4,512,128]{2,1,0:T(8,128)(2,1)S(1)}, bf16[4,512,128]{2,1,0:T(8,128)(2,1)S(1)}, u32[]{:S(2)}, u32[]{:S(2)}) collective-permute-start(bf16[4,512,128]{2,1,0:T(8,128)(2,1)S(1)} %node0.1.refs_2_.refs_1_), channel_id=1, source_target_pairs={{0,5},{2,7},{4,9},{5,0},{6,11},{7,2},{8,13},{9,4},{10,15},{11,6},{... | collective-permute-start | bytes 1572872 | tf_op jit(solution)/shard_map/ppermute | solution.py:38
  89.4 28.2 %collective-permute-start.13 = (bf16[512,512]{1,0:T(8,128)(2,1)S(1)}, bf16[512,512]{1,0:T(8,128)(2,1)S(1)}, u32[]{:S(2)}, u32[]{:S(2)}) collective-permute-start(bf16[512,512]{1,0:T(8,128)(2,1)S(1)} %far1.1.refs_2_), channel_id=1, source_target_pairs={{0,1},{1,0},{2,3},{3,2},{4,5},{5,4},{6,7},{7,6},{8,9},{9,8},{10,11... | collective-permute-start | bytes 1572872 | tf_op jit(solution)/shard_map/ppermute | solution.py:31
  119.4 6.6 %collective-permute-start.14 = (bf16[512,128]{1,0:T(8,128)(2,1)S(1)}, bf16[512,128]{1,0:T(8,128)(2,1)S(1)}, u32[]{:S(2)}, u32[]{:S(2)}) collective-permute-start(bf16[512,128]{1,0:T(8,128)(2,1)S(1)} %get-tuple-element.58), channel_id=1, source_target_pairs={{0,2},{1,3},{2,0},{3,1},{4,6},{5,7},{6,4},{7,5},{8,10},{9,11},{10,... | collective-permute-start | bytes 393224 | tf_op jit(solution)/shard_map/ppermute | solution.py:31

commit v11 on v7

--- a/solution.py
+++ b/solution.py
@@ -15,7 +15,7 @@
 STRAIGHT = (0, 1, 2, 3)
 FROM_NEXT = (3, 2, 1, 0)
 FROM_BEYOND = (2, 3, 0, 1)
-UNROLL = 4
+UNROLL = 2
 LIST = 32
 VMEM = pl.BlockSpec(memory_space=pltpu.VMEM)
 SMEM = pl.BlockSpec(memory_space=pltpu.SMEM)

time: 120 us -> 123 us (1.025); the launches traced: 119 us -> 120 us
  waiting for transfers between devices: 55.1 us -> 49.6 us
  Pallas kernels: 23.1 us -> 27.5 us
  starting transfers between devices: 40.4 us -> 42.7 us
    pallas_call x9, Pallas kernels: 23.1 us -> 27.5 us  [call(): pl.pallas_call(kernel, out_shape=outs, grid=(1,), in_specs=spaces, out_sp...]
    ppermute x4, waiting for transfers between devices: 35.8 us -> 31.7 us  [swap_with(): lax.ppermute(value, BOTH, [(i, t) for i, t in pairs if 0 <= t < total])]
    ppermute x10, starting transfers between devices: 23.6 us -> 25.8 us  [exchange(): return lax.ppermute(value, BOTH, [(i, i ^ mask) for i in range(total)])]
    ppermute x10, waiting for transfers between devices: 11.4 us -> 10.1 us  [exchange(): return lax.ppermute(value, BOTH, [(i, i ^ mask) for i in range(total)])]
  transfers between devices with their start and end apart: 15 -> 15, of which waited for: 7 -> 8; matrix products, arithmetic and copies ran while one was open for 0% -> 0% of each run, Pallas kernels for 11% -> 13%
where the time goes in v11:
time: 123 us; the launch traced here: 120 us
  waiting for transfers between devices  49.6 us (40%)
  starting transfers between devices  42.7 us (35%)
  Pallas kernels  27.5 us (22%)
    ppermute x4, waiting for transfers between devices, swap_with(): lax.ppermute(value, BOTH, [(i, t) for i, t in pairs if 0 <= t < total])  31.7 us
    pallas_call x9, Pallas kernels, call(): pl.pallas_call(kernel, out_shape=outs, grid=(1,), in_specs=spaces, out_sp...  27.5 us
    ppermute x10, starting transfers between devices, exchange(): return lax.ppermute(value, BOTH, [(i, i ^ mask) for i in range(total)])  25.8 us
    ppermute x10, waiting for transfers between devices, exchange(): return lax.ppermute(value, BOTH, [(i, i ^ mask) for i in range(total)])  10.1 us
    ppermute x1, starting transfers between devices, from_other_side(): return lax.ppermute(value, BOTH, pairs)  9.13 us
    ppermute x1, waiting for transfers between devices, from_other_side(): return lax.ppermute(value, BOTH, pairs)  7.86 us
    ppermute x4, starting transfers between devices, swap_with(): lax.ppermute(value, BOTH, [(i, t) for i, t in pairs if 0 <= t < total])  7.68 us
  transfers between devices with their start and end apart: 15, of which 8 were waited for; matrix products, arithmetic and copies ran while one was open for 0% of the time, Pallas kernels for 13%

profile of v11, /device:TPU:6, one launch (start us, length us, event | category | flops | bytes accessed | tf_op | source)
XLA Modules:
  0.0 120.5 jit_solution(9844481700945446341)
XLA Ops:
  0.0 2.5 %packs.1 = (bf16[2624,128]{1,0:T(8,128)(2,1)}, bf16[2560,128]{1,0:T(8,128)(2,1)}) custom-call(bf16[2,512,128]{2,1,0:T(8,128)(2,1)} %src_ref.2, bf16[2,512,128]{2,1,0:T(8,128)(2,1)} %dst_ref.2, bf16[2,1024,128]{2,1,0:T(8,128)(2,1)} %in_ref.1, bf16[2,512,128]{2,1,0:T(8,128)(2,1)} %out_w_ref.1, f32[2,4,128]{2,1,0:T(4,128)} %vec_ref.1, f32[2,128]{1,0:T(2,128)} %gain_ref.1), custom_call_target="tpu_custom_call" | custom-call | flops 2000000000 | bytes 1048576 | tf_op jit(solution)/shard_map/packs/pallas_call | solution.py:250
  2.5 1.9 %collective-permute-start.2 = (bf16[2624,128]{1,0:T(8,128)(2,1)}, bf16[2624,128]{1,0:T(8,128)(2,1)S(1)}, u32[]{:S(2)}, u32[]{:S(2)}) collective-permute-start(bf16[2624,128]{1,0:T(8,128)(2,1)} %get-tuple-element.32.refs_8_.refs_12_.refs_16_.refs_9_), channel_id=1, source_target_pairs={{0,1},{1,0},{2,3},{3,2},{4,5},{5,4},{6,7},{7,6},{8,9},{9,8},{10,11... | collective-permute-start | bytes 2015240 | tf_op jit(solution)/shard_map/ppermute | solution.py:31
  4.5 4.3 %collective-permute-start.1 = (bf16[2624,128]{1,0:T(8,128)(2,1)}, bf16[2624,128]{1,0:T(8,128)(2,1)S(1)}, u32[]{:S(2)}, u32[]{:S(2)}) collective-permute-start(bf16[2624,128]{1,0:T(8,128)(2,1)} %get-tuple-element.32.refs_8_.refs_12_.refs_16_.refs_9_), channel_id=1, source_target_pairs={{0,2},{1,3},{2,0},{3,1},{4,6},{5,7},{6,4},{7,5},{8,10},{9,11},{10,... | collective-permute-start | bytes 2015240 | tf_op jit(solution)/shard_map/ppermute | solution.py:31
  8.8 2.1 %collective-permute-start.4 = (bf16[2560,128]{1,0:T(8,128)(2,1)}, bf16[2560,128]{1,0:T(8,128)(2,1)S(1)}, u32[]{:S(2)}, u32[]{:S(2)}) collective-permute-start(bf16[2560,128]{1,0:T(8,128)(2,1)} %get-tuple-element.34.refs_8_.refs_12_.refs_9_.refs_16_), channel_id=1, source_target_pairs={{0,1},{1,0},{2,3},{3,2},{4,5},{5,4},{6,7},{7,6},{8,9},{9,8},{10,11... | collective-permute-start | bytes 1966088 | tf_op jit(solution)/shard_map/ppermute | solution.py:31
  10.9 9.1 %collective-permute-start.3 = (bf16[2560,128]{1,0:T(8,128)(2,1)}, bf16[2560,128]{1,0:T(8,128)(2,1)S(1)}, u32[]{:S(2)}, u32[]{:S(2)}) collective-permute-start(bf16[2560,128]{1,0:T(8,128)(2,1)} %get-tuple-element.34.refs_8_.refs_12_.refs_9_.refs_16_), channel_id=1, source_target_pairs={{0,14},{1,15},{2,4},{3,5},{4,2},{5,3},{6,8},{7,9},{8,6},{9,7},{10,... | collective-permute-start | bytes 1966088 | tf_op jit(solution)/shard_map/ppermute | solution.py:49
  20.1 1.9 %collective-permute-start = (bf16[512,128]{1,0:T(8,128)(2,1)S(1)}, bf16[512,128]{1,0:T(8,128)(2,1)S(1)}, u32[]{:S(2)}, u32[]{:S(2)}) collective-permute-start(bf16[512,128]{1,0:T(8,128)(2,1)S(1)} %get-tuple-element.60), channel_id=1, source_target_pairs={{0,2},{1,3},{2,0},{3,1},{4,6},{5,7},{6,4},{7,5},{8,10},{9,11},{10,... | collective-permute-start | bytes 393224 | tf_op jit(solution)/shard_map/ppermute | solution.py:31
  22.2 2.2 %one_hots.1 = (bf16[25,128,256]{2,1,0:T(8,128)(2,1)S(1)}, bf16[25,128,128]{2,1,0:T(8,128)(2,1)S(1)}, f32[512,128]{1,0:T(8,128)S(1)}, s32[4,32]{1,0:T(4,128)S(1)}) custom-call(s32[5]{0:T(128)S(1)} %stack.30.place_ref.refs_0_, s32[8,6]{1,0:T(8,128)S(1)} %copy-done.5, s32[8,6]{1,0:T(8,128)S(1)} %copy-done.6, s32[8,6,128]{2,1,0:T(8,128)S(1)} %copy.15.src_ref, ...), custom_call_target="tpu_custom_call" | custom-call | flops 3000000000 | bytes 1048576 | tf_op jit(solution)/shard_map/one_hots/pallas_call | solution.py:250
  24.5 3.0 %collective-permute-done = bf16[512,128]{1,0:T(8,128)(2,1)S(1)} collective-permute-done((bf16[512,128]{1,0:T(8,128)(2,1)S(1)}, bf16[512,128]{1,0:T(8,128)(2,1)S(1)}, u32[]{:S(2)}, u32[]{:S(2)}) %collective-permute-start) | collective-permute-done | bytes 131104 | tf_op jit(solution)/shard_map/ppermute | solution.py:31
  27.6 7.9 %collective-permute-done.3.refs_10_.refs_14_.refs_11_.refs_18_ = bf16[2560,128]{1,0:T(8,128)(2,1)S(1)} collective-permute-done((bf16[2560,128]{1,0:T(8,128)(2,1)}, bf16[2560,128]{1,0:T(8,128)(2,1)S(1)}, u32[]{:S(2)}, u32[]{:S(2)}) %collective-permute-start.3) | collective-permute-done | bytes 655392 | tf_op jit(solution)/shard_map/ppermute | solution.py:49
  35.4 1.9 %collective-permute-start.5 = (bf16[2,512,128]{2,1,0:T(8,128)(2,1)S(1)}, bf16[2,512,128]{2,1,0:T(8,128)(2,1)S(1)}, u32[]{:S(2)}, u32[]{:S(2)}) collective-permute-start(bf16[2,512,128]{2,1,0:T(8,128)(2,1)S(1)} %pad_maximum_fusion), channel_id=1, source_target_pairs={{0,1},{1,0},{2,3},{3,2},{4,5},{5,4},{6,7},{7,6},{8,9},{9,8},{10,11... | collective-permute-start | bytes 786440 | tf_op jit(solution)/shard_map/ppermute | solution.py:31
  37.4 1.5 %collective-permute-done.5 = bf16[2,512,128]{2,1,0:T(8,128)(2,1)S(1)} collective-permute-done((bf16[2,512,128]{2,1,0:T(8,128)(2,1)S(1)}, bf16[2,512,128]{2,1,0:T(8,128)(2,1)S(1)}, u32[]{:S(2)}, u32[]{:S(2)}) %collective-permute-start.5) | collective-permute-done | bytes 262176 | tf_op jit(solution)/shard_map/ppermute | solution.py:31
  38.9 2.0 %collective-permute-start.8 = (bf16[2624,128]{1,0:T(8,128)(2,1)S(1)}, bf16[2624,128]{1,0:T(8,128)(2,1)S(1)}, u32[]{:S(2)}, u32[]{:S(2)}) collective-permute-start(bf16[2624,128]{1,0:T(8,128)(2,1)S(1)} %collective-permute-done.1.refs_10_.refs_14_.refs_18_.refs_11_), channel_id=1, source_target_pairs={{0,1},{1,0},{2,3},{3,2},{4,5},{5,4},{6,7},{7,6},{8,9},{9,8},{10,11... | collective-permute-start | bytes 2015240 | tf_op jit(solution)/shard_map/ppermute | solution.py:31
  40.9 1.9 %collective-permute-start.7 = (bf16[4,512,128]{2,1,0:T(8,128)(2,1)S(1)}, bf16[4,512,128]{2,1,0:T(8,128)(2,1)S(1)}, u32[]{:S(2)}, u32[]{:S(2)}) collective-permute-start(bf16[4,512,128]{2,1,0:T(8,128)(2,1)S(1)} %constant_dynamic-update-slice_fusion.refs_2_.refs_1_), channel_id=1, source_target_pairs={{0,3},{2,5},{3,0},{4,7},{5,2},{6,9},{7,4},{8,11},{9,6},{10,13},{11... | collective-permute-start | bytes 1572872 | tf_op jit(solution)/shard_map/ppermute | solution.py:38
  42.9 1.9 %collective-permute-start.6 = (bf16[4,512,128]{2,1,0:T(8,128)(2,1)S(1)}, bf16[4,512,128]{2,1,0:T(8,128)(2,1)S(1)}, u32[]{:S(2)}, u32[]{:S(2)}) collective-permute-start(bf16[4,512,128]{2,1,0:T(8,128)(2,1)S(1)} %constant_dynamic-update-slice_fusion.refs_2_.refs_1_), channel_id=1, source_target_pairs={{0,5},{2,7},{4,9},{5,0},{6,11},{7,2},{8,13},{9,4},{10,15},{11,6},{... | collective-permute-start | bytes 1572872 | tf_op jit(solution)/shard_map/ppermute | solution.py:38
  44.8 17.9 %collective-permute-done.7.refs_3_ = bf16[4,512,128]{2,1,0:T(8,128)(2,1)S(1)} collective-permute-done((bf16[4,512,128]{2,1,0:T(8,128)(2,1)S(1)}, bf16[4,512,128]{2,1,0:T(8,128)(2,1)S(1)}, u32[]{:S(2)}, u32[]{:S(2)}) %collective-permute-start.7) | collective-permute-done | bytes 524320 | tf_op jit(solution)/shard_map/ppermute | solution.py:38
  62.7 5.5 %near0.1 = (f32[512,512]{1,0:T(8,128)S(1)}, bf16[512,512]{1,0:T(8,128)(2,1)S(1)}, f32[4,16,128]{2,1,0:T(8,128)S(1)}) custom-call(s32[5]{0:T(128)S(1)} %stack.30.place_ref.refs_0_, s32[4,32]{1,0:T(4,128)S(1)} %get-tuple-element.38.refs_1_, bf16[4,512,128]{2,1,0:T(8,128)(2,1)S(1)} %constant_dynamic-update-slice_fusion.refs_2_.refs_1_, ...), custom_call_target="tpu_custom_call" | custom-call | flops 5000000000 | bytes 1048576 | tf_op jit(solution)/shard_map/near0/pallas_call | solution.py:250
  68.2 3.4 %far0.1.refs_2_ = bf16[512,512]{1,0:T(8,128)(2,1)S(1)} custom-call(s32[5]{0:T(128)S(1)} %stack.30.place_ref.refs_0_, s32[4,32]{1,0:T(4,128)S(1)} %get-tuple-element.38.refs_1_, bf16[4,512,128]{2,1,0:T(8,128)(2,1)S(1)} %collective-permute-done.6.refs_2_, bf16[8,128,512]{2,1,0:T(8,128)(2,1)S(1)} %bitcast.11, f32[2,2,512]{2,1,0:T(2,128)S(1)} %copy-done.2, ...), custom_call_target="tpu_custom_call" | custom-call | flops 3000000000 | bytes 1048576 | tf_op jit(solution)/shard_map/far0/pallas_call | solution.py:250
  71.7 1.9 %collective-permute-start.9 = (bf16[512,512]{1,0:T(8,128)(2,1)S(1)}, bf16[512,512]{1,0:T(8,128)(2,1)S(1)}, u32[]{:S(2)}, u32[]{:S(2)}) collective-permute-start(bf16[512,512]{1,0:T(8,128)(2,1)S(1)} %far0.1.refs_2_), channel_id=1, source_target_pairs={{0,1},{1,0},{2,3},{3,2},{4,5},{5,4},{6,7},{7,6},{8,9},{9,8},{10,11... | collective-permute-start | bytes 1572872 | tf_op jit(solution)/shard_map/ppermute | solution.py:31
  73.6 2.4 %collective-permute-start.12 = (bf16[2560,128]{1,0:T(8,128)(2,1)S(1)}, bf16[2560,128]{1,0:T(8,128)(2,1)S(1)}, u32[]{:S(2)}, u32[]{:S(2)}) collective-permute-start(bf16[2560,128]{1,0:T(8,128)(2,1)S(1)} %collective-permute-done.3.refs_10_.refs_14_.refs_11_.refs_18_), channel_id=1, source_target_pairs={{0,1},{1,0},{2,3},{3,2},{4,5},{5,4},{6,7},{7,6},{8,9},{9,8},{10,11... | collective-permute-start | bytes 1966088 | tf_op jit(solution)/shard_map/ppermute | solution.py:31
  76.0 1.9 %node0.1.refs_2_.refs_1_ = bf16[4,512,128]{2,1,0:T(8,128)(2,1)S(1)} custom-call(s32[5]{0:T(128)S(1)} %stack.30.place_ref.refs_0_, bf16[4,512,128]{2,1,0:T(8,128)(2,1)S(1)} %constant_dynamic-update-slice_fusion.refs_2_.refs_1_, bf16[512,512]{1,0:T(8,128)(2,1)S(1)} %far0.1.refs_2_, bf16[512,512]{1,0:T(8,128)(2,1)S(1)} %collective-permute-done.9.refs_3_, ...), custom_call_target="tpu_custom_call" | custom-call | flops 2000000000 | bytes 1048576 | tf_op jit(solution)/shard_map/node0/pallas_call | solution.py:250
  77.9 1.9 %collective-permute-start.11 = (bf16[4,512,128]{2,1,0:T(8,128)(2,1)S(1)}, bf16[4,512,128]{2,1,0:T(8,128)(2,1)S(1)}, u32[]{:S(2)}, u32[]{:S(2)}) collective-permute-start(bf16[4,512,128]{2,1,0:T(8,128)(2,1)S(1)} %node0.1.refs_2_.refs_1_), channel_id=1, source_target_pairs={{0,3},{2,5},{3,0},{4,7},{5,2},{6,9},{7,4},{8,11},{9,6},{10,13},{11... | collective-permute-start | bytes 1572872 | tf_op jit(solution)/shard_map/ppermute | solution.py:38
  79.9 1.9 %collective-permute-start.10 = (bf16[4,512,128]{2,1,0:T(8,128)(2,1)S(1)}, bf16[4,512,128]{2,1,0:T(8,128)(2,1)S(1)}, u32[]{:S(2)}, u32[]{:S(2)}) collective-permute-start(bf16[4,512,128]{2,1,0:T(8,128)(2,1)S(1)} %node0.1.refs_2_.refs_1_), channel_id=1, source_target_pairs={{0,5},{2,7},{4,9},{5,0},{6,11},{7,2},{8,13},{9,4},{10,15},{11,6},{... | collective-permute-start | bytes 1572872 | tf_op jit(solution)/shard_map/ppermute | solution.py:38
  81.8 6.6 %collective-permute-done.11.refs_3_ = bf16[4,512,128]{2,1,0:T(8,128)(2,1)S(1)} collective-permute-done((bf16[4,512,128]{2,1,0:T(8,128)(2,1)S(1)}, bf16[4,512,128]{2,1,0:T(8,128)(2,1)S(1)}, u32[]{:S(2)}, u32[]{:S(2)}) %collective-permute-start.11) | collective-permute-done | bytes 524320 | tf_op jit(solution)/shard_map/ppermute | solution.py:38
  88.4 5.5 %near1.1 = (f32[512,512]{1,0:T(8,128)S(1)}, bf16[512,512]{1,0:T(8,128)(2,1)S(1)}) custom-call(s32[5]{0:T(128)S(1)} %stack.30.place_ref.refs_0_, s32[4,32]{1,0:T(4,128)S(1)} %get-tuple-element.38.refs_1_, bf16[4,512,128]{2,1,0:T(8,128)(2,1)S(1)} %node0.1.refs_2_.refs_1_, bf16[4,512,128]{2,1,0:T(8,128)(2,1)S(1)} %collective-permute-done.11.refs_3_, ...), custom_call_target="tpu_custom_call" | custom-call | flops 5000000000 | bytes 1048576 | tf_op jit(solution)/shard_map/near1/pallas_call | solution.py:250
  93.9 7.2 %collective-permute-done.10.refs_2_ = bf16[4,512,128]{2,1,0:T(8,128)(2,1)S(1)} collective-permute-done((bf16[4,512,128]{2,1,0:T(8,128)(2,1)S(1)}, bf16[4,512,128]{2,1,0:T(8,128)(2,1)S(1)}, u32[]{:S(2)}, u32[]{:S(2)}) %collective-permute-start.10) | collective-permute-done | bytes 524320 | tf_op jit(solution)/shard_map/ppermute | solution.py:38
  101.1 3.4 %far1.1.refs_2_ = bf16[512,512]{1,0:T(8,128)(2,1)S(1)} custom-call(s32[5]{0:T(128)S(1)} %stack.30.place_ref.refs_0_, s32[4,32]{1,0:T(4,128)S(1)} %get-tuple-element.38.refs_1_, bf16[4,512,128]{2,1,0:T(8,128)(2,1)S(1)} %collective-permute-done.10.refs_2_, bf16[8,128,512]{2,1,0:T(8,128)(2,1)S(1)} %bitcast.13, f32[2,2,512]{2,1,0:T(2,128)S(1)} %copy-done.2, ...), custom_call_target="tpu_custom_call" | custom-call | flops 3000000000 | bytes 1048576 | tf_op jit(solution)/shard_map/far1/pallas_call | solution.py:250
  104.5 2.6 %collective-permute-start.13 = (bf16[512,512]{1,0:T(8,128)(2,1)S(1)}, bf16[512,512]{1,0:T(8,128)(2,1)S(1)}, u32[]{:S(2)}, u32[]{:S(2)}) collective-permute-start(bf16[512,512]{1,0:T(8,128)(2,1)S(1)} %far1.1.refs_2_), channel_id=1, source_target_pairs={{0,1},{1,0},{2,3},{3,2},{4,5},{5,4},{6,7},{7,6},{8,9},{9,8},{10,11... | collective-permute-start | bytes 1572872 | tf_op jit(solution)/shard_map/ppermute | solution.py:31
  107.2 1.5 %collective-permute-done.13.refs_3_ = bf16[512,512]{1,0:T(8,128)(2,1)S(1)} collective-permute-done((bf16[512,512]{1,0:T(8,128)(2,1)S(1)}, bf16[512,512]{1,0:T(8,128)(2,1)S(1)}, u32[]{:S(2)}, u32[]{:S(2)}) %collective-permute-start.13) | collective-permute-done | bytes 524320 | tf_op jit(solution)/shard_map/ppermute | solution.py:31
  108.7 1.8 %node1.1 = (bf16[512,128]{1,0:T(8,128)(2,1)S(1)}, bf16[512,128]{1,0:T(8,128)(2,1)S(1)}) custom-call(s32[5]{0:T(128)S(1)} %stack.30.place_ref.refs_0_, bf16[4,512,128]{2,1,0:T(8,128)(2,1)S(1)} %node0.1.refs_2_.refs_1_, bf16[512,512]{1,0:T(8,128)(2,1)S(1)} %far1.1.refs_2_, bf16[512,512]{1,0:T(8,128)(2,1)S(1)} %collective-permute-done.13.refs_3_, ...), custom_call_target="tpu_custom_call" | custom-call | flops 2000000000 | bytes 1048576 | tf_op jit(solution)/shard_map/node1/pallas_call | solution.py:250
  110.5 4.7 %collective-permute-start.14 = (bf16[512,128]{1,0:T(8,128)(2,1)S(1)}, bf16[512,128]{1,0:T(8,128)(2,1)S(1)}, u32[]{:S(2)}, u32[]{:S(2)}) collective-permute-start(bf16[512,128]{1,0:T(8,128)(2,1)S(1)} %get-tuple-element.58), channel_id=1, source_target_pairs={{0,2},{1,3},{2,0},{3,1},{4,6},{5,7},{6,4},{7,5},{8,10},{9,11},{10,... | collective-permute-start | bytes 393224 | tf_op jit(solution)/shard_map/ppermute | solution.py:31
  115.2 4.0 %collective-permute-done.14.other_ref = bf16[512,128]{1,0:T(8,128)(2,1)S(1)} collective-permute-done((bf16[512,128]{1,0:T(8,128)(2,1)S(1)}, bf16[512,128]{1,0:T(8,128)(2,1)S(1)}, u32[]{:S(2)}, u32[]{:S(2)}) %collective-permute-start.14) | collective-permute-done | bytes 131104 | tf_op jit(solution)/shard_map/ppermute | solution.py:31
  119.2 1.3 %join.1 = bf16[1024,128]{1,0:T(8,128)(2,1)} custom-call(s32[5]{0:T(128)S(1)} %stack.30.place_ref.refs_0_, bf16[512,128]{1,0:T(8,128)(2,1)S(1)} %get-tuple-element.57.own_ref, bf16[512,128]{1,0:T(8,128)(2,1)S(1)} %collective-permute-done.14.other_ref), custom_call_target="tpu_custom_call" | custom-call | flops 2000000000 | bytes 1048576 | tf_op jit(solution)/shard_map/join/pallas_call | solution.py:250
  (34 shorter events, 0.3 us)
Async XLA Ops:
  0.0 20.1 %copy-start.7 = (bf16[1024,128]{1,0:T(8,128)(2,1)S(1)}, bf16[1024,128]{1,0:T(8,128)(2,1)}, u32[]{:S(2)}) copy-start(bf16[1024,128]{1,0:T(8,128)(2,1)} %param.14) | copy-start | bytes 786436
  0.0 22.0 %copy-start.8 = (s32[8,6,128]{2,0,1:T(8,128)S(1)}, s32[8,6,128]{2,0,1:T(8,128)}, u32[]{:S(2)}) copy-start(s32[8,6,128]{2,0,1:T(8,128)} %param.26) | copy-start | bytes 73732
  0.0 22.1 %copy-start.9 = (s32[8,6,128]{2,0,1:T(8,128)S(1)}, s32[8,6,128]{2,0,1:T(8,128)}, u32[]{:S(2)}) copy-start(s32[8,6,128]{2,0,1:T(8,128)} %param.27) | copy-start | bytes 73732
  0.0 22.2 %copy-start.6 = (s32[8,6]{1,0:T(8,128)S(1)}, s32[8,6]{1,0:T(8,128)}, u32[]{:S(2)}) copy-start(s32[8,6]{1,0:T(8,128)} %count_ref.1) | copy-start | bytes 580
  0.0 22.2 %copy-start.5 = (s32[8,6]{1,0:T(8,128)S(1)}, s32[8,6]{1,0:T(8,128)}, u32[]{:S(2)}) copy-start(s32[8,6]{1,0:T(8,128)} %nbr_ref.1) | copy-start | bytes 580
  2.5 6.2 %collective-permute-start.2 = (bf16[2624,128]{1,0:T(8,128)(2,1)}, bf16[2624,128]{1,0:T(8,128)(2,1)S(1)}, u32[]{:S(2)}, u32[]{:S(2)}) collective-permute-start(bf16[2624,128]{1,0:T(8,128)(2,1)} %get-tuple-element.32.refs_8_.refs_12_.refs_16_.refs_9_), channel_id=1, source_target_pairs={{0,1},{1,0},{2,3},{3,2},{4,5},{5,4},{6,7},{7,6},{8,9},{9,8},{10,11... | collective-permute-start | bytes 2015240 | tf_op jit(solution)/shard_map/ppermute | solution.py:31
  4.5 23.1 %collective-permute-start.1 = (bf16[2624,128]{1,0:T(8,128)(2,1)}, bf16[2624,128]{1,0:T(8,128)(2,1)S(1)}, u32[]{:S(2)}, u32[]{:S(2)}) collective-permute-start(bf16[2624,128]{1,0:T(8,128)(2,1)} %get-tuple-element.32.refs_8_.refs_12_.refs_16_.refs_9_), channel_id=1, source_target_pairs={{0,2},{1,3},{2,0},{3,1},{4,6},{5,7},{6,4},{7,5},{8,10},{9,11},{10,... | collective-permute-start | bytes 2015240 | tf_op jit(solution)/shard_map/ppermute | solution.py:31
  8.8 18.8 %collective-permute-start.4 = (bf16[2560,128]{1,0:T(8,128)(2,1)}, bf16[2560,128]{1,0:T(8,128)(2,1)S(1)}, u32[]{:S(2)}, u32[]{:S(2)}) collective-permute-start(bf16[2560,128]{1,0:T(8,128)(2,1)} %get-tuple-element.34.refs_8_.refs_12_.refs_9_.refs_16_), channel_id=1, source_target_pairs={{0,1},{1,0},{2,3},{3,2},{4,5},{5,4},{6,7},{7,6},{8,9},{9,8},{10,11... | collective-permute-start | bytes 1966088 | tf_op jit(solution)/shard_map/ppermute | solution.py:31
  10.9 24.5 %collective-permute-start.3 = (bf16[2560,128]{1,0:T(8,128)(2,1)}, bf16[2560,128]{1,0:T(8,128)(2,1)S(1)}, u32[]{:S(2)}, u32[]{:S(2)}) collective-permute-start(bf16[2560,128]{1,0:T(8,128)(2,1)} %get-tuple-element.34.refs_8_.refs_12_.refs_9_.refs_16_), channel_id=1, source_target_pairs={{0,14},{1,15},{2,4},{3,5},{4,2},{5,3},{6,8},{7,9},{8,6},{9,7},{10,... | collective-permute-start | bytes 1966088 | tf_op jit(solution)/shard_map/ppermute | solution.py:49
  20.1 7.4 %collective-permute-start = (bf16[512,128]{1,0:T(8,128)(2,1)S(1)}, bf16[512,128]{1,0:T(8,128)(2,1)S(1)}, u32[]{:S(2)}, u32[]{:S(2)}) collective-permute-start(bf16[512,128]{1,0:T(8,128)(2,1)S(1)} %get-tuple-element.60), channel_id=1, source_target_pairs={{0,2},{1,3},{2,0},{3,1},{4,6},{5,7},{6,4},{7,5},{8,10},{9,11},{10,... | collective-permute-start | bytes 393224 | tf_op jit(solution)/shard_map/ppermute | solution.py:31
  22.2 40.5 %copy-start = (bf16[2624,128]{1,0:T(8,128)(2,1)S(1)}, bf16[2624,128]{1,0:T(8,128)(2,1)}, u32[]{:S(2)}) copy-start(bf16[2624,128]{1,0:T(8,128)(2,1)} %get-tuple-element.32.refs_8_.refs_12_.refs_16_.refs_9_) | copy-start | bytes 2015236
  22.2 40.5 %copy-start.2 = (f32[2,2,512]{2,1,0:T(2,128)S(1)}, f32[2,2,512]{2,1,0:T(2,128)}, u32[]{:S(2)}) copy-start(f32[2,2,512]{2,1,0:T(2,128)} %refs_6_.3) | copy-start | bytes 24580
  22.2 40.5 %copy-start.4 = (bf16[2,512,512]{2,1,0:T(8,128)(2,1)S(1)}, bf16[2,512,512]{2,1,0:T(8,128)(2,1)}, u32[]{:S(2)}) copy-start(bf16[2,512,512]{2,1,0:T(8,128)(2,1)} %param.17) | copy-start | bytes 3145732
  35.4 3.4 %collective-permute-start.5 = (bf16[2,512,128]{2,1,0:T(8,128)(2,1)S(1)}, bf16[2,512,128]{2,1,0:T(8,128)(2,1)S(1)}, u32[]{:S(2)}, u32[]{:S(2)}) collective-permute-start(bf16[2,512,128]{2,1,0:T(8,128)(2,1)S(1)} %pad_maximum_fusion), channel_id=1, source_target_pairs={{0,1},{1,0},{2,3},{3,2},{4,5},{5,4},{6,7},{7,6},{8,9},{9,8},{10,11... | collective-permute-start | bytes 786440 | tf_op jit(solution)/shard_map/ppermute | solution.py:31
  38.9 23.8 %collective-permute-start.8 = (bf16[2624,128]{1,0:T(8,128)(2,1)S(1)}, bf16[2624,128]{1,0:T(8,128)(2,1)S(1)}, u32[]{:S(2)}, u32[]{:S(2)}) collective-permute-start(bf16[2624,128]{1,0:T(8,128)(2,1)S(1)} %collective-permute-done.1.refs_10_.refs_14_.refs_18_.refs_11_), channel_id=1, source_target_pairs={{0,1},{1,0},{2,3},{3,2},{4,5},{5,4},{6,7},{7,6},{8,9},{9,8},{10,11... | collective-permute-start | bytes 2015240 | tf_op jit(solution)/shard_map/ppermute | solution.py:31
  40.9 21.7 %collective-permute-start.7 = (bf16[4,512,128]{2,1,0:T(8,128)(2,1)S(1)}, bf16[4,512,128]{2,1,0:T(8,128)(2,1)S(1)}, u32[]{:S(2)}, u32[]{:S(2)}) collective-permute-start(bf16[4,512,128]{2,1,0:T(8,128)(2,1)S(1)} %constant_dynamic-update-slice_fusion.refs_2_.refs_1_), channel_id=1, source_target_pairs={{0,3},{2,5},{3,0},{4,7},{5,2},{6,9},{7,4},{8,11},{9,6},{10,13},{11... | collective-permute-start | bytes 1572872 | tf_op jit(solution)/shard_map/ppermute | solution.py:38
  42.9 25.3 %collective-permute-start.6 = (bf16[4,512,128]{2,1,0:T(8,128)(2,1)S(1)}, bf16[4,512,128]{2,1,0:T(8,128)(2,1)S(1)}, u32[]{:S(2)}, u32[]{:S(2)}) collective-permute-start(bf16[4,512,128]{2,1,0:T(8,128)(2,1)S(1)} %constant_dynamic-update-slice_fusion.refs_2_.refs_1_), channel_id=1, source_target_pairs={{0,5},{2,7},{4,9},{5,0},{6,11},{7,2},{8,13},{9,4},{10,15},{11,6},{... | collective-permute-start | bytes 1572872 | tf_op jit(solution)/shard_map/ppermute | solution.py:38
  68.2 7.8 %copy-start.3 = (f32[2,512]{1,0:T(2,128)S(1)}, f32[2,512]{1,0:T(2,128)}, u32[]{:S(2)}) copy-start(f32[2,512]{1,0:T(2,128)} %refs_7_.3) | copy-start | bytes 12292
  71.7 4.3 %collective-permute-start.9 = (bf16[512,512]{1,0:T(8,128)(2,1)S(1)}, bf16[512,512]{1,0:T(8,128)(2,1)S(1)}, u32[]{:S(2)}, u32[]{:S(2)}) collective-permute-start(bf16[512,512]{1,0:T(8,128)(2,1)S(1)} %far0.1.refs_2_), channel_id=1, source_target_pairs={{0,1},{1,0},{2,3},{3,2},{4,5},{5,4},{6,7},{7,6},{8,9},{9,8},{10,11... | collective-permute-start | bytes 1572872 | tf_op jit(solution)/shard_map/ppermute | solution.py:31
  73.6 8.2 %collective-permute-start.12 = (bf16[2560,128]{1,0:T(8,128)(2,1)S(1)}, bf16[2560,128]{1,0:T(8,128)(2,1)S(1)}, u32[]{:S(2)}, u32[]{:S(2)}) collective-permute-start(bf16[2560,128]{1,0:T(8,128)(2,1)S(1)} %collective-permute-done.3.refs_10_.refs_14_.refs_11_.refs_18_), channel_id=1, source_target_pairs={{0,1},{1,0},{2,3},{3,2},{4,5},{5,4},{6,7},{7,6},{8,9},{9,8},{10,11... | collective-permute-start | bytes 1966088 | tf_op jit(solution)/shard_map/ppermute | solution.py:31
  76.0 12.4 %copy-start.1 = (bf16[2560,128]{1,0:T(8,128)(2,1)S(1)}, bf16[2560,128]{1,0:T(8,128)(2,1)}, u32[]{:S(2)}) copy-start(bf16[2560,128]{1,0:T(8,128)(2,1)} %get-tuple-element.34.refs_8_.refs_12_.refs_9_.refs_16_) | copy-start | bytes 1966084
  77.9 10.5 %collective-permute-start.11 = (bf16[4,512,128]{2,1,0:T(8,128)(2,1)S(1)}, bf16[4,512,128]{2,1,0:T(8,128)(2,1)S(1)}, u32[]{:S(2)}, u32[]{:S(2)}) collective-permute-start(bf16[4,512,128]{2,1,0:T(8,128)(2,1)S(1)} %node0.1.refs_2_.refs_1_), channel_id=1, source_target_pairs={{0,3},{2,5},{3,0},{4,7},{5,2},{6,9},{7,4},{8,11},{9,6},{10,13},{11... | collective-permute-start | bytes 1572872 | tf_op jit(solution)/shard_map/ppermute | solution.py:38
  79.9 21.3 %collective-permute-start.10 = (bf16[4,512,128]{2,1,0:T(8,128)(2,1)S(1)}, bf16[4,512,128]{2,1,0:T(8,128)(2,1)S(1)}, u32[]{:S(2)}, u32[]{:S(2)}) collective-permute-start(bf16[4,512,128]{2,1,0:T(8,128)(2,1)S(1)} %node0.1.refs_2_.refs_1_), channel_id=1, source_target_pairs={{0,5},{2,7},{4,9},{5,0},{6,11},{7,2},{8,13},{9,4},{10,15},{11,6},{... | collective-permute-start | bytes 1572872 | tf_op jit(solution)/shard_map/ppermute | solution.py:38
  104.5 4.1 %collective-permute-start.13 = (bf16[512,512]{1,0:T(8,128)(2,1)S(1)}, bf16[512,512]{1,0:T(8,128)(2,1)S(1)}, u32[]{:S(2)}, u32[]{:S(2)}) collective-permute-start(bf16[512,512]{1,0:T(8,128)(2,1)S(1)} %far1.1.refs_2_), channel_id=1, source_target_pairs={{0,1},{1,0},{2,3},{3,2},{4,5},{5,4},{6,7},{7,6},{8,9},{9,8},{10,11... | collective-permute-start | bytes 1572872 | tf_op jit(solution)/shard_map/ppermute | solution.py:31
  110.5 8.7 %collective-permute-start.14 = (bf16[512,128]{1,0:T(8,128)(2,1)S(1)}, bf16[512,128]{1,0:T(8,128)(2,1)S(1)}, u32[]{:S(2)}, u32[]{:S(2)}) collective-permute-start(bf16[512,128]{1,0:T(8,128)(2,1)S(1)} %get-tuple-element.58), channel_id=1, source_target_pairs={{0,2},{1,3},{2,0},{3,1},{4,6},{5,7},{6,4},{7,5},{8,10},{9,11},{10,... | collective-permute-start | bytes 393224 | tf_op jit(solution)/shard_map/ppermute | solution.py:31
